TPU v7x, 256 devices: a whole 4x4x8 slice. The times are simulated.
256 devices in a mesh: replica: 8 (over y, core), fsdp: 32 (over z, x).
Axes of the slice: x: 4, y: 4, z: 8, core: 2. Of those that a mesh axis runs over, the one named last changes fastest.
Arguments:
- grads: bfloat16 [8, 4, 1024, 8192], P('replica', None, 'fsdp'), may hold values from -32 to 32
- left_root: bfloat16 [64, 1024, 1024], P('fsdp'), may hold values from -1 to 2.5
- right_root: bfloat16 [64, 1024, 1024], P('fsdp'), may hold values from -1 to 2.5
- block_slot: int32 [32], replicated, may hold values from 0 to 63, as said below
Outputs:
- updates: bfloat16 [4, 1024, 8192], P(None, 'fsdp')
Inputs may be any that keep to these rules, and one draw needn't show every extreme that they name: block_slot gives the 32 blocks distinct slots; slot q belongs to owner q // 2 of fsdp; some owners hold 2 blocks and as many hold none.
All inputs are finite; a program needn't handle non-finite values.
Results may differ from a plain program's by a relative error of at most 0.02.
Values may be sent and summed in bfloat16 or wider, within the bound.
No kernel may reach another device: no remote copies, remote signals or barrier semaphores. Data moves between devices by JAX's collectives and lax.ppermute only.
A program may use at most 128 MiB of HBM per device.

v0:
```python
import jax
import jax.numpy as jnp
from jax import lax
from jax.sharding import PartitionSpec as P

EPSILON = 1e-06


def owner_table(block_slot, owner_count, slot_count, matrices, col_blocks):
    slot_of = lax.broadcasted_iota(
        jnp.int32, (slot_count, owner_count, 1), 1
    ) * slot_count + lax.broadcasted_iota(jnp.int32, (slot_count, owner_count, 1), 0)
    table = (block_slot[None, None, :] == slot_of).astype(jnp.bfloat16)
    return table.reshape(slot_count, owner_count, matrices, col_blocks)


def graft(block_square, prec_square, preconditioned, entries):
    graft_ratio = jnp.sqrt(block_square / entries + EPSILON) / jnp.sqrt(
        prec_square / entries + EPSILON
    )
    return (preconditioned * graft_ratio[:, None, None]).astype(jnp.bfloat16)


def on_device(grads, left_root, right_root, block_slot):
    owner_count = lax.axis_size("fsdp")
    slot_count = left_root.shape[0]
    left_width = left_root.shape[1]
    block_width = right_root.shape[1]
    gradient = grads[0]
    matrices, row_count, full_width = gradient.shape
    col_blocks = full_width // block_width
    routing = owner_table(block_slot, owner_count, slot_count, matrices, col_blocks)
    entries = left_width * block_width
    summed_grad = lax.psum(gradient.astype(jnp.float32).astype(jnp.bfloat16), "replica")
    summed_grad = summed_grad.reshape(matrices, row_count, col_blocks, block_width)
    outgoing = jnp.einsum(
        "spmj,mrjc->sprc", routing, summed_grad, preferred_element_type=jnp.float32
    ).astype(jnp.bfloat16)
    incoming = lax.all_to_all(outgoing, "fsdp", split_axis=1, concat_axis=1, tiled=True)
    block_whole = incoming.reshape(slot_count, left_width, block_width)
    right_half = jnp.einsum(
        "ski,sic->skc", block_whole, right_root, preferred_element_type=jnp.float32
    ).astype(jnp.bfloat16)
    preconditioned = jnp.einsum(
        "sKk,skc->sKc", left_root, right_half, preferred_element_type=jnp.float32
    )
    block_square = jnp.sum(jnp.square(block_whole.astype(jnp.float32)), axis=(1, 2))
    prec_square = jnp.sum(jnp.square(preconditioned), axis=(1, 2))
    grafted = graft(block_square, prec_square, preconditioned, entries)
    returned = lax.all_to_all(
        grafted.reshape(slot_count, owner_count, row_count, block_width),
        "fsdp",
        split_axis=1,
        concat_axis=1,
        tiled=True,
    )
    placed = jnp.einsum(
        "spmj,sprc->mrjc", routing, returned, preferred_element_type=jnp.float32
    ).astype(jnp.bfloat16)
    return placed.reshape(matrices, row_count, full_width)


def solution(mesh):
    in_specs = (P("replica", None, "fsdp", None), P("fsdp", None, None), P("fsdp", None, None), P())
    out_specs = P(None, "fsdp", None)
    return jax.shard_map(
        on_device, mesh=mesh, in_specs=in_specs, out_specs=out_specs, check_vma=False
    )
```

profile of v0, /device:TPU:1, one launch (start us, length us, event | category | flops | bytes accessed | tf_op | source)
XLA Modules:
  0.0 338.8 jit_solution(16158470646441013639)
XLA Ops:
  6.5 0.0 all-reduce.2.cloned.1.call-start
  6.5 3.0 copy.30
  9.5 0.0 copy-start.1
  9.5 1.5 copy.27
  11.0 0.0 all-reduce.2.cloned.1.call-update
  11.1 0.0 copy-done.1
  11.1 0.1 eq.16
  11.2 72.8 %all-reduce.2.cloned.1.call-done = bf16[4,32,8,1024]{3,2,0,1:T(8,128)(2,1)} async-done(((bf16[4,32,8,1024]{3,2,0,1:T(8,128)(2,1)}), bf16[4,32,8,1024]{3,2,0,1:T(8,128)(2,1)}) %all-reduce.2.cloned.1.call-update) | async-done | bytes 2097168 | tf_op jit(solution)/shard_map/psum | solution.py:34
  84.0 2.9 bitcast_convert_fusion
  86.9 2.3 copy.16
  89.2 101.4 %all_to_all.10 = bf16[2,32,32,1024]{3,2,0,1:T(8,128)(2,1)S(1)} all-to-all(bf16[2,32,32,1024]{3,2,0,1:T(8,128)(2,1)S(1)} %copy.16), channel_id=1, replica_groups=mesh['replica'=8,'fsdp'=32] {'fsdp'}, dimensions={1} | all-to-all | bytes 8388608 | tf_op jit(solution)/shard_map/all_to_all | solution.py:39
  190.6 0.0 copy-start
  190.6 2.0 copy-done
  192.6 2.4 copy.17
  195.0 14.2 %multiply_reduce_fusion = (f32[2]{0:T(128)S(1)}, f32[2,1024,1024]{1,2,0:T(8,128)}) fusion(bf16[2,1024,1024]{2,1,0:T(8,128)(2,1)} %param.5, bf16[2,1024,1024]{2,1,0:T(8,128)(2,1)} %bitcast.39, bf16[2,1024,1024]{2,1,0:T(8,128)(2,1)} %param.6), kind=kOutput, calls=%fused_computation.2 | convolution fusion | flops 8596226048 | bytes 20971528 | tf_op jit(solution)/shard_map/sKk,skc->sKc/dot_general | solution.py:44
  209.1 3.4 multiply_reduce_fusion.1
  212.5 4.7 %multiply_convert_fusion = bf16[2,1024,1024]{1,2,0:T(8,128)(2,1)S(1)} fusion(f32[2,1024,1024]{1,2,0:T(8,128)} %get-tuple-element.6, f32[2]{0:T(128)S(1)} %rsqrt_multiply_fusion), kind=kLoop, calls=%fused_computation.1 | loop fusion | flops 4194304 | bytes 12582920 | tf_op jit(solution)/shard_map/convert_element_type | solution.py:21
  217.2 6.2 %copy.18 = bf16[2,32,32,1024]{3,0,2,1:T(2,128)(2,1)} copy(bf16[2,32,32,1024]{3,2,1,0:T(8,128)(2,1)S(1)} %bitcast.36) | data formatting | bytes 8388608 | tf_op jit(solution)/shard_map/reshape | solution.py:51
  223.5 98.4 %all_to_all.11 = bf16[2,32,32,1024]{3,0,2,1:T(2,128)(2,1)S(1)} all-to-all(bf16[2,32,32,1024]{3,0,2,1:T(2,128)(2,1)} %copy.18), channel_id=1, replica_groups=mesh['replica'=8,'fsdp'=32] {'fsdp'}, dimensions={1} | all-to-all | bytes 8388608 | tf_op jit(solution)/shard_map/all_to_all | solution.py:50
  321.8 4.3 %fusion.6 = bf16[4,32,8,1024]{3,2,0,1:T(8,128)(2,1)} fusion(bf16[2,32,32,1024,1]{3,0,2,1,4:T(2,128)(2,1)S(1)} %bitcast.38, s32[2,32]{1,0:T(2,128)S(1)} %iota_add_fusion, s32[4,8]{1,0:T(4,128)S(1)} %eq.16), kind=kOutput, calls=%fused_computation.10 | convolution fusion | flops 135268352 | bytes 6291840 | tf_op jit(solution)/shard_map/spmj,sprc->mrjc/dot_general | solution.py:57
  326.2 3.3 reshape.44
  329.5 2.5 copy.20
  (3 shorter events, 0.0 us)
Async XLA Ops:
  6.5 77.4 %all-reduce.2.cloned.1.call-start = ((), (), s32[]{:S(2)}) async-start(), calls=%async_computation.2 | async-start | bytes 4194304 | tf_op jit(solution)/shard_map/psum | solution.py:34
  9.5 1.5 copy-start.1
  190.6 2.0 copy-start
Sparse Core Ops, SparseCore 0:
  11.2 72.7 all-reduce.1
where the time goes:
time: 346 us; the launch traced here: 339 us
  blocking collectives  200 us (58%)
  waiting for transfers between devices  72.8 us (21%)
  local copies, waits for them, and re-layouts  23.3 us (7%)
  matrix products  21.4 us (6%)
  between operations  13.4 us (4%)
  other arithmetic  8.1 us (2%)
    all_to_all x1, blocking collectives, on_device(): lax.all_to_all(outgoing, 'fsdp', split_axis=1, concat_axis=1, tiled=True)  101 us
    all_to_all x1, blocking collectives, on_device(): lax.all_to_all(grafted.reshape(slot_count, owner_count, row_count, block_...  98.4 us
    psum x1, waiting for transfers between devices, on_device(): lax.psum(gradient.astype(jnp.float32).astype(jnp.bfloat16), 'replica')  72.8 us
    dot_general x1, matrix products, on_device(): jnp.einsum('sKk,skc->sKc', left_root, right_half, preferred_element_type=...  14.2 us
  transfers between devices with their start and end apart: 1, of which 1 were waited for; matrix products, arithmetic and copies ran while one was open for 0% of the time, Pallas kernels for 0%

commit v1 on v0

v1 whole, which is shorter than its diff:
```python
import functools
import jax
import jax.numpy as jnp
from jax import lax
from jax.experimental import pallas as pl
from jax.experimental.pallas import tpu as pltpu
from jax.sharding import PartitionSpec as P

EPSILON = 1e-06
LANES = 128
TERMS = 6
MIB = 1024 * 1024
VMEM_BYTES = 24 * MIB
bf16, f32 = jnp.bfloat16, jnp.float32

SELF, NEAR, FAR, OPPOSITE = range(4)


def masks(core):
    return 0, 1 + 2 * core, 3 - 2 * core, 2


def chip(place, relative):
    return lax.bitwise_xor(place[0] // 2, jnp.int32(masks(lax.rem(place[0], 2))[relative]))


def strip_columns(place, relative, core, j, width, strip):
    index = 2 * chip(place, relative) + core
    return pl.ds(pl.multiple_of(j * width + index * strip, strip), strip)


def together(copies):
    copies = list(copies)
    for copy in copies:
        copy.start()
    for copy in copies:
        copy.wait()


def strip_copies(place, grads_ref, out_ref, arrived, first, kinds, own, sizes):
    core = lax.rem(place[0], 2)
    core = core if own else 1 - core
    cols = sizes["cols"]
    order = (SELF, NEAR, FAR, OPPOSITE) if own else (SELF, FAR, NEAR, OPPOSITE)
    return [
        pltpu.make_async_copy(
            grads_ref.at[0, :, :, strip_columns(place, order[k], core, j, sizes["width"], sizes["strip"])],
            out_ref.at[n, :, j],
            arrived.at[first + n * cols + j],
        )
        for n, k in enumerate(kinds)
        for j in range(cols)
    ]


def send_kernel(place, grads_ref, send_ref, arrived, *, kinds, **sizes):
    together(strip_copies(place, grads_ref, send_ref, arrived, 0, kinds, False, sizes))


def send_and_keep_kernel(place, grads_ref, send_ref, keep_ref, arrived, *, kinds, kept, **sizes):
    together(
        strip_copies(place, grads_ref, send_ref, arrived, 0, kinds, False, sizes)
        + strip_copies(place, grads_ref, keep_ref, arrived, len(kinds) * sizes["cols"], kept, True, sizes)
    )


def pair_sum_kernel(keep_ref, got_ref, *sum_refs, first):
    for n, sum_ref in enumerate(sum_refs):
        sum_ref[...] = (keep_ref[first + n].astype(f32) + got_ref[n].astype(f32)).astype(bf16)


def add_kernel(x_ref, y_ref, out_ref):
    out_ref[...] = (x_ref[...].astype(f32) + y_ref[...].astype(f32)).astype(bf16)


def route_kernel(slot, *refs):
    *terms, out_ref = refs
    slots = out_ref.shape[1]
    cols = terms[0].shape[1]
    out_ref[...] = jnp.zeros_like(out_ref)
    for m in range(terms[0].shape[0]):
        for j in range(cols):
            q = slot[m * cols + j]
            total = sum(term[m, j].astype(f32) for term in terms)
            out_ref[q // slots, lax.rem(q, slots)] = total.astype(bf16)


def left_kernel(place, left_ref, block_ref, *out_refs):
    *half_refs, square_ref, scratch = out_refs
    owners, slots, rows, strip = block_ref.shape
    for s in range(slots):
        block = block_ref[:, s].reshape(owners * rows, strip)
        wide = block.astype(f32)
        square_ref[s] = jnp.broadcast_to(jnp.sum(wide * wide, keepdims=True), square_ref.shape[1:])
        half = jnp.dot(left_ref[s], block, preferred_element_type=f32)
        scratch[s] = half.reshape(scratch.shape[1:])
        for k, half_ref in enumerate(half_refs):
            half_ref[s] = scratch[s, :, chip(place, k)].reshape(half_ref.shape[1:]).astype(bf16)


def split3(x):
    a = x.astype(bf16).astype(f32)
    b = (x - a).astype(bf16).astype(f32)
    return a, b, x - a - b


def right_kernel(place, *refs):
    own_refs, twin_refs = refs[:4], refs[4:8]
    right_ref, square_ref, back_ref, half_scratch = refs[8:]
    owners, part, wide = back_ref.shape
    slots = right_ref.shape[0]
    width = (wide - LANES) // slots
    strip = own_refs[0].shape[2]
    core = lax.rem(place[0], 2)
    lane = lax.broadcasted_iota(jnp.int32, (part, LANES), 1)
    tail = jnp.zeros((part, LANES), f32)
    for s in range(slots):
        for half_refs, c in ((own_refs, core), (twin_refs, 1 - core)):
            for k, half_ref in enumerate(half_refs):
                r = 2 * chip(place, k) + c
                half_scratch[s, :, pl.ds(pl.multiple_of(r * strip, strip), strip)] = half_ref[s]
        columns = pl.ds(pl.multiple_of(core * width, width), width)
        prec = jnp.dot(half_scratch[s], right_ref[s, :, columns], preferred_element_type=f32)
        back_ref[:, :, s * width : (s + 1) * width] = prec.reshape(owners, part, width).astype(bf16)
        prec_square = jnp.broadcast_to(jnp.sum(prec * prec, keepdims=True), (part, LANES))
        for k, term in enumerate(split3(square_ref[s]) + split3(prec_square)):
            tail = jnp.where(lane == TERMS * s + k, term, tail)
    back_ref[:, :, slots * width :] = jnp.broadcast_to(tail[None], (owners, part, LANES)).astype(bf16)


def select_kernel(slot, back_ref, pair_ref):
    mats, count, part, wide = pair_ref.shape
    width = (wide - LANES) // 2
    lane = lax.broadcasted_iota(jnp.int32, (part, LANES), 1)
    for m in range(mats):
        for p in range(count):
            tails = []
            for h in range(2):
                q = slot[2 * (m * count + p) + h]
                s = lax.rem(q, 2)
                columns = pl.ds(pl.multiple_of(s * width, width), width)
                pair_ref[m, p, :, h * width : (h + 1) * width] = back_ref[q // 2, :, columns]
                tail = back_ref[q // 2, :, 2 * width :].astype(f32)
                tails.append(jnp.where(s == h, tail, pltpu.roll(tail, TERMS if h else LANES - TERMS, 1)))
            pair_ref[m, p, :, 2 * width :] = jnp.where(lane < TERMS, tails[0], tails[1]).astype(bf16)


def stack_kernel(*refs):
    *piece_refs, out_ref = refs
    for k, piece_ref in enumerate(piece_refs):
        out_ref[k] = piece_ref[...]


def finish_kernel(place, first_ref, second_ref, twin_first_ref, twin_second_ref, out_ref, ready, written, *, entries):
    _, mats, count, part, wide = first_ref.shape
    width = (wide - LANES) // 2
    lane = lax.broadcasted_iota(jnp.int32, (count, part, LANES), 2)

    def emit(m, own, twin, ratios, core, odd):
        couples = ((SELF, FAR), (OPPOSITE, NEAR)) if core else ((SELF, NEAR), (OPPOSITE, FAR))
        for couple in couples:
            rows = pl.ds(pl.multiple_of(chip(place, couple[0]) // 2 * 2 * part, 2 * part), 2 * part)
            for p in range(count):
                for h in range(2):
                    for pieces, c in ((own, core), (twin, 1 - core)):
                        tiles = [
                            pieces[k][p, :, h * width : (h + 1) * width].astype(f32) * ratios[h][p]
                            for k in (couple[::-1] if odd else couple)
                        ]
                        at = (2 * p + h) * 2 * width + c * width
                        ready[m, rows, pl.ds(at, width)] = jnp.concatenate(tiles, 0).astype(bf16)

    def write(m):
        return pltpu.make_async_copy(ready.at[m], out_ref.at[m], written.at[m])

    @pl.loop(0, mats)
    def _(m):
        own = [ref.at[n, m] for ref in (first_ref, second_ref) for n in range(2)]
        twin = [ref.at[n, m] for n in range(2) for ref in (twin_first_ref, twin_second_ref)]
        tail = sum(ref[:, :, 2 * width :].astype(f32) for ref in own + twin)
        ratios = []
        for h in range(2):
            terms = [
                jnp.sum(jnp.where((lane >= start) & (lane < start + 3), tail, 0.0), axis=2, keepdims=True)
                for start in (TERMS * h, TERMS * h + 3)
            ]
            ratios.append(jnp.sqrt(terms[0] / entries + EPSILON) / jnp.sqrt(terms[1] / entries + EPSILON))
        for core in range(2):
            for odd in range(2):
                here = (lax.rem(place[0], 2) == core) & (lax.rem(place[0] // 2, 2) == odd)
                pl.when(here)(functools.partial(emit, m, own, twin, ratios, core, odd))
        write(m).start()

    for m in range(mats):
        write(m).wait()


def on_device(grads, left_root, right_root, block_slot):
    owners = lax.axis_size("fsdp")
    reps = lax.axis_size("replica")
    slots, height, width = left_root.shape[0], left_root.shape[1], right_root.shape[1]
    _, mats, rows, full = grads.shape
    cols = full // width
    blocks = mats * cols
    strip = width // reps
    part = rows // 4
    shape = jax.ShapeDtypeStruct

    place = lax.axis_index("replica").reshape(1).astype(jnp.int32)
    def twin(x):
        return lax.ppermute(x, "replica", [(i, i ^ 1) for i in range(reps)])

    def exchange(x, relative):
        perm = [(i, i ^ (2 * masks(i % 2)[relative])) for i in range(reps)]
        return lax.ppermute(x, "replica", perm)

    sizes = dict(cols=cols, width=width, strip=strip)
    def strips(*n):
        return shape((*n, mats, cols, rows, strip), bf16)

    def local(kernel, in_specs, out_specs, out_shape, scratch_shapes=()):
        return pl.pallas_call(
            kernel,
            in_specs=in_specs,
            out_specs=out_specs,
            out_shape=out_shape,
            scratch_shapes=scratch_shapes,
            compiler_params=pltpu.CompilerParams(vmem_limit_bytes=VMEM_BYTES),
        )

    smem, vmem = pl.BlockSpec(memory_space=pltpu.SMEM), pl.BlockSpec(memory_space=pltpu.VMEM)
    hbm = pl.BlockSpec(memory_space=pl.ANY)
    in_hbm = pltpu.with_memory_space_constraint(grads, pltpu.HBM)
    ahead, behind = (OPPOSITE, NEAR), (SELF, FAR)
    send = local(
        functools.partial(send_kernel, kinds=ahead, **sizes),
        [smem, hbm],
        vmem,
        strips(2),
        [pltpu.SemaphoreType.DMA((2 * cols,))],
    )(place, in_hbm)
    got = twin(send)
    send, keep = local(
        functools.partial(send_and_keep_kernel, kinds=behind, kept=ahead + behind, **sizes),
        [smem, hbm],
        [vmem] * 2,
        [strips(2), strips(4)],
        [pltpu.SemaphoreType.DMA((6 * cols,))],
    )(place, in_hbm)
    got = (got, twin(send))
    sums = {}
    for n, kinds in enumerate((ahead, behind)):
        add = local(functools.partial(pair_sum_kernel, first=2 * n), [vmem] * 2, [vmem] * 2, [strips()] * 2)
        sums.update(zip(kinds, add(keep, got[n])))

    onward = exchange(sums[OPPOSITE], NEAR)
    direct = exchange(sums[NEAR], NEAR)
    passed = local(add_kernel, [vmem] * 2, vmem, strips())(sums[FAR], onward)
    last = exchange(passed, FAR)

    outgoing = local(route_kernel, [smem] + [vmem] * 3, vmem, shape((owners, slots, rows, strip), bf16))(
        block_slot, sums[SELF], direct, last
    )
    incoming = lax.all_to_all(outgoing, "fsdp", 0, 0, tiled=True)

    half_shape = shape((slots, owners * part, strip), bf16)
    *halves, square = local(
        left_kernel,
        [smem, vmem, vmem],
        [vmem] * 5,
        [half_shape] * 4 + [shape((slots, part, LANES), f32)],
        [pltpu.VMEM((slots, owners, 4, part, strip), f32)],
    )(place, left_root, incoming)
    halves = [halves[SELF]] + [exchange(halves[k], k) for k in (NEAR, FAR, OPPOSITE)]
    handed = [twin(half) for half in halves]
    handed = [handed[SELF], handed[FAR], handed[NEAR], handed[OPPOSITE]]
    wide = width + LANES
    back = local(
        right_kernel,
        [smem] + [vmem] * 10,
        vmem,
        shape((owners, part, wide), bf16),
        [pltpu.VMEM((slots, owners * part, width), bf16)],
    )(place, *halves, *handed, right_root, square)
    back = lax.all_to_all(back, "fsdp", 0, 0, tiled=True)

    count = cols // 2
    piece = (mats, count, part, wide)
    mine = local(select_kernel, [smem, vmem], vmem, shape(piece, bf16))(block_slot, back)
    near = exchange(mine, NEAR)
    first = local(stack_kernel, [vmem] * 2, vmem, shape((2, *piece), bf16))(mine, near)
    second = exchange(first, FAR)
    return local(
        functools.partial(finish_kernel, entries=height * width),
        [smem] + [vmem] * 4,
        pl.BlockSpec(memory_space=pl.ANY),
        shape((mats, rows, full), bf16),
        [pltpu.VMEM((mats, rows, full), bf16), pltpu.SemaphoreType.DMA((mats,))],
    )(place, first, second, twin(first), twin(second))


def solution(mesh):
    in_specs = (P("replica", None, "fsdp", None), P("fsdp", None, None), P("fsdp", None, None), P())
    return jax.shard_map(
        on_device, mesh=mesh, in_specs=in_specs, out_specs=P(None, "fsdp", None), check_vma=False
    )
```

time: 346 us -> 108 us (0.31); the launches traced: 339 us -> 108 us
  blocking collectives: 200 us -> 45.2 us
  waiting for transfers between devices: 72.8 us -> 21 us
  starting transfers between devices: 0.01 us -> 32.4 us
  local copies, waits for them, and re-layouts: 23.3 us -> 0.02 us
  matrix products: 21.4 us -> 0 us
  between operations: 13.4 us -> 0.1 us
  Pallas kernels: 0 us -> 9.34 us
  other arithmetic: 8.1 us -> 0 us
    all_to_all x2, blocking collectives: 200 us -> 45.2 us  [the longest x1 23.5 us: on_device(): incoming = lax.all_to_all(outgoing, 'fsdp', 0, 0, tiled=True)]
    psum x1 -> x0, waiting for transfers between devices: 72.8 us -> none  [on_device(): lax.psum(gradient.astype(jnp.float32).astype(jnp.bfloat16), 'replica')]
    ppermute x0 -> x16, starting transfers between devices: none -> 32.4 us  [the longest x8 22.7 us: twin(): return lax.ppermute(x, 'replica', [(i, i ^ 1) for i in range(reps)])]
    dot_general x3 -> x0, matrix products: 21.4 us -> none  [the longest x1 14.2 us: on_device(): jnp.einsum('sKk,skc->sKc', left_root, right_half, preferred_element_type=...]
    ppermute x0 -> x16, waiting for transfers between devices: none -> 21 us  [the longest x8 18.4 us: exchange(): return lax.ppermute(x, 'replica', perm)]
    reshape x4 -> x0, local copies, waits for them, and re-layouts: 13.5 us -> none  [the longest x1 6.25 us: on_device(): grafted.reshape(slot_count, owner_count, row_count, block_width)]
    pallas_call x0 -> x11, Pallas kernels: none -> 9.34 us  [the longest x1 1.84 us: on_device(): local(functools.partial(finish_kernel, entries=height * width), [smem] +...]
    unnamed x5 -> x6, local copies, waits for them, and re-layouts: 4.98 us -> 0.02 us
  transfers between devices with their start and end apart: 1 -> 16, of which waited for: 1 -> 7; matrix products, arithmetic and copies ran while one was open for 0% -> 0% of each run, Pallas kernels for 0% -> 2%
where the time goes in v1:
time: 108 us
  blocking collectives  45.2 us (42%)
  starting transfers between devices  32.4 us (30%)
  waiting for transfers between devices  21 us (19%)
  Pallas kernels  9.34 us (9%)
    all_to_all x1, blocking collectives, on_device(): incoming = lax.all_to_all(outgoing, 'fsdp', 0, 0, tiled=True)  23.5 us
    ppermute x8, starting transfers between devices, twin(): return lax.ppermute(x, 'replica', [(i, i ^ 1) for i in range(reps)])  22.7 us
    all_to_all x1, blocking collectives, on_device(): back = lax.all_to_all(back, 'fsdp', 0, 0, tiled=True)  21.8 us
    ppermute x8, waiting for transfers between devices, exchange(): return lax.ppermute(x, 'replica', perm)  18.4 us
    ppermute x8, starting transfers between devices, exchange(): return lax.ppermute(x, 'replica', perm)  9.62 us
    ppermute x8, waiting for transfers between devices, twin(): return lax.ppermute(x, 'replica', [(i, i ^ 1) for i in range(reps)])  2.62 us
  transfers between devices with their start and end apart: 16, of which 7 were waited for; matrix products, arithmetic and copies ran while one was open for 0% of the time, Pallas kernels for 2%

profile of v1, /device:TPU:1, one launch (start us, length us, event | category | flops | bytes accessed | tf_op | source)
XLA Modules:
  0.0 108.0 jit_solution(2915570308641385879)
XLA Ops:
  0.0 1.2 %shard_map.48 = bf16[2,4,8,32,128]{4,3,2,1,0:T(8,128)(2,1)S(1)} custom-call(s32[1]{0:T(128)} %bitcast.place, bf16[1,4,32,8192]{3,2,1,0:T(8,128)(2,1)} %grads_ref.3), custom_call_target="tpu_custom_call" | custom-call | tf_op jit(solution)/shard_map/pallas_call | solution.py:235
  1.2 3.3 %collective-permute-start.1 = (bf16[2,4,8,32,128]{4,3,2,1,0:T(8,128)(2,1)S(1)}, bf16[2,4,8,32,128]{4,3,2,1,0:T(8,128)(2,1)S(1)}, u32[]{:S(2)}, u32[]{:S(2)}) collective-permute-start(bf16[2,4,8,32,128]{4,3,2,1,0:T(8,128)(2,1)S(1)} %shard_map.48), channel_id=1, source_target_pairs={{0,32},{32,0},{64,96},{96,64},{128,160},{160,128},{192,224},{224,1... | collective-permute-start | bytes 1572872 | tf_op jit(solution)/shard_map/ppermute | solution.py:211
  4.5 1.8 %shard_map.46 = (bf16[2,4,8,32,128]{4,3,2,1,0:T(8,128)(2,1)S(1)}, bf16[4,4,8,32,128]{4,3,2,1,0:T(8,128)(2,1)S(1)}) custom-call(s32[1]{0:T(128)} %bitcast.place, bf16[1,4,32,8192]{3,2,1,0:T(8,128)(2,1)} %grads_ref.3), custom_call_target="tpu_custom_call" | custom-call | tf_op jit(solution)/shard_map/pallas_call | solution.py:243
  6.7 1.3 %collective-permute-start.3 = (bf16[4,8,32,128]{3,2,1,0:T(8,128)(2,1)S(1)}, bf16[4,8,32,128]{3,2,1,0:T(8,128)(2,1)S(1)}, u32[]{:S(2)}, u32[]{:S(2)}) collective-permute-start(bf16[4,8,32,128]{3,2,1,0:T(8,128)(2,1)S(1)} %get-tuple-element.21), channel_id=1, source_target_pairs={{0,64},{32,224},{64,0},{96,160},{128,192},{160,96},{192,128},{224,... | collective-permute-start | bytes 786440 | tf_op jit(solution)/shard_map/ppermute | solution.py:215
  8.0 1.5 %collective-permute-start.2 = (bf16[4,8,32,128]{3,2,1,0:T(8,128)(2,1)S(1)}, bf16[4,8,32,128]{3,2,1,0:T(8,128)(2,1)S(1)}, u32[]{:S(2)}, u32[]{:S(2)}) collective-permute-start(bf16[4,8,32,128]{3,2,1,0:T(8,128)(2,1)S(1)} %get-tuple-element.19), channel_id=1, source_target_pairs={{0,64},{32,224},{64,0},{96,160},{128,192},{160,96},{192,128},{224,... | collective-permute-start | bytes 786440 | tf_op jit(solution)/shard_map/ppermute | solution.py:215
  9.6 3.6 %collective-permute-done.3.y_ref = bf16[4,8,32,128]{3,2,1,0:T(8,128)(2,1)S(1)} collective-permute-done((bf16[4,8,32,128]{3,2,1,0:T(8,128)(2,1)S(1)}, bf16[4,8,32,128]{3,2,1,0:T(8,128)(2,1)S(1)}, u32[]{:S(2)}, u32[]{:S(2)}) %collective-permute-start.3) | collective-permute-done | bytes 262176 | tf_op jit(solution)/shard_map/ppermute | solution.py:215
  13.4 2.6 %collective-permute-done.2.refs_1_ = bf16[4,8,32,128]{3,2,1,0:T(8,128)(2,1)S(1)} collective-permute-done((bf16[4,8,32,128]{3,2,1,0:T(8,128)(2,1)S(1)}, bf16[4,8,32,128]{3,2,1,0:T(8,128)(2,1)S(1)}, u32[]{:S(2)}, u32[]{:S(2)}) %collective-permute-start.2) | collective-permute-done | bytes 262176 | tf_op jit(solution)/shard_map/ppermute | solution.py:215
  16.0 2.9 %collective-permute-done.4.refs_2_ = bf16[4,8,32,128]{3,2,1,0:T(8,128)(2,1)S(1)} collective-permute-done((bf16[4,8,32,128]{3,2,1,0:T(8,128)(2,1)S(1)}, bf16[4,8,32,128]{3,2,1,0:T(8,128)(2,1)S(1)}, u32[]{:S(2)}, u32[]{:S(2)}) %collective-permute-start.4) | collective-permute-done | bytes 262176 | tf_op jit(solution)/shard_map/ppermute | solution.py:215
  19.7 23.5 %all_to_all.10.block_ref = bf16[32,2,32,128]{3,2,1,0:T(8,128)(2,1)S(1)} all-to-all(bf16[32,2,32,128]{3,2,1,0:T(8,128)(2,1)S(1)} %shard_map.51), channel_id=1, replica_groups=mesh['replica'=8,'fsdp'=32] {'fsdp'}, dimensions={0} | all-to-all | bytes 1048576 | tf_op jit(solution)/shard_map/all_to_all | solution.py:264
  43.1 1.4 %shard_map.52 = (bf16[2,256,128]{2,1,0:T(8,128)(2,1)S(1)}, bf16[2,256,128]{2,1,0:T(8,128)(2,1)S(1)}, bf16[2,256,128]{2,1,0:T(8,128)(2,1)S(1)}, bf16[2,256,128]{2,1,0:T(8,128)(2,1)S(1)}, f32[2,8,128]{2,1,0:T(8,128)S(1)}) custom-call(s32[1]{0:T(128)} %bitcast.place, bf16[2,1024,1024]{2,1,0:T(8,128)(2,1)S(1)} %copy-done, ...), custom_call_target="tpu_custom_call" | custom-call | tf_op jit(solution)/shard_map/pallas_call | solution.py:267
  44.6 2.6 %collective-permute-start.5 = (bf16[2,256,128]{2,1,0:T(8,128)(2,1)S(1)}, bf16[2,256,128]{2,1,0:T(8,128)(2,1)S(1)}, u32[]{:S(2)}, u32[]{:S(2)}) collective-permute-start(bf16[2,256,128]{2,1,0:T(8,128)(2,1)S(1)} %get-tuple-element.23), channel_id=1, source_target_pairs={{0,64},{32,224},{64,0},{96,160},{128,192},{160,96},{192,128},{224,... | collective-permute-start | bytes 393224 | tf_op jit(solution)/shard_map/ppermute | solution.py:215
  47.2 1.3 %collective-permute-start.6 = (bf16[2,256,128]{2,1,0:T(8,128)(2,1)S(1)}, bf16[2,256,128]{2,1,0:T(8,128)(2,1)S(1)}, u32[]{:S(2)}, u32[]{:S(2)}) collective-permute-start(bf16[2,256,128]{2,1,0:T(8,128)(2,1)S(1)} %get-tuple-element.24), channel_id=1, source_target_pairs={{0,192},{32,96},{64,128},{96,32},{128,64},{160,224},{192,0},{224,1... | collective-permute-start | bytes 393224 | tf_op jit(solution)/shard_map/ppermute | solution.py:215
  49.0 5.0 %collective-permute-start.8 = (bf16[2,256,128]{2,1,0:T(8,128)(2,1)S(1)}, bf16[2,256,128]{2,1,0:T(8,128)(2,1)S(1)}, u32[]{:S(2)}, u32[]{:S(2)}) collective-permute-start(bf16[2,256,128]{2,1,0:T(8,128)(2,1)S(1)} %get-tuple-element.22.refs_0_), channel_id=1, source_target_pairs={{0,32},{32,0},{64,96},{96,64},{128,160},{160,128},{192,224},{224,1... | collective-permute-start | bytes 393224 | tf_op jit(solution)/shard_map/ppermute | solution.py:211
  54.5 2.5 %collective-permute-start.9 = (bf16[2,256,128]{2,1,0:T(8,128)(2,1)S(1)}, bf16[2,256,128]{2,1,0:T(8,128)(2,1)S(1)}, u32[]{:S(2)}, u32[]{:S(2)}) collective-permute-start(bf16[2,256,128]{2,1,0:T(8,128)(2,1)S(1)} %collective-permute-done.6.refs_2_), channel_id=1, source_target_pairs={{0,32},{32,0},{64,96},{96,64},{128,160},{160,128},{192,224},{224,1... | collective-permute-start | bytes 393224 | tf_op jit(solution)/shard_map/ppermute | solution.py:211
  57.0 2.5 %collective-permute-start.11 = (bf16[2,256,128]{2,1,0:T(8,128)(2,1)S(1)}, bf16[2,256,128]{2,1,0:T(8,128)(2,1)S(1)}, u32[]{:S(2)}, u32[]{:S(2)}) collective-permute-start(bf16[2,256,128]{2,1,0:T(8,128)(2,1)S(1)} %collective-permute-done.7.refs_3_), channel_id=1, source_target_pairs={{0,32},{32,0},{64,96},{96,64},{128,160},{160,128},{192,224},{224,1... | collective-permute-start | bytes 393224 | tf_op jit(solution)/shard_map/ppermute | solution.py:211
  60.5 1.2 %shard_map.53 = bf16[32,8,1152]{2,1,0:T(8,128)(2,1)S(1)} custom-call(s32[1]{0:T(128)} %bitcast.place, bf16[2,256,128]{2,1,0:T(8,128)(2,1)S(1)} %get-tuple-element.22.refs_0_, bf16[2,256,128]{2,1,0:T(8,128)(2,1)S(1)} %collective-permute-done.5.refs_1_, bf16[2,256,128]{2,1,0:T(8,128)(2,1)S(1)} %collective-permute-done.6.refs_2_, ...), custom_call_target="tpu_custom_call" | custom-call | tf_op jit(solution)/shard_map/pallas_call | solution.py:278
  61.7 21.8 %all_to_all.11.back_ref = bf16[32,8,1152]{2,1,0:T(8,128)(2,1)S(1)} all-to-all(bf16[32,8,1152]{2,1,0:T(8,128)(2,1)S(1)} %shard_map.53), channel_id=1, replica_groups=mesh['replica'=8,'fsdp'=32] {'fsdp'}, dimensions={0} | all-to-all | bytes 1179648 | tf_op jit(solution)/shard_map/all_to_all | solution.py:285
  84.3 2.2 %collective-permute-start.12 = (bf16[4,4,8,1152]{3,2,1,0:T(8,128)(2,1)S(1)}, bf16[4,4,8,1152]{3,2,1,0:T(8,128)(2,1)S(1)}, u32[]{:S(2)}, u32[]{:S(2)}) collective-permute-start(bf16[4,4,8,1152]{3,2,1,0:T(8,128)(2,1)S(1)} %shard_map.54.refs_0_), channel_id=1, source_target_pairs={{0,64},{32,224},{64,0},{96,160},{128,192},{160,96},{192,128},{224,... | collective-permute-start | bytes 884744 | tf_op jit(solution)/shard_map/ppermute | solution.py:215
  86.5 4.6 %collective-permute-done.12.refs_1_ = bf16[4,4,8,1152]{3,2,1,0:T(8,128)(2,1)S(1)} collective-permute-done((bf16[4,4,8,1152]{3,2,1,0:T(8,128)(2,1)S(1)}, bf16[4,4,8,1152]{3,2,1,0:T(8,128)(2,1)S(1)}, u32[]{:S(2)}, u32[]{:S(2)}) %collective-permute-start.12) | collective-permute-done | bytes 294944 | tf_op jit(solution)/shard_map/ppermute | solution.py:215
  91.3 4.4 %collective-permute-start.14 = (bf16[2,4,4,8,1152]{4,3,2,1,0:T(8,128)(2,1)S(1)}, bf16[2,4,4,8,1152]{4,3,2,1,0:T(8,128)(2,1)S(1)}, u32[]{:S(2)}, u32[]{:S(2)}) collective-permute-start(bf16[2,4,4,8,1152]{4,3,2,1,0:T(8,128)(2,1)S(1)} %shard_map.55.first_ref), channel_id=1, source_target_pairs={{0,32},{32,0},{64,96},{96,64},{128,160},{160,128},{192,224},{224,1... | collective-permute-start | bytes 1769480 | tf_op jit(solution)/shard_map/ppermute | solution.py:211
  95.7 4.6 %collective-permute-done.13.second_ref = bf16[2,4,4,8,1152]{4,3,2,1,0:T(8,128)(2,1)S(1)} collective-permute-done((bf16[2,4,4,8,1152]{4,3,2,1,0:T(8,128)(2,1)S(1)}, bf16[2,4,4,8,1152]{4,3,2,1,0:T(8,128)(2,1)S(1)}, u32[]{:S(2)}, u32[]{:S(2)}) %collective-permute-start.13) | collective-permute-done | bytes 589856 | tf_op jit(solution)/shard_map/ppermute | solution.py:215
  100.3 4.3 %collective-permute-start.15 = (bf16[2,4,4,8,1152]{4,3,2,1,0:T(8,128)(2,1)S(1)}, bf16[2,4,4,8,1152]{4,3,2,1,0:T(8,128)(2,1)S(1)}, u32[]{:S(2)}, u32[]{:S(2)}) collective-permute-start(bf16[2,4,4,8,1152]{4,3,2,1,0:T(8,128)(2,1)S(1)} %collective-permute-done.13.second_ref), channel_id=1, source_target_pairs={{0,32},{32,0},{64,96},{96,64},{128,160},{160,128},{192,224},{224,1... | collective-permute-start | bytes 1769480 | tf_op jit(solution)/shard_map/ppermute | solution.py:211
  104.6 1.6 %collective-permute-done.15.twin_second_ref = bf16[2,4,4,8,1152]{4,3,2,1,0:T(8,128)(2,1)S(1)} collective-permute-done((bf16[2,4,4,8,1152]{4,3,2,1,0:T(8,128)(2,1)S(1)}, bf16[2,4,4,8,1152]{4,3,2,1,0:T(8,128)(2,1)S(1)}, u32[]{:S(2)}, u32[]{:S(2)}) %collective-permute-start.15) | collective-permute-done | bytes 589856 | tf_op jit(solution)/shard_map/ppermute | solution.py:211
  106.2 1.8 %shard_map.56 = bf16[4,32,8192]{2,1,0:T(8,128)(2,1)} custom-call(s32[1]{0:T(128)} %bitcast.place, bf16[2,4,4,8,1152]{4,3,2,1,0:T(8,128)(2,1)S(1)} %shard_map.55.first_ref, bf16[2,4,4,8,1152]{4,3,2,1,0:T(8,128)(2,1)S(1)} %collective-permute-done.13.second_ref, bf16[2,4,4,8,1152]{4,3,2,1,0:T(8,128)(2,1)S(1)} %collective-permute-done.14.twin_first_ref, ...), custom_call_target="tpu_custom_call" | custom-call | tf_op jit(solution)/shard_map/pallas_call | solution.py:293
  (27 shorter events, 4.5 us)
Async XLA Ops:
  0.0 18.9 %copy-start.2 = (s32[32]{0:T(128)S(1)}, s32[32]{0:T(128)}, u32[]{:S(2)}) copy-start(s32[32]{0:T(128)} %slot.3) | copy-start | bytes 388
  1.2 42.0 %copy-start = (bf16[2,1024,1024]{2,1,0:T(8,128)(2,1)S(1)}, bf16[2,1024,1024]{2,1,0:T(8,128)(2,1)}, u32[]{:S(2)}) copy-start(bf16[2,1024,1024]{2,1,0:T(8,128)(2,1)} %left_ref.1) | copy-start | bytes 12582916
  1.2 5.4 %collective-permute-start.1 = (bf16[2,4,8,32,128]{4,3,2,1,0:T(8,128)(2,1)S(1)}, bf16[2,4,8,32,128]{4,3,2,1,0:T(8,128)(2,1)S(1)}, u32[]{:S(2)}, u32[]{:S(2)}) collective-permute-start(bf16[2,4,8,32,128]{4,3,2,1,0:T(8,128)(2,1)S(1)} %shard_map.48), channel_id=1, source_target_pairs={{0,32},{32,0},{64,96},{96,64},{128,160},{160,128},{192,224},{224,1... | collective-permute-start | bytes 1572872 | tf_op jit(solution)/shard_map/ppermute | solution.py:211
  6.3 3.1 %collective-permute-start = (bf16[2,4,8,32,128]{4,3,2,1,0:T(8,128)(2,1)S(1)}, bf16[2,4,8,32,128]{4,3,2,1,0:T(8,128)(2,1)S(1)}, u32[]{:S(2)}, u32[]{:S(2)}) collective-permute-start(bf16[2,4,8,32,128]{4,3,2,1,0:T(8,128)(2,1)S(1)} %get-tuple-element.17), channel_id=1, source_target_pairs={{0,32},{32,0},{64,96},{96,64},{128,160},{160,128},{192,224},{224,1... | collective-permute-start | bytes 1572872 | tf_op jit(solution)/shard_map/ppermute | solution.py:211
  6.7 6.5 %collective-permute-start.3 = (bf16[4,8,32,128]{3,2,1,0:T(8,128)(2,1)S(1)}, bf16[4,8,32,128]{3,2,1,0:T(8,128)(2,1)S(1)}, u32[]{:S(2)}, u32[]{:S(2)}) collective-permute-start(bf16[4,8,32,128]{3,2,1,0:T(8,128)(2,1)S(1)} %get-tuple-element.21), channel_id=1, source_target_pairs={{0,64},{32,224},{64,0},{96,160},{128,192},{160,96},{192,128},{224,... | collective-permute-start | bytes 786440 | tf_op jit(solution)/shard_map/ppermute | solution.py:215
  8.0 8.0 %collective-permute-start.2 = (bf16[4,8,32,128]{3,2,1,0:T(8,128)(2,1)S(1)}, bf16[4,8,32,128]{3,2,1,0:T(8,128)(2,1)S(1)}, u32[]{:S(2)}, u32[]{:S(2)}) collective-permute-start(bf16[4,8,32,128]{3,2,1,0:T(8,128)(2,1)S(1)} %get-tuple-element.19), channel_id=1, source_target_pairs={{0,64},{32,224},{64,0},{96,160},{128,192},{160,96},{192,128},{224,... | collective-permute-start | bytes 786440 | tf_op jit(solution)/shard_map/ppermute | solution.py:215
  9.6 50.9 %copy-start.1 = (bf16[2,1024,1024]{2,1,0:T(8,128)(2,1)S(1)}, bf16[2,1024,1024]{2,1,0:T(8,128)(2,1)}, u32[]{:S(2)}) copy-start(bf16[2,1024,1024]{2,1,0:T(8,128)(2,1)} %refs_8_.1) | copy-start | bytes 12582916
  13.3 5.6 %collective-permute-start.4 = (bf16[4,8,32,128]{3,2,1,0:T(8,128)(2,1)S(1)}, bf16[4,8,32,128]{3,2,1,0:T(8,128)(2,1)S(1)}, u32[]{:S(2)}, u32[]{:S(2)}) collective-permute-start(bf16[4,8,32,128]{3,2,1,0:T(8,128)(2,1)S(1)} %shard_map.50), channel_id=1, source_target_pairs={{0,192},{32,96},{64,128},{96,32},{128,64},{160,224},{192,0},{224,1... | collective-permute-start | bytes 786440 | tf_op jit(solution)/shard_map/ppermute | solution.py:215
  44.6 9.4 %collective-permute-start.5 = (bf16[2,256,128]{2,1,0:T(8,128)(2,1)S(1)}, bf16[2,256,128]{2,1,0:T(8,128)(2,1)S(1)}, u32[]{:S(2)}, u32[]{:S(2)}) collective-permute-start(bf16[2,256,128]{2,1,0:T(8,128)(2,1)S(1)} %get-tuple-element.23), channel_id=1, source_target_pairs={{0,64},{32,224},{64,0},{96,160},{128,192},{160,96},{192,128},{224,... | collective-permute-start | bytes 393224 | tf_op jit(solution)/shard_map/ppermute | solution.py:215
  47.2 7.3 %collective-permute-start.6 = (bf16[2,256,128]{2,1,0:T(8,128)(2,1)S(1)}, bf16[2,256,128]{2,1,0:T(8,128)(2,1)S(1)}, u32[]{:S(2)}, u32[]{:S(2)}) collective-permute-start(bf16[2,256,128]{2,1,0:T(8,128)(2,1)S(1)} %get-tuple-element.24), channel_id=1, source_target_pairs={{0,192},{32,96},{64,128},{96,32},{128,64},{160,224},{192,0},{224,1... | collective-permute-start | bytes 393224 | tf_op jit(solution)/shard_map/ppermute | solution.py:215
  48.5 8.6 %collective-permute-start.7 = (bf16[2,256,128]{2,1,0:T(8,128)(2,1)S(1)}, bf16[2,256,128]{2,1,0:T(8,128)(2,1)S(1)}, u32[]{:S(2)}, u32[]{:S(2)}) collective-permute-start(bf16[2,256,128]{2,1,0:T(8,128)(2,1)S(1)} %get-tuple-element.25), channel_id=1, source_target_pairs={{0,128},{32,160},{64,192},{96,224},{128,0},{160,32},{192,64},{224,... | collective-permute-start | bytes 393224 | tf_op jit(solution)/shard_map/ppermute | solution.py:215
  49.0 10.5 %collective-permute-start.8 = (bf16[2,256,128]{2,1,0:T(8,128)(2,1)S(1)}, bf16[2,256,128]{2,1,0:T(8,128)(2,1)S(1)}, u32[]{:S(2)}, u32[]{:S(2)}) collective-permute-start(bf16[2,256,128]{2,1,0:T(8,128)(2,1)S(1)} %get-tuple-element.22.refs_0_), channel_id=1, source_target_pairs={{0,32},{32,0},{64,96},{96,64},{128,160},{160,128},{192,224},{224,1... | collective-permute-start | bytes 393224 | tf_op jit(solution)/shard_map/ppermute | solution.py:211
  54.0 5.6 %collective-permute-start.10 = (bf16[2,256,128]{2,1,0:T(8,128)(2,1)S(1)}, bf16[2,256,128]{2,1,0:T(8,128)(2,1)S(1)}, u32[]{:S(2)}, u32[]{:S(2)}) collective-permute-start(bf16[2,256,128]{2,1,0:T(8,128)(2,1)S(1)} %collective-permute-done.5.refs_1_), channel_id=1, source_target_pairs={{0,32},{32,0},{64,96},{96,64},{128,160},{160,128},{192,224},{224,1... | collective-permute-start | bytes 393224 | tf_op jit(solution)/shard_map/ppermute | solution.py:211
  54.5 5.0 %collective-permute-start.9 = (bf16[2,256,128]{2,1,0:T(8,128)(2,1)S(1)}, bf16[2,256,128]{2,1,0:T(8,128)(2,1)S(1)}, u32[]{:S(2)}, u32[]{:S(2)}) collective-permute-start(bf16[2,256,128]{2,1,0:T(8,128)(2,1)S(1)} %collective-permute-done.6.refs_2_), channel_id=1, source_target_pairs={{0,32},{32,0},{64,96},{96,64},{128,160},{160,128},{192,224},{224,1... | collective-permute-start | bytes 393224 | tf_op jit(solution)/shard_map/ppermute | solution.py:211
  57.0 3.5 %collective-permute-start.11 = (bf16[2,256,128]{2,1,0:T(8,128)(2,1)S(1)}, bf16[2,256,128]{2,1,0:T(8,128)(2,1)S(1)}, u32[]{:S(2)}, u32[]{:S(2)}) collective-permute-start(bf16[2,256,128]{2,1,0:T(8,128)(2,1)S(1)} %collective-permute-done.7.refs_3_), channel_id=1, source_target_pairs={{0,32},{32,0},{64,96},{96,64},{128,160},{160,128},{192,224},{224,1... | collective-permute-start | bytes 393224 | tf_op jit(solution)/shard_map/ppermute | solution.py:211
  84.3 6.8 %collective-permute-start.12 = (bf16[4,4,8,1152]{3,2,1,0:T(8,128)(2,1)S(1)}, bf16[4,4,8,1152]{3,2,1,0:T(8,128)(2,1)S(1)}, u32[]{:S(2)}, u32[]{:S(2)}) collective-permute-start(bf16[4,4,8,1152]{3,2,1,0:T(8,128)(2,1)S(1)} %shard_map.54.refs_0_), channel_id=1, source_target_pairs={{0,64},{32,224},{64,0},{96,160},{128,192},{160,96},{192,128},{224,... | collective-permute-start | bytes 884744 | tf_op jit(solution)/shard_map/ppermute | solution.py:215
  91.2 9.1 %collective-permute-start.13 = (bf16[2,4,4,8,1152]{4,3,2,1,0:T(8,128)(2,1)S(1)}, bf16[2,4,4,8,1152]{4,3,2,1,0:T(8,128)(2,1)S(1)}, u32[]{:S(2)}, u32[]{:S(2)}) collective-permute-start(bf16[2,4,4,8,1152]{4,3,2,1,0:T(8,128)(2,1)S(1)} %shard_map.55.first_ref), channel_id=1, source_target_pairs={{0,192},{32,96},{64,128},{96,32},{128,64},{160,224},{192,0},{224,1... | collective-permute-start | bytes 1769480 | tf_op jit(solution)/shard_map/ppermute | solution.py:215
  91.3 13.3 %collective-permute-start.14 = (bf16[2,4,4,8,1152]{4,3,2,1,0:T(8,128)(2,1)S(1)}, bf16[2,4,4,8,1152]{4,3,2,1,0:T(8,128)(2,1)S(1)}, u32[]{:S(2)}, u32[]{:S(2)}) collective-permute-start(bf16[2,4,4,8,1152]{4,3,2,1,0:T(8,128)(2,1)S(1)} %shard_map.55.first_ref), channel_id=1, source_target_pairs={{0,32},{32,0},{64,96},{96,64},{128,160},{160,128},{192,224},{224,1... | collective-permute-start | bytes 1769480 | tf_op jit(solution)/shard_map/ppermute | solution.py:211
  100.3 5.9 %collective-permute-start.15 = (bf16[2,4,4,8,1152]{4,3,2,1,0:T(8,128)(2,1)S(1)}, bf16[2,4,4,8,1152]{4,3,2,1,0:T(8,128)(2,1)S(1)}, u32[]{:S(2)}, u32[]{:S(2)}) collective-permute-start(bf16[2,4,4,8,1152]{4,3,2,1,0:T(8,128)(2,1)S(1)} %collective-permute-done.13.second_ref), channel_id=1, source_target_pairs={{0,32},{32,0},{64,96},{96,64},{128,160},{160,128},{192,224},{224,1... | collective-permute-start | bytes 1769480 | tf_op jit(solution)/shard_map/ppermute | solution.py:211

commit v2 on v1

--- a/solution.py
+++ b/solution.py
@@ -37,36 +37,27 @@
         copy.wait()
 
 
-def strip_copies(place, grads_ref, out_ref, arrived, first, kinds, own, sizes):
-    core = lax.rem(place[0], 2)
-    core = core if own else 1 - core
-    cols = sizes["cols"]
-    order = (SELF, NEAR, FAR, OPPOSITE) if own else (SELF, FAR, NEAR, OPPOSITE)
-    return [
+def send_kernel(place, grads_ref, send_ref, arrived, *, kinds, cols, width, strip):
+    other = 1 - lax.rem(place[0], 2)
+    order = (SELF, FAR, NEAR, OPPOSITE)
+    together(
         pltpu.make_async_copy(
-            grads_ref.at[0, :, :, strip_columns(place, order[k], core, j, sizes["width"], sizes["strip"])],
-            out_ref.at[n, :, j],
-            arrived.at[first + n * cols + j],
+            grads_ref.at[0, :, :, strip_columns(place, order[k], other, j, width, strip)],
+            send_ref.at[n, :, j],
+            arrived.at[n * cols + j],
         )
         for n, k in enumerate(kinds)
         for j in range(cols)
-    ]
-
-
-def send_kernel(place, grads_ref, send_ref, arrived, *, kinds, **sizes):
-    together(strip_copies(place, grads_ref, send_ref, arrived, 0, kinds, False, sizes))
-
-
-def send_and_keep_kernel(place, grads_ref, send_ref, keep_ref, arrived, *, kinds, kept, **sizes):
-    together(
-        strip_copies(place, grads_ref, send_ref, arrived, 0, kinds, False, sizes)
-        + strip_copies(place, grads_ref, keep_ref, arrived, len(kinds) * sizes["cols"], kept, True, sizes)
     )
 
 
-def pair_sum_kernel(keep_ref, got_ref, *sum_refs, first):
-    for n, sum_ref in enumerate(sum_refs):
-        sum_ref[...] = (keep_ref[first + n].astype(f32) + got_ref[n].astype(f32)).astype(bf16)
+def pair_sum_kernel(place, grads_ref, got_ref, *sum_refs, kinds, cols, width, strip):
+    core = lax.rem(place[0], 2)
+    for n, (k, sum_ref) in enumerate(zip(kinds, sum_refs)):
+        for m in range(grads_ref.shape[1]):
+            for j in range(cols):
+                piece = grads_ref[0, m, :, strip_columns(place, k, core, j, width, strip)]
+                sum_ref[m, j] = (piece.astype(f32) + got_ref[n, m, j].astype(f32)).astype(bf16)
 
 
 def add_kernel(x_ref, y_ref, out_ref):
@@ -145,14 +136,10 @@
             pair_ref[m, p, :, 2 * width :] = jnp.where(lane < TERMS, tails[0], tails[1]).astype(bf16)
 
 
-def stack_kernel(*refs):
-    *piece_refs, out_ref = refs
-    for k, piece_ref in enumerate(piece_refs):
-        out_ref[k] = piece_ref[...]
-
-
-def finish_kernel(place, first_ref, second_ref, twin_first_ref, twin_second_ref, out_ref, ready, written, *, entries):
-    _, mats, count, part, wide = first_ref.shape
+def finish_kernel(place, *refs, entries):
+    own_refs, twin_refs = refs[:4], refs[4:8]
+    out_ref, ready, written = refs[8:]
+    mats, count, part, wide = own_refs[0].shape
     width = (wide - LANES) // 2
     lane = lax.broadcasted_iota(jnp.int32, (count, part, LANES), 2)
 
@@ -175,8 +162,8 @@
 
     @pl.loop(0, mats)
     def _(m):
-        own = [ref.at[n, m] for ref in (first_ref, second_ref) for n in range(2)]
-        twin = [ref.at[n, m] for n in range(2) for ref in (twin_first_ref, twin_second_ref)]
+        own = [ref.at[m] for ref in own_refs]
+        twin = [ref.at[m] for ref in twin_refs]
         tail = sum(ref[:, :, 2 * width :].astype(f32) for ref in own + twin)
         ratios = []
         for h in range(2):
@@ -229,29 +216,20 @@
         )
 
     smem, vmem = pl.BlockSpec(memory_space=pltpu.SMEM), pl.BlockSpec(memory_space=pltpu.VMEM)
-    hbm = pl.BlockSpec(memory_space=pl.ANY)
-    in_hbm = pltpu.with_memory_space_constraint(grads, pltpu.HBM)
-    ahead, behind = (OPPOSITE, NEAR), (SELF, FAR)
-    send = local(
-        functools.partial(send_kernel, kinds=ahead, **sizes),
-        [smem, hbm],
-        vmem,
-        strips(2),
-        [pltpu.SemaphoreType.DMA((2 * cols,))],
-    )(place, in_hbm)
-    got = twin(send)
-    send, keep = local(
-        functools.partial(send_and_keep_kernel, kinds=behind, kept=ahead + behind, **sizes),
-        [smem, hbm],
-        [vmem] * 2,
-        [strips(2), strips(4)],
-        [pltpu.SemaphoreType.DMA((6 * cols,))],
-    )(place, in_hbm)
-    got = (got, twin(send))
     sums = {}
-    for n, kinds in enumerate((ahead, behind)):
-        add = local(functools.partial(pair_sum_kernel, first=2 * n), [vmem] * 2, [vmem] * 2, [strips()] * 2)
-        sums.update(zip(kinds, add(keep, got[n])))
+    for kinds in ((OPPOSITE, NEAR), (SELF, FAR)):
+        send = local(
+            functools.partial(send_kernel, kinds=kinds, **sizes),
+            [smem, pl.BlockSpec(memory_space=pl.ANY)],
+            vmem,
+            strips(2),
+            [pltpu.SemaphoreType.DMA((2 * cols,))],
+        )(place, pltpu.with_memory_space_constraint(grads, pltpu.HBM))
+        got = twin(send)
+        found = local(
+            functools.partial(pair_sum_kernel, kinds=kinds, **sizes), [smem, vmem, vmem], [vmem] * 2, [strips()] * 2
+        )(place, grads, got)
+        sums.update(zip(kinds, found))
 
     onward = exchange(sums[OPPOSITE], NEAR)
     direct = exchange(sums[NEAR], NEAR)
@@ -288,15 +266,17 @@
     piece = (mats, count, part, wide)
     mine = local(select_kernel, [smem, vmem], vmem, shape(piece, bf16))(block_slot, back)
     near = exchange(mine, NEAR)
-    first = local(stack_kernel, [vmem] * 2, vmem, shape((2, *piece), bf16))(mine, near)
-    second = exchange(first, FAR)
+    far = exchange(mine, FAR)
+    opposite = exchange(near, FAR)
+    own = [mine, near, far, opposite]
+    other = [twin(x) for x in (mine, far, near, opposite)]
     return local(
         functools.partial(finish_kernel, entries=height * width),
-        [smem] + [vmem] * 4,
+        [smem] + [vmem] * 8,
         pl.BlockSpec(memory_space=pl.ANY),
         shape((mats, rows, full), bf16),
         [pltpu.VMEM((mats, rows, full), bf16), pltpu.SemaphoreType.DMA((mats,))],
-    )(place, first, second, twin(first), twin(second))
+    )(place, *own, *other)
 
 
 def solution(mesh):

time: 108 us -> 107 us (level)
  waiting for transfers between devices: 21 us -> 17.3 us
  starting transfers between devices: 32.4 us -> 35.2 us
    ppermute x8 -> x9, waiting for transfers between devices: 18.4 us -> 14.9 us  [exchange(): return lax.ppermute(x, 'replica', perm)]
    ppermute x8 -> x10, starting transfers between devices: 22.7 us -> 26.1 us  [twin(): return lax.ppermute(x, 'replica', [(i, i ^ 1) for i in range(reps)])]
    pallas_call x5 -> x4, Pallas kernels: 3.27 us -> 2.77 us  [the longest x2 2.44 us: on_device(): local(functools.partial(send_kernel, kinds=kinds, **sizes), [smem, pl.Blo...]
    ppermute x8 -> x9, starting transfers between devices: 9.62 us -> 9.16 us  [exchange(): return lax.ppermute(x, 'replica', perm)]
    ppermute x8 -> x10, waiting for transfers between devices: 2.62 us -> 2.43 us  [twin(): return lax.ppermute(x, 'replica', [(i, i ^ 1) for i in range(reps)])]
  transfers between devices with their start and end apart: 16 -> 19, of which waited for: 7 -> 8; matrix products, arithmetic and copies ran while one was open for 0% -> 0% of each run, Pallas kernels for 2% -> 1%
where the time goes in v2:
time: 107 us
  blocking collectives  45.3 us (42%)
  starting transfers between devices  35.2 us (33%)
  waiting for transfers between devices  17.3 us (16%)
  Pallas kernels  8.84 us (8%)
    ppermute x10, starting transfers between devices, twin(): return lax.ppermute(x, 'replica', [(i, i ^ 1) for i in range(reps)])  26.1 us
    all_to_all x1, blocking collectives, on_device(): incoming = lax.all_to_all(outgoing, 'fsdp', 0, 0, tiled=True)  23.5 us
    all_to_all x1, blocking collectives, on_device(): back = lax.all_to_all(back, 'fsdp', 0, 0, tiled=True)  21.8 us
    ppermute x9, waiting for transfers between devices, exchange(): return lax.ppermute(x, 'replica', perm)  14.9 us
    ppermute x9, starting transfers between devices, exchange(): return lax.ppermute(x, 'replica', perm)  9.16 us
    pallas_call x2, Pallas kernels, on_device(): local(functools.partial(send_kernel, kinds=kinds, **sizes), [smem, pl.Blo...  2.44 us
    ppermute x10, waiting for transfers between devices, twin(): return lax.ppermute(x, 'replica', [(i, i ^ 1) for i in range(reps)])  2.43 us
  transfers between devices with their start and end apart: 19, of which 8 were waited for; matrix products, arithmetic and copies ran while one was open for 0% of the time, Pallas kernels for 1%

profile of v2, /device:TPU:1, one launch (start us, length us, event | category | flops | bytes accessed | tf_op | source)
XLA Modules:
  0.0 106.9 jit_solution(17280811634333514185)
XLA Ops:
  0.0 1.3 %shard_map.48 = bf16[2,4,8,32,128]{4,3,2,1,0:T(8,128)(2,1)S(1)} custom-call(s32[1]{0:T(128)} %bitcast.place, bf16[1,4,32,8192]{3,2,1,0:T(8,128)(2,1)} %grads_ref.7), custom_call_target="tpu_custom_call" | custom-call | tf_op jit(solution)/shard_map/pallas_call | solution.py:221
  1.3 3.3 %collective-permute-start.1 = (bf16[2,4,8,32,128]{4,3,2,1,0:T(8,128)(2,1)S(1)}, bf16[2,4,8,32,128]{4,3,2,1,0:T(8,128)(2,1)S(1)}, u32[]{:S(2)}, u32[]{:S(2)}) collective-permute-start(bf16[2,4,8,32,128]{4,3,2,1,0:T(8,128)(2,1)S(1)} %shard_map.48), channel_id=1, source_target_pairs={{0,32},{32,0},{64,96},{96,64},{128,160},{160,128},{192,224},{224,1... | collective-permute-start | bytes 1572872 | tf_op jit(solution)/shard_map/ppermute | solution.py:198
  4.6 1.1 %shard_map.46 = bf16[2,4,8,32,128]{4,3,2,1,0:T(8,128)(2,1)S(1)} custom-call(s32[1]{0:T(128)} %bitcast.place, bf16[1,4,32,8192]{3,2,1,0:T(8,128)(2,1)} %grads_ref.7), custom_call_target="tpu_custom_call" | custom-call | tf_op jit(solution)/shard_map/pallas_call | solution.py:221
  6.4 1.1 %collective-permute-start.3 = (bf16[4,8,32,128]{3,2,1,0:T(8,128)(2,1)S(1)}, bf16[4,8,32,128]{3,2,1,0:T(8,128)(2,1)S(1)}, u32[]{:S(2)}, u32[]{:S(2)}) collective-permute-start(bf16[4,8,32,128]{3,2,1,0:T(8,128)(2,1)S(1)} %get-tuple-element.17), channel_id=1, source_target_pairs={{0,64},{32,224},{64,0},{96,160},{128,192},{160,96},{192,128},{224,... | collective-permute-start | bytes 786440 | tf_op jit(solution)/shard_map/ppermute | solution.py:202
  7.4 1.7 %collective-permute-start.2 = (bf16[4,8,32,128]{3,2,1,0:T(8,128)(2,1)S(1)}, bf16[4,8,32,128]{3,2,1,0:T(8,128)(2,1)S(1)}, u32[]{:S(2)}, u32[]{:S(2)}) collective-permute-start(bf16[4,8,32,128]{3,2,1,0:T(8,128)(2,1)S(1)} %get-tuple-element.15), channel_id=1, source_target_pairs={{0,64},{32,224},{64,0},{96,160},{128,192},{160,96},{192,128},{224,... | collective-permute-start | bytes 786440 | tf_op jit(solution)/shard_map/ppermute | solution.py:202
  9.3 3.6 %collective-permute-done.3.y_ref = bf16[4,8,32,128]{3,2,1,0:T(8,128)(2,1)S(1)} collective-permute-done((bf16[4,8,32,128]{3,2,1,0:T(8,128)(2,1)S(1)}, bf16[4,8,32,128]{3,2,1,0:T(8,128)(2,1)S(1)}, u32[]{:S(2)}, u32[]{:S(2)}) %collective-permute-start.3) | collective-permute-done | bytes 262176 | tf_op jit(solution)/shard_map/ppermute | solution.py:202
  13.0 2.6 %collective-permute-done.2.refs_1_ = bf16[4,8,32,128]{3,2,1,0:T(8,128)(2,1)S(1)} collective-permute-done((bf16[4,8,32,128]{3,2,1,0:T(8,128)(2,1)S(1)}, bf16[4,8,32,128]{3,2,1,0:T(8,128)(2,1)S(1)}, u32[]{:S(2)}, u32[]{:S(2)}) %collective-permute-start.2) | collective-permute-done | bytes 262176 | tf_op jit(solution)/shard_map/ppermute | solution.py:202
  15.7 2.9 %collective-permute-done.4.refs_2_ = bf16[4,8,32,128]{3,2,1,0:T(8,128)(2,1)S(1)} collective-permute-done((bf16[4,8,32,128]{3,2,1,0:T(8,128)(2,1)S(1)}, bf16[4,8,32,128]{3,2,1,0:T(8,128)(2,1)S(1)}, u32[]{:S(2)}, u32[]{:S(2)}) %collective-permute-start.4) | collective-permute-done | bytes 262176 | tf_op jit(solution)/shard_map/ppermute | solution.py:202
  19.3 23.5 %all_to_all.10.block_ref = bf16[32,2,32,128]{3,2,1,0:T(8,128)(2,1)S(1)} all-to-all(bf16[32,2,32,128]{3,2,1,0:T(8,128)(2,1)S(1)} %shard_map.51), channel_id=1, replica_groups=mesh['replica'=8,'fsdp'=32] {'fsdp'}, dimensions={0} | all-to-all | bytes 1048576 | tf_op jit(solution)/shard_map/all_to_all | solution.py:242
  42.8 1.4 %shard_map.52 = (bf16[2,256,128]{2,1,0:T(8,128)(2,1)S(1)}, bf16[2,256,128]{2,1,0:T(8,128)(2,1)S(1)}, bf16[2,256,128]{2,1,0:T(8,128)(2,1)S(1)}, bf16[2,256,128]{2,1,0:T(8,128)(2,1)S(1)}, f32[2,8,128]{2,1,0:T(8,128)S(1)}) custom-call(s32[1]{0:T(128)} %bitcast.place, bf16[2,1024,1024]{2,1,0:T(8,128)(2,1)S(1)} %copy-done.1, ...), custom_call_target="tpu_custom_call" | custom-call | tf_op jit(solution)/shard_map/pallas_call | solution.py:245
  44.2 2.6 %collective-permute-start.5 = (bf16[2,256,128]{2,1,0:T(8,128)(2,1)S(1)}, bf16[2,256,128]{2,1,0:T(8,128)(2,1)S(1)}, u32[]{:S(2)}, u32[]{:S(2)}) collective-permute-start(bf16[2,256,128]{2,1,0:T(8,128)(2,1)S(1)} %get-tuple-element.19), channel_id=1, source_target_pairs={{0,64},{32,224},{64,0},{96,160},{128,192},{160,96},{192,128},{224,... | collective-permute-start | bytes 393224 | tf_op jit(solution)/shard_map/ppermute | solution.py:202
  48.3 5.1 %collective-permute-start.8 = (bf16[2,256,128]{2,1,0:T(8,128)(2,1)S(1)}, bf16[2,256,128]{2,1,0:T(8,128)(2,1)S(1)}, u32[]{:S(2)}, u32[]{:S(2)}) collective-permute-start(bf16[2,256,128]{2,1,0:T(8,128)(2,1)S(1)} %get-tuple-element.18.refs_0_), channel_id=1, source_target_pairs={{0,32},{32,0},{64,96},{96,64},{128,160},{160,128},{192,224},{224,1... | collective-permute-start | bytes 393224 | tf_op jit(solution)/shard_map/ppermute | solution.py:198
  54.2 2.2 %collective-permute-start.9 = (bf16[2,256,128]{2,1,0:T(8,128)(2,1)S(1)}, bf16[2,256,128]{2,1,0:T(8,128)(2,1)S(1)}, u32[]{:S(2)}, u32[]{:S(2)}) collective-permute-start(bf16[2,256,128]{2,1,0:T(8,128)(2,1)S(1)} %collective-permute-done.6.refs_2_), channel_id=1, source_target_pairs={{0,32},{32,0},{64,96},{96,64},{128,160},{160,128},{192,224},{224,1... | collective-permute-start | bytes 393224 | tf_op jit(solution)/shard_map/ppermute | solution.py:198
  56.4 2.5 %collective-permute-start.11 = (bf16[2,256,128]{2,1,0:T(8,128)(2,1)S(1)}, bf16[2,256,128]{2,1,0:T(8,128)(2,1)S(1)}, u32[]{:S(2)}, u32[]{:S(2)}) collective-permute-start(bf16[2,256,128]{2,1,0:T(8,128)(2,1)S(1)} %collective-permute-done.7.refs_3_), channel_id=1, source_target_pairs={{0,32},{32,0},{64,96},{96,64},{128,160},{160,128},{192,224},{224,1... | collective-permute-start | bytes 393224 | tf_op jit(solution)/shard_map/ppermute | solution.py:198
  58.9 1.0 collective-permute-done.11.refs_7_
  59.8 1.2 %shard_map.53 = bf16[32,8,1152]{2,1,0:T(8,128)(2,1)S(1)} custom-call(s32[1]{0:T(128)} %bitcast.place, bf16[2,256,128]{2,1,0:T(8,128)(2,1)S(1)} %get-tuple-element.18.refs_0_, bf16[2,256,128]{2,1,0:T(8,128)(2,1)S(1)} %collective-permute-done.5.refs_1_, bf16[2,256,128]{2,1,0:T(8,128)(2,1)S(1)} %collective-permute-done.6.refs_2_, ...), custom_call_target="tpu_custom_call" | custom-call | tf_op jit(solution)/shard_map/pallas_call | solution.py:256
  61.0 21.8 %all_to_all.11.back_ref = bf16[32,8,1152]{2,1,0:T(8,128)(2,1)S(1)} all-to-all(bf16[32,8,1152]{2,1,0:T(8,128)(2,1)S(1)} %shard_map.53), channel_id=1, replica_groups=mesh['replica'=8,'fsdp'=32] {'fsdp'}, dimensions={0} | all-to-all | bytes 1179648 | tf_op jit(solution)/shard_map/all_to_all | solution.py:263
  83.6 2.2 %collective-permute-start.12 = (bf16[4,4,8,1152]{3,2,1,0:T(8,128)(2,1)S(1)}, bf16[4,4,8,1152]{3,2,1,0:T(8,128)(2,1)S(1)}, u32[]{:S(2)}, u32[]{:S(2)}) collective-permute-start(bf16[4,4,8,1152]{3,2,1,0:T(8,128)(2,1)S(1)} %shard_map.54.refs_0_), channel_id=1, source_target_pairs={{0,64},{32,224},{64,0},{96,160},{128,192},{160,96},{192,128},{224,... | collective-permute-start | bytes 884744 | tf_op jit(solution)/shard_map/ppermute | solution.py:202
  85.8 4.7 %collective-permute-done.12.refs_1_ = bf16[4,4,8,1152]{3,2,1,0:T(8,128)(2,1)S(1)} collective-permute-done((bf16[4,4,8,1152]{3,2,1,0:T(8,128)(2,1)S(1)}, bf16[4,4,8,1152]{3,2,1,0:T(8,128)(2,1)S(1)}, u32[]{:S(2)}, u32[]{:S(2)}) %collective-permute-start.12) | collective-permute-done | bytes 294944 | tf_op jit(solution)/shard_map/ppermute | solution.py:202
  90.5 5.6 %collective-permute-start.15 = (bf16[4,4,8,1152]{3,2,1,0:T(8,128)(2,1)S(1)}, bf16[4,4,8,1152]{3,2,1,0:T(8,128)(2,1)S(1)}, u32[]{:S(2)}, u32[]{:S(2)}) collective-permute-start(bf16[4,4,8,1152]{3,2,1,0:T(8,128)(2,1)S(1)} %shard_map.54.refs_0_), channel_id=1, source_target_pairs={{0,32},{32,0},{64,96},{96,64},{128,160},{160,128},{192,224},{224,1... | collective-permute-start | bytes 884744 | tf_op jit(solution)/shard_map/ppermute | solution.py:198
  96.6 1.1 %collective-permute-done.14.refs_3_ = bf16[4,4,8,1152]{3,2,1,0:T(8,128)(2,1)S(1)} collective-permute-done((bf16[4,4,8,1152]{3,2,1,0:T(8,128)(2,1)S(1)}, bf16[4,4,8,1152]{3,2,1,0:T(8,128)(2,1)S(1)}, u32[]{:S(2)}, u32[]{:S(2)}) %collective-permute-start.14) | collective-permute-done | bytes 294944 | tf_op jit(solution)/shard_map/ppermute | solution.py:202
  97.7 6.0 %collective-permute-start.18 = (bf16[4,4,8,1152]{3,2,1,0:T(8,128)(2,1)S(1)}, bf16[4,4,8,1152]{3,2,1,0:T(8,128)(2,1)S(1)}, u32[]{:S(2)}, u32[]{:S(2)}) collective-permute-start(bf16[4,4,8,1152]{3,2,1,0:T(8,128)(2,1)S(1)} %collective-permute-done.14.refs_3_), channel_id=1, source_target_pairs={{0,32},{32,0},{64,96},{96,64},{128,160},{160,128},{192,224},{224,1... | collective-permute-start | bytes 884744 | tf_op jit(solution)/shard_map/ppermute | solution.py:198
  103.7 1.2 %collective-permute-done.18.refs_7_ = bf16[4,4,8,1152]{3,2,1,0:T(8,128)(2,1)S(1)} collective-permute-done((bf16[4,4,8,1152]{3,2,1,0:T(8,128)(2,1)S(1)}, bf16[4,4,8,1152]{3,2,1,0:T(8,128)(2,1)S(1)}, u32[]{:S(2)}, u32[]{:S(2)}) %collective-permute-start.18) | collective-permute-done | bytes 294944 | tf_op jit(solution)/shard_map/ppermute | solution.py:198
  104.9 1.8 %shard_map.55 = bf16[4,32,8192]{2,1,0:T(8,128)(2,1)} custom-call(s32[1]{0:T(128)} %bitcast.place, bf16[4,4,8,1152]{3,2,1,0:T(8,128)(2,1)S(1)} %shard_map.54.refs_0_, bf16[4,4,8,1152]{3,2,1,0:T(8,128)(2,1)S(1)} %collective-permute-done.12.refs_1_, bf16[4,4,8,1152]{3,2,1,0:T(8,128)(2,1)S(1)} %collective-permute-done.13.refs_2_, ...), custom_call_target="tpu_custom_call" | custom-call | tf_op jit(solution)/shard_map/pallas_call | solution.py:273
  (34 shorter events, 5.3 us)
Async XLA Ops:
  0.0 6.2 %copy-start = (bf16[1,4,32,8192]{3,2,1,0:T(8,128)(2,1)S(1)}, bf16[1,4,32,8192]{3,2,1,0:T(8,128)(2,1)}, u32[]{:S(2)}) copy-start(bf16[1,4,32,8192]{3,2,1,0:T(8,128)(2,1)} %grads_ref.7) | copy-start | bytes 6291460
  1.3 17.2 %copy-start.3 = (s32[32]{0:T(128)S(1)}, s32[32]{0:T(128)}, u32[]{:S(2)}) copy-start(s32[32]{0:T(128)} %slot.3) | copy-start | bytes 388
  1.3 4.9 %collective-permute-start.1 = (bf16[2,4,8,32,128]{4,3,2,1,0:T(8,128)(2,1)S(1)}, bf16[2,4,8,32,128]{4,3,2,1,0:T(8,128)(2,1)S(1)}, u32[]{:S(2)}, u32[]{:S(2)}) collective-permute-start(bf16[2,4,8,32,128]{4,3,2,1,0:T(8,128)(2,1)S(1)} %shard_map.48), channel_id=1, source_target_pairs={{0,32},{32,0},{64,96},{96,64},{128,160},{160,128},{192,224},{224,1... | collective-permute-start | bytes 1572872 | tf_op jit(solution)/shard_map/ppermute | solution.py:198
  5.8 37.0 %copy-start.1 = (bf16[2,1024,1024]{2,1,0:T(8,128)(2,1)S(1)}, bf16[2,1024,1024]{2,1,0:T(8,128)(2,1)}, u32[]{:S(2)}) copy-start(bf16[2,1024,1024]{2,1,0:T(8,128)(2,1)} %left_ref.1) | copy-start | bytes 12582916
  5.8 3.3 %collective-permute-start = (bf16[2,4,8,32,128]{4,3,2,1,0:T(8,128)(2,1)S(1)}, bf16[2,4,8,32,128]{4,3,2,1,0:T(8,128)(2,1)S(1)}, u32[]{:S(2)}, u32[]{:S(2)}) collective-permute-start(bf16[2,4,8,32,128]{4,3,2,1,0:T(8,128)(2,1)S(1)} %shard_map.46), channel_id=1, source_target_pairs={{0,32},{32,0},{64,96},{96,64},{128,160},{160,128},{192,224},{224,1... | collective-permute-start | bytes 1572872 | tf_op jit(solution)/shard_map/ppermute | solution.py:198
  6.4 6.5 %collective-permute-start.3 = (bf16[4,8,32,128]{3,2,1,0:T(8,128)(2,1)S(1)}, bf16[4,8,32,128]{3,2,1,0:T(8,128)(2,1)S(1)}, u32[]{:S(2)}, u32[]{:S(2)}) collective-permute-start(bf16[4,8,32,128]{3,2,1,0:T(8,128)(2,1)S(1)} %get-tuple-element.17), channel_id=1, source_target_pairs={{0,64},{32,224},{64,0},{96,160},{128,192},{160,96},{192,128},{224,... | collective-permute-start | bytes 786440 | tf_op jit(solution)/shard_map/ppermute | solution.py:202
  7.4 8.2 %collective-permute-start.2 = (bf16[4,8,32,128]{3,2,1,0:T(8,128)(2,1)S(1)}, bf16[4,8,32,128]{3,2,1,0:T(8,128)(2,1)S(1)}, u32[]{:S(2)}, u32[]{:S(2)}) collective-permute-start(bf16[4,8,32,128]{3,2,1,0:T(8,128)(2,1)S(1)} %get-tuple-element.15), channel_id=1, source_target_pairs={{0,64},{32,224},{64,0},{96,160},{128,192},{160,96},{192,128},{224,... | collective-permute-start | bytes 786440 | tf_op jit(solution)/shard_map/ppermute | solution.py:202
  9.3 50.5 %copy-start.2 = (bf16[2,1024,1024]{2,1,0:T(8,128)(2,1)S(1)}, bf16[2,1024,1024]{2,1,0:T(8,128)(2,1)}, u32[]{:S(2)}) copy-start(bf16[2,1024,1024]{2,1,0:T(8,128)(2,1)} %refs_8_.1) | copy-start | bytes 12582916
  12.9 5.6 %collective-permute-start.4 = (bf16[4,8,32,128]{3,2,1,0:T(8,128)(2,1)S(1)}, bf16[4,8,32,128]{3,2,1,0:T(8,128)(2,1)S(1)}, u32[]{:S(2)}, u32[]{:S(2)}) collective-permute-start(bf16[4,8,32,128]{3,2,1,0:T(8,128)(2,1)S(1)} %shard_map.50), channel_id=1, source_target_pairs={{0,192},{32,96},{64,128},{96,32},{128,64},{160,224},{192,0},{224,1... | collective-permute-start | bytes 786440 | tf_op jit(solution)/shard_map/ppermute | solution.py:202
  44.2 9.2 %collective-permute-start.5 = (bf16[2,256,128]{2,1,0:T(8,128)(2,1)S(1)}, bf16[2,256,128]{2,1,0:T(8,128)(2,1)S(1)}, u32[]{:S(2)}, u32[]{:S(2)}) collective-permute-start(bf16[2,256,128]{2,1,0:T(8,128)(2,1)S(1)} %get-tuple-element.19), channel_id=1, source_target_pairs={{0,64},{32,224},{64,0},{96,160},{128,192},{160,96},{192,128},{224,... | collective-permute-start | bytes 393224 | tf_op jit(solution)/shard_map/ppermute | solution.py:202
  46.9 7.3 %collective-permute-start.6 = (bf16[2,256,128]{2,1,0:T(8,128)(2,1)S(1)}, bf16[2,256,128]{2,1,0:T(8,128)(2,1)S(1)}, u32[]{:S(2)}, u32[]{:S(2)}) collective-permute-start(bf16[2,256,128]{2,1,0:T(8,128)(2,1)S(1)} %get-tuple-element.20), channel_id=1, source_target_pairs={{0,192},{32,96},{64,128},{96,32},{128,64},{160,224},{192,0},{224,1... | collective-permute-start | bytes 393224 | tf_op jit(solution)/shard_map/ppermute | solution.py:202
  47.8 8.6 %collective-permute-start.7 = (bf16[2,256,128]{2,1,0:T(8,128)(2,1)S(1)}, bf16[2,256,128]{2,1,0:T(8,128)(2,1)S(1)}, u32[]{:S(2)}, u32[]{:S(2)}) collective-permute-start(bf16[2,256,128]{2,1,0:T(8,128)(2,1)S(1)} %get-tuple-element.21), channel_id=1, source_target_pairs={{0,128},{32,160},{64,192},{96,224},{128,0},{160,32},{192,64},{224,... | collective-permute-start | bytes 393224 | tf_op jit(solution)/shard_map/ppermute | solution.py:202
  48.3 10.5 %collective-permute-start.8 = (bf16[2,256,128]{2,1,0:T(8,128)(2,1)S(1)}, bf16[2,256,128]{2,1,0:T(8,128)(2,1)S(1)}, u32[]{:S(2)}, u32[]{:S(2)}) collective-permute-start(bf16[2,256,128]{2,1,0:T(8,128)(2,1)S(1)} %get-tuple-element.18.refs_0_), channel_id=1, source_target_pairs={{0,32},{32,0},{64,96},{96,64},{128,160},{160,128},{192,224},{224,1... | collective-permute-start | bytes 393224 | tf_op jit(solution)/shard_map/ppermute | solution.py:198
  53.4 5.4 %collective-permute-start.10 = (bf16[2,256,128]{2,1,0:T(8,128)(2,1)S(1)}, bf16[2,256,128]{2,1,0:T(8,128)(2,1)S(1)}, u32[]{:S(2)}, u32[]{:S(2)}) collective-permute-start(bf16[2,256,128]{2,1,0:T(8,128)(2,1)S(1)} %collective-permute-done.5.refs_1_), channel_id=1, source_target_pairs={{0,32},{32,0},{64,96},{96,64},{128,160},{160,128},{192,224},{224,1... | collective-permute-start | bytes 393224 | tf_op jit(solution)/shard_map/ppermute | solution.py:198
  54.2 4.7 %collective-permute-start.9 = (bf16[2,256,128]{2,1,0:T(8,128)(2,1)S(1)}, bf16[2,256,128]{2,1,0:T(8,128)(2,1)S(1)}, u32[]{:S(2)}, u32[]{:S(2)}) collective-permute-start(bf16[2,256,128]{2,1,0:T(8,128)(2,1)S(1)} %collective-permute-done.6.refs_2_), channel_id=1, source_target_pairs={{0,32},{32,0},{64,96},{96,64},{128,160},{160,128},{192,224},{224,1... | collective-permute-start | bytes 393224 | tf_op jit(solution)/shard_map/ppermute | solution.py:198
  56.4 3.5 %collective-permute-start.11 = (bf16[2,256,128]{2,1,0:T(8,128)(2,1)S(1)}, bf16[2,256,128]{2,1,0:T(8,128)(2,1)S(1)}, u32[]{:S(2)}, u32[]{:S(2)}) collective-permute-start(bf16[2,256,128]{2,1,0:T(8,128)(2,1)S(1)} %collective-permute-done.7.refs_3_), channel_id=1, source_target_pairs={{0,32},{32,0},{64,96},{96,64},{128,160},{160,128},{192,224},{224,1... | collective-permute-start | bytes 393224 | tf_op jit(solution)/shard_map/ppermute | solution.py:198
  83.6 6.8 %collective-permute-start.12 = (bf16[4,4,8,1152]{3,2,1,0:T(8,128)(2,1)S(1)}, bf16[4,4,8,1152]{3,2,1,0:T(8,128)(2,1)S(1)}, u32[]{:S(2)}, u32[]{:S(2)}) collective-permute-start(bf16[4,4,8,1152]{3,2,1,0:T(8,128)(2,1)S(1)} %shard_map.54.refs_0_), channel_id=1, source_target_pairs={{0,64},{32,224},{64,0},{96,160},{128,192},{160,96},{192,128},{224,... | collective-permute-start | bytes 884744 | tf_op jit(solution)/shard_map/ppermute | solution.py:202
  85.8 10.3 %collective-permute-start.13 = (bf16[4,4,8,1152]{3,2,1,0:T(8,128)(2,1)S(1)}, bf16[4,4,8,1152]{3,2,1,0:T(8,128)(2,1)S(1)}, u32[]{:S(2)}, u32[]{:S(2)}) collective-permute-start(bf16[4,4,8,1152]{3,2,1,0:T(8,128)(2,1)S(1)} %shard_map.54.refs_0_), channel_id=1, source_target_pairs={{0,192},{32,96},{64,128},{96,32},{128,64},{160,224},{192,0},{224,1... | collective-permute-start | bytes 884744 | tf_op jit(solution)/shard_map/ppermute | solution.py:202
  90.5 7.2 %collective-permute-start.14 = (bf16[4,4,8,1152]{3,2,1,0:T(8,128)(2,1)S(1)}, bf16[4,4,8,1152]{3,2,1,0:T(8,128)(2,1)S(1)}, u32[]{:S(2)}, u32[]{:S(2)}) collective-permute-start(bf16[4,4,8,1152]{3,2,1,0:T(8,128)(2,1)S(1)} %collective-permute-done.12.refs_1_), channel_id=1, source_target_pairs={{0,192},{32,96},{64,128},{96,32},{128,64},{160,224},{192,0},{224,1... | collective-permute-start | bytes 884744 | tf_op jit(solution)/shard_map/ppermute | solution.py:202
  90.5 13.3 %collective-permute-start.15 = (bf16[4,4,8,1152]{3,2,1,0:T(8,128)(2,1)S(1)}, bf16[4,4,8,1152]{3,2,1,0:T(8,128)(2,1)S(1)}, u32[]{:S(2)}, u32[]{:S(2)}) collective-permute-start(bf16[4,4,8,1152]{3,2,1,0:T(8,128)(2,1)S(1)} %shard_map.54.refs_0_), channel_id=1, source_target_pairs={{0,32},{32,0},{64,96},{96,64},{128,160},{160,128},{192,224},{224,1... | collective-permute-start | bytes 884744 | tf_op jit(solution)/shard_map/ppermute | solution.py:198
  96.1 7.7 %collective-permute-start.17 = (bf16[4,4,8,1152]{3,2,1,0:T(8,128)(2,1)S(1)}, bf16[4,4,8,1152]{3,2,1,0:T(8,128)(2,1)S(1)}, u32[]{:S(2)}, u32[]{:S(2)}) collective-permute-start(bf16[4,4,8,1152]{3,2,1,0:T(8,128)(2,1)S(1)} %collective-permute-done.12.refs_1_), channel_id=1, source_target_pairs={{0,32},{32,0},{64,96},{96,64},{128,160},{160,128},{192,224},{224,1... | collective-permute-start | bytes 884744 | tf_op jit(solution)/shard_map/ppermute | solution.py:198
  96.1 7.7 %collective-permute-start.16 = (bf16[4,4,8,1152]{3,2,1,0:T(8,128)(2,1)S(1)}, bf16[4,4,8,1152]{3,2,1,0:T(8,128)(2,1)S(1)}, u32[]{:S(2)}, u32[]{:S(2)}) collective-permute-start(bf16[4,4,8,1152]{3,2,1,0:T(8,128)(2,1)S(1)} %collective-permute-done.13.refs_2_), channel_id=1, source_target_pairs={{0,32},{32,0},{64,96},{96,64},{128,160},{160,128},{192,224},{224,1... | collective-permute-start | bytes 884744 | tf_op jit(solution)/shard_map/ppermute | solution.py:198
  97.7 7.2 %collective-permute-start.18 = (bf16[4,4,8,1152]{3,2,1,0:T(8,128)(2,1)S(1)}, bf16[4,4,8,1152]{3,2,1,0:T(8,128)(2,1)S(1)}, u32[]{:S(2)}, u32[]{:S(2)}) collective-permute-start(bf16[4,4,8,1152]{3,2,1,0:T(8,128)(2,1)S(1)} %collective-permute-done.14.refs_3_), channel_id=1, source_target_pairs={{0,32},{32,0},{64,96},{96,64},{128,160},{160,128},{192,224},{224,1... | collective-permute-start | bytes 884744 | tf_op jit(solution)/shard_map/ppermute | solution.py:198

commit v3 on v2

--- a/solution.py
+++ b/solution.py
@@ -14,10 +14,12 @@
 bf16, f32 = jnp.bfloat16, jnp.float32
 
 SELF, NEAR, FAR, OPPOSITE = range(4)
+ORDER = (SELF, OPPOSITE, NEAR, FAR)
+TWIN_ORDER = (SELF, OPPOSITE, FAR, NEAR)
 
 
 def masks(core):
-    return 0, 1 + 2 * core, 3 - 2 * core, 2
+    return 0, 3 - 2 * core, 1 + 2 * core, 2
 
 
 def chip(place, relative):
@@ -85,7 +87,7 @@
         square_ref[s] = jnp.broadcast_to(jnp.sum(wide * wide, keepdims=True), square_ref.shape[1:])
         half = jnp.dot(left_ref[s], block, preferred_element_type=f32)
         scratch[s] = half.reshape(scratch.shape[1:])
-        for k, half_ref in enumerate(half_refs):
+        for k, half_ref in zip(ORDER, half_refs):
             half_ref[s] = scratch[s, :, chip(place, k)].reshape(half_ref.shape[1:]).astype(bf16)
 
 
@@ -107,7 +109,7 @@
     tail = jnp.zeros((part, LANES), f32)
     for s in range(slots):
         for half_refs, c in ((own_refs, core), (twin_refs, 1 - core)):
-            for k, half_ref in enumerate(half_refs):
+            for k, half_ref in zip(ORDER, half_refs):
                 r = 2 * chip(place, k) + c
                 half_scratch[s, :, pl.ds(pl.multiple_of(r * strip, strip), strip)] = half_ref[s]
         columns = pl.ds(pl.multiple_of(core * width, width), width)
@@ -144,7 +146,7 @@
     lane = lax.broadcasted_iota(jnp.int32, (count, part, LANES), 2)
 
     def emit(m, own, twin, ratios, core, odd):
-        couples = ((SELF, FAR), (OPPOSITE, NEAR)) if core else ((SELF, NEAR), (OPPOSITE, FAR))
+        couples = ((SELF, NEAR), (OPPOSITE, FAR)) if core else ((SELF, FAR), (OPPOSITE, NEAR))
         for couple in couples:
             rows = pl.ds(pl.multiple_of(chip(place, couple[0]) // 2 * 2 * part, 2 * part), 2 * part)
             for p in range(count):
@@ -249,9 +251,8 @@
         [half_shape] * 4 + [shape((slots, part, LANES), f32)],
         [pltpu.VMEM((slots, owners, 4, part, strip), f32)],
     )(place, left_root, incoming)
-    halves = [halves[SELF]] + [exchange(halves[k], k) for k in (NEAR, FAR, OPPOSITE)]
-    handed = [twin(half) for half in halves]
-    handed = [handed[SELF], handed[FAR], handed[NEAR], handed[OPPOSITE]]
+    halves = [half if k == SELF else exchange(half, k) for k, half in zip(ORDER, halves)]
+    handed = [twin(halves[ORDER.index(k)]) for k in TWIN_ORDER]
     wide = width + LANES
     back = local(
         right_kernel,
@@ -266,10 +267,12 @@
     piece = (mats, count, part, wide)
     mine = local(select_kernel, [smem, vmem], vmem, shape(piece, bf16))(block_slot, back)
     near = exchange(mine, NEAR)
-    far = exchange(mine, FAR)
+    shared = twin(mine)
+    later, shared = lax.optimization_barrier((mine, shared))
+    far = exchange(later, FAR)
     opposite = exchange(near, FAR)
     own = [mine, near, far, opposite]
-    other = [twin(x) for x in (mine, far, near, opposite)]
+    other = [shared] + [twin(x) for x in (far, near, opposite)]
     return local(
         functools.partial(finish_kernel, entries=height * width),
         [smem] + [vmem] * 8,

time: 107 us -> 107 us (level)
  starting transfers between devices: 35.2 us -> 29.7 us
  waiting for transfers between devices: 17.3 us -> 20.5 us
  blocking collectives: 45.3 us -> 47.7 us
    ppermute x10, starting transfers between devices: 26.1 us -> 19.6 us  [twin(): return lax.ppermute(x, 'replica', [(i, i ^ 1) for i in range(reps)])]
    ppermute x9, waiting for transfers between devices: 14.9 us -> 16.5 us  [exchange(): return lax.ppermute(x, 'replica', perm)]
    ppermute x10, waiting for transfers between devices: 2.43 us -> 3.99 us  [twin(): return lax.ppermute(x, 'replica', [(i, i ^ 1) for i in range(reps)])]
    all_to_all x1, blocking collectives: 21.8 us -> 23 us  [on_device(): back = lax.all_to_all(back, 'fsdp', 0, 0, tiled=True)]
    all_to_all x1, blocking collectives: 23.5 us -> 24.7 us  [on_device(): incoming = lax.all_to_all(outgoing, 'fsdp', 0, 0, tiled=True)]
  transfers between devices with their start and end apart: 19 -> 19, of which waited for: 8 -> 10; matrix products, arithmetic and copies ran while one was open for 0% -> 0% of each run, Pallas kernels for 1% -> 1%
where the time goes in v3:
time: 107 us
  blocking collectives  47.7 us (45%)
  starting transfers between devices  29.7 us (28%)
  waiting for transfers between devices  20.5 us (19%)
  Pallas kernels  8.84 us (8%)
    all_to_all x1, blocking collectives, on_device(): incoming = lax.all_to_all(outgoing, 'fsdp', 0, 0, tiled=True)  24.7 us
    all_to_all x1, blocking collectives, on_device(): back = lax.all_to_all(back, 'fsdp', 0, 0, tiled=True)  23 us
    ppermute x10, starting transfers between devices, twin(): return lax.ppermute(x, 'replica', [(i, i ^ 1) for i in range(reps)])  19.6 us
    ppermute x9, waiting for transfers between devices, exchange(): return lax.ppermute(x, 'replica', perm)  16.5 us
    ppermute x9, starting transfers between devices, exchange(): return lax.ppermute(x, 'replica', perm)  10 us
    ppermute x10, waiting for transfers between devices, twin(): return lax.ppermute(x, 'replica', [(i, i ^ 1) for i in range(reps)])  3.99 us
    pallas_call x2, Pallas kernels, on_device(): local(functools.partial(send_kernel, kinds=kinds, **sizes), [smem, pl.Blo...  2.44 us
  transfers between devices with their start and end apart: 19, of which 10 were waited for; matrix products, arithmetic and copies ran while one was open for 0% of the time, Pallas kernels for 1%

profile of v3, /device:TPU:1, one launch (start us, length us, event | category | flops | bytes accessed | tf_op | source)
XLA Modules:
  0.0 107.0 jit_solution(1719760822361020958)
XLA Ops:
  0.0 1.3 %shard_map.48 = bf16[2,4,8,32,128]{4,3,2,1,0:T(8,128)(2,1)S(1)} custom-call(s32[1]{0:T(128)} %bitcast.place, bf16[1,4,32,8192]{3,2,1,0:T(8,128)(2,1)} %grads_ref.7), custom_call_target="tpu_custom_call" | custom-call | tf_op jit(solution)/shard_map/pallas_call | solution.py:223
  1.3 3.3 %collective-permute-start.1 = (bf16[2,4,8,32,128]{4,3,2,1,0:T(8,128)(2,1)S(1)}, bf16[2,4,8,32,128]{4,3,2,1,0:T(8,128)(2,1)S(1)}, u32[]{:S(2)}, u32[]{:S(2)}) collective-permute-start(bf16[2,4,8,32,128]{4,3,2,1,0:T(8,128)(2,1)S(1)} %shard_map.48), channel_id=1, source_target_pairs={{0,32},{32,0},{64,96},{96,64},{128,160},{160,128},{192,224},{224,1... | collective-permute-start | bytes 1572872 | tf_op jit(solution)/shard_map/ppermute | solution.py:200
  6.5 1.5 %collective-permute-start.2 = (bf16[4,8,32,128]{3,2,1,0:T(8,128)(2,1)S(1)}, bf16[4,8,32,128]{3,2,1,0:T(8,128)(2,1)S(1)}, u32[]{:S(2)}, u32[]{:S(2)}) collective-permute-start(bf16[4,8,32,128]{3,2,1,0:T(8,128)(2,1)S(1)} %get-tuple-element.17), channel_id=1, source_target_pairs={{0,192},{32,96},{64,128},{96,32},{128,64},{160,224},{192,0},{224,1... | collective-permute-start | bytes 786440 | tf_op jit(solution)/shard_map/ppermute | solution.py:204
  8.1 3.9 %collective-permute-done.3.y_ref = bf16[4,8,32,128]{3,2,1,0:T(8,128)(2,1)S(1)} collective-permute-done((bf16[4,8,32,128]{3,2,1,0:T(8,128)(2,1)S(1)}, bf16[4,8,32,128]{3,2,1,0:T(8,128)(2,1)S(1)}, u32[]{:S(2)}, u32[]{:S(2)}) %collective-permute-start.3) | collective-permute-done | bytes 262176 | tf_op jit(solution)/shard_map/ppermute | solution.py:204
  13.1 1.7 %collective-permute-done.2.refs_1_ = bf16[4,8,32,128]{3,2,1,0:T(8,128)(2,1)S(1)} collective-permute-done((bf16[4,8,32,128]{3,2,1,0:T(8,128)(2,1)S(1)}, bf16[4,8,32,128]{3,2,1,0:T(8,128)(2,1)S(1)}, u32[]{:S(2)}, u32[]{:S(2)}) %collective-permute-start.2) | collective-permute-done | bytes 262176 | tf_op jit(solution)/shard_map/ppermute | solution.py:204
  14.8 4.6 %collective-permute-done.4.refs_2_ = bf16[4,8,32,128]{3,2,1,0:T(8,128)(2,1)S(1)} collective-permute-done((bf16[4,8,32,128]{3,2,1,0:T(8,128)(2,1)S(1)}, bf16[4,8,32,128]{3,2,1,0:T(8,128)(2,1)S(1)}, u32[]{:S(2)}, u32[]{:S(2)}) %collective-permute-start.4) | collective-permute-done | bytes 262176 | tf_op jit(solution)/shard_map/ppermute | solution.py:204
  20.1 24.7 %all_to_all.10.block_ref = bf16[32,2,32,128]{3,2,1,0:T(8,128)(2,1)S(1)} all-to-all(bf16[32,2,32,128]{3,2,1,0:T(8,128)(2,1)S(1)} %shard_map.51), channel_id=1, replica_groups=mesh['replica'=8,'fsdp'=32] {'fsdp'}, dimensions={0} | all-to-all | bytes 1048576 | tf_op jit(solution)/shard_map/all_to_all | solution.py:244
  44.8 1.4 %shard_map.52 = (bf16[2,256,128]{2,1,0:T(8,128)(2,1)S(1)}, bf16[2,256,128]{2,1,0:T(8,128)(2,1)S(1)}, bf16[2,256,128]{2,1,0:T(8,128)(2,1)S(1)}, bf16[2,256,128]{2,1,0:T(8,128)(2,1)S(1)}, f32[2,8,128]{2,1,0:T(8,128)S(1)}) custom-call(s32[1]{0:T(128)} %bitcast.place, bf16[2,1024,1024]{2,1,0:T(8,128)(2,1)S(1)} %copy-done.1, ...), custom_call_target="tpu_custom_call" | custom-call | tf_op jit(solution)/shard_map/pallas_call | solution.py:247
  46.2 1.4 %collective-permute-start.5 = (bf16[2,256,128]{2,1,0:T(8,128)(2,1)S(1)}, bf16[2,256,128]{2,1,0:T(8,128)(2,1)S(1)}, u32[]{:S(2)}, u32[]{:S(2)}) collective-permute-start(bf16[2,256,128]{2,1,0:T(8,128)(2,1)S(1)} %get-tuple-element.21), channel_id=1, source_target_pairs={{0,128},{32,160},{64,192},{96,224},{128,0},{160,32},{192,64},{224,... | collective-permute-start | bytes 393224 | tf_op jit(solution)/shard_map/ppermute | solution.py:204
  47.6 1.5 %collective-permute-start.6 = (bf16[2,256,128]{2,1,0:T(8,128)(2,1)S(1)}, bf16[2,256,128]{2,1,0:T(8,128)(2,1)S(1)}, u32[]{:S(2)}, u32[]{:S(2)}) collective-permute-start(bf16[2,256,128]{2,1,0:T(8,128)(2,1)S(1)} %get-tuple-element.22), channel_id=1, source_target_pairs={{0,192},{32,96},{64,128},{96,32},{128,64},{160,224},{192,0},{224,1... | collective-permute-start | bytes 393224 | tf_op jit(solution)/shard_map/ppermute | solution.py:204
  49.6 3.9 %collective-permute-start.8 = (bf16[2,256,128]{2,1,0:T(8,128)(2,1)S(1)}, bf16[2,256,128]{2,1,0:T(8,128)(2,1)S(1)}, u32[]{:S(2)}, u32[]{:S(2)}) collective-permute-start(bf16[2,256,128]{2,1,0:T(8,128)(2,1)S(1)} %get-tuple-element.20.refs_0_), channel_id=1, source_target_pairs={{0,32},{32,0},{64,96},{96,64},{128,160},{160,128},{192,224},{224,1... | collective-permute-start | bytes 393224 | tf_op jit(solution)/shard_map/ppermute | solution.py:200
  53.4 2.8 %collective-permute-start.9 = (bf16[2,256,128]{2,1,0:T(8,128)(2,1)S(1)}, bf16[2,256,128]{2,1,0:T(8,128)(2,1)S(1)}, u32[]{:S(2)}, u32[]{:S(2)}) collective-permute-start(bf16[2,256,128]{2,1,0:T(8,128)(2,1)S(1)} %collective-permute-done.5.refs_1_), channel_id=1, source_target_pairs={{0,32},{32,0},{64,96},{96,64},{128,160},{160,128},{192,224},{224,1... | collective-permute-start | bytes 393224 | tf_op jit(solution)/shard_map/ppermute | solution.py:200
  56.2 1.8 %collective-permute-start.11 = (bf16[2,256,128]{2,1,0:T(8,128)(2,1)S(1)}, bf16[2,256,128]{2,1,0:T(8,128)(2,1)S(1)}, u32[]{:S(2)}, u32[]{:S(2)}) collective-permute-start(bf16[2,256,128]{2,1,0:T(8,128)(2,1)S(1)} %collective-permute-done.6.refs_2_), channel_id=1, source_target_pairs={{0,32},{32,0},{64,96},{96,64},{128,160},{160,128},{192,224},{224,1... | collective-permute-start | bytes 393224 | tf_op jit(solution)/shard_map/ppermute | solution.py:200
  60.5 23.0 %all_to_all.11.back_ref = bf16[32,8,1152]{2,1,0:T(8,128)(2,1)S(1)} all-to-all(bf16[32,8,1152]{2,1,0:T(8,128)(2,1)S(1)} %shard_map.53), channel_id=1, replica_groups=mesh['replica'=8,'fsdp'=32] {'fsdp'}, dimensions={0} | all-to-all | bytes 1179648 | tf_op jit(solution)/shard_map/all_to_all | solution.py:264
  84.4 2.1 %collective-permute-start.13 = (bf16[4,4,8,1152]{3,2,1,0:T(8,128)(2,1)S(1)}, bf16[4,4,8,1152]{3,2,1,0:T(8,128)(2,1)S(1)}, u32[]{:S(2)}, u32[]{:S(2)}) collective-permute-start(bf16[4,4,8,1152]{3,2,1,0:T(8,128)(2,1)S(1)} %shard_map.54.refs_0_), channel_id=1, source_target_pairs={{0,32},{32,0},{64,96},{96,64},{128,160},{160,128},{192,224},{224,1... | collective-permute-start | bytes 884744 | tf_op jit(solution)/shard_map/ppermute | solution.py:200
  86.5 1.2 %collective-permute-done.13.refs_4_ = bf16[4,4,8,1152]{3,2,1,0:T(8,128)(2,1)S(1)} collective-permute-done((bf16[4,4,8,1152]{3,2,1,0:T(8,128)(2,1)S(1)}, bf16[4,4,8,1152]{3,2,1,0:T(8,128)(2,1)S(1)}, u32[]{:S(2)}, u32[]{:S(2)}) %collective-permute-start.13) | collective-permute-done | bytes 294944 | tf_op jit(solution)/shard_map/ppermute | solution.py:200
  87.7 1.7 %collective-permute-start.14 = (bf16[4,4,8,1152]{3,2,1,0:T(8,128)(2,1)S(1)}, bf16[4,4,8,1152]{3,2,1,0:T(8,128)(2,1)S(1)}, u32[]{:S(2)}, u32[]{:S(2)}) collective-permute-start(bf16[4,4,8,1152]{3,2,1,0:T(8,128)(2,1)S(1)} %shard_map.54.refs_0_), channel_id=1, source_target_pairs={{0,64},{32,224},{64,0},{96,160},{128,192},{160,96},{192,128},{224,... | collective-permute-start | bytes 884744 | tf_op jit(solution)/shard_map/ppermute | solution.py:204
  89.4 3.4 %collective-permute-done.12.refs_1_ = bf16[4,4,8,1152]{3,2,1,0:T(8,128)(2,1)S(1)} collective-permute-done((bf16[4,4,8,1152]{3,2,1,0:T(8,128)(2,1)S(1)}, bf16[4,4,8,1152]{3,2,1,0:T(8,128)(2,1)S(1)}, u32[]{:S(2)}, u32[]{:S(2)}) %collective-permute-start.12) | collective-permute-done | bytes 294944 | tf_op jit(solution)/shard_map/ppermute | solution.py:204
  92.8 2.3 %collective-permute-start.15 = (bf16[4,4,8,1152]{3,2,1,0:T(8,128)(2,1)S(1)}, bf16[4,4,8,1152]{3,2,1,0:T(8,128)(2,1)S(1)}, u32[]{:S(2)}, u32[]{:S(2)}) collective-permute-start(bf16[4,4,8,1152]{3,2,1,0:T(8,128)(2,1)S(1)} %collective-permute-done.12.refs_1_), channel_id=1, source_target_pairs={{0,64},{32,224},{64,0},{96,160},{128,192},{160,96},{192,128},{224,... | collective-permute-start | bytes 884744 | tf_op jit(solution)/shard_map/ppermute | solution.py:204
  95.1 1.9 %collective-permute-start.17 = (bf16[4,4,8,1152]{3,2,1,0:T(8,128)(2,1)S(1)}, bf16[4,4,8,1152]{3,2,1,0:T(8,128)(2,1)S(1)}, u32[]{:S(2)}, u32[]{:S(2)}) collective-permute-start(bf16[4,4,8,1152]{3,2,1,0:T(8,128)(2,1)S(1)} %collective-permute-done.12.refs_1_), channel_id=1, source_target_pairs={{0,32},{32,0},{64,96},{96,64},{128,160},{160,128},{192,224},{224,1... | collective-permute-start | bytes 884744 | tf_op jit(solution)/shard_map/ppermute | solution.py:200
  97.1 3.0 %collective-permute-done.15.refs_3_ = bf16[4,4,8,1152]{3,2,1,0:T(8,128)(2,1)S(1)} collective-permute-done((bf16[4,4,8,1152]{3,2,1,0:T(8,128)(2,1)S(1)}, bf16[4,4,8,1152]{3,2,1,0:T(8,128)(2,1)S(1)}, u32[]{:S(2)}, u32[]{:S(2)}) %collective-permute-start.15) | collective-permute-done | bytes 294944 | tf_op jit(solution)/shard_map/ppermute | solution.py:204
  100.1 3.6 %collective-permute-start.18 = (bf16[4,4,8,1152]{3,2,1,0:T(8,128)(2,1)S(1)}, bf16[4,4,8,1152]{3,2,1,0:T(8,128)(2,1)S(1)}, u32[]{:S(2)}, u32[]{:S(2)}) collective-permute-start(bf16[4,4,8,1152]{3,2,1,0:T(8,128)(2,1)S(1)} %collective-permute-done.15.refs_3_), channel_id=1, source_target_pairs={{0,32},{32,0},{64,96},{96,64},{128,160},{160,128},{192,224},{224,1... | collective-permute-start | bytes 884744 | tf_op jit(solution)/shard_map/ppermute | solution.py:200
  103.8 1.2 %collective-permute-done.18.refs_7_ = bf16[4,4,8,1152]{3,2,1,0:T(8,128)(2,1)S(1)} collective-permute-done((bf16[4,4,8,1152]{3,2,1,0:T(8,128)(2,1)S(1)}, bf16[4,4,8,1152]{3,2,1,0:T(8,128)(2,1)S(1)}, u32[]{:S(2)}, u32[]{:S(2)}) %collective-permute-start.18) | collective-permute-done | bytes 294944 | tf_op jit(solution)/shard_map/ppermute | solution.py:200
  105.0 1.8 %shard_map.55 = bf16[4,32,8192]{2,1,0:T(8,128)(2,1)} custom-call(s32[1]{0:T(128)} %bitcast.place, bf16[4,4,8,1152]{3,2,1,0:T(8,128)(2,1)S(1)} %shard_map.54.refs_0_, bf16[4,4,8,1152]{3,2,1,0:T(8,128)(2,1)S(1)} %collective-permute-done.12.refs_1_, bf16[4,4,8,1152]{3,2,1,0:T(8,128)(2,1)S(1)} %collective-permute-done.14.refs_2_, ...), custom_call_target="tpu_custom_call" | custom-call | tf_op jit(solution)/shard_map/pallas_call | solution.py:276
  (34 shorter events, 7.8 us)
Async XLA Ops:
  0.0 6.2 %copy-start = (bf16[1,4,32,8192]{3,2,1,0:T(8,128)(2,1)S(1)}, bf16[1,4,32,8192]{3,2,1,0:T(8,128)(2,1)}, u32[]{:S(2)}) copy-start(bf16[1,4,32,8192]{3,2,1,0:T(8,128)(2,1)} %grads_ref.7) | copy-start | bytes 6291460
  1.3 18.0 %copy-start.3 = (s32[32]{0:T(128)S(1)}, s32[32]{0:T(128)}, u32[]{:S(2)}) copy-start(s32[32]{0:T(128)} %slot.3) | copy-start | bytes 388
  1.3 4.9 %collective-permute-start.1 = (bf16[2,4,8,32,128]{4,3,2,1,0:T(8,128)(2,1)S(1)}, bf16[2,4,8,32,128]{4,3,2,1,0:T(8,128)(2,1)S(1)}, u32[]{:S(2)}, u32[]{:S(2)}) collective-permute-start(bf16[2,4,8,32,128]{4,3,2,1,0:T(8,128)(2,1)S(1)} %shard_map.48), channel_id=1, source_target_pairs={{0,32},{32,0},{64,96},{96,64},{128,160},{160,128},{192,224},{224,1... | collective-permute-start | bytes 1572872 | tf_op jit(solution)/shard_map/ppermute | solution.py:200
  5.8 39.0 %copy-start.1 = (bf16[2,1024,1024]{2,1,0:T(8,128)(2,1)S(1)}, bf16[2,1024,1024]{2,1,0:T(8,128)(2,1)}, u32[]{:S(2)}) copy-start(bf16[2,1024,1024]{2,1,0:T(8,128)(2,1)} %left_ref.1) | copy-start | bytes 12582916
  5.8 2.1 %collective-permute-start = (bf16[2,4,8,32,128]{4,3,2,1,0:T(8,128)(2,1)S(1)}, bf16[2,4,8,32,128]{4,3,2,1,0:T(8,128)(2,1)S(1)}, u32[]{:S(2)}, u32[]{:S(2)}) collective-permute-start(bf16[2,4,8,32,128]{4,3,2,1,0:T(8,128)(2,1)S(1)} %shard_map.46), channel_id=1, source_target_pairs={{0,32},{32,0},{64,96},{96,64},{128,160},{160,128},{192,224},{224,1... | collective-permute-start | bytes 1572872 | tf_op jit(solution)/shard_map/ppermute | solution.py:200
  6.4 5.6 %collective-permute-start.3 = (bf16[4,8,32,128]{3,2,1,0:T(8,128)(2,1)S(1)}, bf16[4,8,32,128]{3,2,1,0:T(8,128)(2,1)S(1)}, u32[]{:S(2)}, u32[]{:S(2)}) collective-permute-start(bf16[4,8,32,128]{3,2,1,0:T(8,128)(2,1)S(1)} %get-tuple-element.19), channel_id=1, source_target_pairs={{0,192},{32,96},{64,128},{96,32},{128,64},{160,224},{192,0},{224,1... | collective-permute-start | bytes 786440 | tf_op jit(solution)/shard_map/ppermute | solution.py:204
  6.5 8.3 %collective-permute-start.2 = (bf16[4,8,32,128]{3,2,1,0:T(8,128)(2,1)S(1)}, bf16[4,8,32,128]{3,2,1,0:T(8,128)(2,1)S(1)}, u32[]{:S(2)}, u32[]{:S(2)}) collective-permute-start(bf16[4,8,32,128]{3,2,1,0:T(8,128)(2,1)S(1)} %get-tuple-element.17), channel_id=1, source_target_pairs={{0,192},{32,96},{64,128},{96,32},{128,64},{160,224},{192,0},{224,1... | collective-permute-start | bytes 786440 | tf_op jit(solution)/shard_map/ppermute | solution.py:204
  8.1 51.3 %copy-start.2 = (bf16[2,1024,1024]{2,1,0:T(8,128)(2,1)S(1)}, bf16[2,1024,1024]{2,1,0:T(8,128)(2,1)}, u32[]{:S(2)}) copy-start(bf16[2,1024,1024]{2,1,0:T(8,128)(2,1)} %refs_8_.1) | copy-start | bytes 12582916
  12.0 7.3 %collective-permute-start.4 = (bf16[4,8,32,128]{3,2,1,0:T(8,128)(2,1)S(1)}, bf16[4,8,32,128]{3,2,1,0:T(8,128)(2,1)S(1)}, u32[]{:S(2)}, u32[]{:S(2)}) collective-permute-start(bf16[4,8,32,128]{3,2,1,0:T(8,128)(2,1)S(1)} %shard_map.50), channel_id=1, source_target_pairs={{0,64},{32,224},{64,0},{96,160},{128,192},{160,96},{192,128},{224,... | collective-permute-start | bytes 786440 | tf_op jit(solution)/shard_map/ppermute | solution.py:204
  46.2 7.2 %collective-permute-start.5 = (bf16[2,256,128]{2,1,0:T(8,128)(2,1)S(1)}, bf16[2,256,128]{2,1,0:T(8,128)(2,1)S(1)}, u32[]{:S(2)}, u32[]{:S(2)}) collective-permute-start(bf16[2,256,128]{2,1,0:T(8,128)(2,1)S(1)} %get-tuple-element.21), channel_id=1, source_target_pairs={{0,128},{32,160},{64,192},{96,224},{128,0},{160,32},{192,64},{224,... | collective-permute-start | bytes 393224 | tf_op jit(solution)/shard_map/ppermute | solution.py:204
  47.6 8.6 %collective-permute-start.6 = (bf16[2,256,128]{2,1,0:T(8,128)(2,1)S(1)}, bf16[2,256,128]{2,1,0:T(8,128)(2,1)S(1)}, u32[]{:S(2)}, u32[]{:S(2)}) collective-permute-start(bf16[2,256,128]{2,1,0:T(8,128)(2,1)S(1)} %get-tuple-element.22), channel_id=1, source_target_pairs={{0,192},{32,96},{64,128},{96,32},{128,64},{160,224},{192,0},{224,1... | collective-permute-start | bytes 393224 | tf_op jit(solution)/shard_map/ppermute | solution.py:204
  49.1 8.9 %collective-permute-start.7 = (bf16[2,256,128]{2,1,0:T(8,128)(2,1)S(1)}, bf16[2,256,128]{2,1,0:T(8,128)(2,1)S(1)}, u32[]{:S(2)}, u32[]{:S(2)}) collective-permute-start(bf16[2,256,128]{2,1,0:T(8,128)(2,1)S(1)} %get-tuple-element.23), channel_id=1, source_target_pairs={{0,64},{32,224},{64,0},{96,160},{128,192},{160,96},{192,128},{224,... | collective-permute-start | bytes 393224 | tf_op jit(solution)/shard_map/ppermute | solution.py:204
  49.6 8.4 %collective-permute-start.8 = (bf16[2,256,128]{2,1,0:T(8,128)(2,1)S(1)}, bf16[2,256,128]{2,1,0:T(8,128)(2,1)S(1)}, u32[]{:S(2)}, u32[]{:S(2)}) collective-permute-start(bf16[2,256,128]{2,1,0:T(8,128)(2,1)S(1)} %get-tuple-element.20.refs_0_), channel_id=1, source_target_pairs={{0,32},{32,0},{64,96},{96,64},{128,160},{160,128},{192,224},{224,1... | collective-permute-start | bytes 393224 | tf_op jit(solution)/shard_map/ppermute | solution.py:200
  53.4 4.6 %collective-permute-start.9 = (bf16[2,256,128]{2,1,0:T(8,128)(2,1)S(1)}, bf16[2,256,128]{2,1,0:T(8,128)(2,1)S(1)}, u32[]{:S(2)}, u32[]{:S(2)}) collective-permute-start(bf16[2,256,128]{2,1,0:T(8,128)(2,1)S(1)} %collective-permute-done.5.refs_1_), channel_id=1, source_target_pairs={{0,32},{32,0},{64,96},{96,64},{128,160},{160,128},{192,224},{224,1... | collective-permute-start | bytes 393224 | tf_op jit(solution)/shard_map/ppermute | solution.py:200
  56.2 2.8 %collective-permute-start.11 = (bf16[2,256,128]{2,1,0:T(8,128)(2,1)S(1)}, bf16[2,256,128]{2,1,0:T(8,128)(2,1)S(1)}, u32[]{:S(2)}, u32[]{:S(2)}) collective-permute-start(bf16[2,256,128]{2,1,0:T(8,128)(2,1)S(1)} %collective-permute-done.6.refs_2_), channel_id=1, source_target_pairs={{0,32},{32,0},{64,96},{96,64},{128,160},{160,128},{192,224},{224,1... | collective-permute-start | bytes 393224 | tf_op jit(solution)/shard_map/ppermute | solution.py:200
  58.0 1.3 %collective-permute-start.10 = (bf16[2,256,128]{2,1,0:T(8,128)(2,1)S(1)}, bf16[2,256,128]{2,1,0:T(8,128)(2,1)S(1)}, u32[]{:S(2)}, u32[]{:S(2)}) collective-permute-start(bf16[2,256,128]{2,1,0:T(8,128)(2,1)S(1)} %collective-permute-done.7.refs_3_), channel_id=1, source_target_pairs={{0,32},{32,0},{64,96},{96,64},{128,160},{160,128},{192,224},{224,1... | collective-permute-start | bytes 393224 | tf_op jit(solution)/shard_map/ppermute | solution.py:200
  84.4 3.3 %collective-permute-start.13 = (bf16[4,4,8,1152]{3,2,1,0:T(8,128)(2,1)S(1)}, bf16[4,4,8,1152]{3,2,1,0:T(8,128)(2,1)S(1)}, u32[]{:S(2)}, u32[]{:S(2)}) collective-permute-start(bf16[4,4,8,1152]{3,2,1,0:T(8,128)(2,1)S(1)} %shard_map.54.refs_0_), channel_id=1, source_target_pairs={{0,32},{32,0},{64,96},{96,64},{128,160},{160,128},{192,224},{224,1... | collective-permute-start | bytes 884744 | tf_op jit(solution)/shard_map/ppermute | solution.py:200
  86.5 6.4 %collective-permute-start.12 = (bf16[4,4,8,1152]{3,2,1,0:T(8,128)(2,1)S(1)}, bf16[4,4,8,1152]{3,2,1,0:T(8,128)(2,1)S(1)}, u32[]{:S(2)}, u32[]{:S(2)}) collective-permute-start(bf16[4,4,8,1152]{3,2,1,0:T(8,128)(2,1)S(1)} %shard_map.54.refs_0_), channel_id=1, source_target_pairs={{0,192},{32,96},{64,128},{96,32},{128,64},{160,224},{192,0},{224,1... | collective-permute-start | bytes 884744 | tf_op jit(solution)/shard_map/ppermute | solution.py:204
  87.7 9.4 %collective-permute-start.14 = (bf16[4,4,8,1152]{3,2,1,0:T(8,128)(2,1)S(1)}, bf16[4,4,8,1152]{3,2,1,0:T(8,128)(2,1)S(1)}, u32[]{:S(2)}, u32[]{:S(2)}) collective-permute-start(bf16[4,4,8,1152]{3,2,1,0:T(8,128)(2,1)S(1)} %shard_map.54.refs_0_), channel_id=1, source_target_pairs={{0,64},{32,224},{64,0},{96,160},{128,192},{160,96},{192,128},{224,... | collective-permute-start | bytes 884744 | tf_op jit(solution)/shard_map/ppermute | solution.py:204
  92.8 7.3 %collective-permute-start.15 = (bf16[4,4,8,1152]{3,2,1,0:T(8,128)(2,1)S(1)}, bf16[4,4,8,1152]{3,2,1,0:T(8,128)(2,1)S(1)}, u32[]{:S(2)}, u32[]{:S(2)}) collective-permute-start(bf16[4,4,8,1152]{3,2,1,0:T(8,128)(2,1)S(1)} %collective-permute-done.12.refs_1_), channel_id=1, source_target_pairs={{0,64},{32,224},{64,0},{96,160},{128,192},{160,96},{192,128},{224,... | collective-permute-start | bytes 884744 | tf_op jit(solution)/shard_map/ppermute | solution.py:204
  95.1 8.7 %collective-permute-start.17 = (bf16[4,4,8,1152]{3,2,1,0:T(8,128)(2,1)S(1)}, bf16[4,4,8,1152]{3,2,1,0:T(8,128)(2,1)S(1)}, u32[]{:S(2)}, u32[]{:S(2)}) collective-permute-start(bf16[4,4,8,1152]{3,2,1,0:T(8,128)(2,1)S(1)} %collective-permute-done.12.refs_1_), channel_id=1, source_target_pairs={{0,32},{32,0},{64,96},{96,64},{128,160},{160,128},{192,224},{224,1... | collective-permute-start | bytes 884744 | tf_op jit(solution)/shard_map/ppermute | solution.py:200
  97.1 6.7 %collective-permute-start.16 = (bf16[4,4,8,1152]{3,2,1,0:T(8,128)(2,1)S(1)}, bf16[4,4,8,1152]{3,2,1,0:T(8,128)(2,1)S(1)}, u32[]{:S(2)}, u32[]{:S(2)}) collective-permute-start(bf16[4,4,8,1152]{3,2,1,0:T(8,128)(2,1)S(1)} %collective-permute-done.14.refs_2_), channel_id=1, source_target_pairs={{0,32},{32,0},{64,96},{96,64},{128,160},{160,128},{192,224},{224,1... | collective-permute-start | bytes 884744 | tf_op jit(solution)/shard_map/ppermute | solution.py:200
  100.1 4.9 %collective-permute-start.18 = (bf16[4,4,8,1152]{3,2,1,0:T(8,128)(2,1)S(1)}, bf16[4,4,8,1152]{3,2,1,0:T(8,128)(2,1)S(1)}, u32[]{:S(2)}, u32[]{:S(2)}) collective-permute-start(bf16[4,4,8,1152]{3,2,1,0:T(8,128)(2,1)S(1)} %collective-permute-done.15.refs_3_), channel_id=1, source_target_pairs={{0,32},{32,0},{64,96},{96,64},{128,160},{160,128},{192,224},{224,1... | collective-permute-start | bytes 884744 | tf_op jit(solution)/shard_map/ppermute | solution.py:200

commit v4 on v3

--- a/solution.py
+++ b/solution.py
@@ -19,7 +19,7 @@
 
 
 def masks(core):
-    return 0, 3 - 2 * core, 1 + 2 * core, 2
+    return 0, 1 + 2 * core, 3 - 2 * core, 2
 
 
 def chip(place, relative):
@@ -121,63 +121,71 @@
     back_ref[:, :, slots * width :] = jnp.broadcast_to(tail[None], (owners, part, LANES)).astype(bf16)
 
 
-def select_kernel(slot, back_ref, pair_ref):
-    mats, count, part, wide = pair_ref.shape
+def select_kernel(slot, back_ref, tiles_ref):
+    part, wide = back_ref.shape[1:]
     width = (wide - LANES) // 2
+    each = width // LANES
+    blocks = (tiles_ref.shape[0] - 2) // each
     lane = lax.broadcasted_iota(jnp.int32, (part, LANES), 1)
-    for m in range(mats):
-        for p in range(count):
-            tails = []
-            for h in range(2):
-                q = slot[2 * (m * count + p) + h]
-                s = lax.rem(q, 2)
-                columns = pl.ds(pl.multiple_of(s * width, width), width)
-                pair_ref[m, p, :, h * width : (h + 1) * width] = back_ref[q // 2, :, columns]
-                tail = back_ref[q // 2, :, 2 * width :].astype(f32)
-                tails.append(jnp.where(s == h, tail, pltpu.roll(tail, TERMS if h else LANES - TERMS, 1)))
-            pair_ref[m, p, :, 2 * width :] = jnp.where(lane < TERMS, tails[0], tails[1]).astype(bf16)
+    line = lax.broadcasted_iota(jnp.int32, (part, LANES), 0)
+    terms = [jnp.zeros((part, LANES), f32)] * 2
+    for b in range(blocks):
+        q, h, pair = slot[b], b % 2, b // 2
+        s = lax.rem(q, 2)
+        for t in range(each):
+            columns = pl.ds(pl.multiple_of(s * width + t * LANES, LANES), LANES)
+            tiles_ref[b * each + t] = back_ref[q // 2, :, columns]
+        tail = back_ref[q // 2, :, 2 * width :].astype(f32)
+        tail = jnp.where(s == h, tail, pltpu.roll(tail, TERMS if h else LANES - TERMS, 1))
+        here = (line == pair % part) & (lane >= TERMS * h) & (lane < TERMS * (h + 1))
+        terms[pair // part] = jnp.where(here, tail, terms[pair // part])
+    for n in range(2):
+        tiles_ref[blocks * each + n] = terms[n].astype(bf16)
 
 
 def finish_kernel(place, *refs, entries):
     own_refs, twin_refs = refs[:4], refs[4:8]
-    out_ref, ready, written = refs[8:]
-    mats, count, part, wide = own_refs[0].shape
-    width = (wide - LANES) // 2
-    lane = lax.broadcasted_iota(jnp.int32, (count, part, LANES), 2)
-
-    def emit(m, own, twin, ratios, core, odd):
-        couples = ((SELF, NEAR), (OPPOSITE, FAR)) if core else ((SELF, FAR), (OPPOSITE, NEAR))
+    out_ref, ready, ratios, written = refs[8:]
+    part = own_refs[0].shape[1]
+    mats, rows, full = ready.shape
+    blocks = ratios.shape[0]
+    each = (own_refs[0].shape[0] - 2) // blocks
+    count = blocks // mats
+    lane = lax.broadcasted_iota(jnp.int32, (part, LANES), 1)
+    for n in range(2):
+        tail = sum(ref[blocks * each + n].astype(f32) for ref in own_refs + twin_refs)
+        for h in range(2):
+            block_square, prec_square = [
+                jnp.sum(jnp.where((lane >= start) & (lane < start + 3), tail, 0.0), axis=1, keepdims=True)
+                for start in (TERMS * h, TERMS * h + 3)
+            ]
+            ratio = jnp.sqrt(block_square / entries + EPSILON) / jnp.sqrt(prec_square / entries + EPSILON)
+            for line in range(part):
+                ratios[2 * (n * part + line) + h] = jnp.broadcast_to(ratio[line : line + 1], (part, LANES))
+
+    def emit(m, core, odd):
+        couples = ((SELF, FAR), (OPPOSITE, NEAR)) if core else ((SELF, NEAR), (OPPOSITE, FAR))
         for couple in couples:
-            rows = pl.ds(pl.multiple_of(chip(place, couple[0]) // 2 * 2 * part, 2 * part), 2 * part)
-            for p in range(count):
-                for h in range(2):
-                    for pieces, c in ((own, core), (twin, 1 - core)):
+            at = pl.ds(pl.multiple_of(chip(place, couple[0]) // 2 * 2 * part, 2 * part), 2 * part)
+            for j in range(count):
+                b = m * count + j
+                for refs, c in ((own_refs, core), (twin_refs, 1 - core)):
+                    for t in range(each):
                         tiles = [
-                            pieces[k][p, :, h * width : (h + 1) * width].astype(f32) * ratios[h][p]
-                            for k in (couple[::-1] if odd else couple)
+                            refs[k][b * each + t].astype(f32) * ratios[b] for k in (couple[::-1] if odd else couple)
                         ]
-                        at = (2 * p + h) * 2 * width + c * width
-                        ready[m, rows, pl.ds(at, width)] = jnp.concatenate(tiles, 0).astype(bf16)
+                        columns = pl.ds(((2 * j + c) * each + t) * LANES, LANES)
+                        ready[m, at, columns] = jnp.concatenate(tiles, 0).astype(bf16)
 
     def write(m):
         return pltpu.make_async_copy(ready.at[m], out_ref.at[m], written.at[m])
 
     @pl.loop(0, mats)
     def _(m):
-        own = [ref.at[m] for ref in own_refs]
-        twin = [ref.at[m] for ref in twin_refs]
-        tail = sum(ref[:, :, 2 * width :].astype(f32) for ref in own + twin)
-        ratios = []
-        for h in range(2):
-            terms = [
-                jnp.sum(jnp.where((lane >= start) & (lane < start + 3), tail, 0.0), axis=2, keepdims=True)
-                for start in (TERMS * h, TERMS * h + 3)
-            ]
-            ratios.append(jnp.sqrt(terms[0] / entries + EPSILON) / jnp.sqrt(terms[1] / entries + EPSILON))
         for core in range(2):
             for odd in range(2):
                 here = (lax.rem(place[0], 2) == core) & (lax.rem(place[0] // 2, 2) == odd)
-                pl.when(here)(functools.partial(emit, m, own, twin, ratios, core, odd))
+                pl.when(here)(functools.partial(emit, m, core, odd))
         write(m).start()
 
     for m in range(mats):
@@ -263,22 +271,23 @@
     )(place, *halves, *handed, right_root, square)
     back = lax.all_to_all(back, "fsdp", 0, 0, tiled=True)
 
-    count = cols // 2
-    piece = (mats, count, part, wide)
-    mine = local(select_kernel, [smem, vmem], vmem, shape(piece, bf16))(block_slot, back)
+    tiles = blocks * (width // 2 // LANES) + 2
+    mine = local(select_kernel, [smem, vmem], vmem, shape((tiles, part, LANES), bf16))(block_slot, back)
     near = exchange(mine, NEAR)
-    shared = twin(mine)
-    later, shared = lax.optimization_barrier((mine, shared))
-    far = exchange(later, FAR)
+    far = exchange(mine, FAR)
     opposite = exchange(near, FAR)
     own = [mine, near, far, opposite]
-    other = [shared] + [twin(x) for x in (far, near, opposite)]
+    other = [twin(x) for x in (mine, far, near, opposite)]
     return local(
         functools.partial(finish_kernel, entries=height * width),
         [smem] + [vmem] * 8,
         pl.BlockSpec(memory_space=pl.ANY),
         shape((mats, rows, full), bf16),
-        [pltpu.VMEM((mats, rows, full), bf16), pltpu.SemaphoreType.DMA((mats,))],
+        [
+            pltpu.VMEM((mats, rows, full), bf16),
+            pltpu.VMEM((blocks, part, LANES), f32),
+            pltpu.SemaphoreType.DMA((mats,)),
+        ],
     )(place, *own, *other)
 
 

time: 107 us -> 104 us (0.972)
  waiting for transfers between devices: 20.5 us -> 17.3 us
  blocking collectives: 47.7 us -> 45 us
  starting transfers between devices: 29.7 us -> 32.2 us
    ppermute x10, starting transfers between devices: 19.6 us -> 24 us  [twin(): return lax.ppermute(x, 'replica', [(i, i ^ 1) for i in range(reps)])]
    ppermute x9, starting transfers between devices: 10 us -> 8.22 us  [exchange(): return lax.ppermute(x, 'replica', perm)]
    ppermute x10, waiting for transfers between devices: 3.99 us -> 2.39 us  [twin(): return lax.ppermute(x, 'replica', [(i, i ^ 1) for i in range(reps)])]
    ppermute x9, waiting for transfers between devices: 16.5 us -> 15 us  [exchange(): return lax.ppermute(x, 'replica', perm)]
    all_to_all x1, blocking collectives: 23 us -> 21.5 us  [on_device(): back = lax.all_to_all(back, 'fsdp', 0, 0, tiled=True)]
    all_to_all x1, blocking collectives: 24.7 us -> 23.5 us  [on_device(): incoming = lax.all_to_all(outgoing, 'fsdp', 0, 0, tiled=True)]
  transfers between devices with their start and end apart: 19 -> 19, of which waited for: 10 -> 7; matrix products, arithmetic and copies ran while one was open for 0% -> 0% of each run, Pallas kernels for 1% -> 1%
where the time goes in v4:
time: 104 us
  blocking collectives  45 us (43%)
  starting transfers between devices  32.2 us (31%)
  waiting for transfers between devices  17.3 us (17%)
  Pallas kernels  8.81 us (8%)
    ppermute x10, starting transfers between devices, twin(): return lax.ppermute(x, 'replica', [(i, i ^ 1) for i in range(reps)])  24 us
    all_to_all x1, blocking collectives, on_device(): incoming = lax.all_to_all(outgoing, 'fsdp', 0, 0, tiled=True)  23.5 us
    all_to_all x1, blocking collectives, on_device(): back = lax.all_to_all(back, 'fsdp', 0, 0, tiled=True)  21.5 us
    ppermute x9, waiting for transfers between devices, exchange(): return lax.ppermute(x, 'replica', perm)  15 us
    ppermute x9, starting transfers between devices, exchange(): return lax.ppermute(x, 'replica', perm)  8.22 us
    pallas_call x2, Pallas kernels, on_device(): local(functools.partial(send_kernel, kinds=kinds, **sizes), [smem, pl.Blo...  2.44 us
    ppermute x10, waiting for transfers between devices, twin(): return lax.ppermute(x, 'replica', [(i, i ^ 1) for i in range(reps)])  2.39 us
  transfers between devices with their start and end apart: 19, of which 7 were waited for; matrix products, arithmetic and copies ran while one was open for 0% of the time, Pallas kernels for 1%

profile of v4, /device:TPU:1, one launch (start us, length us, event | category | flops | bytes accessed | tf_op | source)
XLA Modules:
  0.0 103.7 jit_solution(9468966853191562473)
XLA Ops:
  0.0 1.3 %shard_map.48 = bf16[2,4,8,32,128]{4,3,2,1,0:T(8,128)(2,1)S(1)} custom-call(s32[1]{0:T(128)} %bitcast.place, bf16[1,4,32,8192]{3,2,1,0:T(8,128)(2,1)} %grads_ref.7), custom_call_target="tpu_custom_call" | custom-call | tf_op jit(solution)/shard_map/pallas_call | solution.py:231
  1.3 3.3 %collective-permute-start.1 = (bf16[2,4,8,32,128]{4,3,2,1,0:T(8,128)(2,1)S(1)}, bf16[2,4,8,32,128]{4,3,2,1,0:T(8,128)(2,1)S(1)}, u32[]{:S(2)}, u32[]{:S(2)}) collective-permute-start(bf16[2,4,8,32,128]{4,3,2,1,0:T(8,128)(2,1)S(1)} %shard_map.48), channel_id=1, source_target_pairs={{0,32},{32,0},{64,96},{96,64},{128,160},{160,128},{192,224},{224,1... | collective-permute-start | bytes 1572872 | tf_op jit(solution)/shard_map/ppermute | solution.py:208
  4.6 1.1 %shard_map.46 = bf16[2,4,8,32,128]{4,3,2,1,0:T(8,128)(2,1)S(1)} custom-call(s32[1]{0:T(128)} %bitcast.place, bf16[1,4,32,8192]{3,2,1,0:T(8,128)(2,1)} %grads_ref.7), custom_call_target="tpu_custom_call" | custom-call | tf_op jit(solution)/shard_map/pallas_call | solution.py:231
  6.4 1.1 %collective-permute-start.3 = (bf16[4,8,32,128]{3,2,1,0:T(8,128)(2,1)S(1)}, bf16[4,8,32,128]{3,2,1,0:T(8,128)(2,1)S(1)}, u32[]{:S(2)}, u32[]{:S(2)}) collective-permute-start(bf16[4,8,32,128]{3,2,1,0:T(8,128)(2,1)S(1)} %get-tuple-element.17), channel_id=1, source_target_pairs={{0,64},{32,224},{64,0},{96,160},{128,192},{160,96},{192,128},{224,... | collective-permute-start | bytes 786440 | tf_op jit(solution)/shard_map/ppermute | solution.py:212
  7.4 1.7 %collective-permute-start.2 = (bf16[4,8,32,128]{3,2,1,0:T(8,128)(2,1)S(1)}, bf16[4,8,32,128]{3,2,1,0:T(8,128)(2,1)S(1)}, u32[]{:S(2)}, u32[]{:S(2)}) collective-permute-start(bf16[4,8,32,128]{3,2,1,0:T(8,128)(2,1)S(1)} %get-tuple-element.15), channel_id=1, source_target_pairs={{0,64},{32,224},{64,0},{96,160},{128,192},{160,96},{192,128},{224,... | collective-permute-start | bytes 786440 | tf_op jit(solution)/shard_map/ppermute | solution.py:212
  9.3 3.6 %collective-permute-done.3.y_ref = bf16[4,8,32,128]{3,2,1,0:T(8,128)(2,1)S(1)} collective-permute-done((bf16[4,8,32,128]{3,2,1,0:T(8,128)(2,1)S(1)}, bf16[4,8,32,128]{3,2,1,0:T(8,128)(2,1)S(1)}, u32[]{:S(2)}, u32[]{:S(2)}) %collective-permute-start.3) | collective-permute-done | bytes 262176 | tf_op jit(solution)/shard_map/ppermute | solution.py:212
  13.0 2.6 %collective-permute-done.2.refs_1_ = bf16[4,8,32,128]{3,2,1,0:T(8,128)(2,1)S(1)} collective-permute-done((bf16[4,8,32,128]{3,2,1,0:T(8,128)(2,1)S(1)}, bf16[4,8,32,128]{3,2,1,0:T(8,128)(2,1)S(1)}, u32[]{:S(2)}, u32[]{:S(2)}) %collective-permute-start.2) | collective-permute-done | bytes 262176 | tf_op jit(solution)/shard_map/ppermute | solution.py:212
  15.7 2.9 %collective-permute-done.4.refs_2_ = bf16[4,8,32,128]{3,2,1,0:T(8,128)(2,1)S(1)} collective-permute-done((bf16[4,8,32,128]{3,2,1,0:T(8,128)(2,1)S(1)}, bf16[4,8,32,128]{3,2,1,0:T(8,128)(2,1)S(1)}, u32[]{:S(2)}, u32[]{:S(2)}) %collective-permute-start.4) | collective-permute-done | bytes 262176 | tf_op jit(solution)/shard_map/ppermute | solution.py:212
  19.3 23.5 %all_to_all.10.block_ref = bf16[32,2,32,128]{3,2,1,0:T(8,128)(2,1)S(1)} all-to-all(bf16[32,2,32,128]{3,2,1,0:T(8,128)(2,1)S(1)} %shard_map.51), channel_id=1, replica_groups=mesh['replica'=8,'fsdp'=32] {'fsdp'}, dimensions={0} | all-to-all | bytes 1048576 | tf_op jit(solution)/shard_map/all_to_all | solution.py:252
  42.8 1.4 %shard_map.52 = (bf16[2,256,128]{2,1,0:T(8,128)(2,1)S(1)}, bf16[2,256,128]{2,1,0:T(8,128)(2,1)S(1)}, bf16[2,256,128]{2,1,0:T(8,128)(2,1)S(1)}, bf16[2,256,128]{2,1,0:T(8,128)(2,1)S(1)}, f32[2,8,128]{2,1,0:T(8,128)S(1)}) custom-call(s32[1]{0:T(128)} %bitcast.place, bf16[2,1024,1024]{2,1,0:T(8,128)(2,1)S(1)} %copy-done.1, ...), custom_call_target="tpu_custom_call" | custom-call | tf_op jit(solution)/shard_map/pallas_call | solution.py:255
  44.2 3.9 %collective-permute-start.5 = (bf16[2,256,128]{2,1,0:T(8,128)(2,1)S(1)}, bf16[2,256,128]{2,1,0:T(8,128)(2,1)S(1)}, u32[]{:S(2)}, u32[]{:S(2)}) collective-permute-start(bf16[2,256,128]{2,1,0:T(8,128)(2,1)S(1)} %get-tuple-element.19), channel_id=1, source_target_pairs={{0,128},{32,160},{64,192},{96,224},{128,0},{160,32},{192,64},{224,... | collective-permute-start | bytes 393224 | tf_op jit(solution)/shard_map/ppermute | solution.py:212
  48.1 0.8 collective-permute-start.6
  48.9 4.2 %collective-permute-start.8 = (bf16[2,256,128]{2,1,0:T(8,128)(2,1)S(1)}, bf16[2,256,128]{2,1,0:T(8,128)(2,1)S(1)}, u32[]{:S(2)}, u32[]{:S(2)}) collective-permute-start(bf16[2,256,128]{2,1,0:T(8,128)(2,1)S(1)} %get-tuple-element.18.refs_0_), channel_id=1, source_target_pairs={{0,32},{32,0},{64,96},{96,64},{128,160},{160,128},{192,224},{224,1... | collective-permute-start | bytes 393224 | tf_op jit(solution)/shard_map/ppermute | solution.py:208
  53.1 3.4 %collective-permute-start.9 = (bf16[2,256,128]{2,1,0:T(8,128)(2,1)S(1)}, bf16[2,256,128]{2,1,0:T(8,128)(2,1)S(1)}, u32[]{:S(2)}, u32[]{:S(2)}) collective-permute-start(bf16[2,256,128]{2,1,0:T(8,128)(2,1)S(1)} %collective-permute-done.5.refs_1_), channel_id=1, source_target_pairs={{0,32},{32,0},{64,96},{96,64},{128,160},{160,128},{192,224},{224,1... | collective-permute-start | bytes 393224 | tf_op jit(solution)/shard_map/ppermute | solution.py:208
  57.2 1.8 %collective-permute-start.10 = (bf16[2,256,128]{2,1,0:T(8,128)(2,1)S(1)}, bf16[2,256,128]{2,1,0:T(8,128)(2,1)S(1)}, u32[]{:S(2)}, u32[]{:S(2)}) collective-permute-start(bf16[2,256,128]{2,1,0:T(8,128)(2,1)S(1)} %collective-permute-done.7.refs_3_), channel_id=1, source_target_pairs={{0,32},{32,0},{64,96},{96,64},{128,160},{160,128},{192,224},{224,1... | collective-permute-start | bytes 393224 | tf_op jit(solution)/shard_map/ppermute | solution.py:208
  59.0 1.0 collective-permute-done.10.refs_6_
  60.0 1.1 %shard_map.53 = bf16[32,8,1152]{2,1,0:T(8,128)(2,1)S(1)} custom-call(s32[1]{0:T(128)} %bitcast.place, bf16[2,256,128]{2,1,0:T(8,128)(2,1)S(1)} %get-tuple-element.18.refs_0_, bf16[2,256,128]{2,1,0:T(8,128)(2,1)S(1)} %collective-permute-done.5.refs_1_, bf16[2,256,128]{2,1,0:T(8,128)(2,1)S(1)} %collective-permute-done.6.refs_2_, ...), custom_call_target="tpu_custom_call" | custom-call | tf_op jit(solution)/shard_map/pallas_call | solution.py:265
  61.1 21.5 %all_to_all.11.back_ref = bf16[32,8,1152]{2,1,0:T(8,128)(2,1)S(1)} all-to-all(bf16[32,8,1152]{2,1,0:T(8,128)(2,1)S(1)} %shard_map.53), channel_id=1, replica_groups=mesh['replica'=8,'fsdp'=32] {'fsdp'}, dimensions={0} | all-to-all | bytes 1179648 | tf_op jit(solution)/shard_map/all_to_all | solution.py:272
  82.7 1.0 shard_map.54.refs_0_
  84.3 5.9 %collective-permute-done.12.refs_1_ = bf16[130,8,128]{2,1,0:T(8,128)(2,1)S(1)} collective-permute-done((bf16[130,8,128]{2,1,0:T(8,128)(2,1)S(1)}, bf16[130,8,128]{2,1,0:T(8,128)(2,1)S(1)}, u32[]{:S(2)}, u32[]{:S(2)}) %collective-permute-start.12) | collective-permute-done | bytes 266272 | tf_op jit(solution)/shard_map/ppermute | solution.py:212
  90.2 5.9 %collective-permute-start.15 = (bf16[130,8,128]{2,1,0:T(8,128)(2,1)S(1)}, bf16[130,8,128]{2,1,0:T(8,128)(2,1)S(1)}, u32[]{:S(2)}, u32[]{:S(2)}) collective-permute-start(bf16[130,8,128]{2,1,0:T(8,128)(2,1)S(1)} %shard_map.54.refs_0_), channel_id=1, source_target_pairs={{0,32},{32,0},{64,96},{96,64},{128,160},{160,128},{192,224},{224,1... | collective-permute-start | bytes 798728 | tf_op jit(solution)/shard_map/ppermute | solution.py:208
  96.6 4.1 %collective-permute-start.18 = (bf16[130,8,128]{2,1,0:T(8,128)(2,1)S(1)}, bf16[130,8,128]{2,1,0:T(8,128)(2,1)S(1)}, u32[]{:S(2)}, u32[]{:S(2)}) collective-permute-start(bf16[130,8,128]{2,1,0:T(8,128)(2,1)S(1)} %collective-permute-done.14.refs_3_), channel_id=1, source_target_pairs={{0,32},{32,0},{64,96},{96,64},{128,160},{160,128},{192,224},{224,1... | collective-permute-start | bytes 798728 | tf_op jit(solution)/shard_map/ppermute | solution.py:208
  100.7 1.2 %collective-permute-done.18.refs_7_ = bf16[130,8,128]{2,1,0:T(8,128)(2,1)S(1)} collective-permute-done((bf16[130,8,128]{2,1,0:T(8,128)(2,1)S(1)}, bf16[130,8,128]{2,1,0:T(8,128)(2,1)S(1)}, u32[]{:S(2)}, u32[]{:S(2)}) %collective-permute-start.18) | collective-permute-done | bytes 266272 | tf_op jit(solution)/shard_map/ppermute | solution.py:208
  101.9 1.7 %shard_map.55 = bf16[4,32,8192]{2,1,0:T(8,128)(2,1)} custom-call(s32[1]{0:T(128)} %bitcast.place, bf16[130,8,128]{2,1,0:T(8,128)(2,1)S(1)} %shard_map.54.refs_0_, bf16[130,8,128]{2,1,0:T(8,128)(2,1)S(1)} %collective-permute-done.12.refs_1_, bf16[130,8,128]{2,1,0:T(8,128)(2,1)S(1)} %collective-permute-done.13.refs_2_, ...), custom_call_target="tpu_custom_call" | custom-call | tf_op jit(solution)/shard_map/pallas_call | solution.py:281
  (34 shorter events, 3.6 us)
Async XLA Ops:
  0.0 6.2 %copy-start = (bf16[1,4,32,8192]{3,2,1,0:T(8,128)(2,1)S(1)}, bf16[1,4,32,8192]{3,2,1,0:T(8,128)(2,1)}, u32[]{:S(2)}) copy-start(bf16[1,4,32,8192]{3,2,1,0:T(8,128)(2,1)} %grads_ref.7) | copy-start | bytes 6291460
  1.3 17.2 %copy-start.3 = (s32[32]{0:T(128)S(1)}, s32[32]{0:T(128)}, u32[]{:S(2)}) copy-start(s32[32]{0:T(128)} %slot.3) | copy-start | bytes 388
  1.3 4.9 %collective-permute-start.1 = (bf16[2,4,8,32,128]{4,3,2,1,0:T(8,128)(2,1)S(1)}, bf16[2,4,8,32,128]{4,3,2,1,0:T(8,128)(2,1)S(1)}, u32[]{:S(2)}, u32[]{:S(2)}) collective-permute-start(bf16[2,4,8,32,128]{4,3,2,1,0:T(8,128)(2,1)S(1)} %shard_map.48), channel_id=1, source_target_pairs={{0,32},{32,0},{64,96},{96,64},{128,160},{160,128},{192,224},{224,1... | collective-permute-start | bytes 1572872 | tf_op jit(solution)/shard_map/ppermute | solution.py:208
  5.8 37.0 %copy-start.1 = (bf16[2,1024,1024]{2,1,0:T(8,128)(2,1)S(1)}, bf16[2,1024,1024]{2,1,0:T(8,128)(2,1)}, u32[]{:S(2)}) copy-start(bf16[2,1024,1024]{2,1,0:T(8,128)(2,1)} %left_ref.1) | copy-start | bytes 12582916
  5.8 3.3 %collective-permute-start = (bf16[2,4,8,32,128]{4,3,2,1,0:T(8,128)(2,1)S(1)}, bf16[2,4,8,32,128]{4,3,2,1,0:T(8,128)(2,1)S(1)}, u32[]{:S(2)}, u32[]{:S(2)}) collective-permute-start(bf16[2,4,8,32,128]{4,3,2,1,0:T(8,128)(2,1)S(1)} %shard_map.46), channel_id=1, source_target_pairs={{0,32},{32,0},{64,96},{96,64},{128,160},{160,128},{192,224},{224,1... | collective-permute-start | bytes 1572872 | tf_op jit(solution)/shard_map/ppermute | solution.py:208
  6.4 6.5 %collective-permute-start.3 = (bf16[4,8,32,128]{3,2,1,0:T(8,128)(2,1)S(1)}, bf16[4,8,32,128]{3,2,1,0:T(8,128)(2,1)S(1)}, u32[]{:S(2)}, u32[]{:S(2)}) collective-permute-start(bf16[4,8,32,128]{3,2,1,0:T(8,128)(2,1)S(1)} %get-tuple-element.17), channel_id=1, source_target_pairs={{0,64},{32,224},{64,0},{96,160},{128,192},{160,96},{192,128},{224,... | collective-permute-start | bytes 786440 | tf_op jit(solution)/shard_map/ppermute | solution.py:212
  7.4 8.2 %collective-permute-start.2 = (bf16[4,8,32,128]{3,2,1,0:T(8,128)(2,1)S(1)}, bf16[4,8,32,128]{3,2,1,0:T(8,128)(2,1)S(1)}, u32[]{:S(2)}, u32[]{:S(2)}) collective-permute-start(bf16[4,8,32,128]{3,2,1,0:T(8,128)(2,1)S(1)} %get-tuple-element.15), channel_id=1, source_target_pairs={{0,64},{32,224},{64,0},{96,160},{128,192},{160,96},{192,128},{224,... | collective-permute-start | bytes 786440 | tf_op jit(solution)/shard_map/ppermute | solution.py:212
  9.3 50.7 %copy-start.2 = (bf16[2,1024,1024]{2,1,0:T(8,128)(2,1)S(1)}, bf16[2,1024,1024]{2,1,0:T(8,128)(2,1)}, u32[]{:S(2)}) copy-start(bf16[2,1024,1024]{2,1,0:T(8,128)(2,1)} %refs_8_.1) | copy-start | bytes 12582916
  12.9 5.6 %collective-permute-start.4 = (bf16[4,8,32,128]{3,2,1,0:T(8,128)(2,1)S(1)}, bf16[4,8,32,128]{3,2,1,0:T(8,128)(2,1)S(1)}, u32[]{:S(2)}, u32[]{:S(2)}) collective-permute-start(bf16[4,8,32,128]{3,2,1,0:T(8,128)(2,1)S(1)} %shard_map.50), channel_id=1, source_target_pairs={{0,192},{32,96},{64,128},{96,32},{128,64},{160,224},{192,0},{224,1... | collective-permute-start | bytes 786440 | tf_op jit(solution)/shard_map/ppermute | solution.py:212
  44.2 8.8 %collective-permute-start.5 = (bf16[2,256,128]{2,1,0:T(8,128)(2,1)S(1)}, bf16[2,256,128]{2,1,0:T(8,128)(2,1)S(1)}, u32[]{:S(2)}, u32[]{:S(2)}) collective-permute-start(bf16[2,256,128]{2,1,0:T(8,128)(2,1)S(1)} %get-tuple-element.19), channel_id=1, source_target_pairs={{0,128},{32,160},{64,192},{96,224},{128,0},{160,32},{192,64},{224,... | collective-permute-start | bytes 393224 | tf_op jit(solution)/shard_map/ppermute | solution.py:212
  48.1 8.3 %collective-permute-start.6 = (bf16[2,256,128]{2,1,0:T(8,128)(2,1)S(1)}, bf16[2,256,128]{2,1,0:T(8,128)(2,1)S(1)}, u32[]{:S(2)}, u32[]{:S(2)}) collective-permute-start(bf16[2,256,128]{2,1,0:T(8,128)(2,1)S(1)} %get-tuple-element.20), channel_id=1, source_target_pairs={{0,64},{32,224},{64,0},{96,160},{128,192},{160,96},{192,128},{224,... | collective-permute-start | bytes 393224 | tf_op jit(solution)/shard_map/ppermute | solution.py:212
  48.9 8.2 %collective-permute-start.7 = (bf16[2,256,128]{2,1,0:T(8,128)(2,1)S(1)}, bf16[2,256,128]{2,1,0:T(8,128)(2,1)S(1)}, u32[]{:S(2)}, u32[]{:S(2)}) collective-permute-start(bf16[2,256,128]{2,1,0:T(8,128)(2,1)S(1)} %get-tuple-element.21), channel_id=1, source_target_pairs={{0,192},{32,96},{64,128},{96,32},{128,64},{160,224},{192,0},{224,1... | collective-permute-start | bytes 393224 | tf_op jit(solution)/shard_map/ppermute | solution.py:212
  48.9 10.1 %collective-permute-start.8 = (bf16[2,256,128]{2,1,0:T(8,128)(2,1)S(1)}, bf16[2,256,128]{2,1,0:T(8,128)(2,1)S(1)}, u32[]{:S(2)}, u32[]{:S(2)}) collective-permute-start(bf16[2,256,128]{2,1,0:T(8,128)(2,1)S(1)} %get-tuple-element.18.refs_0_), channel_id=1, source_target_pairs={{0,32},{32,0},{64,96},{96,64},{128,160},{160,128},{192,224},{224,1... | collective-permute-start | bytes 393224 | tf_op jit(solution)/shard_map/ppermute | solution.py:208
  53.1 5.9 %collective-permute-start.9 = (bf16[2,256,128]{2,1,0:T(8,128)(2,1)S(1)}, bf16[2,256,128]{2,1,0:T(8,128)(2,1)S(1)}, u32[]{:S(2)}, u32[]{:S(2)}) collective-permute-start(bf16[2,256,128]{2,1,0:T(8,128)(2,1)S(1)} %collective-permute-done.5.refs_1_), channel_id=1, source_target_pairs={{0,32},{32,0},{64,96},{96,64},{128,160},{160,128},{192,224},{224,1... | collective-permute-start | bytes 393224 | tf_op jit(solution)/shard_map/ppermute | solution.py:208
  56.5 2.5 %collective-permute-start.11 = (bf16[2,256,128]{2,1,0:T(8,128)(2,1)S(1)}, bf16[2,256,128]{2,1,0:T(8,128)(2,1)S(1)}, u32[]{:S(2)}, u32[]{:S(2)}) collective-permute-start(bf16[2,256,128]{2,1,0:T(8,128)(2,1)S(1)} %collective-permute-done.6.refs_2_), channel_id=1, source_target_pairs={{0,32},{32,0},{64,96},{96,64},{128,160},{160,128},{192,224},{224,1... | collective-permute-start | bytes 393224 | tf_op jit(solution)/shard_map/ppermute | solution.py:208
  57.2 2.8 %collective-permute-start.10 = (bf16[2,256,128]{2,1,0:T(8,128)(2,1)S(1)}, bf16[2,256,128]{2,1,0:T(8,128)(2,1)S(1)}, u32[]{:S(2)}, u32[]{:S(2)}) collective-permute-start(bf16[2,256,128]{2,1,0:T(8,128)(2,1)S(1)} %collective-permute-done.7.refs_3_), channel_id=1, source_target_pairs={{0,32},{32,0},{64,96},{96,64},{128,160},{160,128},{192,224},{224,1... | collective-permute-start | bytes 393224 | tf_op jit(solution)/shard_map/ppermute | solution.py:208
  83.6 6.5 %collective-permute-start.12 = (bf16[130,8,128]{2,1,0:T(8,128)(2,1)S(1)}, bf16[130,8,128]{2,1,0:T(8,128)(2,1)S(1)}, u32[]{:S(2)}, u32[]{:S(2)}) collective-permute-start(bf16[130,8,128]{2,1,0:T(8,128)(2,1)S(1)} %shard_map.54.refs_0_), channel_id=1, source_target_pairs={{0,64},{32,224},{64,0},{96,160},{128,192},{160,96},{192,128},{224,... | collective-permute-start | bytes 798728 | tf_op jit(solution)/shard_map/ppermute | solution.py:212
  84.3 11.8 %collective-permute-start.13 = (bf16[130,8,128]{2,1,0:T(8,128)(2,1)S(1)}, bf16[130,8,128]{2,1,0:T(8,128)(2,1)S(1)}, u32[]{:S(2)}, u32[]{:S(2)}) collective-permute-start(bf16[130,8,128]{2,1,0:T(8,128)(2,1)S(1)} %shard_map.54.refs_0_), channel_id=1, source_target_pairs={{0,192},{32,96},{64,128},{96,32},{128,64},{160,224},{192,0},{224,1... | collective-permute-start | bytes 798728 | tf_op jit(solution)/shard_map/ppermute | solution.py:212
  90.2 6.4 %collective-permute-start.14 = (bf16[130,8,128]{2,1,0:T(8,128)(2,1)S(1)}, bf16[130,8,128]{2,1,0:T(8,128)(2,1)S(1)}, u32[]{:S(2)}, u32[]{:S(2)}) collective-permute-start(bf16[130,8,128]{2,1,0:T(8,128)(2,1)S(1)} %collective-permute-done.12.refs_1_), channel_id=1, source_target_pairs={{0,192},{32,96},{64,128},{96,32},{128,64},{160,224},{192,0},{224,1... | collective-permute-start | bytes 798728 | tf_op jit(solution)/shard_map/ppermute | solution.py:212
  90.2 10.5 %collective-permute-start.15 = (bf16[130,8,128]{2,1,0:T(8,128)(2,1)S(1)}, bf16[130,8,128]{2,1,0:T(8,128)(2,1)S(1)}, u32[]{:S(2)}, u32[]{:S(2)}) collective-permute-start(bf16[130,8,128]{2,1,0:T(8,128)(2,1)S(1)} %shard_map.54.refs_0_), channel_id=1, source_target_pairs={{0,32},{32,0},{64,96},{96,64},{128,160},{160,128},{192,224},{224,1... | collective-permute-start | bytes 798728 | tf_op jit(solution)/shard_map/ppermute | solution.py:208
  96.1 4.6 %collective-permute-start.17 = (bf16[130,8,128]{2,1,0:T(8,128)(2,1)S(1)}, bf16[130,8,128]{2,1,0:T(8,128)(2,1)S(1)}, u32[]{:S(2)}, u32[]{:S(2)}) collective-permute-start(bf16[130,8,128]{2,1,0:T(8,128)(2,1)S(1)} %collective-permute-done.12.refs_1_), channel_id=1, source_target_pairs={{0,32},{32,0},{64,96},{96,64},{128,160},{160,128},{192,224},{224,1... | collective-permute-start | bytes 798728 | tf_op jit(solution)/shard_map/ppermute | solution.py:208
  96.1 4.6 %collective-permute-start.16 = (bf16[130,8,128]{2,1,0:T(8,128)(2,1)S(1)}, bf16[130,8,128]{2,1,0:T(8,128)(2,1)S(1)}, u32[]{:S(2)}, u32[]{:S(2)}) collective-permute-start(bf16[130,8,128]{2,1,0:T(8,128)(2,1)S(1)} %collective-permute-done.13.refs_2_), channel_id=1, source_target_pairs={{0,32},{32,0},{64,96},{96,64},{128,160},{160,128},{192,224},{224,1... | collective-permute-start | bytes 798728 | tf_op jit(solution)/shard_map/ppermute | solution.py:208
  96.6 5.3 %collective-permute-start.18 = (bf16[130,8,128]{2,1,0:T(8,128)(2,1)S(1)}, bf16[130,8,128]{2,1,0:T(8,128)(2,1)S(1)}, u32[]{:S(2)}, u32[]{:S(2)}) collective-permute-start(bf16[130,8,128]{2,1,0:T(8,128)(2,1)S(1)} %collective-permute-done.14.refs_3_), channel_id=1, source_target_pairs={{0,32},{32,0},{64,96},{96,64},{128,160},{160,128},{192,224},{224,1... | collective-permute-start | bytes 798728 | tf_op jit(solution)/shard_map/ppermute | solution.py:208

commit v5 on v4

--- a/solution.py
+++ b/solution.py
@@ -121,39 +121,58 @@
     back_ref[:, :, slots * width :] = jnp.broadcast_to(tail[None], (owners, part, LANES)).astype(bf16)
 
 
-def select_kernel(slot, back_ref, tiles_ref):
+def select_kernel(slot, back_ref, tiles_ref, *, first):
     part, wide = back_ref.shape[1:]
     width = (wide - LANES) // 2
     each = width // LANES
-    blocks = (tiles_ref.shape[0] - 2) // each
+    blocks = (tiles_ref.shape[0] - 1) // each
     lane = lax.broadcasted_iota(jnp.int32, (part, LANES), 1)
     line = lax.broadcasted_iota(jnp.int32, (part, LANES), 0)
-    terms = [jnp.zeros((part, LANES), f32)] * 2
+    terms = jnp.zeros((part, LANES), f32)
     for b in range(blocks):
-        q, h, pair = slot[b], b % 2, b // 2
+        q, h = slot[first + b], b % 2
         s = lax.rem(q, 2)
         for t in range(each):
             columns = pl.ds(pl.multiple_of(s * width + t * LANES, LANES), LANES)
             tiles_ref[b * each + t] = back_ref[q // 2, :, columns]
         tail = back_ref[q // 2, :, 2 * width :].astype(f32)
         tail = jnp.where(s == h, tail, pltpu.roll(tail, TERMS if h else LANES - TERMS, 1))
-        here = (line == pair % part) & (lane >= TERMS * h) & (lane < TERMS * (h + 1))
-        terms[pair // part] = jnp.where(here, tail, terms[pair // part])
+        here = (line == b // 2) & (lane >= TERMS * h) & (lane < TERMS * (h + 1))
+        terms = jnp.where(here, tail, terms)
+    tiles_ref[blocks * each] = terms.astype(bf16)
+
+
+def finish_kernel(place, *refs, entries):
+    out_ref, ready, ratios, written = refs[16:]
+    part = refs[0].shape[1]
+    mats, rows, full = ready.shape
+    blocks = ratios.shape[0] // 2
+    each = (refs[0].shape[0] - 1) // blocks
+    some = mats // 2
+    count = blocks // some
+    lane = lax.broadcasted_iota(jnp.int32, (part, LANES), 1)
+
+    def emit(m, row, own_refs, twin_refs, core, odd):
+        couples = ((SELF, FAR), (OPPOSITE, NEAR)) if core else ((SELF, NEAR), (OPPOSITE, FAR))
+        for couple in couples:
+            at = pl.ds(pl.multiple_of(chip(place, couple[0]) // 2 * 2 * part, 2 * part), 2 * part)
+            for j in range(count):
+                b = m * count + j
+                for found, c in ((own_refs, core), (twin_refs, 1 - core)):
+                    for t in range(each):
+                        tiles = [
+                            found[k][b * each + t].astype(f32) * ratios[row * count + j]
+                            for k in (couple[::-1] if odd else couple)
+                        ]
+                        columns = pl.ds(((2 * j + c) * each + t) * LANES, LANES)
+                        ready[row, at, columns] = jnp.concatenate(tiles, 0).astype(bf16)
+
+    def write(m):
+        return pltpu.make_async_copy(ready.at[m], out_ref.at[m], written.at[m])
+
     for n in range(2):
-        tiles_ref[blocks * each + n] = terms[n].astype(bf16)
-
-
-def finish_kernel(place, *refs, entries):
-    own_refs, twin_refs = refs[:4], refs[4:8]
-    out_ref, ready, ratios, written = refs[8:]
-    part = own_refs[0].shape[1]
-    mats, rows, full = ready.shape
-    blocks = ratios.shape[0]
-    each = (own_refs[0].shape[0] - 2) // blocks
-    count = blocks // mats
-    lane = lax.broadcasted_iota(jnp.int32, (part, LANES), 1)
-    for n in range(2):
-        tail = sum(ref[blocks * each + n].astype(f32) for ref in own_refs + twin_refs)
+        own_refs, twin_refs = refs[8 * n : 8 * n + 4], refs[8 * n + 4 : 8 * n + 8]
+        tail = sum(ref[blocks * each].astype(f32) for ref in own_refs + twin_refs)
         for h in range(2):
             block_square, prec_square = [
                 jnp.sum(jnp.where((lane >= start) & (lane < start + 3), tail, 0.0), axis=1, keepdims=True)
@@ -161,32 +180,15 @@
             ]
             ratio = jnp.sqrt(block_square / entries + EPSILON) / jnp.sqrt(prec_square / entries + EPSILON)
             for line in range(part):
-                ratios[2 * (n * part + line) + h] = jnp.broadcast_to(ratio[line : line + 1], (part, LANES))
-
-    def emit(m, core, odd):
-        couples = ((SELF, FAR), (OPPOSITE, NEAR)) if core else ((SELF, NEAR), (OPPOSITE, FAR))
-        for couple in couples:
-            at = pl.ds(pl.multiple_of(chip(place, couple[0]) // 2 * 2 * part, 2 * part), 2 * part)
-            for j in range(count):
-                b = m * count + j
-                for refs, c in ((own_refs, core), (twin_refs, 1 - core)):
-                    for t in range(each):
-                        tiles = [
-                            refs[k][b * each + t].astype(f32) * ratios[b] for k in (couple[::-1] if odd else couple)
-                        ]
-                        columns = pl.ds(((2 * j + c) * each + t) * LANES, LANES)
-                        ready[m, at, columns] = jnp.concatenate(tiles, 0).astype(bf16)
-
-    def write(m):
-        return pltpu.make_async_copy(ready.at[m], out_ref.at[m], written.at[m])
-
-    @pl.loop(0, mats)
-    def _(m):
-        for core in range(2):
-            for odd in range(2):
-                here = (lax.rem(place[0], 2) == core) & (lax.rem(place[0] // 2, 2) == odd)
-                pl.when(here)(functools.partial(emit, m, core, odd))
-        write(m).start()
+                ratios[blocks * n + 2 * line + h] = jnp.broadcast_to(ratio[line : line + 1], (part, LANES))
+
+        @pl.loop(0, some)
+        def _(m):
+            for core in range(2):
+                for odd in range(2):
+                    here = (lax.rem(place[0], 2) == core) & (lax.rem(place[0] // 2, 2) == odd)
+                    pl.when(here)(functools.partial(emit, m, some * n + m, own_refs, twin_refs, core, odd))
+            write(some * n + m).start()
 
     for m in range(mats):
         write(m).wait()
@@ -271,16 +273,24 @@
     )(place, *halves, *handed, right_root, square)
     back = lax.all_to_all(back, "fsdp", 0, 0, tiled=True)
 
-    tiles = blocks * (width // 2 // LANES) + 2
-    mine = local(select_kernel, [smem, vmem], vmem, shape((tiles, part, LANES), bf16))(block_slot, back)
-    near = exchange(mine, NEAR)
-    far = exchange(mine, FAR)
-    opposite = exchange(near, FAR)
-    own = [mine, near, far, opposite]
-    other = [twin(x) for x in (mine, far, near, opposite)]
+    some = blocks // 2
+    tiles = some * (width // 2 // LANES) + 1
+    parts = [
+        local(functools.partial(select_kernel, first=n * some), [smem, vmem], vmem, shape((tiles, part, LANES), bf16))(
+            block_slot, back
+        )
+        for n in range(2)
+    ]
+    near = [exchange(x, NEAR) for x in parts]
+    far = [exchange(lax.optimization_barrier((x, y))[0], FAR) for x, y in zip(parts, near)]
+    opposite = [exchange(x, FAR) for x in near]
+    pieces = []
+    for n in range(2):
+        pieces += [parts[n], near[n], far[n], opposite[n]]
+        pieces += [twin(x) for x in (parts[n], far[n], near[n], opposite[n])]
     return local(
         functools.partial(finish_kernel, entries=height * width),
-        [smem] + [vmem] * 8,
+        [smem] + [vmem] * 16,
         pl.BlockSpec(memory_space=pl.ANY),
         shape((mats, rows, full), bf16),
         [
@@ -288,7 +298,7 @@
             pltpu.VMEM((blocks, part, LANES), f32),
             pltpu.SemaphoreType.DMA((mats,)),
         ],
-    )(place, *own, *other)
+    )(place, *pieces)
 
 
 def solution(mesh):

time: 104 us -> 105 us (level)
  starting transfers between devices: 32.2 us -> 37.4 us
  waiting for transfers between devices: 17.3 us -> 12.7 us
    ppermute x9 -> x12, starting transfers between devices: 8.22 us -> 14.1 us  [exchange(): return lax.ppermute(x, 'replica', perm)]
    ppermute x9 -> x12, waiting for transfers between devices: 15 us -> 10.5 us  [exchange(): return lax.ppermute(x, 'replica', perm)]
    ppermute x10 -> x14, starting transfers between devices: 24 us -> 23.3 us  [twin(): return lax.ppermute(x, 'replica', [(i, i ^ 1) for i in range(reps)])]
    ppermute x10 -> x14, waiting for transfers between devices: 2.39 us -> 2.21 us  [twin(): return lax.ppermute(x, 'replica', [(i, i ^ 1) for i in range(reps)])]
  transfers between devices with their start and end apart: 19 -> 26, of which waited for: 7 -> 10; matrix products, arithmetic and copies ran while one was open for 0% -> 0% of each run, Pallas kernels for 1% -> 2%
where the time goes in v5:
time: 105 us
  blocking collectives  45 us (43%)
  starting transfers between devices  37.4 us (36%)
  waiting for transfers between devices  12.7 us (12%)
  Pallas kernels  9.49 us (9%)
    all_to_all x1, blocking collectives, on_device(): incoming = lax.all_to_all(outgoing, 'fsdp', 0, 0, tiled=True)  23.5 us
    ppermute x14, starting transfers between devices, twin(): return lax.ppermute(x, 'replica', [(i, i ^ 1) for i in range(reps)])  23.3 us
    all_to_all x1, blocking collectives, on_device(): back = lax.all_to_all(back, 'fsdp', 0, 0, tiled=True)  21.5 us
    ppermute x12, starting transfers between devices, exchange(): return lax.ppermute(x, 'replica', perm)  14.1 us
    ppermute x12, waiting for transfers between devices, exchange(): return lax.ppermute(x, 'replica', perm)  10.5 us
    pallas_call x2, Pallas kernels, on_device(): local(functools.partial(send_kernel, kinds=kinds, **sizes), [smem, pl.Blo...  2.44 us
    ppermute x14, waiting for transfers between devices, twin(): return lax.ppermute(x, 'replica', [(i, i ^ 1) for i in range(reps)])  2.21 us
  transfers between devices with their start and end apart: 26, of which 10 were waited for; matrix products, arithmetic and copies ran while one was open for 0% of the time, Pallas kernels for 2%

profile of v5, /device:TPU:1, one launch (start us, length us, event | category | flops | bytes accessed | tf_op | source)
XLA Modules:
  0.0 105.0 jit_solution(6044068833534156983)
XLA Ops:
  0.0 1.3 %shard_map.48 = bf16[2,4,8,32,128]{4,3,2,1,0:T(8,128)(2,1)S(1)} custom-call(s32[1]{0:T(128)} %bitcast.place, bf16[1,4,32,8192]{3,2,1,0:T(8,128)(2,1)} %grads_ref.7), custom_call_target="tpu_custom_call" | custom-call | tf_op jit(solution)/shard_map/pallas_call | solution.py:233
  1.3 3.3 %collective-permute-start.1 = (bf16[2,4,8,32,128]{4,3,2,1,0:T(8,128)(2,1)S(1)}, bf16[2,4,8,32,128]{4,3,2,1,0:T(8,128)(2,1)S(1)}, u32[]{:S(2)}, u32[]{:S(2)}) collective-permute-start(bf16[2,4,8,32,128]{4,3,2,1,0:T(8,128)(2,1)S(1)} %shard_map.48), channel_id=1, source_target_pairs={{0,32},{32,0},{64,96},{96,64},{128,160},{160,128},{192,224},{224,1... | collective-permute-start | bytes 1572872 | tf_op jit(solution)/shard_map/ppermute | solution.py:210
  4.6 1.1 %shard_map.46 = bf16[2,4,8,32,128]{4,3,2,1,0:T(8,128)(2,1)S(1)} custom-call(s32[1]{0:T(128)} %bitcast.place, bf16[1,4,32,8192]{3,2,1,0:T(8,128)(2,1)} %grads_ref.7), custom_call_target="tpu_custom_call" | custom-call | tf_op jit(solution)/shard_map/pallas_call | solution.py:233
  7.4 1.7 %collective-permute-start.2 = (bf16[4,8,32,128]{3,2,1,0:T(8,128)(2,1)S(1)}, bf16[4,8,32,128]{3,2,1,0:T(8,128)(2,1)S(1)}, u32[]{:S(2)}, u32[]{:S(2)}) collective-permute-start(bf16[4,8,32,128]{3,2,1,0:T(8,128)(2,1)S(1)} %get-tuple-element.17), channel_id=1, source_target_pairs={{0,64},{32,224},{64,0},{96,160},{128,192},{160,96},{192,128},{224,... | collective-permute-start | bytes 786440 | tf_op jit(solution)/shard_map/ppermute | solution.py:214
  9.3 3.6 %collective-permute-done.3.y_ref = bf16[4,8,32,128]{3,2,1,0:T(8,128)(2,1)S(1)} collective-permute-done((bf16[4,8,32,128]{3,2,1,0:T(8,128)(2,1)S(1)}, bf16[4,8,32,128]{3,2,1,0:T(8,128)(2,1)S(1)}, u32[]{:S(2)}, u32[]{:S(2)}) %collective-permute-start.3) | collective-permute-done | bytes 262176 | tf_op jit(solution)/shard_map/ppermute | solution.py:214
  13.0 2.6 %collective-permute-done.2.refs_1_ = bf16[4,8,32,128]{3,2,1,0:T(8,128)(2,1)S(1)} collective-permute-done((bf16[4,8,32,128]{3,2,1,0:T(8,128)(2,1)S(1)}, bf16[4,8,32,128]{3,2,1,0:T(8,128)(2,1)S(1)}, u32[]{:S(2)}, u32[]{:S(2)}) %collective-permute-start.2) | collective-permute-done | bytes 262176 | tf_op jit(solution)/shard_map/ppermute | solution.py:214
  15.7 2.9 %collective-permute-done.4.refs_2_ = bf16[4,8,32,128]{3,2,1,0:T(8,128)(2,1)S(1)} collective-permute-done((bf16[4,8,32,128]{3,2,1,0:T(8,128)(2,1)S(1)}, bf16[4,8,32,128]{3,2,1,0:T(8,128)(2,1)S(1)}, u32[]{:S(2)}, u32[]{:S(2)}) %collective-permute-start.4) | collective-permute-done | bytes 262176 | tf_op jit(solution)/shard_map/ppermute | solution.py:214
  19.3 23.5 %all_to_all.10.block_ref = bf16[32,2,32,128]{3,2,1,0:T(8,128)(2,1)S(1)} all-to-all(bf16[32,2,32,128]{3,2,1,0:T(8,128)(2,1)S(1)} %shard_map.51), channel_id=1, replica_groups=mesh['replica'=8,'fsdp'=32] {'fsdp'}, dimensions={0} | all-to-all | bytes 1048576 | tf_op jit(solution)/shard_map/all_to_all | solution.py:254
  42.8 1.4 %shard_map.52 = (bf16[2,256,128]{2,1,0:T(8,128)(2,1)S(1)}, bf16[2,256,128]{2,1,0:T(8,128)(2,1)S(1)}, bf16[2,256,128]{2,1,0:T(8,128)(2,1)S(1)}, bf16[2,256,128]{2,1,0:T(8,128)(2,1)S(1)}, f32[2,8,128]{2,1,0:T(8,128)S(1)}) custom-call(s32[1]{0:T(128)} %bitcast.place, bf16[2,1024,1024]{2,1,0:T(8,128)(2,1)S(1)} %copy-done.1, ...), custom_call_target="tpu_custom_call" | custom-call | tf_op jit(solution)/shard_map/pallas_call | solution.py:257
  44.2 3.9 %collective-permute-start.5 = (bf16[2,256,128]{2,1,0:T(8,128)(2,1)S(1)}, bf16[2,256,128]{2,1,0:T(8,128)(2,1)S(1)}, u32[]{:S(2)}, u32[]{:S(2)}) collective-permute-start(bf16[2,256,128]{2,1,0:T(8,128)(2,1)S(1)} %get-tuple-element.21), channel_id=1, source_target_pairs={{0,128},{32,160},{64,192},{96,224},{128,0},{160,32},{192,64},{224,... | collective-permute-start | bytes 393224 | tf_op jit(solution)/shard_map/ppermute | solution.py:214
  48.9 4.2 %collective-permute-start.8 = (bf16[2,256,128]{2,1,0:T(8,128)(2,1)S(1)}, bf16[2,256,128]{2,1,0:T(8,128)(2,1)S(1)}, u32[]{:S(2)}, u32[]{:S(2)}) collective-permute-start(bf16[2,256,128]{2,1,0:T(8,128)(2,1)S(1)} %get-tuple-element.20.refs_0_), channel_id=1, source_target_pairs={{0,32},{32,0},{64,96},{96,64},{128,160},{160,128},{192,224},{224,1... | collective-permute-start | bytes 393224 | tf_op jit(solution)/shard_map/ppermute | solution.py:210
  53.1 3.4 %collective-permute-start.9 = (bf16[2,256,128]{2,1,0:T(8,128)(2,1)S(1)}, bf16[2,256,128]{2,1,0:T(8,128)(2,1)S(1)}, u32[]{:S(2)}, u32[]{:S(2)}) collective-permute-start(bf16[2,256,128]{2,1,0:T(8,128)(2,1)S(1)} %collective-permute-done.5.refs_1_), channel_id=1, source_target_pairs={{0,32},{32,0},{64,96},{96,64},{128,160},{160,128},{192,224},{224,1... | collective-permute-start | bytes 393224 | tf_op jit(solution)/shard_map/ppermute | solution.py:210
  57.2 1.8 %collective-permute-start.10 = (bf16[2,256,128]{2,1,0:T(8,128)(2,1)S(1)}, bf16[2,256,128]{2,1,0:T(8,128)(2,1)S(1)}, u32[]{:S(2)}, u32[]{:S(2)}) collective-permute-start(bf16[2,256,128]{2,1,0:T(8,128)(2,1)S(1)} %collective-permute-done.7.refs_3_), channel_id=1, source_target_pairs={{0,32},{32,0},{64,96},{96,64},{128,160},{160,128},{192,224},{224,1... | collective-permute-start | bytes 393224 | tf_op jit(solution)/shard_map/ppermute | solution.py:210
  60.0 1.1 %shard_map.53 = bf16[32,8,1152]{2,1,0:T(8,128)(2,1)S(1)} custom-call(s32[1]{0:T(128)} %bitcast.place, bf16[2,256,128]{2,1,0:T(8,128)(2,1)S(1)} %get-tuple-element.20.refs_0_, bf16[2,256,128]{2,1,0:T(8,128)(2,1)S(1)} %collective-permute-done.5.refs_1_, bf16[2,256,128]{2,1,0:T(8,128)(2,1)S(1)} %collective-permute-done.6.refs_2_, ...), custom_call_target="tpu_custom_call" | custom-call | tf_op jit(solution)/shard_map/pallas_call | solution.py:267
  61.1 21.5 %all_to_all.11.back_ref = bf16[32,8,1152]{2,1,0:T(8,128)(2,1)S(1)} all-to-all(bf16[32,8,1152]{2,1,0:T(8,128)(2,1)S(1)} %shard_map.53), channel_id=1, replica_groups=mesh['replica'=8,'fsdp'=32] {'fsdp'}, dimensions={0} | all-to-all | bytes 1179648 | tf_op jit(solution)/shard_map/all_to_all | solution.py:274
  84.9 2.2 %collective-permute-start.19 = (bf16[65,8,128]{2,1,0:T(8,128)(2,1)S(1)}, bf16[65,8,128]{2,1,0:T(8,128)(2,1)S(1)}, u32[]{:S(2)}, u32[]{:S(2)}) collective-permute-start(bf16[65,8,128]{2,1,0:T(8,128)(2,1)S(1)} %shard_map.55.refs_8_), channel_id=1, source_target_pairs={{0,64},{32,224},{64,0},{96,160},{128,192},{160,96},{192,128},{224,... | collective-permute-start | bytes 399368 | tf_op jit(solution)/shard_map/ppermute | solution.py:214
  87.1 1.7 %collective-permute-start.15 = (bf16[65,8,128]{2,1,0:T(8,128)(2,1)S(1)}, bf16[65,8,128]{2,1,0:T(8,128)(2,1)S(1)}, u32[]{:S(2)}, u32[]{:S(2)}) collective-permute-start(bf16[65,8,128]{2,1,0:T(8,128)(2,1)S(1)} %shard_map.54.refs_0_), channel_id=1, source_target_pairs={{0,32},{32,0},{64,96},{96,64},{128,160},{160,128},{192,224},{224,1... | collective-permute-start | bytes 399368 | tf_op jit(solution)/shard_map/ppermute | solution.py:210
  90.0 2.6 %collective-permute-start.17 = (bf16[65,8,128]{2,1,0:T(8,128)(2,1)S(1)}, bf16[65,8,128]{2,1,0:T(8,128)(2,1)S(1)}, u32[]{:S(2)}, u32[]{:S(2)}) collective-permute-start(bf16[65,8,128]{2,1,0:T(8,128)(2,1)S(1)} %collective-permute-done.12.refs_1_), channel_id=1, source_target_pairs={{0,32},{32,0},{64,96},{96,64},{128,160},{160,128},{192,224},{224,1... | collective-permute-start | bytes 399368 | tf_op jit(solution)/shard_map/ppermute | solution.py:210
  92.6 2.2 %collective-permute-start.14 = (bf16[65,8,128]{2,1,0:T(8,128)(2,1)S(1)}, bf16[65,8,128]{2,1,0:T(8,128)(2,1)S(1)}, u32[]{:S(2)}, u32[]{:S(2)}) collective-permute-start(bf16[65,8,128]{2,1,0:T(8,128)(2,1)S(1)} %collective-permute-done.12.refs_1_), channel_id=1, source_target_pairs={{0,192},{32,96},{64,128},{96,32},{128,64},{160,224},{192,0},{224,1... | collective-permute-start | bytes 399368 | tf_op jit(solution)/shard_map/ppermute | solution.py:214
  94.9 1.4 %collective-permute-start.21 = (bf16[65,8,128]{2,1,0:T(8,128)(2,1)S(1)}, bf16[65,8,128]{2,1,0:T(8,128)(2,1)S(1)}, u32[]{:S(2)}, u32[]{:S(2)}) collective-permute-start(bf16[65,8,128]{2,1,0:T(8,128)(2,1)S(1)} %collective-permute-done.19.refs_9_), channel_id=1, source_target_pairs={{0,192},{32,96},{64,128},{96,32},{128,64},{160,224},{192,0},{224,1... | collective-permute-start | bytes 399368 | tf_op jit(solution)/shard_map/ppermute | solution.py:214
  97.5 1.4 %collective-permute-start.18 = (bf16[65,8,128]{2,1,0:T(8,128)(2,1)S(1)}, bf16[65,8,128]{2,1,0:T(8,128)(2,1)S(1)}, u32[]{:S(2)}, u32[]{:S(2)}) collective-permute-start(bf16[65,8,128]{2,1,0:T(8,128)(2,1)S(1)} %collective-permute-done.14.refs_3_), channel_id=1, source_target_pairs={{0,32},{32,0},{64,96},{96,64},{128,160},{160,128},{192,224},{224,1... | collective-permute-start | bytes 399368 | tf_op jit(solution)/shard_map/ppermute | solution.py:210
  99.0 1.3 %collective-permute-start.23 = (bf16[65,8,128]{2,1,0:T(8,128)(2,1)S(1)}, bf16[65,8,128]{2,1,0:T(8,128)(2,1)S(1)}, u32[]{:S(2)}, u32[]{:S(2)}) collective-permute-start(bf16[65,8,128]{2,1,0:T(8,128)(2,1)S(1)} %collective-permute-done.20.refs_10_), channel_id=1, source_target_pairs={{0,32},{32,0},{64,96},{96,64},{128,160},{160,128},{192,224},{224,1... | collective-permute-start | bytes 399368 | tf_op jit(solution)/shard_map/ppermute | solution.py:210
  100.4 1.7 %collective-permute-start.25 = (bf16[65,8,128]{2,1,0:T(8,128)(2,1)S(1)}, bf16[65,8,128]{2,1,0:T(8,128)(2,1)S(1)}, u32[]{:S(2)}, u32[]{:S(2)}) collective-permute-start(bf16[65,8,128]{2,1,0:T(8,128)(2,1)S(1)} %collective-permute-done.21.refs_11_), channel_id=1, source_target_pairs={{0,32},{32,0},{64,96},{96,64},{128,160},{160,128},{192,224},{224,1... | collective-permute-start | bytes 399368 | tf_op jit(solution)/shard_map/ppermute | solution.py:210
  103.1 1.7 %shard_map.56 = bf16[4,32,8192]{2,1,0:T(8,128)(2,1)} custom-call(s32[1]{0:T(128)} %bitcast.place, bf16[65,8,128]{2,1,0:T(8,128)(2,1)S(1)} %shard_map.54.refs_0_, bf16[65,8,128]{2,1,0:T(8,128)(2,1)S(1)} %collective-permute-done.12.refs_1_, bf16[65,8,128]{2,1,0:T(8,128)(2,1)S(1)} %collective-permute-done.13.refs_2_, ...), custom_call_target="tpu_custom_call" | custom-call | tf_op jit(solution)/shard_map/pallas_call | solution.py:291
  (49 shorter events, 11.1 us)
Async XLA Ops:
  1.3 4.9 %collective-permute-start.1 = (bf16[2,4,8,32,128]{4,3,2,1,0:T(8,128)(2,1)S(1)}, bf16[2,4,8,32,128]{4,3,2,1,0:T(8,128)(2,1)S(1)}, u32[]{:S(2)}, u32[]{:S(2)}) collective-permute-start(bf16[2,4,8,32,128]{4,3,2,1,0:T(8,128)(2,1)S(1)} %shard_map.48), channel_id=1, source_target_pairs={{0,32},{32,0},{64,96},{96,64},{128,160},{160,128},{192,224},{224,1... | collective-permute-start | bytes 1572872 | tf_op jit(solution)/shard_map/ppermute | solution.py:210
  5.8 3.3 %collective-permute-start = (bf16[2,4,8,32,128]{4,3,2,1,0:T(8,128)(2,1)S(1)}, bf16[2,4,8,32,128]{4,3,2,1,0:T(8,128)(2,1)S(1)}, u32[]{:S(2)}, u32[]{:S(2)}) collective-permute-start(bf16[2,4,8,32,128]{4,3,2,1,0:T(8,128)(2,1)S(1)} %shard_map.46), channel_id=1, source_target_pairs={{0,32},{32,0},{64,96},{96,64},{128,160},{160,128},{192,224},{224,1... | collective-permute-start | bytes 1572872 | tf_op jit(solution)/shard_map/ppermute | solution.py:210
  6.4 6.5 %collective-permute-start.3 = (bf16[4,8,32,128]{3,2,1,0:T(8,128)(2,1)S(1)}, bf16[4,8,32,128]{3,2,1,0:T(8,128)(2,1)S(1)}, u32[]{:S(2)}, u32[]{:S(2)}) collective-permute-start(bf16[4,8,32,128]{3,2,1,0:T(8,128)(2,1)S(1)} %get-tuple-element.19), channel_id=1, source_target_pairs={{0,64},{32,224},{64,0},{96,160},{128,192},{160,96},{192,128},{224,... | collective-permute-start | bytes 786440 | tf_op jit(solution)/shard_map/ppermute | solution.py:214
  7.4 8.2 %collective-permute-start.2 = (bf16[4,8,32,128]{3,2,1,0:T(8,128)(2,1)S(1)}, bf16[4,8,32,128]{3,2,1,0:T(8,128)(2,1)S(1)}, u32[]{:S(2)}, u32[]{:S(2)}) collective-permute-start(bf16[4,8,32,128]{3,2,1,0:T(8,128)(2,1)S(1)} %get-tuple-element.17), channel_id=1, source_target_pairs={{0,64},{32,224},{64,0},{96,160},{128,192},{160,96},{192,128},{224,... | collective-permute-start | bytes 786440 | tf_op jit(solution)/shard_map/ppermute | solution.py:214
  12.9 5.6 %collective-permute-start.4 = (bf16[4,8,32,128]{3,2,1,0:T(8,128)(2,1)S(1)}, bf16[4,8,32,128]{3,2,1,0:T(8,128)(2,1)S(1)}, u32[]{:S(2)}, u32[]{:S(2)}) collective-permute-start(bf16[4,8,32,128]{3,2,1,0:T(8,128)(2,1)S(1)} %shard_map.50), channel_id=1, source_target_pairs={{0,192},{32,96},{64,128},{96,32},{128,64},{160,224},{192,0},{224,1... | collective-permute-start | bytes 786440 | tf_op jit(solution)/shard_map/ppermute | solution.py:214
  44.2 8.8 %collective-permute-start.5 = (bf16[2,256,128]{2,1,0:T(8,128)(2,1)S(1)}, bf16[2,256,128]{2,1,0:T(8,128)(2,1)S(1)}, u32[]{:S(2)}, u32[]{:S(2)}) collective-permute-start(bf16[2,256,128]{2,1,0:T(8,128)(2,1)S(1)} %get-tuple-element.21), channel_id=1, source_target_pairs={{0,128},{32,160},{64,192},{96,224},{128,0},{160,32},{192,64},{224,... | collective-permute-start | bytes 393224 | tf_op jit(solution)/shard_map/ppermute | solution.py:214
  48.1 8.3 %collective-permute-start.6 = (bf16[2,256,128]{2,1,0:T(8,128)(2,1)S(1)}, bf16[2,256,128]{2,1,0:T(8,128)(2,1)S(1)}, u32[]{:S(2)}, u32[]{:S(2)}) collective-permute-start(bf16[2,256,128]{2,1,0:T(8,128)(2,1)S(1)} %get-tuple-element.22), channel_id=1, source_target_pairs={{0,64},{32,224},{64,0},{96,160},{128,192},{160,96},{192,128},{224,... | collective-permute-start | bytes 393224 | tf_op jit(solution)/shard_map/ppermute | solution.py:214
  48.9 8.2 %collective-permute-start.7 = (bf16[2,256,128]{2,1,0:T(8,128)(2,1)S(1)}, bf16[2,256,128]{2,1,0:T(8,128)(2,1)S(1)}, u32[]{:S(2)}, u32[]{:S(2)}) collective-permute-start(bf16[2,256,128]{2,1,0:T(8,128)(2,1)S(1)} %get-tuple-element.23), channel_id=1, source_target_pairs={{0,192},{32,96},{64,128},{96,32},{128,64},{160,224},{192,0},{224,1... | collective-permute-start | bytes 393224 | tf_op jit(solution)/shard_map/ppermute | solution.py:214
  48.9 10.1 %collective-permute-start.8 = (bf16[2,256,128]{2,1,0:T(8,128)(2,1)S(1)}, bf16[2,256,128]{2,1,0:T(8,128)(2,1)S(1)}, u32[]{:S(2)}, u32[]{:S(2)}) collective-permute-start(bf16[2,256,128]{2,1,0:T(8,128)(2,1)S(1)} %get-tuple-element.20.refs_0_), channel_id=1, source_target_pairs={{0,32},{32,0},{64,96},{96,64},{128,160},{160,128},{192,224},{224,1... | collective-permute-start | bytes 393224 | tf_op jit(solution)/shard_map/ppermute | solution.py:210
  53.1 5.9 %collective-permute-start.9 = (bf16[2,256,128]{2,1,0:T(8,128)(2,1)S(1)}, bf16[2,256,128]{2,1,0:T(8,128)(2,1)S(1)}, u32[]{:S(2)}, u32[]{:S(2)}) collective-permute-start(bf16[2,256,128]{2,1,0:T(8,128)(2,1)S(1)} %collective-permute-done.5.refs_1_), channel_id=1, source_target_pairs={{0,32},{32,0},{64,96},{96,64},{128,160},{160,128},{192,224},{224,1... | collective-permute-start | bytes 393224 | tf_op jit(solution)/shard_map/ppermute | solution.py:210
  57.2 2.8 %collective-permute-start.10 = (bf16[2,256,128]{2,1,0:T(8,128)(2,1)S(1)}, bf16[2,256,128]{2,1,0:T(8,128)(2,1)S(1)}, u32[]{:S(2)}, u32[]{:S(2)}) collective-permute-start(bf16[2,256,128]{2,1,0:T(8,128)(2,1)S(1)} %collective-permute-done.7.refs_3_), channel_id=1, source_target_pairs={{0,32},{32,0},{64,96},{96,64},{128,160},{160,128},{192,224},{224,1... | collective-permute-start | bytes 393224 | tf_op jit(solution)/shard_map/ppermute | solution.py:210
  83.5 5.3 %collective-permute-start.12 = (bf16[65,8,128]{2,1,0:T(8,128)(2,1)S(1)}, bf16[65,8,128]{2,1,0:T(8,128)(2,1)S(1)}, u32[]{:S(2)}, u32[]{:S(2)}) collective-permute-start(bf16[65,8,128]{2,1,0:T(8,128)(2,1)S(1)} %shard_map.54.refs_0_), channel_id=1, source_target_pairs={{0,64},{32,224},{64,0},{96,160},{128,192},{160,96},{192,128},{224,... | collective-permute-start | bytes 399368 | tf_op jit(solution)/shard_map/ppermute | solution.py:214
  84.9 5.1 %collective-permute-start.19 = (bf16[65,8,128]{2,1,0:T(8,128)(2,1)S(1)}, bf16[65,8,128]{2,1,0:T(8,128)(2,1)S(1)}, u32[]{:S(2)}, u32[]{:S(2)}) collective-permute-start(bf16[65,8,128]{2,1,0:T(8,128)(2,1)S(1)} %shard_map.55.refs_8_), channel_id=1, source_target_pairs={{0,64},{32,224},{64,0},{96,160},{128,192},{160,96},{192,128},{224,... | collective-permute-start | bytes 399368 | tf_op jit(solution)/shard_map/ppermute | solution.py:214
  87.1 7.8 %collective-permute-start.15 = (bf16[65,8,128]{2,1,0:T(8,128)(2,1)S(1)}, bf16[65,8,128]{2,1,0:T(8,128)(2,1)S(1)}, u32[]{:S(2)}, u32[]{:S(2)}) collective-permute-start(bf16[65,8,128]{2,1,0:T(8,128)(2,1)S(1)} %shard_map.54.refs_0_), channel_id=1, source_target_pairs={{0,32},{32,0},{64,96},{96,64},{128,160},{160,128},{192,224},{224,1... | collective-permute-start | bytes 399368 | tf_op jit(solution)/shard_map/ppermute | solution.py:210
  88.7 6.1 %collective-permute-start.22 = (bf16[65,8,128]{2,1,0:T(8,128)(2,1)S(1)}, bf16[65,8,128]{2,1,0:T(8,128)(2,1)S(1)}, u32[]{:S(2)}, u32[]{:S(2)}) collective-permute-start(bf16[65,8,128]{2,1,0:T(8,128)(2,1)S(1)} %shard_map.55.refs_8_), channel_id=1, source_target_pairs={{0,32},{32,0},{64,96},{96,64},{128,160},{160,128},{192,224},{224,1... | collective-permute-start | bytes 399368 | tf_op jit(solution)/shard_map/ppermute | solution.py:210
  88.7 7.6 %collective-permute-start.13 = (bf16[65,8,128]{2,1,0:T(8,128)(2,1)S(1)}, bf16[65,8,128]{2,1,0:T(8,128)(2,1)S(1)}, u32[]{:S(2)}, u32[]{:S(2)}) collective-permute-start(bf16[65,8,128]{2,1,0:T(8,128)(2,1)S(1)} %shard_map.54.refs_0_), channel_id=1, source_target_pairs={{0,192},{32,96},{64,128},{96,32},{128,64},{160,224},{192,0},{224,1... | collective-permute-start | bytes 399368 | tf_op jit(solution)/shard_map/ppermute | solution.py:214
  90.0 7.3 %collective-permute-start.17 = (bf16[65,8,128]{2,1,0:T(8,128)(2,1)S(1)}, bf16[65,8,128]{2,1,0:T(8,128)(2,1)S(1)}, u32[]{:S(2)}, u32[]{:S(2)}) collective-permute-start(bf16[65,8,128]{2,1,0:T(8,128)(2,1)S(1)} %collective-permute-done.12.refs_1_), channel_id=1, source_target_pairs={{0,32},{32,0},{64,96},{96,64},{128,160},{160,128},{192,224},{224,1... | collective-permute-start | bytes 399368 | tf_op jit(solution)/shard_map/ppermute | solution.py:210
  92.6 4.8 %collective-permute-start.14 = (bf16[65,8,128]{2,1,0:T(8,128)(2,1)S(1)}, bf16[65,8,128]{2,1,0:T(8,128)(2,1)S(1)}, u32[]{:S(2)}, u32[]{:S(2)}) collective-permute-start(bf16[65,8,128]{2,1,0:T(8,128)(2,1)S(1)} %collective-permute-done.12.refs_1_), channel_id=1, source_target_pairs={{0,192},{32,96},{64,128},{96,32},{128,64},{160,224},{192,0},{224,1... | collective-permute-start | bytes 399368 | tf_op jit(solution)/shard_map/ppermute | solution.py:214
  94.8 4.1 %collective-permute-start.20 = (bf16[65,8,128]{2,1,0:T(8,128)(2,1)S(1)}, bf16[65,8,128]{2,1,0:T(8,128)(2,1)S(1)}, u32[]{:S(2)}, u32[]{:S(2)}) collective-permute-start(bf16[65,8,128]{2,1,0:T(8,128)(2,1)S(1)} %shard_map.55.refs_8_), channel_id=1, source_target_pairs={{0,192},{32,96},{64,128},{96,32},{128,64},{160,224},{192,0},{224,1... | collective-permute-start | bytes 399368 | tf_op jit(solution)/shard_map/ppermute | solution.py:214
  94.9 5.5 %collective-permute-start.21 = (bf16[65,8,128]{2,1,0:T(8,128)(2,1)S(1)}, bf16[65,8,128]{2,1,0:T(8,128)(2,1)S(1)}, u32[]{:S(2)}, u32[]{:S(2)}) collective-permute-start(bf16[65,8,128]{2,1,0:T(8,128)(2,1)S(1)} %collective-permute-done.19.refs_9_), channel_id=1, source_target_pairs={{0,192},{32,96},{64,128},{96,32},{128,64},{160,224},{192,0},{224,1... | collective-permute-start | bytes 399368 | tf_op jit(solution)/shard_map/ppermute | solution.py:214
  96.3 5.8 %collective-permute-start.24 = (bf16[65,8,128]{2,1,0:T(8,128)(2,1)S(1)}, bf16[65,8,128]{2,1,0:T(8,128)(2,1)S(1)}, u32[]{:S(2)}, u32[]{:S(2)}) collective-permute-start(bf16[65,8,128]{2,1,0:T(8,128)(2,1)S(1)} %collective-permute-done.19.refs_9_), channel_id=1, source_target_pairs={{0,32},{32,0},{64,96},{96,64},{128,160},{160,128},{192,224},{224,1... | collective-permute-start | bytes 399368 | tf_op jit(solution)/shard_map/ppermute | solution.py:210
  97.3 4.8 %collective-permute-start.16 = (bf16[65,8,128]{2,1,0:T(8,128)(2,1)S(1)}, bf16[65,8,128]{2,1,0:T(8,128)(2,1)S(1)}, u32[]{:S(2)}, u32[]{:S(2)}) collective-permute-start(bf16[65,8,128]{2,1,0:T(8,128)(2,1)S(1)} %collective-permute-done.13.refs_2_), channel_id=1, source_target_pairs={{0,32},{32,0},{64,96},{96,64},{128,160},{160,128},{192,224},{224,1... | collective-permute-start | bytes 399368 | tf_op jit(solution)/shard_map/ppermute | solution.py:210
  97.5 4.6 %collective-permute-start.18 = (bf16[65,8,128]{2,1,0:T(8,128)(2,1)S(1)}, bf16[65,8,128]{2,1,0:T(8,128)(2,1)S(1)}, u32[]{:S(2)}, u32[]{:S(2)}) collective-permute-start(bf16[65,8,128]{2,1,0:T(8,128)(2,1)S(1)} %collective-permute-done.14.refs_3_), channel_id=1, source_target_pairs={{0,32},{32,0},{64,96},{96,64},{128,160},{160,128},{192,224},{224,1... | collective-permute-start | bytes 399368 | tf_op jit(solution)/shard_map/ppermute | solution.py:210
  99.0 3.1 %collective-permute-start.23 = (bf16[65,8,128]{2,1,0:T(8,128)(2,1)S(1)}, bf16[65,8,128]{2,1,0:T(8,128)(2,1)S(1)}, u32[]{:S(2)}, u32[]{:S(2)}) collective-permute-start(bf16[65,8,128]{2,1,0:T(8,128)(2,1)S(1)} %collective-permute-done.20.refs_10_), channel_id=1, source_target_pairs={{0,32},{32,0},{64,96},{96,64},{128,160},{160,128},{192,224},{224,1... | collective-permute-start | bytes 399368 | tf_op jit(solution)/shard_map/ppermute | solution.py:210
  (6 other events, 116.4 us)

commit v6 on v4

--- a/solution.py
+++ b/solution.py
@@ -16,6 +16,14 @@
 SELF, NEAR, FAR, OPPOSITE = range(4)
 ORDER = (SELF, OPPOSITE, NEAR, FAR)
 TWIN_ORDER = (SELF, OPPOSITE, FAR, NEAR)
+
+
+CHIPS_X, CHIPS_Z, STEP_Z = 4, 8, 3
+
+
+def place_of(owner):
+    z, x = owner // CHIPS_X, owner % CHIPS_X
+    return x * CHIPS_Z + STEP_Z * z % CHIPS_Z
 
 
 def masks(core):
@@ -75,14 +83,14 @@
         for j in range(cols):
             q = slot[m * cols + j]
             total = sum(term[m, j].astype(f32) for term in terms)
-            out_ref[q // slots, lax.rem(q, slots)] = total.astype(bf16)
+            out_ref[place_of(q // slots), lax.rem(q, slots)] = total.astype(bf16)
 
 
 def left_kernel(place, left_ref, block_ref, *out_refs):
     *half_refs, square_ref, scratch = out_refs
     owners, slots, rows, strip = block_ref.shape
     for s in range(slots):
-        block = block_ref[:, s].reshape(owners * rows, strip)
+        block = jnp.concatenate([block_ref[place_of(owner), s] for owner in range(owners)], axis=0)
         wide = block.astype(f32)
         square_ref[s] = jnp.broadcast_to(jnp.sum(wide * wide, keepdims=True), square_ref.shape[1:])
         half = jnp.dot(left_ref[s], block, preferred_element_type=f32)
@@ -114,7 +122,9 @@
                 half_scratch[s, :, pl.ds(pl.multiple_of(r * strip, strip), strip)] = half_ref[s]
         columns = pl.ds(pl.multiple_of(core * width, width), width)
         prec = jnp.dot(half_scratch[s], right_ref[s, :, columns], preferred_element_type=f32)
-        back_ref[:, :, s * width : (s + 1) * width] = prec.reshape(owners, part, width).astype(bf16)
+        rows = prec.reshape(owners, part, width).astype(bf16)
+        for owner in range(owners):
+            back_ref[place_of(owner), :, s * width : (s + 1) * width] = rows[owner]
         prec_square = jnp.broadcast_to(jnp.sum(prec * prec, keepdims=True), (part, LANES))
         for k, term in enumerate(split3(square_ref[s]) + split3(prec_square)):
             tail = jnp.where(lane == TERMS * s + k, term, tail)
@@ -134,8 +144,8 @@
         s = lax.rem(q, 2)
         for t in range(each):
             columns = pl.ds(pl.multiple_of(s * width + t * LANES, LANES), LANES)
-            tiles_ref[b * each + t] = back_ref[q // 2, :, columns]
-        tail = back_ref[q // 2, :, 2 * width :].astype(f32)
+            tiles_ref[b * each + t] = back_ref[place_of(q // 2), :, columns]
+        tail = back_ref[place_of(q // 2), :, 2 * width :].astype(f32)
         tail = jnp.where(s == h, tail, pltpu.roll(tail, TERMS if h else LANES - TERMS, 1))
         here = (line == pair % part) & (lane >= TERMS * h) & (lane < TERMS * (h + 1))
         terms[pair // part] = jnp.where(here, tail, terms[pair // part])
@@ -249,7 +259,8 @@
     outgoing = local(route_kernel, [smem] + [vmem] * 3, vmem, shape((owners, slots, rows, strip), bf16))(
         block_slot, sums[SELF], direct, last
     )
-    incoming = lax.all_to_all(outgoing, "fsdp", 0, 0, tiled=True)
+    ring = [sorted(range(owners), key=place_of)]
+    incoming = lax.all_to_all(outgoing, "fsdp", 0, 0, tiled=True, axis_index_groups=ring)
 
     half_shape = shape((slots, owners * part, strip), bf16)
     *halves, square = local(
@@ -269,7 +280,7 @@
         shape((owners, part, wide), bf16),
         [pltpu.VMEM((slots, owners * part, width), bf16)],
     )(place, *halves, *handed, right_root, square)
-    back = lax.all_to_all(back, "fsdp", 0, 0, tiled=True)
+    back = lax.all_to_all(back, "fsdp", 0, 0, tiled=True, axis_index_groups=ring)
 
     tiles = blocks * (width // 2 // LANES) + 2
     mine = local(select_kernel, [smem, vmem], vmem, shape((tiles, part, LANES), bf16))(block_slot, back)

time: 104 us -> 104 us (level)
  starting transfers between devices: 32.2 us -> 34.3 us
  blocking collectives: 45 us -> 43.1 us
    all_to_all x2, blocking collectives: 45 us -> 43.1 us  [the longest x1 22.5 us: on_device(): lax.all_to_all(outgoing, 'fsdp', 0, 0, tiled=True, axis_index_groups=ring)]
    ppermute x10, starting transfers between devices: 24 us -> 25.8 us  [twin(): return lax.ppermute(x, 'replica', [(i, i ^ 1) for i in range(reps)])]
where the time goes in v6:
time: 104 us
  blocking collectives  43.1 us (41%)
  starting transfers between devices  34.3 us (33%)
  waiting for transfers between devices  16.8 us (16%)
  Pallas kernels  9.32 us (9%)
    ppermute x10, starting transfers between devices, twin(): return lax.ppermute(x, 'replica', [(i, i ^ 1) for i in range(reps)])  25.8 us
    all_to_all x1, blocking collectives, on_device(): lax.all_to_all(outgoing, 'fsdp', 0, 0, tiled=True, axis_index_groups=ring)  22.5 us
    all_to_all x1, blocking collectives, on_device(): lax.all_to_all(back, 'fsdp', 0, 0, tiled=True, axis_index_groups=ring)  20.6 us
    ppermute x9, waiting for transfers between devices, exchange(): return lax.ppermute(x, 'replica', perm)  14.4 us
    ppermute x9, starting transfers between devices, exchange(): return lax.ppermute(x, 'replica', perm)  8.57 us
    pallas_call x2, Pallas kernels, on_device(): local(functools.partial(send_kernel, kinds=kinds, **sizes), [smem, pl.Blo...  2.44 us
    ppermute x10, waiting for transfers between devices, twin(): return lax.ppermute(x, 'replica', [(i, i ^ 1) for i in range(reps)])  2.39 us
  transfers between devices with their start and end apart: 19, of which 7 were waited for; matrix products, arithmetic and copies ran while one was open for 0% of the time, Pallas kernels for 1%

profile of v6, /device:TPU:1, one launch (start us, length us, event | category | flops | bytes accessed | tf_op | source)
XLA Modules:
  0.0 103.8 jit_solution(51473058387289054)
XLA Ops:
  0.0 1.3 %shard_map.48 = bf16[2,4,8,32,128]{4,3,2,1,0:T(8,128)(2,1)S(1)} custom-call(s32[1]{0:T(128)} %bitcast.place, bf16[1,4,32,8192]{3,2,1,0:T(8,128)(2,1)} %grads_ref.7), custom_call_target="tpu_custom_call" | custom-call | tf_op jit(solution)/shard_map/pallas_call | solution.py:241
  1.3 3.3 %collective-permute-start.1 = (bf16[2,4,8,32,128]{4,3,2,1,0:T(8,128)(2,1)S(1)}, bf16[2,4,8,32,128]{4,3,2,1,0:T(8,128)(2,1)S(1)}, u32[]{:S(2)}, u32[]{:S(2)}) collective-permute-start(bf16[2,4,8,32,128]{4,3,2,1,0:T(8,128)(2,1)S(1)} %shard_map.48), channel_id=1, source_target_pairs={{0,32},{32,0},{64,96},{96,64},{128,160},{160,128},{192,224},{224,1... | collective-permute-start | bytes 1572872 | tf_op jit(solution)/shard_map/ppermute | solution.py:218
  4.6 1.1 %shard_map.46 = bf16[2,4,8,32,128]{4,3,2,1,0:T(8,128)(2,1)S(1)} custom-call(s32[1]{0:T(128)} %bitcast.place, bf16[1,4,32,8192]{3,2,1,0:T(8,128)(2,1)} %grads_ref.7), custom_call_target="tpu_custom_call" | custom-call | tf_op jit(solution)/shard_map/pallas_call | solution.py:241
  6.4 1.1 %collective-permute-start.3 = (bf16[4,8,32,128]{3,2,1,0:T(8,128)(2,1)S(1)}, bf16[4,8,32,128]{3,2,1,0:T(8,128)(2,1)S(1)}, u32[]{:S(2)}, u32[]{:S(2)}) collective-permute-start(bf16[4,8,32,128]{3,2,1,0:T(8,128)(2,1)S(1)} %get-tuple-element.17), channel_id=1, source_target_pairs={{0,64},{32,224},{64,0},{96,160},{128,192},{160,96},{192,128},{224,... | collective-permute-start | bytes 786440 | tf_op jit(solution)/shard_map/ppermute | solution.py:222
  7.4 1.7 %collective-permute-start.2 = (bf16[4,8,32,128]{3,2,1,0:T(8,128)(2,1)S(1)}, bf16[4,8,32,128]{3,2,1,0:T(8,128)(2,1)S(1)}, u32[]{:S(2)}, u32[]{:S(2)}) collective-permute-start(bf16[4,8,32,128]{3,2,1,0:T(8,128)(2,1)S(1)} %get-tuple-element.15), channel_id=1, source_target_pairs={{0,64},{32,224},{64,0},{96,160},{128,192},{160,96},{192,128},{224,... | collective-permute-start | bytes 786440 | tf_op jit(solution)/shard_map/ppermute | solution.py:222
  9.3 3.6 %collective-permute-done.3.y_ref = bf16[4,8,32,128]{3,2,1,0:T(8,128)(2,1)S(1)} collective-permute-done((bf16[4,8,32,128]{3,2,1,0:T(8,128)(2,1)S(1)}, bf16[4,8,32,128]{3,2,1,0:T(8,128)(2,1)S(1)}, u32[]{:S(2)}, u32[]{:S(2)}) %collective-permute-start.3) | collective-permute-done | bytes 262176 | tf_op jit(solution)/shard_map/ppermute | solution.py:222
  13.0 2.6 %collective-permute-done.2.refs_1_ = bf16[4,8,32,128]{3,2,1,0:T(8,128)(2,1)S(1)} collective-permute-done((bf16[4,8,32,128]{3,2,1,0:T(8,128)(2,1)S(1)}, bf16[4,8,32,128]{3,2,1,0:T(8,128)(2,1)S(1)}, u32[]{:S(2)}, u32[]{:S(2)}) %collective-permute-start.2) | collective-permute-done | bytes 262176 | tf_op jit(solution)/shard_map/ppermute | solution.py:222
  15.7 2.9 %collective-permute-done.4.refs_2_ = bf16[4,8,32,128]{3,2,1,0:T(8,128)(2,1)S(1)} collective-permute-done((bf16[4,8,32,128]{3,2,1,0:T(8,128)(2,1)S(1)}, bf16[4,8,32,128]{3,2,1,0:T(8,128)(2,1)S(1)}, u32[]{:S(2)}, u32[]{:S(2)}) %collective-permute-start.4) | collective-permute-done | bytes 262176 | tf_op jit(solution)/shard_map/ppermute | solution.py:222
  19.6 22.5 %all_to_all.10.block_ref = bf16[32,2,32,128]{3,2,1,0:T(8,128)(2,1)S(1)} all-to-all(bf16[32,2,32,128]{3,2,1,0:T(8,128)(2,1)S(1)} %shard_map.51), channel_id=1, replica_groups={{0,12,24,4,16,28,8,20,1,13,25,5,17,29,9,21,2,14,26,6,18,30,10,22,3,15,2..., dimensions={0} | all-to-all | bytes 1048576 | tf_op jit(solution)/shard_map/all_to_all | solution.py:263
  42.1 1.4 %shard_map.52 = (bf16[2,256,128]{2,1,0:T(8,128)(2,1)S(1)}, bf16[2,256,128]{2,1,0:T(8,128)(2,1)S(1)}, bf16[2,256,128]{2,1,0:T(8,128)(2,1)S(1)}, bf16[2,256,128]{2,1,0:T(8,128)(2,1)S(1)}, f32[2,8,128]{2,1,0:T(8,128)S(1)}) custom-call(s32[1]{0:T(128)} %bitcast.place, bf16[2,1024,1024]{2,1,0:T(8,128)(2,1)S(1)} %copy-done.1, ...), custom_call_target="tpu_custom_call" | custom-call | tf_op jit(solution)/shard_map/pallas_call | solution.py:266
  43.5 3.7 %collective-permute-start.5 = (bf16[2,256,128]{2,1,0:T(8,128)(2,1)S(1)}, bf16[2,256,128]{2,1,0:T(8,128)(2,1)S(1)}, u32[]{:S(2)}, u32[]{:S(2)}) collective-permute-start(bf16[2,256,128]{2,1,0:T(8,128)(2,1)S(1)} %get-tuple-element.19), channel_id=1, source_target_pairs={{0,128},{32,160},{64,192},{96,224},{128,0},{160,32},{192,64},{224,... | collective-permute-start | bytes 393224 | tf_op jit(solution)/shard_map/ppermute | solution.py:222
  48.0 5.2 %collective-permute-start.8 = (bf16[2,256,128]{2,1,0:T(8,128)(2,1)S(1)}, bf16[2,256,128]{2,1,0:T(8,128)(2,1)S(1)}, u32[]{:S(2)}, u32[]{:S(2)}) collective-permute-start(bf16[2,256,128]{2,1,0:T(8,128)(2,1)S(1)} %get-tuple-element.18.refs_0_), channel_id=1, source_target_pairs={{0,32},{32,0},{64,96},{96,64},{128,160},{160,128},{192,224},{224,1... | collective-permute-start | bytes 393224 | tf_op jit(solution)/shard_map/ppermute | solution.py:218
  53.1 2.4 %collective-permute-start.9 = (bf16[2,256,128]{2,1,0:T(8,128)(2,1)S(1)}, bf16[2,256,128]{2,1,0:T(8,128)(2,1)S(1)}, u32[]{:S(2)}, u32[]{:S(2)}) collective-permute-start(bf16[2,256,128]{2,1,0:T(8,128)(2,1)S(1)} %collective-permute-done.5.refs_1_), channel_id=1, source_target_pairs={{0,32},{32,0},{64,96},{96,64},{128,160},{160,128},{192,224},{224,1... | collective-permute-start | bytes 393224 | tf_op jit(solution)/shard_map/ppermute | solution.py:218
  55.5 1.7 %collective-permute-start.11 = (bf16[2,256,128]{2,1,0:T(8,128)(2,1)S(1)}, bf16[2,256,128]{2,1,0:T(8,128)(2,1)S(1)}, u32[]{:S(2)}, u32[]{:S(2)}) collective-permute-start(bf16[2,256,128]{2,1,0:T(8,128)(2,1)S(1)} %collective-permute-done.6.refs_2_), channel_id=1, source_target_pairs={{0,32},{32,0},{64,96},{96,64},{128,160},{160,128},{192,224},{224,1... | collective-permute-start | bytes 393224 | tf_op jit(solution)/shard_map/ppermute | solution.py:218
  57.2 1.8 %collective-permute-start.10 = (bf16[2,256,128]{2,1,0:T(8,128)(2,1)S(1)}, bf16[2,256,128]{2,1,0:T(8,128)(2,1)S(1)}, u32[]{:S(2)}, u32[]{:S(2)}) collective-permute-start(bf16[2,256,128]{2,1,0:T(8,128)(2,1)S(1)} %collective-permute-done.7.refs_3_), channel_id=1, source_target_pairs={{0,32},{32,0},{64,96},{96,64},{128,160},{160,128},{192,224},{224,1... | collective-permute-start | bytes 393224 | tf_op jit(solution)/shard_map/ppermute | solution.py:218
  60.0 1.1 %shard_map.53 = bf16[32,8,1152]{2,1,0:T(8,128)(2,1)S(1)} custom-call(s32[1]{0:T(128)} %bitcast.place, bf16[2,256,128]{2,1,0:T(8,128)(2,1)S(1)} %get-tuple-element.18.refs_0_, bf16[2,256,128]{2,1,0:T(8,128)(2,1)S(1)} %collective-permute-done.5.refs_1_, bf16[2,256,128]{2,1,0:T(8,128)(2,1)S(1)} %collective-permute-done.6.refs_2_, ...), custom_call_target="tpu_custom_call" | custom-call | tf_op jit(solution)/shard_map/pallas_call | solution.py:276
  61.2 20.6 %all_to_all.11.back_ref = bf16[32,8,1152]{2,1,0:T(8,128)(2,1)S(1)} all-to-all(bf16[32,8,1152]{2,1,0:T(8,128)(2,1)S(1)} %shard_map.53), channel_id=1, replica_groups={{0,12,24,4,16,28,8,20,1,13,25,5,17,29,9,21,2,14,26,6,18,30,10,22,3,15,2..., dimensions={0} | all-to-all | bytes 1179648 | tf_op jit(solution)/shard_map/all_to_all | solution.py:283
  81.7 1.2 %shard_map.54.refs_0_ = bf16[130,8,128]{2,1,0:T(8,128)(2,1)S(1)} custom-call(s32[32]{0:T(128)S(1)} %copy-done.3, bf16[32,8,1152]{2,1,0:T(8,128)(2,1)S(1)} %all_to_all.11.back_ref), custom_call_target="tpu_custom_call" | custom-call | tf_op jit(solution)/shard_map/pallas_call | solution.py:286
  83.0 1.2 %collective-permute-start.12 = (bf16[130,8,128]{2,1,0:T(8,128)(2,1)S(1)}, bf16[130,8,128]{2,1,0:T(8,128)(2,1)S(1)}, u32[]{:S(2)}, u32[]{:S(2)}) collective-permute-start(bf16[130,8,128]{2,1,0:T(8,128)(2,1)S(1)} %shard_map.54.refs_0_), channel_id=1, source_target_pairs={{0,64},{32,224},{64,0},{96,160},{128,192},{160,96},{192,128},{224,... | collective-permute-start | bytes 798728 | tf_op jit(solution)/shard_map/ppermute | solution.py:222
  84.2 5.3 %collective-permute-done.12.refs_1_ = bf16[130,8,128]{2,1,0:T(8,128)(2,1)S(1)} collective-permute-done((bf16[130,8,128]{2,1,0:T(8,128)(2,1)S(1)}, bf16[130,8,128]{2,1,0:T(8,128)(2,1)S(1)}, u32[]{:S(2)}, u32[]{:S(2)}) %collective-permute-start.12) | collective-permute-done | bytes 266272 | tf_op jit(solution)/shard_map/ppermute | solution.py:222
  89.5 6.0 %collective-permute-start.15 = (bf16[130,8,128]{2,1,0:T(8,128)(2,1)S(1)}, bf16[130,8,128]{2,1,0:T(8,128)(2,1)S(1)}, u32[]{:S(2)}, u32[]{:S(2)}) collective-permute-start(bf16[130,8,128]{2,1,0:T(8,128)(2,1)S(1)} %shard_map.54.refs_0_), channel_id=1, source_target_pairs={{0,32},{32,0},{64,96},{96,64},{128,160},{160,128},{192,224},{224,1... | collective-permute-start | bytes 798728 | tf_op jit(solution)/shard_map/ppermute | solution.py:218
  96.1 4.7 %collective-permute-start.18 = (bf16[130,8,128]{2,1,0:T(8,128)(2,1)S(1)}, bf16[130,8,128]{2,1,0:T(8,128)(2,1)S(1)}, u32[]{:S(2)}, u32[]{:S(2)}) collective-permute-start(bf16[130,8,128]{2,1,0:T(8,128)(2,1)S(1)} %collective-permute-done.14.refs_3_), channel_id=1, source_target_pairs={{0,32},{32,0},{64,96},{96,64},{128,160},{160,128},{192,224},{224,1... | collective-permute-start | bytes 798728 | tf_op jit(solution)/shard_map/ppermute | solution.py:218
  100.8 1.2 %collective-permute-done.18.refs_7_ = bf16[130,8,128]{2,1,0:T(8,128)(2,1)S(1)} collective-permute-done((bf16[130,8,128]{2,1,0:T(8,128)(2,1)S(1)}, bf16[130,8,128]{2,1,0:T(8,128)(2,1)S(1)}, u32[]{:S(2)}, u32[]{:S(2)}) %collective-permute-start.18) | collective-permute-done | bytes 266272 | tf_op jit(solution)/shard_map/ppermute | solution.py:218
  102.0 1.7 %shard_map.55 = bf16[4,32,8192]{2,1,0:T(8,128)(2,1)} custom-call(s32[1]{0:T(128)} %bitcast.place, bf16[130,8,128]{2,1,0:T(8,128)(2,1)S(1)} %shard_map.54.refs_0_, bf16[130,8,128]{2,1,0:T(8,128)(2,1)S(1)} %collective-permute-done.12.refs_1_, bf16[130,8,128]{2,1,0:T(8,128)(2,1)S(1)} %collective-permute-done.13.refs_2_, ...), custom_call_target="tpu_custom_call" | custom-call | tf_op jit(solution)/shard_map/pallas_call | solution.py:292
  (34 shorter events, 4.3 us)
Async XLA Ops:
  0.0 6.2 %copy-start = (bf16[1,4,32,8192]{3,2,1,0:T(8,128)(2,1)S(1)}, bf16[1,4,32,8192]{3,2,1,0:T(8,128)(2,1)}, u32[]{:S(2)}) copy-start(bf16[1,4,32,8192]{3,2,1,0:T(8,128)(2,1)} %grads_ref.7) | copy-start | bytes 6291460
  1.3 17.2 %copy-start.3 = (s32[32]{0:T(128)S(1)}, s32[32]{0:T(128)}, u32[]{:S(2)}) copy-start(s32[32]{0:T(128)} %slot.3) | copy-start | bytes 388
  1.3 4.9 %collective-permute-start.1 = (bf16[2,4,8,32,128]{4,3,2,1,0:T(8,128)(2,1)S(1)}, bf16[2,4,8,32,128]{4,3,2,1,0:T(8,128)(2,1)S(1)}, u32[]{:S(2)}, u32[]{:S(2)}) collective-permute-start(bf16[2,4,8,32,128]{4,3,2,1,0:T(8,128)(2,1)S(1)} %shard_map.48), channel_id=1, source_target_pairs={{0,32},{32,0},{64,96},{96,64},{128,160},{160,128},{192,224},{224,1... | collective-permute-start | bytes 1572872 | tf_op jit(solution)/shard_map/ppermute | solution.py:218
  5.8 36.3 %copy-start.1 = (bf16[2,1024,1024]{2,1,0:T(8,128)(2,1)S(1)}, bf16[2,1024,1024]{2,1,0:T(8,128)(2,1)}, u32[]{:S(2)}) copy-start(bf16[2,1024,1024]{2,1,0:T(8,128)(2,1)} %left_ref.1) | copy-start | bytes 12582916
  5.8 3.3 %collective-permute-start = (bf16[2,4,8,32,128]{4,3,2,1,0:T(8,128)(2,1)S(1)}, bf16[2,4,8,32,128]{4,3,2,1,0:T(8,128)(2,1)S(1)}, u32[]{:S(2)}, u32[]{:S(2)}) collective-permute-start(bf16[2,4,8,32,128]{4,3,2,1,0:T(8,128)(2,1)S(1)} %shard_map.46), channel_id=1, source_target_pairs={{0,32},{32,0},{64,96},{96,64},{128,160},{160,128},{192,224},{224,1... | collective-permute-start | bytes 1572872 | tf_op jit(solution)/shard_map/ppermute | solution.py:218
  6.4 6.5 %collective-permute-start.3 = (bf16[4,8,32,128]{3,2,1,0:T(8,128)(2,1)S(1)}, bf16[4,8,32,128]{3,2,1,0:T(8,128)(2,1)S(1)}, u32[]{:S(2)}, u32[]{:S(2)}) collective-permute-start(bf16[4,8,32,128]{3,2,1,0:T(8,128)(2,1)S(1)} %get-tuple-element.17), channel_id=1, source_target_pairs={{0,64},{32,224},{64,0},{96,160},{128,192},{160,96},{192,128},{224,... | collective-permute-start | bytes 786440 | tf_op jit(solution)/shard_map/ppermute | solution.py:222
  7.4 8.2 %collective-permute-start.2 = (bf16[4,8,32,128]{3,2,1,0:T(8,128)(2,1)S(1)}, bf16[4,8,32,128]{3,2,1,0:T(8,128)(2,1)S(1)}, u32[]{:S(2)}, u32[]{:S(2)}) collective-permute-start(bf16[4,8,32,128]{3,2,1,0:T(8,128)(2,1)S(1)} %get-tuple-element.15), channel_id=1, source_target_pairs={{0,64},{32,224},{64,0},{96,160},{128,192},{160,96},{192,128},{224,... | collective-permute-start | bytes 786440 | tf_op jit(solution)/shard_map/ppermute | solution.py:222
  9.3 50.7 %copy-start.2 = (bf16[2,1024,1024]{2,1,0:T(8,128)(2,1)S(1)}, bf16[2,1024,1024]{2,1,0:T(8,128)(2,1)}, u32[]{:S(2)}) copy-start(bf16[2,1024,1024]{2,1,0:T(8,128)(2,1)} %refs_8_.1) | copy-start | bytes 12582916
  12.9 5.6 %collective-permute-start.4 = (bf16[4,8,32,128]{3,2,1,0:T(8,128)(2,1)S(1)}, bf16[4,8,32,128]{3,2,1,0:T(8,128)(2,1)S(1)}, u32[]{:S(2)}, u32[]{:S(2)}) collective-permute-start(bf16[4,8,32,128]{3,2,1,0:T(8,128)(2,1)S(1)} %shard_map.50), channel_id=1, source_target_pairs={{0,192},{32,96},{64,128},{96,32},{128,64},{160,224},{192,0},{224,1... | collective-permute-start | bytes 786440 | tf_op jit(solution)/shard_map/ppermute | solution.py:222
  43.5 9.6 %collective-permute-start.5 = (bf16[2,256,128]{2,1,0:T(8,128)(2,1)S(1)}, bf16[2,256,128]{2,1,0:T(8,128)(2,1)S(1)}, u32[]{:S(2)}, u32[]{:S(2)}) collective-permute-start(bf16[2,256,128]{2,1,0:T(8,128)(2,1)S(1)} %get-tuple-element.19), channel_id=1, source_target_pairs={{0,128},{32,160},{64,192},{96,224},{128,0},{160,32},{192,64},{224,... | collective-permute-start | bytes 393224 | tf_op jit(solution)/shard_map/ppermute | solution.py:222
  47.2 8.3 %collective-permute-start.6 = (bf16[2,256,128]{2,1,0:T(8,128)(2,1)S(1)}, bf16[2,256,128]{2,1,0:T(8,128)(2,1)S(1)}, u32[]{:S(2)}, u32[]{:S(2)}) collective-permute-start(bf16[2,256,128]{2,1,0:T(8,128)(2,1)S(1)} %get-tuple-element.20), channel_id=1, source_target_pairs={{0,64},{32,224},{64,0},{96,160},{128,192},{160,96},{192,128},{224,... | collective-permute-start | bytes 393224 | tf_op jit(solution)/shard_map/ppermute | solution.py:222
  48.0 9.2 %collective-permute-start.7 = (bf16[2,256,128]{2,1,0:T(8,128)(2,1)S(1)}, bf16[2,256,128]{2,1,0:T(8,128)(2,1)S(1)}, u32[]{:S(2)}, u32[]{:S(2)}) collective-permute-start(bf16[2,256,128]{2,1,0:T(8,128)(2,1)S(1)} %get-tuple-element.21), channel_id=1, source_target_pairs={{0,192},{32,96},{64,128},{96,32},{128,64},{160,224},{192,0},{224,1... | collective-permute-start | bytes 393224 | tf_op jit(solution)/shard_map/ppermute | solution.py:222
  48.0 11.1 %collective-permute-start.8 = (bf16[2,256,128]{2,1,0:T(8,128)(2,1)S(1)}, bf16[2,256,128]{2,1,0:T(8,128)(2,1)S(1)}, u32[]{:S(2)}, u32[]{:S(2)}) collective-permute-start(bf16[2,256,128]{2,1,0:T(8,128)(2,1)S(1)} %get-tuple-element.18.refs_0_), channel_id=1, source_target_pairs={{0,32},{32,0},{64,96},{96,64},{128,160},{160,128},{192,224},{224,1... | collective-permute-start | bytes 393224 | tf_op jit(solution)/shard_map/ppermute | solution.py:218
  53.1 5.9 %collective-permute-start.9 = (bf16[2,256,128]{2,1,0:T(8,128)(2,1)S(1)}, bf16[2,256,128]{2,1,0:T(8,128)(2,1)S(1)}, u32[]{:S(2)}, u32[]{:S(2)}) collective-permute-start(bf16[2,256,128]{2,1,0:T(8,128)(2,1)S(1)} %collective-permute-done.5.refs_1_), channel_id=1, source_target_pairs={{0,32},{32,0},{64,96},{96,64},{128,160},{160,128},{192,224},{224,1... | collective-permute-start | bytes 393224 | tf_op jit(solution)/shard_map/ppermute | solution.py:218
  55.5 3.5 %collective-permute-start.11 = (bf16[2,256,128]{2,1,0:T(8,128)(2,1)S(1)}, bf16[2,256,128]{2,1,0:T(8,128)(2,1)S(1)}, u32[]{:S(2)}, u32[]{:S(2)}) collective-permute-start(bf16[2,256,128]{2,1,0:T(8,128)(2,1)S(1)} %collective-permute-done.6.refs_2_), channel_id=1, source_target_pairs={{0,32},{32,0},{64,96},{96,64},{128,160},{160,128},{192,224},{224,1... | collective-permute-start | bytes 393224 | tf_op jit(solution)/shard_map/ppermute | solution.py:218
  57.2 2.8 %collective-permute-start.10 = (bf16[2,256,128]{2,1,0:T(8,128)(2,1)S(1)}, bf16[2,256,128]{2,1,0:T(8,128)(2,1)S(1)}, u32[]{:S(2)}, u32[]{:S(2)}) collective-permute-start(bf16[2,256,128]{2,1,0:T(8,128)(2,1)S(1)} %collective-permute-done.7.refs_3_), channel_id=1, source_target_pairs={{0,32},{32,0},{64,96},{96,64},{128,160},{160,128},{192,224},{224,1... | collective-permute-start | bytes 393224 | tf_op jit(solution)/shard_map/ppermute | solution.py:218
  83.0 6.6 %collective-permute-start.12 = (bf16[130,8,128]{2,1,0:T(8,128)(2,1)S(1)}, bf16[130,8,128]{2,1,0:T(8,128)(2,1)S(1)}, u32[]{:S(2)}, u32[]{:S(2)}) collective-permute-start(bf16[130,8,128]{2,1,0:T(8,128)(2,1)S(1)} %shard_map.54.refs_0_), channel_id=1, source_target_pairs={{0,64},{32,224},{64,0},{96,160},{128,192},{160,96},{192,128},{224,... | collective-permute-start | bytes 798728 | tf_op jit(solution)/shard_map/ppermute | solution.py:222
  84.1 11.5 %collective-permute-start.13 = (bf16[130,8,128]{2,1,0:T(8,128)(2,1)S(1)}, bf16[130,8,128]{2,1,0:T(8,128)(2,1)S(1)}, u32[]{:S(2)}, u32[]{:S(2)}) collective-permute-start(bf16[130,8,128]{2,1,0:T(8,128)(2,1)S(1)} %shard_map.54.refs_0_), channel_id=1, source_target_pairs={{0,192},{32,96},{64,128},{96,32},{128,64},{160,224},{192,0},{224,1... | collective-permute-start | bytes 798728 | tf_op jit(solution)/shard_map/ppermute | solution.py:222
  89.5 6.6 %collective-permute-start.14 = (bf16[130,8,128]{2,1,0:T(8,128)(2,1)S(1)}, bf16[130,8,128]{2,1,0:T(8,128)(2,1)S(1)}, u32[]{:S(2)}, u32[]{:S(2)}) collective-permute-start(bf16[130,8,128]{2,1,0:T(8,128)(2,1)S(1)} %collective-permute-done.12.refs_1_), channel_id=1, source_target_pairs={{0,192},{32,96},{64,128},{96,32},{128,64},{160,224},{192,0},{224,1... | collective-permute-start | bytes 798728 | tf_op jit(solution)/shard_map/ppermute | solution.py:222
  89.5 11.3 %collective-permute-start.15 = (bf16[130,8,128]{2,1,0:T(8,128)(2,1)S(1)}, bf16[130,8,128]{2,1,0:T(8,128)(2,1)S(1)}, u32[]{:S(2)}, u32[]{:S(2)}) collective-permute-start(bf16[130,8,128]{2,1,0:T(8,128)(2,1)S(1)} %shard_map.54.refs_0_), channel_id=1, source_target_pairs={{0,32},{32,0},{64,96},{96,64},{128,160},{160,128},{192,224},{224,1... | collective-permute-start | bytes 798728 | tf_op jit(solution)/shard_map/ppermute | solution.py:218
  95.6 5.2 %collective-permute-start.17 = (bf16[130,8,128]{2,1,0:T(8,128)(2,1)S(1)}, bf16[130,8,128]{2,1,0:T(8,128)(2,1)S(1)}, u32[]{:S(2)}, u32[]{:S(2)}) collective-permute-start(bf16[130,8,128]{2,1,0:T(8,128)(2,1)S(1)} %collective-permute-done.12.refs_1_), channel_id=1, source_target_pairs={{0,32},{32,0},{64,96},{96,64},{128,160},{160,128},{192,224},{224,1... | collective-permute-start | bytes 798728 | tf_op jit(solution)/shard_map/ppermute | solution.py:218
  95.6 5.2 %collective-permute-start.16 = (bf16[130,8,128]{2,1,0:T(8,128)(2,1)S(1)}, bf16[130,8,128]{2,1,0:T(8,128)(2,1)S(1)}, u32[]{:S(2)}, u32[]{:S(2)}) collective-permute-start(bf16[130,8,128]{2,1,0:T(8,128)(2,1)S(1)} %collective-permute-done.13.refs_2_), channel_id=1, source_target_pairs={{0,32},{32,0},{64,96},{96,64},{128,160},{160,128},{192,224},{224,1... | collective-permute-start | bytes 798728 | tf_op jit(solution)/shard_map/ppermute | solution.py:218
  96.1 5.9 %collective-permute-start.18 = (bf16[130,8,128]{2,1,0:T(8,128)(2,1)S(1)}, bf16[130,8,128]{2,1,0:T(8,128)(2,1)S(1)}, u32[]{:S(2)}, u32[]{:S(2)}) collective-permute-start(bf16[130,8,128]{2,1,0:T(8,128)(2,1)S(1)} %collective-permute-done.14.refs_3_), channel_id=1, source_target_pairs={{0,32},{32,0},{64,96},{96,64},{128,160},{160,128},{192,224},{224,1... | collective-permute-start | bytes 798728 | tf_op jit(solution)/shard_map/ppermute | solution.py:218

commit v7 on v4

--- a/solution.py
+++ b/solution.py
@@ -26,9 +26,8 @@
     return lax.bitwise_xor(place[0] // 2, jnp.int32(masks(lax.rem(place[0], 2))[relative]))
 
 
-def strip_columns(place, relative, core, j, width, strip):
-    index = 2 * chip(place, relative) + core
-    return pl.ds(pl.multiple_of(j * width + index * strip, strip), strip)
+def strip_index(place, relative, core):
+    return 2 * chip(place, relative) + core
 
 
 def together(copies):
@@ -39,27 +38,22 @@
         copy.wait()
 
 
-def send_kernel(place, grads_ref, send_ref, arrived, *, kinds, cols, width, strip):
+def send_kernel(place, grads_ref, send_ref, arrived, *, kinds):
     other = 1 - lax.rem(place[0], 2)
     order = (SELF, FAR, NEAR, OPPOSITE)
     together(
         pltpu.make_async_copy(
-            grads_ref.at[0, :, :, strip_columns(place, order[k], other, j, width, strip)],
-            send_ref.at[n, :, j],
-            arrived.at[n * cols + j],
+            grads_ref.at[:, :, :, strip_index(place, order[k], other)], send_ref.at[n], arrived.at[n]
         )
         for n, k in enumerate(kinds)
-        for j in range(cols)
     )
 
 
-def pair_sum_kernel(place, grads_ref, got_ref, *sum_refs, kinds, cols, width, strip):
+def pair_sum_kernel(place, grads_ref, got_ref, *sum_refs, kinds):
     core = lax.rem(place[0], 2)
     for n, (k, sum_ref) in enumerate(zip(kinds, sum_refs)):
-        for m in range(grads_ref.shape[1]):
-            for j in range(cols):
-                piece = grads_ref[0, m, :, strip_columns(place, k, core, j, width, strip)]
-                sum_ref[m, j] = (piece.astype(f32) + got_ref[n, m, j].astype(f32)).astype(bf16)
+        piece = grads_ref[:, :, :, strip_index(place, k, core)]
+        sum_ref[...] = (piece.astype(f32) + got_ref[n].astype(f32)).astype(bf16)
 
 
 def add_kernel(x_ref, y_ref, out_ref):
@@ -69,13 +63,13 @@
 def route_kernel(slot, *refs):
     *terms, out_ref = refs
     slots = out_ref.shape[1]
-    cols = terms[0].shape[1]
+    cols = terms[0].shape[2]
     out_ref[...] = jnp.zeros_like(out_ref)
     for m in range(terms[0].shape[0]):
         for j in range(cols):
             q = slot[m * cols + j]
-            total = sum(term[m, j].astype(f32) for term in terms)
-            out_ref[q // slots, lax.rem(q, slots)] = total.astype(bf16)
+            total = sum(term[m, :, j].astype(f32) for term in terms)
+            out_ref[q // slots, lax.rem(q, slots)] = total.reshape(out_ref.shape[2:]).astype(bf16)
 
 
 def left_kernel(place, left_ref, block_ref, *out_refs):
@@ -166,7 +160,8 @@
     def emit(m, core, odd):
         couples = ((SELF, FAR), (OPPOSITE, NEAR)) if core else ((SELF, NEAR), (OPPOSITE, FAR))
         for couple in couples:
-            at = pl.ds(pl.multiple_of(chip(place, couple[0]) // 2 * 2 * part, 2 * part), 2 * part)
+            side = chip(place, couple[0]) // 2
+            at = lines(side)
             for j in range(count):
                 b = m * count + j
                 for refs, c in ((own_refs, core), (twin_refs, 1 - core)):
@@ -176,9 +171,13 @@
                         ]
                         columns = pl.ds(((2 * j + c) * each + t) * LANES, LANES)
                         ready[m, at, columns] = jnp.concatenate(tiles, 0).astype(bf16)
-
-    def write(m):
-        return pltpu.make_async_copy(ready.at[m], out_ref.at[m], written.at[m])
+            write(m, side).start()
+
+    def lines(side):
+        return pl.ds(pl.multiple_of(side * 2 * part, 2 * part), 2 * part)
+
+    def write(m, side):
+        return pltpu.make_async_copy(ready.at[m, lines(side)], out_ref.at[m, lines(side)], written.at[m, side])
 
     @pl.loop(0, mats)
     def _(m):
@@ -186,10 +185,10 @@
             for odd in range(2):
                 here = (lax.rem(place[0], 2) == core) & (lax.rem(place[0] // 2, 2) == odd)
                 pl.when(here)(functools.partial(emit, m, core, odd))
-        write(m).start()
 
     for m in range(mats):
-        write(m).wait()
+        for side in range(2):
+            write(m, side).wait()
 
 
 def on_device(grads, left_root, right_root, block_slot):
@@ -211,9 +210,11 @@
         perm = [(i, i ^ (2 * masks(i % 2)[relative])) for i in range(reps)]
         return lax.ppermute(x, "replica", perm)
 
-    sizes = dict(cols=cols, width=width, strip=strip)
+    group = 8
+    tiles = grads.reshape(mats, rows // group, group, cols, reps, strip).transpose(0, 1, 3, 4, 2, 5)
+
     def strips(*n):
-        return shape((*n, mats, cols, rows, strip), bf16)
+        return shape((*n, mats, rows // group, cols, group, strip), bf16)
 
     def local(kernel, in_specs, out_specs, out_shape, scratch_shapes=()):
         return pl.pallas_call(
@@ -229,16 +230,16 @@
     sums = {}
     for kinds in ((OPPOSITE, NEAR), (SELF, FAR)):
         send = local(
-            functools.partial(send_kernel, kinds=kinds, **sizes),
+            functools.partial(send_kernel, kinds=kinds),
             [smem, pl.BlockSpec(memory_space=pl.ANY)],
             vmem,
             strips(2),
-            [pltpu.SemaphoreType.DMA((2 * cols,))],
-        )(place, pltpu.with_memory_space_constraint(grads, pltpu.HBM))
+            [pltpu.SemaphoreType.DMA((2,))],
+        )(place, pltpu.with_memory_space_constraint(tiles, pltpu.HBM))
         got = twin(send)
         found = local(
-            functools.partial(pair_sum_kernel, kinds=kinds, **sizes), [smem, vmem, vmem], [vmem] * 2, [strips()] * 2
-        )(place, grads, got)
+            functools.partial(pair_sum_kernel, kinds=kinds), [smem, vmem, vmem], [vmem] * 2, [strips()] * 2
+        )(place, tiles, got)
         sums.update(zip(kinds, found))
 
     onward = exchange(sums[OPPOSITE], NEAR)
@@ -286,7 +287,7 @@
         [
             pltpu.VMEM((mats, rows, full), bf16),
             pltpu.VMEM((blocks, part, LANES), f32),
-            pltpu.SemaphoreType.DMA((mats,)),
+            pltpu.SemaphoreType.DMA((mats, 2)),
         ],
     )(place, *own, *other)
 

time: 104 us -> 104 us (level)
  no operation moved by 1% of the time
where the time goes in v7:
time: 104 us
  blocking collectives  45 us (43%)
  starting transfers between devices  32.2 us (31%)
  waiting for transfers between devices  17.4 us (17%)
  Pallas kernels  8.56 us (8%)
    ppermute x10, starting transfers between devices, twin(): return lax.ppermute(x, 'replica', [(i, i ^ 1) for i in range(reps)])  24 us
    all_to_all x1, blocking collectives, on_device(): incoming = lax.all_to_all(outgoing, 'fsdp', 0, 0, tiled=True)  23.5 us
    all_to_all x1, blocking collectives, on_device(): back = lax.all_to_all(back, 'fsdp', 0, 0, tiled=True)  21.5 us
    ppermute x9, waiting for transfers between devices, exchange(): return lax.ppermute(x, 'replica', perm)  14.9 us
    ppermute x9, starting transfers between devices, exchange(): return lax.ppermute(x, 'replica', perm)  8.22 us
    ppermute x10, waiting for transfers between devices, twin(): return lax.ppermute(x, 'replica', [(i, i ^ 1) for i in range(reps)])  2.5 us
    pallas_call x2, Pallas kernels, on_device(): local(functools.partial(send_kernel, kinds=kinds), [smem, pl.BlockSpec(me...  2.26 us
  transfers between devices with their start and end apart: 19, of which 7 were waited for; matrix products, arithmetic and copies ran while one was open for 0% of the time, Pallas kernels for 1%

profile of v7, /device:TPU:1, one launch (start us, length us, event | category | flops | bytes accessed | tf_op | source)
XLA Modules:
  0.0 103.5 jit_solution(13845494655449787889)
XLA Ops:
  0.0 1.2 %shard_map.48 = bf16[2,4,4,8,8,128]{5,4,3,2,1,0:T(8,128)(2,1)S(1)} custom-call(s32[1]{0:T(128)} %bitcast.place, bf16[4,4,8,8,8,128]{5,4,3,2,1,0:T(8,128)(2,1)} %bitcast.4), custom_call_target="tpu_custom_call" | custom-call | tf_op jit(solution)/shard_map/pallas_call | solution.py:232
  1.2 3.3 %collective-permute-start.1 = (bf16[2,4,4,8,8,128]{5,4,3,2,1,0:T(8,128)(2,1)S(1)}, bf16[2,4,4,8,8,128]{5,4,3,2,1,0:T(8,128)(2,1)S(1)}, u32[]{:S(2)}, u32[]{:S(2)}) collective-permute-start(bf16[2,4,4,8,8,128]{5,4,3,2,1,0:T(8,128)(2,1)S(1)} %shard_map.48), channel_id=1, source_target_pairs={{0,32},{32,0},{64,96},{96,64},{128,160},{160,128},{192,224},{224,1... | collective-permute-start | bytes 1572872 | tf_op jit(solution)/shard_map/ppermute | solution.py:207
  4.6 1.1 %shard_map.46 = bf16[2,4,4,8,8,128]{5,4,3,2,1,0:T(8,128)(2,1)S(1)} custom-call(s32[1]{0:T(128)} %bitcast.place, bf16[4,4,8,8,8,128]{5,4,3,2,1,0:T(8,128)(2,1)} %bitcast.5), custom_call_target="tpu_custom_call" | custom-call | tf_op jit(solution)/shard_map/pallas_call | solution.py:232
  6.3 1.1 %collective-permute-start.3 = (bf16[4,4,8,8,128]{4,3,2,1,0:T(8,128)(2,1)S(1)}, bf16[4,4,8,8,128]{4,3,2,1,0:T(8,128)(2,1)S(1)}, u32[]{:S(2)}, u32[]{:S(2)}) collective-permute-start(bf16[4,4,8,8,128]{4,3,2,1,0:T(8,128)(2,1)S(1)} %get-tuple-element.17), channel_id=1, source_target_pairs={{0,64},{32,224},{64,0},{96,160},{128,192},{160,96},{192,128},{224,... | collective-permute-start | bytes 786440 | tf_op jit(solution)/shard_map/ppermute | solution.py:211
  7.3 1.7 %collective-permute-start.2 = (bf16[4,4,8,8,128]{4,3,2,1,0:T(8,128)(2,1)S(1)}, bf16[4,4,8,8,128]{4,3,2,1,0:T(8,128)(2,1)S(1)}, u32[]{:S(2)}, u32[]{:S(2)}) collective-permute-start(bf16[4,4,8,8,128]{4,3,2,1,0:T(8,128)(2,1)S(1)} %get-tuple-element.15), channel_id=1, source_target_pairs={{0,64},{32,224},{64,0},{96,160},{128,192},{160,96},{192,128},{224,... | collective-permute-start | bytes 786440 | tf_op jit(solution)/shard_map/ppermute | solution.py:211
  9.2 3.6 %collective-permute-done.3.y_ref = bf16[4,4,8,8,128]{4,3,2,1,0:T(8,128)(2,1)S(1)} collective-permute-done((bf16[4,4,8,8,128]{4,3,2,1,0:T(8,128)(2,1)S(1)}, bf16[4,4,8,8,128]{4,3,2,1,0:T(8,128)(2,1)S(1)}, u32[]{:S(2)}, u32[]{:S(2)}) %collective-permute-start.3) | collective-permute-done | bytes 262176 | tf_op jit(solution)/shard_map/ppermute | solution.py:211
  13.0 2.6 %collective-permute-done.2.refs_1_ = bf16[4,4,8,8,128]{4,3,2,1,0:T(8,128)(2,1)S(1)} collective-permute-done((bf16[4,4,8,8,128]{4,3,2,1,0:T(8,128)(2,1)S(1)}, bf16[4,4,8,8,128]{4,3,2,1,0:T(8,128)(2,1)S(1)}, u32[]{:S(2)}, u32[]{:S(2)}) %collective-permute-start.2) | collective-permute-done | bytes 262176 | tf_op jit(solution)/shard_map/ppermute | solution.py:211
  15.6 2.9 %collective-permute-done.4.refs_2_ = bf16[4,4,8,8,128]{4,3,2,1,0:T(8,128)(2,1)S(1)} collective-permute-done((bf16[4,4,8,8,128]{4,3,2,1,0:T(8,128)(2,1)S(1)}, bf16[4,4,8,8,128]{4,3,2,1,0:T(8,128)(2,1)S(1)}, u32[]{:S(2)}, u32[]{:S(2)}) %collective-permute-start.4) | collective-permute-done | bytes 262176 | tf_op jit(solution)/shard_map/ppermute | solution.py:211
  19.2 23.5 %all_to_all.10.block_ref = bf16[32,2,32,128]{3,2,1,0:T(8,128)(2,1)S(1)} all-to-all(bf16[32,2,32,128]{3,2,1,0:T(8,128)(2,1)S(1)} %shard_map.51), channel_id=1, replica_groups=mesh['replica'=8,'fsdp'=32] {'fsdp'}, dimensions={0} | all-to-all | bytes 1048576 | tf_op jit(solution)/shard_map/all_to_all | solution.py:253
  42.7 1.4 %shard_map.52 = (bf16[2,256,128]{2,1,0:T(8,128)(2,1)S(1)}, bf16[2,256,128]{2,1,0:T(8,128)(2,1)S(1)}, bf16[2,256,128]{2,1,0:T(8,128)(2,1)S(1)}, bf16[2,256,128]{2,1,0:T(8,128)(2,1)S(1)}, f32[2,8,128]{2,1,0:T(8,128)S(1)}) custom-call(s32[1]{0:T(128)} %bitcast.place, bf16[2,1024,1024]{2,1,0:T(8,128)(2,1)S(1)} %copy-done.1, ...), custom_call_target="tpu_custom_call" | custom-call | tf_op jit(solution)/shard_map/pallas_call | solution.py:256
  44.2 3.9 %collective-permute-start.5 = (bf16[2,256,128]{2,1,0:T(8,128)(2,1)S(1)}, bf16[2,256,128]{2,1,0:T(8,128)(2,1)S(1)}, u32[]{:S(2)}, u32[]{:S(2)}) collective-permute-start(bf16[2,256,128]{2,1,0:T(8,128)(2,1)S(1)} %get-tuple-element.19), channel_id=1, source_target_pairs={{0,128},{32,160},{64,192},{96,224},{128,0},{160,32},{192,64},{224,... | collective-permute-start | bytes 393224 | tf_op jit(solution)/shard_map/ppermute | solution.py:211
  48.1 0.8 collective-permute-start.6
  48.8 4.2 %collective-permute-start.8 = (bf16[2,256,128]{2,1,0:T(8,128)(2,1)S(1)}, bf16[2,256,128]{2,1,0:T(8,128)(2,1)S(1)}, u32[]{:S(2)}, u32[]{:S(2)}) collective-permute-start(bf16[2,256,128]{2,1,0:T(8,128)(2,1)S(1)} %get-tuple-element.18.refs_0_), channel_id=1, source_target_pairs={{0,32},{32,0},{64,96},{96,64},{128,160},{160,128},{192,224},{224,1... | collective-permute-start | bytes 393224 | tf_op jit(solution)/shard_map/ppermute | solution.py:207
  53.0 3.4 %collective-permute-start.9 = (bf16[2,256,128]{2,1,0:T(8,128)(2,1)S(1)}, bf16[2,256,128]{2,1,0:T(8,128)(2,1)S(1)}, u32[]{:S(2)}, u32[]{:S(2)}) collective-permute-start(bf16[2,256,128]{2,1,0:T(8,128)(2,1)S(1)} %collective-permute-done.5.refs_1_), channel_id=1, source_target_pairs={{0,32},{32,0},{64,96},{96,64},{128,160},{160,128},{192,224},{224,1... | collective-permute-start | bytes 393224 | tf_op jit(solution)/shard_map/ppermute | solution.py:207
  57.1 1.8 %collective-permute-start.10 = (bf16[2,256,128]{2,1,0:T(8,128)(2,1)S(1)}, bf16[2,256,128]{2,1,0:T(8,128)(2,1)S(1)}, u32[]{:S(2)}, u32[]{:S(2)}) collective-permute-start(bf16[2,256,128]{2,1,0:T(8,128)(2,1)S(1)} %collective-permute-done.7.refs_3_), channel_id=1, source_target_pairs={{0,32},{32,0},{64,96},{96,64},{128,160},{160,128},{192,224},{224,1... | collective-permute-start | bytes 393224 | tf_op jit(solution)/shard_map/ppermute | solution.py:207
  58.9 1.0 collective-permute-done.10.refs_6_
  59.9 1.2 %shard_map.53 = bf16[32,8,1152]{2,1,0:T(8,128)(2,1)S(1)} custom-call(s32[1]{0:T(128)} %bitcast.place, bf16[2,256,128]{2,1,0:T(8,128)(2,1)S(1)} %get-tuple-element.18.refs_0_, bf16[2,256,128]{2,1,0:T(8,128)(2,1)S(1)} %collective-permute-done.5.refs_1_, bf16[2,256,128]{2,1,0:T(8,128)(2,1)S(1)} %collective-permute-done.6.refs_2_, ...), custom_call_target="tpu_custom_call" | custom-call | tf_op jit(solution)/shard_map/pallas_call | solution.py:266
  61.0 21.5 %all_to_all.11.back_ref = bf16[32,8,1152]{2,1,0:T(8,128)(2,1)S(1)} all-to-all(bf16[32,8,1152]{2,1,0:T(8,128)(2,1)S(1)} %shard_map.53), channel_id=1, replica_groups=mesh['replica'=8,'fsdp'=32] {'fsdp'}, dimensions={0} | all-to-all | bytes 1179648 | tf_op jit(solution)/shard_map/all_to_all | solution.py:273
  82.6 1.0 shard_map.54.refs_0_
  84.2 5.8 %collective-permute-done.12.refs_1_ = bf16[130,8,128]{2,1,0:T(8,128)(2,1)S(1)} collective-permute-done((bf16[130,8,128]{2,1,0:T(8,128)(2,1)S(1)}, bf16[130,8,128]{2,1,0:T(8,128)(2,1)S(1)}, u32[]{:S(2)}, u32[]{:S(2)}) %collective-permute-start.12) | collective-permute-done | bytes 266272 | tf_op jit(solution)/shard_map/ppermute | solution.py:211
  90.1 5.9 %collective-permute-start.15 = (bf16[130,8,128]{2,1,0:T(8,128)(2,1)S(1)}, bf16[130,8,128]{2,1,0:T(8,128)(2,1)S(1)}, u32[]{:S(2)}, u32[]{:S(2)}) collective-permute-start(bf16[130,8,128]{2,1,0:T(8,128)(2,1)S(1)} %shard_map.54.refs_0_), channel_id=1, source_target_pairs={{0,32},{32,0},{64,96},{96,64},{128,160},{160,128},{192,224},{224,1... | collective-permute-start | bytes 798728 | tf_op jit(solution)/shard_map/ppermute | solution.py:207
  96.5 4.1 %collective-permute-start.18 = (bf16[130,8,128]{2,1,0:T(8,128)(2,1)S(1)}, bf16[130,8,128]{2,1,0:T(8,128)(2,1)S(1)}, u32[]{:S(2)}, u32[]{:S(2)}) collective-permute-start(bf16[130,8,128]{2,1,0:T(8,128)(2,1)S(1)} %collective-permute-done.14.refs_3_), channel_id=1, source_target_pairs={{0,32},{32,0},{64,96},{96,64},{128,160},{160,128},{192,224},{224,1... | collective-permute-start | bytes 798728 | tf_op jit(solution)/shard_map/ppermute | solution.py:207
  100.6 1.2 %collective-permute-done.18.refs_7_ = bf16[130,8,128]{2,1,0:T(8,128)(2,1)S(1)} collective-permute-done((bf16[130,8,128]{2,1,0:T(8,128)(2,1)S(1)}, bf16[130,8,128]{2,1,0:T(8,128)(2,1)S(1)}, u32[]{:S(2)}, u32[]{:S(2)}) %collective-permute-start.18) | collective-permute-done | bytes 266272 | tf_op jit(solution)/shard_map/ppermute | solution.py:207
  101.8 1.6 %shard_map.55 = bf16[4,32,8192]{2,1,0:T(8,128)(2,1)} custom-call(s32[1]{0:T(128)} %bitcast.place, bf16[130,8,128]{2,1,0:T(8,128)(2,1)S(1)} %shard_map.54.refs_0_, bf16[130,8,128]{2,1,0:T(8,128)(2,1)S(1)} %collective-permute-done.12.refs_1_, bf16[130,8,128]{2,1,0:T(8,128)(2,1)S(1)} %collective-permute-done.13.refs_2_, ...), custom_call_target="tpu_custom_call" | custom-call | tf_op jit(solution)/shard_map/pallas_call | solution.py:282
  (34 shorter events, 3.7 us)
Async XLA Ops:
  0.0 6.1 %copy-start = (bf16[1,4,32,8192]{3,2,1,0:T(8,128)(2,1)S(1)}, bf16[1,4,32,8192]{3,2,1,0:T(8,128)(2,1)}, u32[]{:S(2)}) copy-start(bf16[1,4,32,8192]{3,2,1,0:T(8,128)(2,1)} %param.4) | copy-start | bytes 6291460
  1.2 17.2 %copy-start.3 = (s32[32]{0:T(128)S(1)}, s32[32]{0:T(128)}, u32[]{:S(2)}) copy-start(s32[32]{0:T(128)} %slot.3) | copy-start | bytes 388
  1.2 4.9 %collective-permute-start.1 = (bf16[2,4,4,8,8,128]{5,4,3,2,1,0:T(8,128)(2,1)S(1)}, bf16[2,4,4,8,8,128]{5,4,3,2,1,0:T(8,128)(2,1)S(1)}, u32[]{:S(2)}, u32[]{:S(2)}) collective-permute-start(bf16[2,4,4,8,8,128]{5,4,3,2,1,0:T(8,128)(2,1)S(1)} %shard_map.48), channel_id=1, source_target_pairs={{0,32},{32,0},{64,96},{96,64},{128,160},{160,128},{192,224},{224,1... | collective-permute-start | bytes 1572872 | tf_op jit(solution)/shard_map/ppermute | solution.py:207
  5.6 37.1 %copy-start.1 = (bf16[2,1024,1024]{2,1,0:T(8,128)(2,1)S(1)}, bf16[2,1024,1024]{2,1,0:T(8,128)(2,1)}, u32[]{:S(2)}) copy-start(bf16[2,1024,1024]{2,1,0:T(8,128)(2,1)} %left_ref.1) | copy-start | bytes 12582916
  5.6 3.4 %collective-permute-start = (bf16[2,4,4,8,8,128]{5,4,3,2,1,0:T(8,128)(2,1)S(1)}, bf16[2,4,4,8,8,128]{5,4,3,2,1,0:T(8,128)(2,1)S(1)}, u32[]{:S(2)}, u32[]{:S(2)}) collective-permute-start(bf16[2,4,4,8,8,128]{5,4,3,2,1,0:T(8,128)(2,1)S(1)} %shard_map.46), channel_id=1, source_target_pairs={{0,32},{32,0},{64,96},{96,64},{128,160},{160,128},{192,224},{224,1... | collective-permute-start | bytes 1572872 | tf_op jit(solution)/shard_map/ppermute | solution.py:207
  6.3 6.5 %collective-permute-start.3 = (bf16[4,4,8,8,128]{4,3,2,1,0:T(8,128)(2,1)S(1)}, bf16[4,4,8,8,128]{4,3,2,1,0:T(8,128)(2,1)S(1)}, u32[]{:S(2)}, u32[]{:S(2)}) collective-permute-start(bf16[4,4,8,8,128]{4,3,2,1,0:T(8,128)(2,1)S(1)} %get-tuple-element.17), channel_id=1, source_target_pairs={{0,64},{32,224},{64,0},{96,160},{128,192},{160,96},{192,128},{224,... | collective-permute-start | bytes 786440 | tf_op jit(solution)/shard_map/ppermute | solution.py:211
  7.3 8.2 %collective-permute-start.2 = (bf16[4,4,8,8,128]{4,3,2,1,0:T(8,128)(2,1)S(1)}, bf16[4,4,8,8,128]{4,3,2,1,0:T(8,128)(2,1)S(1)}, u32[]{:S(2)}, u32[]{:S(2)}) collective-permute-start(bf16[4,4,8,8,128]{4,3,2,1,0:T(8,128)(2,1)S(1)} %get-tuple-element.15), channel_id=1, source_target_pairs={{0,64},{32,224},{64,0},{96,160},{128,192},{160,96},{192,128},{224,... | collective-permute-start | bytes 786440 | tf_op jit(solution)/shard_map/ppermute | solution.py:211
  9.2 50.7 %copy-start.2 = (bf16[2,1024,1024]{2,1,0:T(8,128)(2,1)S(1)}, bf16[2,1024,1024]{2,1,0:T(8,128)(2,1)}, u32[]{:S(2)}) copy-start(bf16[2,1024,1024]{2,1,0:T(8,128)(2,1)} %refs_8_.1) | copy-start | bytes 12582916
  12.9 5.6 %collective-permute-start.4 = (bf16[4,4,8,8,128]{4,3,2,1,0:T(8,128)(2,1)S(1)}, bf16[4,4,8,8,128]{4,3,2,1,0:T(8,128)(2,1)S(1)}, u32[]{:S(2)}, u32[]{:S(2)}) collective-permute-start(bf16[4,4,8,8,128]{4,3,2,1,0:T(8,128)(2,1)S(1)} %shard_map.50), channel_id=1, source_target_pairs={{0,192},{32,96},{64,128},{96,32},{128,64},{160,224},{192,0},{224,1... | collective-permute-start | bytes 786440 | tf_op jit(solution)/shard_map/ppermute | solution.py:211
  44.2 8.8 %collective-permute-start.5 = (bf16[2,256,128]{2,1,0:T(8,128)(2,1)S(1)}, bf16[2,256,128]{2,1,0:T(8,128)(2,1)S(1)}, u32[]{:S(2)}, u32[]{:S(2)}) collective-permute-start(bf16[2,256,128]{2,1,0:T(8,128)(2,1)S(1)} %get-tuple-element.19), channel_id=1, source_target_pairs={{0,128},{32,160},{64,192},{96,224},{128,0},{160,32},{192,64},{224,... | collective-permute-start | bytes 393224 | tf_op jit(solution)/shard_map/ppermute | solution.py:211
  48.1 8.3 %collective-permute-start.6 = (bf16[2,256,128]{2,1,0:T(8,128)(2,1)S(1)}, bf16[2,256,128]{2,1,0:T(8,128)(2,1)S(1)}, u32[]{:S(2)}, u32[]{:S(2)}) collective-permute-start(bf16[2,256,128]{2,1,0:T(8,128)(2,1)S(1)} %get-tuple-element.20), channel_id=1, source_target_pairs={{0,64},{32,224},{64,0},{96,160},{128,192},{160,96},{192,128},{224,... | collective-permute-start | bytes 393224 | tf_op jit(solution)/shard_map/ppermute | solution.py:211
  48.8 8.2 %collective-permute-start.7 = (bf16[2,256,128]{2,1,0:T(8,128)(2,1)S(1)}, bf16[2,256,128]{2,1,0:T(8,128)(2,1)S(1)}, u32[]{:S(2)}, u32[]{:S(2)}) collective-permute-start(bf16[2,256,128]{2,1,0:T(8,128)(2,1)S(1)} %get-tuple-element.21), channel_id=1, source_target_pairs={{0,192},{32,96},{64,128},{96,32},{128,64},{160,224},{192,0},{224,1... | collective-permute-start | bytes 393224 | tf_op jit(solution)/shard_map/ppermute | solution.py:211
  48.8 10.1 %collective-permute-start.8 = (bf16[2,256,128]{2,1,0:T(8,128)(2,1)S(1)}, bf16[2,256,128]{2,1,0:T(8,128)(2,1)S(1)}, u32[]{:S(2)}, u32[]{:S(2)}) collective-permute-start(bf16[2,256,128]{2,1,0:T(8,128)(2,1)S(1)} %get-tuple-element.18.refs_0_), channel_id=1, source_target_pairs={{0,32},{32,0},{64,96},{96,64},{128,160},{160,128},{192,224},{224,1... | collective-permute-start | bytes 393224 | tf_op jit(solution)/shard_map/ppermute | solution.py:207
  53.0 5.9 %collective-permute-start.9 = (bf16[2,256,128]{2,1,0:T(8,128)(2,1)S(1)}, bf16[2,256,128]{2,1,0:T(8,128)(2,1)S(1)}, u32[]{:S(2)}, u32[]{:S(2)}) collective-permute-start(bf16[2,256,128]{2,1,0:T(8,128)(2,1)S(1)} %collective-permute-done.5.refs_1_), channel_id=1, source_target_pairs={{0,32},{32,0},{64,96},{96,64},{128,160},{160,128},{192,224},{224,1... | collective-permute-start | bytes 393224 | tf_op jit(solution)/shard_map/ppermute | solution.py:207
  56.4 2.5 %collective-permute-start.11 = (bf16[2,256,128]{2,1,0:T(8,128)(2,1)S(1)}, bf16[2,256,128]{2,1,0:T(8,128)(2,1)S(1)}, u32[]{:S(2)}, u32[]{:S(2)}) collective-permute-start(bf16[2,256,128]{2,1,0:T(8,128)(2,1)S(1)} %collective-permute-done.6.refs_2_), channel_id=1, source_target_pairs={{0,32},{32,0},{64,96},{96,64},{128,160},{160,128},{192,224},{224,1... | collective-permute-start | bytes 393224 | tf_op jit(solution)/shard_map/ppermute | solution.py:207
  57.1 2.8 %collective-permute-start.10 = (bf16[2,256,128]{2,1,0:T(8,128)(2,1)S(1)}, bf16[2,256,128]{2,1,0:T(8,128)(2,1)S(1)}, u32[]{:S(2)}, u32[]{:S(2)}) collective-permute-start(bf16[2,256,128]{2,1,0:T(8,128)(2,1)S(1)} %collective-permute-done.7.refs_3_), channel_id=1, source_target_pairs={{0,32},{32,0},{64,96},{96,64},{128,160},{160,128},{192,224},{224,1... | collective-permute-start | bytes 393224 | tf_op jit(solution)/shard_map/ppermute | solution.py:207
  83.5 6.5 %collective-permute-start.12 = (bf16[130,8,128]{2,1,0:T(8,128)(2,1)S(1)}, bf16[130,8,128]{2,1,0:T(8,128)(2,1)S(1)}, u32[]{:S(2)}, u32[]{:S(2)}) collective-permute-start(bf16[130,8,128]{2,1,0:T(8,128)(2,1)S(1)} %shard_map.54.refs_0_), channel_id=1, source_target_pairs={{0,64},{32,224},{64,0},{96,160},{128,192},{160,96},{192,128},{224,... | collective-permute-start | bytes 798728 | tf_op jit(solution)/shard_map/ppermute | solution.py:211
  84.1 11.9 %collective-permute-start.13 = (bf16[130,8,128]{2,1,0:T(8,128)(2,1)S(1)}, bf16[130,8,128]{2,1,0:T(8,128)(2,1)S(1)}, u32[]{:S(2)}, u32[]{:S(2)}) collective-permute-start(bf16[130,8,128]{2,1,0:T(8,128)(2,1)S(1)} %shard_map.54.refs_0_), channel_id=1, source_target_pairs={{0,192},{32,96},{64,128},{96,32},{128,64},{160,224},{192,0},{224,1... | collective-permute-start | bytes 798728 | tf_op jit(solution)/shard_map/ppermute | solution.py:211
  90.1 6.4 %collective-permute-start.14 = (bf16[130,8,128]{2,1,0:T(8,128)(2,1)S(1)}, bf16[130,8,128]{2,1,0:T(8,128)(2,1)S(1)}, u32[]{:S(2)}, u32[]{:S(2)}) collective-permute-start(bf16[130,8,128]{2,1,0:T(8,128)(2,1)S(1)} %collective-permute-done.12.refs_1_), channel_id=1, source_target_pairs={{0,192},{32,96},{64,128},{96,32},{128,64},{160,224},{192,0},{224,1... | collective-permute-start | bytes 798728 | tf_op jit(solution)/shard_map/ppermute | solution.py:211
  90.1 10.5 %collective-permute-start.15 = (bf16[130,8,128]{2,1,0:T(8,128)(2,1)S(1)}, bf16[130,8,128]{2,1,0:T(8,128)(2,1)S(1)}, u32[]{:S(2)}, u32[]{:S(2)}) collective-permute-start(bf16[130,8,128]{2,1,0:T(8,128)(2,1)S(1)} %shard_map.54.refs_0_), channel_id=1, source_target_pairs={{0,32},{32,0},{64,96},{96,64},{128,160},{160,128},{192,224},{224,1... | collective-permute-start | bytes 798728 | tf_op jit(solution)/shard_map/ppermute | solution.py:207
  96.0 4.6 %collective-permute-start.17 = (bf16[130,8,128]{2,1,0:T(8,128)(2,1)S(1)}, bf16[130,8,128]{2,1,0:T(8,128)(2,1)S(1)}, u32[]{:S(2)}, u32[]{:S(2)}) collective-permute-start(bf16[130,8,128]{2,1,0:T(8,128)(2,1)S(1)} %collective-permute-done.12.refs_1_), channel_id=1, source_target_pairs={{0,32},{32,0},{64,96},{96,64},{128,160},{160,128},{192,224},{224,1... | collective-permute-start | bytes 798728 | tf_op jit(solution)/shard_map/ppermute | solution.py:207
  96.0 4.6 %collective-permute-start.16 = (bf16[130,8,128]{2,1,0:T(8,128)(2,1)S(1)}, bf16[130,8,128]{2,1,0:T(8,128)(2,1)S(1)}, u32[]{:S(2)}, u32[]{:S(2)}) collective-permute-start(bf16[130,8,128]{2,1,0:T(8,128)(2,1)S(1)} %collective-permute-done.13.refs_2_), channel_id=1, source_target_pairs={{0,32},{32,0},{64,96},{96,64},{128,160},{160,128},{192,224},{224,1... | collective-permute-start | bytes 798728 | tf_op jit(solution)/shard_map/ppermute | solution.py:207
  96.5 5.2 %collective-permute-start.18 = (bf16[130,8,128]{2,1,0:T(8,128)(2,1)S(1)}, bf16[130,8,128]{2,1,0:T(8,128)(2,1)S(1)}, u32[]{:S(2)}, u32[]{:S(2)}) collective-permute-start(bf16[130,8,128]{2,1,0:T(8,128)(2,1)S(1)} %collective-permute-done.14.refs_3_), channel_id=1, source_target_pairs={{0,32},{32,0},{64,96},{96,64},{128,160},{160,128},{192,224},{224,1... | collective-permute-start | bytes 798728 | tf_op jit(solution)/shard_map/ppermute | solution.py:207

commit v8 on v7

--- a/solution.py
+++ b/solution.py
@@ -16,6 +16,7 @@
 SELF, NEAR, FAR, OPPOSITE = range(4)
 ORDER = (SELF, OPPOSITE, NEAR, FAR)
 TWIN_ORDER = (SELF, OPPOSITE, FAR, NEAR)
+LAST = NEAR
 
 
 def masks(core):
@@ -91,23 +92,39 @@
     return a, b, x - a - b
 
 
+def right_columns(place, right_ref):
+    width = right_ref.shape[2] // 2
+    return pl.ds(pl.multiple_of(lax.rem(place[0], 2) * width, width), width)
+
+
+def strip_lines(place, relative, core, strip):
+    return pl.ds(pl.multiple_of(strip_index(place, relative, core) * strip, strip), strip)
+
+
 def right_kernel(place, *refs):
-    own_refs, twin_refs = refs[:4], refs[4:8]
-    right_ref, square_ref, back_ref, half_scratch = refs[8:]
+    *half_refs, right_ref, prec_ref, half_scratch = refs
+    slots, _, strip = half_refs[0].shape
+    core = lax.rem(place[0], 2)
+    known = [(core, k) for k in ORDER] + [(1 - core, k) for k in ORDER if k != LAST]
+    for s in range(slots):
+        half_scratch[s, :, strip_lines(place, LAST, 1 - core, strip)] = jnp.zeros(half_refs[0].shape[1:], bf16)
+        for half_ref, (c, k) in zip(half_refs, known):
+            half_scratch[s, :, strip_lines(place, k, c, strip)] = half_ref[s]
+        prec_ref[s] = jnp.dot(
+            half_scratch[s], right_ref[s, :, right_columns(place, right_ref)], preferred_element_type=f32
+        )
+
+
+def last_strip_kernel(place, half_ref, right_ref, prec_ref, square_ref, back_ref):
     owners, part, wide = back_ref.shape
-    slots = right_ref.shape[0]
+    slots, _, strip = half_ref.shape
     width = (wide - LANES) // slots
-    strip = own_refs[0].shape[2]
-    core = lax.rem(place[0], 2)
     lane = lax.broadcasted_iota(jnp.int32, (part, LANES), 1)
     tail = jnp.zeros((part, LANES), f32)
+    lines = strip_lines(place, LAST, 1 - lax.rem(place[0], 2), strip)
     for s in range(slots):
-        for half_refs, c in ((own_refs, core), (twin_refs, 1 - core)):
-            for k, half_ref in zip(ORDER, half_refs):
-                r = 2 * chip(place, k) + c
-                half_scratch[s, :, pl.ds(pl.multiple_of(r * strip, strip), strip)] = half_ref[s]
-        columns = pl.ds(pl.multiple_of(core * width, width), width)
-        prec = jnp.dot(half_scratch[s], right_ref[s, :, columns], preferred_element_type=f32)
+        root = right_ref[s, lines, right_columns(place, right_ref)]
+        prec = prec_ref[s] + jnp.dot(half_ref[s], root, preferred_element_type=f32)
         back_ref[:, :, s * width : (s + 1) * width] = prec.reshape(owners, part, width).astype(bf16)
         prec_square = jnp.broadcast_to(jnp.sum(prec * prec, keepdims=True), (part, LANES))
         for k, term in enumerate(split3(square_ref[s]) + split3(prec_square)):
@@ -263,13 +280,17 @@
     halves = [half if k == SELF else exchange(half, k) for k, half in zip(ORDER, halves)]
     handed = [twin(halves[ORDER.index(k)]) for k in TWIN_ORDER]
     wide = width + LANES
-    back = local(
+    last = handed.pop(ORDER.index(LAST))
+    prec = local(
         right_kernel,
-        [smem] + [vmem] * 10,
+        [smem] + [vmem] * 8,
         vmem,
-        shape((owners, part, wide), bf16),
+        shape((slots, owners * part, width // 2), f32),
         [pltpu.VMEM((slots, owners * part, width), bf16)],
-    )(place, *halves, *handed, right_root, square)
+    )(place, *halves, *handed, right_root)
+    back = local(last_strip_kernel, [smem] + [vmem] * 4, vmem, shape((owners, part, wide), bf16))(
+        place, last, right_root, prec, square
+    )
     back = lax.all_to_all(back, "fsdp", 0, 0, tiled=True)
 
     tiles = blocks * (width // 2 // LANES) + 2

time: 104 us -> 104 us (level)
  starting transfers between devices: 32.2 us -> 34 us
  waiting for transfers between devices: 17.4 us -> 15.8 us
    ppermute x10, starting transfers between devices: 24 us -> 25.2 us  [twin(): return lax.ppermute(x, 'replica', [(i, i ^ 1) for i in range(reps)])]
  transfers between devices with their start and end apart: 19 -> 19, of which waited for: 7 -> 6; matrix products, arithmetic and copies ran while one was open for 0% -> 0% of each run, Pallas kernels for 1% -> 2%
where the time goes in v8:
time: 104 us
  blocking collectives  45 us (43%)
  starting transfers between devices  34 us (33%)
  waiting for transfers between devices  15.8 us (15%)
  Pallas kernels  8.85 us (9%)
    ppermute x10, starting transfers between devices, twin(): return lax.ppermute(x, 'replica', [(i, i ^ 1) for i in range(reps)])  25.2 us
    all_to_all x1, blocking collectives, on_device(): incoming = lax.all_to_all(outgoing, 'fsdp', 0, 0, tiled=True)  23.5 us
    all_to_all x1, blocking collectives, on_device(): back = lax.all_to_all(back, 'fsdp', 0, 0, tiled=True)  21.5 us
    ppermute x9, waiting for transfers between devices, exchange(): return lax.ppermute(x, 'replica', perm)  14.3 us
    ppermute x9, starting transfers between devices, exchange(): return lax.ppermute(x, 'replica', perm)  8.88 us
    pallas_call x2, Pallas kernels, on_device(): local(functools.partial(send_kernel, kinds=kinds), [smem, pl.BlockSpec(me...  2.26 us
  transfers between devices with their start and end apart: 19, of which 6 were waited for; matrix products, arithmetic and copies ran while one was open for 0% of the time, Pallas kernels for 2%

profile of v8, /device:TPU:1, one launch (start us, length us, event | category | flops | bytes accessed | tf_op | source)
XLA Modules:
  0.0 104.0 jit_solution(4198312812344066734)
XLA Ops:
  0.0 1.2 %shard_map.48 = bf16[2,4,4,8,8,128]{5,4,3,2,1,0:T(8,128)(2,1)S(1)} custom-call(s32[1]{0:T(128)} %bitcast.place, bf16[4,4,8,8,8,128]{5,4,3,2,1,0:T(8,128)(2,1)} %bitcast.4), custom_call_target="tpu_custom_call" | custom-call | tf_op jit(solution)/shard_map/pallas_call | solution.py:249
  1.2 3.3 %collective-permute-start.1 = (bf16[2,4,4,8,8,128]{5,4,3,2,1,0:T(8,128)(2,1)S(1)}, bf16[2,4,4,8,8,128]{5,4,3,2,1,0:T(8,128)(2,1)S(1)}, u32[]{:S(2)}, u32[]{:S(2)}) collective-permute-start(bf16[2,4,4,8,8,128]{5,4,3,2,1,0:T(8,128)(2,1)S(1)} %shard_map.48), channel_id=1, source_target_pairs={{0,32},{32,0},{64,96},{96,64},{128,160},{160,128},{192,224},{224,1... | collective-permute-start | bytes 1572872 | tf_op jit(solution)/shard_map/ppermute | solution.py:224
  4.6 1.1 %shard_map.46 = bf16[2,4,4,8,8,128]{5,4,3,2,1,0:T(8,128)(2,1)S(1)} custom-call(s32[1]{0:T(128)} %bitcast.place, bf16[4,4,8,8,8,128]{5,4,3,2,1,0:T(8,128)(2,1)} %bitcast.5), custom_call_target="tpu_custom_call" | custom-call | tf_op jit(solution)/shard_map/pallas_call | solution.py:249
  6.3 1.1 %collective-permute-start.3 = (bf16[4,4,8,8,128]{4,3,2,1,0:T(8,128)(2,1)S(1)}, bf16[4,4,8,8,128]{4,3,2,1,0:T(8,128)(2,1)S(1)}, u32[]{:S(2)}, u32[]{:S(2)}) collective-permute-start(bf16[4,4,8,8,128]{4,3,2,1,0:T(8,128)(2,1)S(1)} %get-tuple-element.17), channel_id=1, source_target_pairs={{0,64},{32,224},{64,0},{96,160},{128,192},{160,96},{192,128},{224,... | collective-permute-start | bytes 786440 | tf_op jit(solution)/shard_map/ppermute | solution.py:228
  7.3 1.7 %collective-permute-start.2 = (bf16[4,4,8,8,128]{4,3,2,1,0:T(8,128)(2,1)S(1)}, bf16[4,4,8,8,128]{4,3,2,1,0:T(8,128)(2,1)S(1)}, u32[]{:S(2)}, u32[]{:S(2)}) collective-permute-start(bf16[4,4,8,8,128]{4,3,2,1,0:T(8,128)(2,1)S(1)} %get-tuple-element.15), channel_id=1, source_target_pairs={{0,64},{32,224},{64,0},{96,160},{128,192},{160,96},{192,128},{224,... | collective-permute-start | bytes 786440 | tf_op jit(solution)/shard_map/ppermute | solution.py:228
  9.2 3.6 %collective-permute-done.3.y_ref = bf16[4,4,8,8,128]{4,3,2,1,0:T(8,128)(2,1)S(1)} collective-permute-done((bf16[4,4,8,8,128]{4,3,2,1,0:T(8,128)(2,1)S(1)}, bf16[4,4,8,8,128]{4,3,2,1,0:T(8,128)(2,1)S(1)}, u32[]{:S(2)}, u32[]{:S(2)}) %collective-permute-start.3) | collective-permute-done | bytes 262176 | tf_op jit(solution)/shard_map/ppermute | solution.py:228
  13.0 2.6 %collective-permute-done.2.refs_1_ = bf16[4,4,8,8,128]{4,3,2,1,0:T(8,128)(2,1)S(1)} collective-permute-done((bf16[4,4,8,8,128]{4,3,2,1,0:T(8,128)(2,1)S(1)}, bf16[4,4,8,8,128]{4,3,2,1,0:T(8,128)(2,1)S(1)}, u32[]{:S(2)}, u32[]{:S(2)}) %collective-permute-start.2) | collective-permute-done | bytes 262176 | tf_op jit(solution)/shard_map/ppermute | solution.py:228
  15.6 2.9 %collective-permute-done.4.refs_2_ = bf16[4,4,8,8,128]{4,3,2,1,0:T(8,128)(2,1)S(1)} collective-permute-done((bf16[4,4,8,8,128]{4,3,2,1,0:T(8,128)(2,1)S(1)}, bf16[4,4,8,8,128]{4,3,2,1,0:T(8,128)(2,1)S(1)}, u32[]{:S(2)}, u32[]{:S(2)}) %collective-permute-start.4) | collective-permute-done | bytes 262176 | tf_op jit(solution)/shard_map/ppermute | solution.py:228
  19.2 23.5 %all_to_all.10.block_ref = bf16[32,2,32,128]{3,2,1,0:T(8,128)(2,1)S(1)} all-to-all(bf16[32,2,32,128]{3,2,1,0:T(8,128)(2,1)S(1)} %shard_map.51), channel_id=1, replica_groups=mesh['replica'=8,'fsdp'=32] {'fsdp'}, dimensions={0} | all-to-all | bytes 1048576 | tf_op jit(solution)/shard_map/all_to_all | solution.py:270
  42.7 1.4 %shard_map.52 = (bf16[2,256,128]{2,1,0:T(8,128)(2,1)S(1)}, bf16[2,256,128]{2,1,0:T(8,128)(2,1)S(1)}, bf16[2,256,128]{2,1,0:T(8,128)(2,1)S(1)}, bf16[2,256,128]{2,1,0:T(8,128)(2,1)S(1)}, f32[2,8,128]{2,1,0:T(8,128)S(1)}) custom-call(s32[1]{0:T(128)} %bitcast.place, bf16[2,1024,1024]{2,1,0:T(8,128)(2,1)S(1)} %copy-done.2, ...), custom_call_target="tpu_custom_call" | custom-call | tf_op jit(solution)/shard_map/pallas_call | solution.py:273
  44.2 3.9 %collective-permute-start.7 = (bf16[2,256,128]{2,1,0:T(8,128)(2,1)S(1)}, bf16[2,256,128]{2,1,0:T(8,128)(2,1)S(1)}, u32[]{:S(2)}, u32[]{:S(2)}) collective-permute-start(bf16[2,256,128]{2,1,0:T(8,128)(2,1)S(1)} %get-tuple-element.20), channel_id=1, source_target_pairs={{0,128},{32,160},{64,192},{96,224},{128,0},{160,32},{192,64},{224,... | collective-permute-start | bytes 393224 | tf_op jit(solution)/shard_map/ppermute | solution.py:228
  48.1 0.8 collective-permute-start.8
  48.8 4.2 %collective-permute-start.9 = (bf16[2,256,128]{2,1,0:T(8,128)(2,1)S(1)}, bf16[2,256,128]{2,1,0:T(8,128)(2,1)S(1)}, u32[]{:S(2)}, u32[]{:S(2)}) collective-permute-start(bf16[2,256,128]{2,1,0:T(8,128)(2,1)S(1)} %get-tuple-element.19.refs_0_), channel_id=1, source_target_pairs={{0,32},{32,0},{64,96},{96,64},{128,160},{160,128},{192,224},{224,1... | collective-permute-start | bytes 393224 | tf_op jit(solution)/shard_map/ppermute | solution.py:224
  53.0 3.4 %collective-permute-start.10 = (bf16[2,256,128]{2,1,0:T(8,128)(2,1)S(1)}, bf16[2,256,128]{2,1,0:T(8,128)(2,1)S(1)}, u32[]{:S(2)}, u32[]{:S(2)}) collective-permute-start(bf16[2,256,128]{2,1,0:T(8,128)(2,1)S(1)} %collective-permute-done.7.refs_1_), channel_id=1, source_target_pairs={{0,32},{32,0},{64,96},{96,64},{128,160},{160,128},{192,224},{224,1... | collective-permute-start | bytes 393224 | tf_op jit(solution)/shard_map/ppermute | solution.py:224
  57.1 1.8 %collective-permute-start.6 = (bf16[2,256,128]{2,1,0:T(8,128)(2,1)S(1)}, bf16[2,256,128]{2,1,0:T(8,128)(2,1)S(1)}, u32[]{:S(2)}, u32[]{:S(2)}) collective-permute-start(bf16[2,256,128]{2,1,0:T(8,128)(2,1)S(1)} %collective-permute-done.5.refs_3_), channel_id=1, source_target_pairs={{0,32},{32,0},{64,96},{96,64},{128,160},{160,128},{192,224},{224,1... | collective-permute-start | bytes 393224 | tf_op jit(solution)/shard_map/ppermute | solution.py:224
  58.9 0.9 shard_map.53.prec_ref
  60.4 21.5 %all_to_all.11.back_ref = bf16[32,8,1152]{2,1,0:T(8,128)(2,1)S(1)} all-to-all(bf16[32,8,1152]{2,1,0:T(8,128)(2,1)S(1)} %shard_map.54), channel_id=1, replica_groups=mesh['replica'=8,'fsdp'=32] {'fsdp'}, dimensions={0} | all-to-all | bytes 1179648 | tf_op jit(solution)/shard_map/all_to_all | solution.py:294
  81.9 1.0 shard_map.55.refs_0_
  82.9 1.3 %collective-permute-start.12 = (bf16[130,8,128]{2,1,0:T(8,128)(2,1)S(1)}, bf16[130,8,128]{2,1,0:T(8,128)(2,1)S(1)}, u32[]{:S(2)}, u32[]{:S(2)}) collective-permute-start(bf16[130,8,128]{2,1,0:T(8,128)(2,1)S(1)} %shard_map.55.refs_0_), channel_id=1, source_target_pairs={{0,64},{32,224},{64,0},{96,160},{128,192},{160,96},{192,128},{224,... | collective-permute-start | bytes 798728 | tf_op jit(solution)/shard_map/ppermute | solution.py:228
  84.2 5.2 %collective-permute-done.12.refs_1_ = bf16[130,8,128]{2,1,0:T(8,128)(2,1)S(1)} collective-permute-done((bf16[130,8,128]{2,1,0:T(8,128)(2,1)S(1)}, bf16[130,8,128]{2,1,0:T(8,128)(2,1)S(1)}, u32[]{:S(2)}, u32[]{:S(2)}) %collective-permute-start.12) | collective-permute-done | bytes 266272 | tf_op jit(solution)/shard_map/ppermute | solution.py:228
  89.4 5.8 %collective-permute-start.15 = (bf16[130,8,128]{2,1,0:T(8,128)(2,1)S(1)}, bf16[130,8,128]{2,1,0:T(8,128)(2,1)S(1)}, u32[]{:S(2)}, u32[]{:S(2)}) collective-permute-start(bf16[130,8,128]{2,1,0:T(8,128)(2,1)S(1)} %shard_map.55.refs_0_), channel_id=1, source_target_pairs={{0,32},{32,0},{64,96},{96,64},{128,160},{160,128},{192,224},{224,1... | collective-permute-start | bytes 798728 | tf_op jit(solution)/shard_map/ppermute | solution.py:224
  95.8 5.3 %collective-permute-start.18 = (bf16[130,8,128]{2,1,0:T(8,128)(2,1)S(1)}, bf16[130,8,128]{2,1,0:T(8,128)(2,1)S(1)}, u32[]{:S(2)}, u32[]{:S(2)}) collective-permute-start(bf16[130,8,128]{2,1,0:T(8,128)(2,1)S(1)} %collective-permute-done.14.refs_3_), channel_id=1, source_target_pairs={{0,32},{32,0},{64,96},{96,64},{128,160},{160,128},{192,224},{224,1... | collective-permute-start | bytes 798728 | tf_op jit(solution)/shard_map/ppermute | solution.py:224
  101.1 1.2 %collective-permute-done.18.refs_7_ = bf16[130,8,128]{2,1,0:T(8,128)(2,1)S(1)} collective-permute-done((bf16[130,8,128]{2,1,0:T(8,128)(2,1)S(1)}, bf16[130,8,128]{2,1,0:T(8,128)(2,1)S(1)}, u32[]{:S(2)}, u32[]{:S(2)}) %collective-permute-start.18) | collective-permute-done | bytes 266272 | tf_op jit(solution)/shard_map/ppermute | solution.py:224
  102.3 1.6 %shard_map.56 = bf16[4,32,8192]{2,1,0:T(8,128)(2,1)} custom-call(s32[1]{0:T(128)} %bitcast.place, bf16[130,8,128]{2,1,0:T(8,128)(2,1)S(1)} %shard_map.55.refs_0_, bf16[130,8,128]{2,1,0:T(8,128)(2,1)S(1)} %collective-permute-done.12.refs_1_, bf16[130,8,128]{2,1,0:T(8,128)(2,1)S(1)} %collective-permute-done.13.refs_2_, ...), custom_call_target="tpu_custom_call" | custom-call | tf_op jit(solution)/shard_map/pallas_call | solution.py:303
  (35 shorter events, 3.5 us)
Async XLA Ops:
  0.0 6.1 %copy-start = (bf16[1,4,32,8192]{3,2,1,0:T(8,128)(2,1)S(1)}, bf16[1,4,32,8192]{3,2,1,0:T(8,128)(2,1)}, u32[]{:S(2)}) copy-start(bf16[1,4,32,8192]{3,2,1,0:T(8,128)(2,1)} %param.4) | copy-start | bytes 6291460
  1.2 17.2 %copy-start.3 = (s32[32]{0:T(128)S(1)}, s32[32]{0:T(128)}, u32[]{:S(2)}) copy-start(s32[32]{0:T(128)} %slot.3) | copy-start | bytes 388
  1.2 4.9 %collective-permute-start.1 = (bf16[2,4,4,8,8,128]{5,4,3,2,1,0:T(8,128)(2,1)S(1)}, bf16[2,4,4,8,8,128]{5,4,3,2,1,0:T(8,128)(2,1)S(1)}, u32[]{:S(2)}, u32[]{:S(2)}) collective-permute-start(bf16[2,4,4,8,8,128]{5,4,3,2,1,0:T(8,128)(2,1)S(1)} %shard_map.48), channel_id=1, source_target_pairs={{0,32},{32,0},{64,96},{96,64},{128,160},{160,128},{192,224},{224,1... | collective-permute-start | bytes 1572872 | tf_op jit(solution)/shard_map/ppermute | solution.py:224
  5.6 37.1 %copy-start.2 = (bf16[2,1024,1024]{2,1,0:T(8,128)(2,1)S(1)}, bf16[2,1024,1024]{2,1,0:T(8,128)(2,1)}, u32[]{:S(2)}) copy-start(bf16[2,1024,1024]{2,1,0:T(8,128)(2,1)} %left_ref.1) | copy-start | bytes 12582916
  5.6 3.4 %collective-permute-start = (bf16[2,4,4,8,8,128]{5,4,3,2,1,0:T(8,128)(2,1)S(1)}, bf16[2,4,4,8,8,128]{5,4,3,2,1,0:T(8,128)(2,1)S(1)}, u32[]{:S(2)}, u32[]{:S(2)}) collective-permute-start(bf16[2,4,4,8,8,128]{5,4,3,2,1,0:T(8,128)(2,1)S(1)} %shard_map.46), channel_id=1, source_target_pairs={{0,32},{32,0},{64,96},{96,64},{128,160},{160,128},{192,224},{224,1... | collective-permute-start | bytes 1572872 | tf_op jit(solution)/shard_map/ppermute | solution.py:224
  6.3 6.5 %collective-permute-start.3 = (bf16[4,4,8,8,128]{4,3,2,1,0:T(8,128)(2,1)S(1)}, bf16[4,4,8,8,128]{4,3,2,1,0:T(8,128)(2,1)S(1)}, u32[]{:S(2)}, u32[]{:S(2)}) collective-permute-start(bf16[4,4,8,8,128]{4,3,2,1,0:T(8,128)(2,1)S(1)} %get-tuple-element.17), channel_id=1, source_target_pairs={{0,64},{32,224},{64,0},{96,160},{128,192},{160,96},{192,128},{224,... | collective-permute-start | bytes 786440 | tf_op jit(solution)/shard_map/ppermute | solution.py:228
  7.3 8.2 %collective-permute-start.2 = (bf16[4,4,8,8,128]{4,3,2,1,0:T(8,128)(2,1)S(1)}, bf16[4,4,8,8,128]{4,3,2,1,0:T(8,128)(2,1)S(1)}, u32[]{:S(2)}, u32[]{:S(2)}) collective-permute-start(bf16[4,4,8,8,128]{4,3,2,1,0:T(8,128)(2,1)S(1)} %get-tuple-element.15), channel_id=1, source_target_pairs={{0,64},{32,224},{64,0},{96,160},{128,192},{160,96},{192,128},{224,... | collective-permute-start | bytes 786440 | tf_op jit(solution)/shard_map/ppermute | solution.py:228
  9.2 49.7 %copy-start.1 = (bf16[2,1024,1024]{2,1,0:T(8,128)(2,1)S(1)}, bf16[2,1024,1024]{2,1,0:T(8,128)(2,1)}, u32[]{:S(2)}) copy-start(bf16[2,1024,1024]{2,1,0:T(8,128)(2,1)} %right_ref.1) | copy-start | bytes 12582916
  12.9 5.6 %collective-permute-start.4 = (bf16[4,4,8,8,128]{4,3,2,1,0:T(8,128)(2,1)S(1)}, bf16[4,4,8,8,128]{4,3,2,1,0:T(8,128)(2,1)S(1)}, u32[]{:S(2)}, u32[]{:S(2)}) collective-permute-start(bf16[4,4,8,8,128]{4,3,2,1,0:T(8,128)(2,1)S(1)} %shard_map.50), channel_id=1, source_target_pairs={{0,192},{32,96},{64,128},{96,32},{128,64},{160,224},{192,0},{224,1... | collective-permute-start | bytes 786440 | tf_op jit(solution)/shard_map/ppermute | solution.py:228
  44.2 8.8 %collective-permute-start.7 = (bf16[2,256,128]{2,1,0:T(8,128)(2,1)S(1)}, bf16[2,256,128]{2,1,0:T(8,128)(2,1)S(1)}, u32[]{:S(2)}, u32[]{:S(2)}) collective-permute-start(bf16[2,256,128]{2,1,0:T(8,128)(2,1)S(1)} %get-tuple-element.20), channel_id=1, source_target_pairs={{0,128},{32,160},{64,192},{96,224},{128,0},{160,32},{192,64},{224,... | collective-permute-start | bytes 393224 | tf_op jit(solution)/shard_map/ppermute | solution.py:228
  48.1 8.3 %collective-permute-start.8 = (bf16[2,256,128]{2,1,0:T(8,128)(2,1)S(1)}, bf16[2,256,128]{2,1,0:T(8,128)(2,1)S(1)}, u32[]{:S(2)}, u32[]{:S(2)}) collective-permute-start(bf16[2,256,128]{2,1,0:T(8,128)(2,1)S(1)} %get-tuple-element.21), channel_id=1, source_target_pairs={{0,64},{32,224},{64,0},{96,160},{128,192},{160,96},{192,128},{224,... | collective-permute-start | bytes 393224 | tf_op jit(solution)/shard_map/ppermute | solution.py:228
  48.8 8.2 %collective-permute-start.5 = (bf16[2,256,128]{2,1,0:T(8,128)(2,1)S(1)}, bf16[2,256,128]{2,1,0:T(8,128)(2,1)S(1)}, u32[]{:S(2)}, u32[]{:S(2)}) collective-permute-start(bf16[2,256,128]{2,1,0:T(8,128)(2,1)S(1)} %get-tuple-element.18), channel_id=1, source_target_pairs={{0,192},{32,96},{64,128},{96,32},{128,64},{160,224},{192,0},{224,1... | collective-permute-start | bytes 393224 | tf_op jit(solution)/shard_map/ppermute | solution.py:228
  48.8 10.1 %collective-permute-start.9 = (bf16[2,256,128]{2,1,0:T(8,128)(2,1)S(1)}, bf16[2,256,128]{2,1,0:T(8,128)(2,1)S(1)}, u32[]{:S(2)}, u32[]{:S(2)}) collective-permute-start(bf16[2,256,128]{2,1,0:T(8,128)(2,1)S(1)} %get-tuple-element.19.refs_0_), channel_id=1, source_target_pairs={{0,32},{32,0},{64,96},{96,64},{128,160},{160,128},{192,224},{224,1... | collective-permute-start | bytes 393224 | tf_op jit(solution)/shard_map/ppermute | solution.py:224
  53.0 5.9 %collective-permute-start.10 = (bf16[2,256,128]{2,1,0:T(8,128)(2,1)S(1)}, bf16[2,256,128]{2,1,0:T(8,128)(2,1)S(1)}, u32[]{:S(2)}, u32[]{:S(2)}) collective-permute-start(bf16[2,256,128]{2,1,0:T(8,128)(2,1)S(1)} %collective-permute-done.7.refs_1_), channel_id=1, source_target_pairs={{0,32},{32,0},{64,96},{96,64},{128,160},{160,128},{192,224},{224,1... | collective-permute-start | bytes 393224 | tf_op jit(solution)/shard_map/ppermute | solution.py:224
  56.4 2.5 %collective-permute-start.11 = (bf16[2,256,128]{2,1,0:T(8,128)(2,1)S(1)}, bf16[2,256,128]{2,1,0:T(8,128)(2,1)S(1)}, u32[]{:S(2)}, u32[]{:S(2)}) collective-permute-start(bf16[2,256,128]{2,1,0:T(8,128)(2,1)S(1)} %collective-permute-done.8.refs_2_), channel_id=1, source_target_pairs={{0,32},{32,0},{64,96},{96,64},{128,160},{160,128},{192,224},{224,1... | collective-permute-start | bytes 393224 | tf_op jit(solution)/shard_map/ppermute | solution.py:224
  57.1 2.8 %collective-permute-start.6 = (bf16[2,256,128]{2,1,0:T(8,128)(2,1)S(1)}, bf16[2,256,128]{2,1,0:T(8,128)(2,1)S(1)}, u32[]{:S(2)}, u32[]{:S(2)}) collective-permute-start(bf16[2,256,128]{2,1,0:T(8,128)(2,1)S(1)} %collective-permute-done.5.refs_3_), channel_id=1, source_target_pairs={{0,32},{32,0},{64,96},{96,64},{128,160},{160,128},{192,224},{224,1... | collective-permute-start | bytes 393224 | tf_op jit(solution)/shard_map/ppermute | solution.py:224
  82.9 6.5 %collective-permute-start.12 = (bf16[130,8,128]{2,1,0:T(8,128)(2,1)S(1)}, bf16[130,8,128]{2,1,0:T(8,128)(2,1)S(1)}, u32[]{:S(2)}, u32[]{:S(2)}) collective-permute-start(bf16[130,8,128]{2,1,0:T(8,128)(2,1)S(1)} %shard_map.55.refs_0_), channel_id=1, source_target_pairs={{0,64},{32,224},{64,0},{96,160},{128,192},{160,96},{192,128},{224,... | collective-permute-start | bytes 798728 | tf_op jit(solution)/shard_map/ppermute | solution.py:228
  84.2 11.0 %collective-permute-start.13 = (bf16[130,8,128]{2,1,0:T(8,128)(2,1)S(1)}, bf16[130,8,128]{2,1,0:T(8,128)(2,1)S(1)}, u32[]{:S(2)}, u32[]{:S(2)}) collective-permute-start(bf16[130,8,128]{2,1,0:T(8,128)(2,1)S(1)} %shard_map.55.refs_0_), channel_id=1, source_target_pairs={{0,192},{32,96},{64,128},{96,32},{128,64},{160,224},{192,0},{224,1... | collective-permute-start | bytes 798728 | tf_op jit(solution)/shard_map/ppermute | solution.py:228
  89.4 6.4 %collective-permute-start.14 = (bf16[130,8,128]{2,1,0:T(8,128)(2,1)S(1)}, bf16[130,8,128]{2,1,0:T(8,128)(2,1)S(1)}, u32[]{:S(2)}, u32[]{:S(2)}) collective-permute-start(bf16[130,8,128]{2,1,0:T(8,128)(2,1)S(1)} %collective-permute-done.12.refs_1_), channel_id=1, source_target_pairs={{0,192},{32,96},{64,128},{96,32},{128,64},{160,224},{192,0},{224,1... | collective-permute-start | bytes 798728 | tf_op jit(solution)/shard_map/ppermute | solution.py:228
  89.4 11.7 %collective-permute-start.15 = (bf16[130,8,128]{2,1,0:T(8,128)(2,1)S(1)}, bf16[130,8,128]{2,1,0:T(8,128)(2,1)S(1)}, u32[]{:S(2)}, u32[]{:S(2)}) collective-permute-start(bf16[130,8,128]{2,1,0:T(8,128)(2,1)S(1)} %shard_map.55.refs_0_), channel_id=1, source_target_pairs={{0,32},{32,0},{64,96},{96,64},{128,160},{160,128},{192,224},{224,1... | collective-permute-start | bytes 798728 | tf_op jit(solution)/shard_map/ppermute | solution.py:224
  95.2 5.9 %collective-permute-start.17 = (bf16[130,8,128]{2,1,0:T(8,128)(2,1)S(1)}, bf16[130,8,128]{2,1,0:T(8,128)(2,1)S(1)}, u32[]{:S(2)}, u32[]{:S(2)}) collective-permute-start(bf16[130,8,128]{2,1,0:T(8,128)(2,1)S(1)} %collective-permute-done.12.refs_1_), channel_id=1, source_target_pairs={{0,32},{32,0},{64,96},{96,64},{128,160},{160,128},{192,224},{224,1... | collective-permute-start | bytes 798728 | tf_op jit(solution)/shard_map/ppermute | solution.py:224
  95.2 5.8 %collective-permute-start.16 = (bf16[130,8,128]{2,1,0:T(8,128)(2,1)S(1)}, bf16[130,8,128]{2,1,0:T(8,128)(2,1)S(1)}, u32[]{:S(2)}, u32[]{:S(2)}) collective-permute-start(bf16[130,8,128]{2,1,0:T(8,128)(2,1)S(1)} %collective-permute-done.13.refs_2_), channel_id=1, source_target_pairs={{0,32},{32,0},{64,96},{96,64},{128,160},{160,128},{192,224},{224,1... | collective-permute-start | bytes 798728 | tf_op jit(solution)/shard_map/ppermute | solution.py:224
  95.8 6.5 %collective-permute-start.18 = (bf16[130,8,128]{2,1,0:T(8,128)(2,1)S(1)}, bf16[130,8,128]{2,1,0:T(8,128)(2,1)S(1)}, u32[]{:S(2)}, u32[]{:S(2)}) collective-permute-start(bf16[130,8,128]{2,1,0:T(8,128)(2,1)S(1)} %collective-permute-done.14.refs_3_), channel_id=1, source_target_pairs={{0,32},{32,0},{64,96},{96,64},{128,160},{160,128},{192,224},{224,1... | collective-permute-start | bytes 798728 | tf_op jit(solution)/shard_map/ppermute | solution.py:224

commit v9 on v8

--- a/solution.py
+++ b/solution.py
@@ -58,7 +58,7 @@
 
 
 def add_kernel(x_ref, y_ref, out_ref):
-    out_ref[...] = (x_ref[...].astype(f32) + y_ref[...].astype(f32)).astype(bf16)
+    out_ref[...] = (x_ref[...].astype(f32) + y_ref[...].astype(f32)).astype(out_ref.dtype)
 
 
 def route_kernel(slot, *refs):
@@ -74,12 +74,10 @@
 
 
 def left_kernel(place, left_ref, block_ref, *out_refs):
-    *half_refs, square_ref, scratch = out_refs
+    *half_refs, scratch = out_refs
     owners, slots, rows, strip = block_ref.shape
     for s in range(slots):
         block = block_ref[:, s].reshape(owners * rows, strip)
-        wide = block.astype(f32)
-        square_ref[s] = jnp.broadcast_to(jnp.sum(wide * wide, keepdims=True), square_ref.shape[1:])
         half = jnp.dot(left_ref[s], block, preferred_element_type=f32)
         scratch[s] = half.reshape(scratch.shape[1:])
         for k, half_ref in zip(ORDER, half_refs):
@@ -102,7 +100,7 @@
 
 
 def right_kernel(place, *refs):
-    *half_refs, right_ref, prec_ref, half_scratch = refs
+    *half_refs, block_ref, right_ref, prec_ref, square_ref, half_scratch = refs
     slots, _, strip = half_refs[0].shape
     core = lax.rem(place[0], 2)
     known = [(core, k) for k in ORDER] + [(1 - core, k) for k in ORDER if k != LAST]
@@ -113,6 +111,10 @@
         prec_ref[s] = jnp.dot(
             half_scratch[s], right_ref[s, :, right_columns(place, right_ref)], preferred_element_type=f32
         )
+        block = block_ref[:, s].astype(f32)
+        square = jnp.sum(block * block, axis=(0, 1))
+        square = jnp.sum(square.reshape(1, strip), axis=1, keepdims=True)
+        square_ref[s] = jnp.broadcast_to(square, square_ref.shape[1:])
 
 
 def last_strip_kernel(place, half_ref, right_ref, prec_ref, square_ref, back_ref):
@@ -264,30 +266,31 @@
     passed = local(add_kernel, [vmem] * 2, vmem, strips())(sums[FAR], onward)
     last = exchange(passed, FAR)
 
-    outgoing = local(route_kernel, [smem] + [vmem] * 3, vmem, shape((owners, slots, rows, strip), bf16))(
-        block_slot, sums[SELF], direct, last
+    known = local(add_kernel, [vmem] * 2, vmem, shape(direct.shape, f32))(sums[SELF], direct)
+    outgoing = local(route_kernel, [smem] + [vmem] * 2, vmem, shape((owners, slots, rows, strip), bf16))(
+        block_slot, known, last
     )
     incoming = lax.all_to_all(outgoing, "fsdp", 0, 0, tiled=True)
 
     half_shape = shape((slots, owners * part, strip), bf16)
-    *halves, square = local(
+    halves = local(
         left_kernel,
         [smem, vmem, vmem],
-        [vmem] * 5,
-        [half_shape] * 4 + [shape((slots, part, LANES), f32)],
+        [vmem] * 4,
+        [half_shape] * 4,
         [pltpu.VMEM((slots, owners, 4, part, strip), f32)],
     )(place, left_root, incoming)
     halves = [half if k == SELF else exchange(half, k) for k, half in zip(ORDER, halves)]
     handed = [twin(halves[ORDER.index(k)]) for k in TWIN_ORDER]
     wide = width + LANES
     last = handed.pop(ORDER.index(LAST))
-    prec = local(
+    prec, square = local(
         right_kernel,
-        [smem] + [vmem] * 8,
-        vmem,
-        shape((slots, owners * part, width // 2), f32),
+        [smem] + [vmem] * 9,
+        [vmem] * 2,
+        [shape((slots, owners * part, width // 2), f32), shape((slots, part, LANES), f32)],
         [pltpu.VMEM((slots, owners * part, width), bf16)],
-    )(place, *halves, *handed, right_root)
+    )(place, *halves, *handed, incoming, right_root)
     back = local(last_strip_kernel, [smem] + [vmem] * 4, vmem, shape((owners, part, wide), bf16))(
         place, last, right_root, prec, square
     )

time: 104 us -> 104 us (level)
    pallas_call x3 -> x4, Pallas kernels: 3.13 us -> 3.19 us  [the longest x1 1.42 us: on_device(): local(left_kernel, [smem, vmem, vmem], [vmem] * 4, [half_shape] * 4, [plt...]
where the time goes in v9:
time: 104 us
  blocking collectives  45 us (43%)
  starting transfers between devices  34.1 us (33%)
  waiting for transfers between devices  15.7 us (15%)
  Pallas kernels  8.92 us (9%)
    ppermute x10, starting transfers between devices, twin(): return lax.ppermute(x, 'replica', [(i, i ^ 1) for i in range(reps)])  25.2 us
    all_to_all x1, blocking collectives, on_device(): incoming = lax.all_to_all(outgoing, 'fsdp', 0, 0, tiled=True)  23.5 us
    all_to_all x1, blocking collectives, on_device(): back = lax.all_to_all(back, 'fsdp', 0, 0, tiled=True)  21.5 us
    ppermute x9, waiting for transfers between devices, exchange(): return lax.ppermute(x, 'replica', perm)  14.2 us
    ppermute x9, starting transfers between devices, exchange(): return lax.ppermute(x, 'replica', perm)  8.88 us
    pallas_call x2, Pallas kernels, on_device(): local(functools.partial(send_kernel, kinds=kinds), [smem, pl.BlockSpec(me...  2.26 us
  transfers between devices with their start and end apart: 19, of which 6 were waited for; matrix products, arithmetic and copies ran while one was open for 0% of the time, Pallas kernels for 2%

profile of v9, /device:TPU:1, one launch (start us, length us, event | category | flops | bytes accessed | tf_op | source)
XLA Modules:
  0.0 104.1 jit_solution(4076971347964023824)
XLA Ops:
  0.0 1.2 %shard_map.48 = bf16[2,4,4,8,8,128]{5,4,3,2,1,0:T(8,128)(2,1)S(1)} custom-call(s32[1]{0:T(128)} %bitcast.place, bf16[4,4,8,8,8,128]{5,4,3,2,1,0:T(8,128)(2,1)} %bitcast.4), custom_call_target="tpu_custom_call" | custom-call | tf_op jit(solution)/shard_map/pallas_call | solution.py:251
  1.2 3.3 %collective-permute-start.1 = (bf16[2,4,4,8,8,128]{5,4,3,2,1,0:T(8,128)(2,1)S(1)}, bf16[2,4,4,8,8,128]{5,4,3,2,1,0:T(8,128)(2,1)S(1)}, u32[]{:S(2)}, u32[]{:S(2)}) collective-permute-start(bf16[2,4,4,8,8,128]{5,4,3,2,1,0:T(8,128)(2,1)S(1)} %shard_map.48), channel_id=1, source_target_pairs={{0,32},{32,0},{64,96},{96,64},{128,160},{160,128},{192,224},{224,1... | collective-permute-start | bytes 1572872 | tf_op jit(solution)/shard_map/ppermute | solution.py:226
  4.5 1.1 %shard_map.46 = bf16[2,4,4,8,8,128]{5,4,3,2,1,0:T(8,128)(2,1)S(1)} custom-call(s32[1]{0:T(128)} %bitcast.place, bf16[4,4,8,8,8,128]{5,4,3,2,1,0:T(8,128)(2,1)} %bitcast.5), custom_call_target="tpu_custom_call" | custom-call | tf_op jit(solution)/shard_map/pallas_call | solution.py:251
  6.3 1.1 %collective-permute-start.3 = (bf16[4,4,8,8,128]{4,3,2,1,0:T(8,128)(2,1)S(1)}, bf16[4,4,8,8,128]{4,3,2,1,0:T(8,128)(2,1)S(1)}, u32[]{:S(2)}, u32[]{:S(2)}) collective-permute-start(bf16[4,4,8,8,128]{4,3,2,1,0:T(8,128)(2,1)S(1)} %get-tuple-element.18), channel_id=1, source_target_pairs={{0,64},{32,224},{64,0},{96,160},{128,192},{160,96},{192,128},{224,... | collective-permute-start | bytes 786440 | tf_op jit(solution)/shard_map/ppermute | solution.py:230
  7.3 1.7 %collective-permute-start.2 = (bf16[4,4,8,8,128]{4,3,2,1,0:T(8,128)(2,1)S(1)}, bf16[4,4,8,8,128]{4,3,2,1,0:T(8,128)(2,1)S(1)}, u32[]{:S(2)}, u32[]{:S(2)}) collective-permute-start(bf16[4,4,8,8,128]{4,3,2,1,0:T(8,128)(2,1)S(1)} %get-tuple-element.16), channel_id=1, source_target_pairs={{0,64},{32,224},{64,0},{96,160},{128,192},{160,96},{192,128},{224,... | collective-permute-start | bytes 786440 | tf_op jit(solution)/shard_map/ppermute | solution.py:230
  9.2 3.6 %collective-permute-done.3.y_ref = bf16[4,4,8,8,128]{4,3,2,1,0:T(8,128)(2,1)S(1)} collective-permute-done((bf16[4,4,8,8,128]{4,3,2,1,0:T(8,128)(2,1)S(1)}, bf16[4,4,8,8,128]{4,3,2,1,0:T(8,128)(2,1)S(1)}, u32[]{:S(2)}, u32[]{:S(2)}) %collective-permute-start.3) | collective-permute-done | bytes 262176 | tf_op jit(solution)/shard_map/ppermute | solution.py:230
  13.0 2.6 %collective-permute-done.2.y_ref = bf16[4,4,8,8,128]{4,3,2,1,0:T(8,128)(2,1)S(1)} collective-permute-done((bf16[4,4,8,8,128]{4,3,2,1,0:T(8,128)(2,1)S(1)}, bf16[4,4,8,8,128]{4,3,2,1,0:T(8,128)(2,1)S(1)}, u32[]{:S(2)}, u32[]{:S(2)}) %collective-permute-start.2) | collective-permute-done | bytes 262176 | tf_op jit(solution)/shard_map/ppermute | solution.py:230
  15.6 2.8 %collective-permute-done.4.refs_1_ = bf16[4,4,8,8,128]{4,3,2,1,0:T(8,128)(2,1)S(1)} collective-permute-done((bf16[4,4,8,8,128]{4,3,2,1,0:T(8,128)(2,1)S(1)}, bf16[4,4,8,8,128]{4,3,2,1,0:T(8,128)(2,1)S(1)}, u32[]{:S(2)}, u32[]{:S(2)}) %collective-permute-start.4) | collective-permute-done | bytes 262176 | tf_op jit(solution)/shard_map/ppermute | solution.py:230
  18.5 0.8 shard_map.52
  19.2 23.5 %all_to_all.10.block_ref.refs_7_ = bf16[32,2,32,128]{3,2,1,0:T(8,128)(2,1)S(1)} all-to-all(bf16[32,2,32,128]{3,2,1,0:T(8,128)(2,1)S(1)} %shard_map.52), channel_id=1, replica_groups=mesh['replica'=8,'fsdp'=32] {'fsdp'}, dimensions={0} | all-to-all | bytes 1048576 | tf_op jit(solution)/shard_map/all_to_all | solution.py:273
  42.7 1.4 %shard_map.53 = (bf16[2,256,128]{2,1,0:T(8,128)(2,1)S(1)}, bf16[2,256,128]{2,1,0:T(8,128)(2,1)S(1)}, bf16[2,256,128]{2,1,0:T(8,128)(2,1)S(1)}, bf16[2,256,128]{2,1,0:T(8,128)(2,1)S(1)}) custom-call(s32[1]{0:T(128)} %bitcast.place, bf16[2,1024,1024]{2,1,0:T(8,128)(2,1)S(1)} %copy-done.2, bf16[32,2,32,128]{3,2,1,0:T(8,128)(2,1)S(1)} %all_to_all.10.block_ref.refs_7_), custom_call_target="tpu_custom_call" | custom-call | tf_op jit(solution)/shard_map/pallas_call | solution.py:276
  44.2 3.9 %collective-permute-start.7 = (bf16[2,256,128]{2,1,0:T(8,128)(2,1)S(1)}, bf16[2,256,128]{2,1,0:T(8,128)(2,1)S(1)}, u32[]{:S(2)}, u32[]{:S(2)}) collective-permute-start(bf16[2,256,128]{2,1,0:T(8,128)(2,1)S(1)} %get-tuple-element.21), channel_id=1, source_target_pairs={{0,128},{32,160},{64,192},{96,224},{128,0},{160,32},{192,64},{224,... | collective-permute-start | bytes 393224 | tf_op jit(solution)/shard_map/ppermute | solution.py:230
  48.8 4.2 %collective-permute-start.9 = (bf16[2,256,128]{2,1,0:T(8,128)(2,1)S(1)}, bf16[2,256,128]{2,1,0:T(8,128)(2,1)S(1)}, u32[]{:S(2)}, u32[]{:S(2)}) collective-permute-start(bf16[2,256,128]{2,1,0:T(8,128)(2,1)S(1)} %get-tuple-element.20.refs_0_), channel_id=1, source_target_pairs={{0,32},{32,0},{64,96},{96,64},{128,160},{160,128},{192,224},{224,1... | collective-permute-start | bytes 393224 | tf_op jit(solution)/shard_map/ppermute | solution.py:226
  53.0 3.3 %collective-permute-start.10 = (bf16[2,256,128]{2,1,0:T(8,128)(2,1)S(1)}, bf16[2,256,128]{2,1,0:T(8,128)(2,1)S(1)}, u32[]{:S(2)}, u32[]{:S(2)}) collective-permute-start(bf16[2,256,128]{2,1,0:T(8,128)(2,1)S(1)} %collective-permute-done.7.refs_1_), channel_id=1, source_target_pairs={{0,32},{32,0},{64,96},{96,64},{128,160},{160,128},{192,224},{224,1... | collective-permute-start | bytes 393224 | tf_op jit(solution)/shard_map/ppermute | solution.py:226
  57.1 1.8 %collective-permute-start.6 = (bf16[2,256,128]{2,1,0:T(8,128)(2,1)S(1)}, bf16[2,256,128]{2,1,0:T(8,128)(2,1)S(1)}, u32[]{:S(2)}, u32[]{:S(2)}) collective-permute-start(bf16[2,256,128]{2,1,0:T(8,128)(2,1)S(1)} %collective-permute-done.5.refs_3_), channel_id=1, source_target_pairs={{0,32},{32,0},{64,96},{96,64},{128,160},{160,128},{192,224},{224,1... | collective-permute-start | bytes 393224 | tf_op jit(solution)/shard_map/ppermute | solution.py:226
  58.9 0.9 shard_map.54
  60.4 21.5 %all_to_all.11.back_ref = bf16[32,8,1152]{2,1,0:T(8,128)(2,1)S(1)} all-to-all(bf16[32,8,1152]{2,1,0:T(8,128)(2,1)S(1)} %shard_map.55), channel_id=1, replica_groups=mesh['replica'=8,'fsdp'=32] {'fsdp'}, dimensions={0} | all-to-all | bytes 1179648 | tf_op jit(solution)/shard_map/all_to_all | solution.py:297
  81.9 1.0 shard_map.56.refs_0_
  82.9 1.4 %collective-permute-start.12 = (bf16[130,8,128]{2,1,0:T(8,128)(2,1)S(1)}, bf16[130,8,128]{2,1,0:T(8,128)(2,1)S(1)}, u32[]{:S(2)}, u32[]{:S(2)}) collective-permute-start(bf16[130,8,128]{2,1,0:T(8,128)(2,1)S(1)} %shard_map.56.refs_0_), channel_id=1, source_target_pairs={{0,64},{32,224},{64,0},{96,160},{128,192},{160,96},{192,128},{224,... | collective-permute-start | bytes 798728 | tf_op jit(solution)/shard_map/ppermute | solution.py:230
  84.2 5.2 %collective-permute-done.12.refs_1_ = bf16[130,8,128]{2,1,0:T(8,128)(2,1)S(1)} collective-permute-done((bf16[130,8,128]{2,1,0:T(8,128)(2,1)S(1)}, bf16[130,8,128]{2,1,0:T(8,128)(2,1)S(1)}, u32[]{:S(2)}, u32[]{:S(2)}) %collective-permute-start.12) | collective-permute-done | bytes 266272 | tf_op jit(solution)/shard_map/ppermute | solution.py:230
  89.4 5.8 %collective-permute-start.15 = (bf16[130,8,128]{2,1,0:T(8,128)(2,1)S(1)}, bf16[130,8,128]{2,1,0:T(8,128)(2,1)S(1)}, u32[]{:S(2)}, u32[]{:S(2)}) collective-permute-start(bf16[130,8,128]{2,1,0:T(8,128)(2,1)S(1)} %shard_map.56.refs_0_), channel_id=1, source_target_pairs={{0,32},{32,0},{64,96},{96,64},{128,160},{160,128},{192,224},{224,1... | collective-permute-start | bytes 798728 | tf_op jit(solution)/shard_map/ppermute | solution.py:226
  95.8 5.4 %collective-permute-start.18 = (bf16[130,8,128]{2,1,0:T(8,128)(2,1)S(1)}, bf16[130,8,128]{2,1,0:T(8,128)(2,1)S(1)}, u32[]{:S(2)}, u32[]{:S(2)}) collective-permute-start(bf16[130,8,128]{2,1,0:T(8,128)(2,1)S(1)} %collective-permute-done.14.refs_3_), channel_id=1, source_target_pairs={{0,32},{32,0},{64,96},{96,64},{128,160},{160,128},{192,224},{224,1... | collective-permute-start | bytes 798728 | tf_op jit(solution)/shard_map/ppermute | solution.py:226
  101.2 1.2 %collective-permute-done.18.refs_7_ = bf16[130,8,128]{2,1,0:T(8,128)(2,1)S(1)} collective-permute-done((bf16[130,8,128]{2,1,0:T(8,128)(2,1)S(1)}, bf16[130,8,128]{2,1,0:T(8,128)(2,1)S(1)}, u32[]{:S(2)}, u32[]{:S(2)}) %collective-permute-start.18) | collective-permute-done | bytes 266272 | tf_op jit(solution)/shard_map/ppermute | solution.py:226
  102.3 1.6 %shard_map.57 = bf16[4,32,8192]{2,1,0:T(8,128)(2,1)} custom-call(s32[1]{0:T(128)} %bitcast.place, bf16[130,8,128]{2,1,0:T(8,128)(2,1)S(1)} %shard_map.56.refs_0_, bf16[130,8,128]{2,1,0:T(8,128)(2,1)S(1)} %collective-permute-done.12.refs_1_, bf16[130,8,128]{2,1,0:T(8,128)(2,1)S(1)} %collective-permute-done.13.refs_2_, ...), custom_call_target="tpu_custom_call" | custom-call | tf_op jit(solution)/shard_map/pallas_call | solution.py:306
  (36 shorter events, 3.6 us)
Async XLA Ops:
  0.0 6.1 %copy-start = (bf16[1,4,32,8192]{3,2,1,0:T(8,128)(2,1)S(1)}, bf16[1,4,32,8192]{3,2,1,0:T(8,128)(2,1)}, u32[]{:S(2)}) copy-start(bf16[1,4,32,8192]{3,2,1,0:T(8,128)(2,1)} %param.4) | copy-start | bytes 6291460
  1.2 4.9 %collective-permute-start.1 = (bf16[2,4,4,8,8,128]{5,4,3,2,1,0:T(8,128)(2,1)S(1)}, bf16[2,4,4,8,8,128]{5,4,3,2,1,0:T(8,128)(2,1)S(1)}, u32[]{:S(2)}, u32[]{:S(2)}) collective-permute-start(bf16[2,4,4,8,8,128]{5,4,3,2,1,0:T(8,128)(2,1)S(1)} %shard_map.48), channel_id=1, source_target_pairs={{0,32},{32,0},{64,96},{96,64},{128,160},{160,128},{192,224},{224,1... | collective-permute-start | bytes 1572872 | tf_op jit(solution)/shard_map/ppermute | solution.py:226
  5.6 12.9 %copy-start.3 = (s32[32]{0:T(128)S(1)}, s32[32]{0:T(128)}, u32[]{:S(2)}) copy-start(s32[32]{0:T(128)} %slot.3) | copy-start | bytes 388
  5.6 37.1 %copy-start.2 = (bf16[2,1024,1024]{2,1,0:T(8,128)(2,1)S(1)}, bf16[2,1024,1024]{2,1,0:T(8,128)(2,1)}, u32[]{:S(2)}) copy-start(bf16[2,1024,1024]{2,1,0:T(8,128)(2,1)} %left_ref.1) | copy-start | bytes 12582916
  5.6 3.4 %collective-permute-start = (bf16[2,4,4,8,8,128]{5,4,3,2,1,0:T(8,128)(2,1)S(1)}, bf16[2,4,4,8,8,128]{5,4,3,2,1,0:T(8,128)(2,1)S(1)}, u32[]{:S(2)}, u32[]{:S(2)}) collective-permute-start(bf16[2,4,4,8,8,128]{5,4,3,2,1,0:T(8,128)(2,1)S(1)} %shard_map.46), channel_id=1, source_target_pairs={{0,32},{32,0},{64,96},{96,64},{128,160},{160,128},{192,224},{224,1... | collective-permute-start | bytes 1572872 | tf_op jit(solution)/shard_map/ppermute | solution.py:226
  6.3 6.5 %collective-permute-start.3 = (bf16[4,4,8,8,128]{4,3,2,1,0:T(8,128)(2,1)S(1)}, bf16[4,4,8,8,128]{4,3,2,1,0:T(8,128)(2,1)S(1)}, u32[]{:S(2)}, u32[]{:S(2)}) collective-permute-start(bf16[4,4,8,8,128]{4,3,2,1,0:T(8,128)(2,1)S(1)} %get-tuple-element.18), channel_id=1, source_target_pairs={{0,64},{32,224},{64,0},{96,160},{128,192},{160,96},{192,128},{224,... | collective-permute-start | bytes 786440 | tf_op jit(solution)/shard_map/ppermute | solution.py:230
  7.3 8.2 %collective-permute-start.2 = (bf16[4,4,8,8,128]{4,3,2,1,0:T(8,128)(2,1)S(1)}, bf16[4,4,8,8,128]{4,3,2,1,0:T(8,128)(2,1)S(1)}, u32[]{:S(2)}, u32[]{:S(2)}) collective-permute-start(bf16[4,4,8,8,128]{4,3,2,1,0:T(8,128)(2,1)S(1)} %get-tuple-element.16), channel_id=1, source_target_pairs={{0,64},{32,224},{64,0},{96,160},{128,192},{160,96},{192,128},{224,... | collective-permute-start | bytes 786440 | tf_op jit(solution)/shard_map/ppermute | solution.py:230
  12.8 46.1 %copy-start.1 = (bf16[2,1024,1024]{2,1,0:T(8,128)(2,1)S(1)}, bf16[2,1024,1024]{2,1,0:T(8,128)(2,1)}, u32[]{:S(2)}) copy-start(bf16[2,1024,1024]{2,1,0:T(8,128)(2,1)} %right_ref.1) | copy-start | bytes 12582916
  12.9 5.6 %collective-permute-start.4 = (bf16[4,4,8,8,128]{4,3,2,1,0:T(8,128)(2,1)S(1)}, bf16[4,4,8,8,128]{4,3,2,1,0:T(8,128)(2,1)S(1)}, u32[]{:S(2)}, u32[]{:S(2)}) collective-permute-start(bf16[4,4,8,8,128]{4,3,2,1,0:T(8,128)(2,1)S(1)} %shard_map.51), channel_id=1, source_target_pairs={{0,192},{32,96},{64,128},{96,32},{128,64},{160,224},{192,0},{224,1... | collective-permute-start | bytes 786440 | tf_op jit(solution)/shard_map/ppermute | solution.py:230
  44.2 8.8 %collective-permute-start.7 = (bf16[2,256,128]{2,1,0:T(8,128)(2,1)S(1)}, bf16[2,256,128]{2,1,0:T(8,128)(2,1)S(1)}, u32[]{:S(2)}, u32[]{:S(2)}) collective-permute-start(bf16[2,256,128]{2,1,0:T(8,128)(2,1)S(1)} %get-tuple-element.21), channel_id=1, source_target_pairs={{0,128},{32,160},{64,192},{96,224},{128,0},{160,32},{192,64},{224,... | collective-permute-start | bytes 393224 | tf_op jit(solution)/shard_map/ppermute | solution.py:230
  48.0 8.3 %collective-permute-start.8 = (bf16[2,256,128]{2,1,0:T(8,128)(2,1)S(1)}, bf16[2,256,128]{2,1,0:T(8,128)(2,1)S(1)}, u32[]{:S(2)}, u32[]{:S(2)}) collective-permute-start(bf16[2,256,128]{2,1,0:T(8,128)(2,1)S(1)} %get-tuple-element.22), channel_id=1, source_target_pairs={{0,64},{32,224},{64,0},{96,160},{128,192},{160,96},{192,128},{224,... | collective-permute-start | bytes 393224 | tf_op jit(solution)/shard_map/ppermute | solution.py:230
  48.8 8.3 %collective-permute-start.5 = (bf16[2,256,128]{2,1,0:T(8,128)(2,1)S(1)}, bf16[2,256,128]{2,1,0:T(8,128)(2,1)S(1)}, u32[]{:S(2)}, u32[]{:S(2)}) collective-permute-start(bf16[2,256,128]{2,1,0:T(8,128)(2,1)S(1)} %get-tuple-element.19), channel_id=1, source_target_pairs={{0,192},{32,96},{64,128},{96,32},{128,64},{160,224},{192,0},{224,1... | collective-permute-start | bytes 393224 | tf_op jit(solution)/shard_map/ppermute | solution.py:230
  48.8 10.1 %collective-permute-start.9 = (bf16[2,256,128]{2,1,0:T(8,128)(2,1)S(1)}, bf16[2,256,128]{2,1,0:T(8,128)(2,1)S(1)}, u32[]{:S(2)}, u32[]{:S(2)}) collective-permute-start(bf16[2,256,128]{2,1,0:T(8,128)(2,1)S(1)} %get-tuple-element.20.refs_0_), channel_id=1, source_target_pairs={{0,32},{32,0},{64,96},{96,64},{128,160},{160,128},{192,224},{224,1... | collective-permute-start | bytes 393224 | tf_op jit(solution)/shard_map/ppermute | solution.py:226
  53.0 5.9 %collective-permute-start.10 = (bf16[2,256,128]{2,1,0:T(8,128)(2,1)S(1)}, bf16[2,256,128]{2,1,0:T(8,128)(2,1)S(1)}, u32[]{:S(2)}, u32[]{:S(2)}) collective-permute-start(bf16[2,256,128]{2,1,0:T(8,128)(2,1)S(1)} %collective-permute-done.7.refs_1_), channel_id=1, source_target_pairs={{0,32},{32,0},{64,96},{96,64},{128,160},{160,128},{192,224},{224,1... | collective-permute-start | bytes 393224 | tf_op jit(solution)/shard_map/ppermute | solution.py:226
  56.3 2.6 %collective-permute-start.11 = (bf16[2,256,128]{2,1,0:T(8,128)(2,1)S(1)}, bf16[2,256,128]{2,1,0:T(8,128)(2,1)S(1)}, u32[]{:S(2)}, u32[]{:S(2)}) collective-permute-start(bf16[2,256,128]{2,1,0:T(8,128)(2,1)S(1)} %collective-permute-done.8.refs_2_), channel_id=1, source_target_pairs={{0,32},{32,0},{64,96},{96,64},{128,160},{160,128},{192,224},{224,1... | collective-permute-start | bytes 393224 | tf_op jit(solution)/shard_map/ppermute | solution.py:226
  57.1 2.8 %collective-permute-start.6 = (bf16[2,256,128]{2,1,0:T(8,128)(2,1)S(1)}, bf16[2,256,128]{2,1,0:T(8,128)(2,1)S(1)}, u32[]{:S(2)}, u32[]{:S(2)}) collective-permute-start(bf16[2,256,128]{2,1,0:T(8,128)(2,1)S(1)} %collective-permute-done.5.refs_3_), channel_id=1, source_target_pairs={{0,32},{32,0},{64,96},{96,64},{128,160},{160,128},{192,224},{224,1... | collective-permute-start | bytes 393224 | tf_op jit(solution)/shard_map/ppermute | solution.py:226
  82.9 6.5 %collective-permute-start.12 = (bf16[130,8,128]{2,1,0:T(8,128)(2,1)S(1)}, bf16[130,8,128]{2,1,0:T(8,128)(2,1)S(1)}, u32[]{:S(2)}, u32[]{:S(2)}) collective-permute-start(bf16[130,8,128]{2,1,0:T(8,128)(2,1)S(1)} %shard_map.56.refs_0_), channel_id=1, source_target_pairs={{0,64},{32,224},{64,0},{96,160},{128,192},{160,96},{192,128},{224,... | collective-permute-start | bytes 798728 | tf_op jit(solution)/shard_map/ppermute | solution.py:230
  84.2 11.0 %collective-permute-start.13 = (bf16[130,8,128]{2,1,0:T(8,128)(2,1)S(1)}, bf16[130,8,128]{2,1,0:T(8,128)(2,1)S(1)}, u32[]{:S(2)}, u32[]{:S(2)}) collective-permute-start(bf16[130,8,128]{2,1,0:T(8,128)(2,1)S(1)} %shard_map.56.refs_0_), channel_id=1, source_target_pairs={{0,192},{32,96},{64,128},{96,32},{128,64},{160,224},{192,0},{224,1... | collective-permute-start | bytes 798728 | tf_op jit(solution)/shard_map/ppermute | solution.py:230
  89.4 6.3 %collective-permute-start.14 = (bf16[130,8,128]{2,1,0:T(8,128)(2,1)S(1)}, bf16[130,8,128]{2,1,0:T(8,128)(2,1)S(1)}, u32[]{:S(2)}, u32[]{:S(2)}) collective-permute-start(bf16[130,8,128]{2,1,0:T(8,128)(2,1)S(1)} %collective-permute-done.12.refs_1_), channel_id=1, source_target_pairs={{0,192},{32,96},{64,128},{96,32},{128,64},{160,224},{192,0},{224,1... | collective-permute-start | bytes 798728 | tf_op jit(solution)/shard_map/ppermute | solution.py:230
  89.4 11.7 %collective-permute-start.15 = (bf16[130,8,128]{2,1,0:T(8,128)(2,1)S(1)}, bf16[130,8,128]{2,1,0:T(8,128)(2,1)S(1)}, u32[]{:S(2)}, u32[]{:S(2)}) collective-permute-start(bf16[130,8,128]{2,1,0:T(8,128)(2,1)S(1)} %shard_map.56.refs_0_), channel_id=1, source_target_pairs={{0,32},{32,0},{64,96},{96,64},{128,160},{160,128},{192,224},{224,1... | collective-permute-start | bytes 798728 | tf_op jit(solution)/shard_map/ppermute | solution.py:226
  95.3 5.9 %collective-permute-start.17 = (bf16[130,8,128]{2,1,0:T(8,128)(2,1)S(1)}, bf16[130,8,128]{2,1,0:T(8,128)(2,1)S(1)}, u32[]{:S(2)}, u32[]{:S(2)}) collective-permute-start(bf16[130,8,128]{2,1,0:T(8,128)(2,1)S(1)} %collective-permute-done.12.refs_1_), channel_id=1, source_target_pairs={{0,32},{32,0},{64,96},{96,64},{128,160},{160,128},{192,224},{224,1... | collective-permute-start | bytes 798728 | tf_op jit(solution)/shard_map/ppermute | solution.py:226
  95.3 5.9 %collective-permute-start.16 = (bf16[130,8,128]{2,1,0:T(8,128)(2,1)S(1)}, bf16[130,8,128]{2,1,0:T(8,128)(2,1)S(1)}, u32[]{:S(2)}, u32[]{:S(2)}) collective-permute-start(bf16[130,8,128]{2,1,0:T(8,128)(2,1)S(1)} %collective-permute-done.13.refs_2_), channel_id=1, source_target_pairs={{0,32},{32,0},{64,96},{96,64},{128,160},{160,128},{192,224},{224,1... | collective-permute-start | bytes 798728 | tf_op jit(solution)/shard_map/ppermute | solution.py:226
  95.8 6.5 %collective-permute-start.18 = (bf16[130,8,128]{2,1,0:T(8,128)(2,1)S(1)}, bf16[130,8,128]{2,1,0:T(8,128)(2,1)S(1)}, u32[]{:S(2)}, u32[]{:S(2)}) collective-permute-start(bf16[130,8,128]{2,1,0:T(8,128)(2,1)S(1)} %collective-permute-done.14.refs_3_), channel_id=1, source_target_pairs={{0,32},{32,0},{64,96},{96,64},{128,160},{160,128},{192,224},{224,1... | collective-permute-start | bytes 798728 | tf_op jit(solution)/shard_map/ppermute | solution.py:226

commit v10 on v4

--- a/solution.py
+++ b/solution.py
@@ -275,7 +275,7 @@
     mine = local(select_kernel, [smem, vmem], vmem, shape((tiles, part, LANES), bf16))(block_slot, back)
     near = exchange(mine, NEAR)
     far = exchange(mine, FAR)
-    opposite = exchange(near, FAR)
+    opposite = exchange(far, NEAR)
     own = [mine, near, far, opposite]
     other = [twin(x) for x in (mine, far, near, opposite)]
     return local(

time: 104 us -> 105 us (level)
  starting transfers between devices: 32.2 us -> 34.3 us
  waiting for transfers between devices: 17.3 us -> 15.9 us
    ppermute x9, waiting for transfers between devices: 15 us -> 13.6 us  [exchange(): return lax.ppermute(x, 'replica', perm)]
    ppermute x9, starting transfers between devices: 8.22 us -> 9.39 us  [exchange(): return lax.ppermute(x, 'replica', perm)]
  transfers between devices with their start and end apart: 19 -> 19, of which waited for: 7 -> 8; matrix products, arithmetic and copies ran while one was open for 0% -> 0% of each run, Pallas kernels for 1% -> 1%
where the time goes in v10:
time: 105 us; the launch traced here: 104 us
  blocking collectives  45 us (43%)
  starting transfers between devices  34.3 us (33%)
  waiting for transfers between devices  15.9 us (15%)
  Pallas kernels  8.79 us (8%)
    ppermute x10, starting transfers between devices, twin(): return lax.ppermute(x, 'replica', [(i, i ^ 1) for i in range(reps)])  24.9 us
    all_to_all x1, blocking collectives, on_device(): incoming = lax.all_to_all(outgoing, 'fsdp', 0, 0, tiled=True)  23.5 us
    all_to_all x1, blocking collectives, on_device(): back = lax.all_to_all(back, 'fsdp', 0, 0, tiled=True)  21.5 us
    ppermute x9, waiting for transfers between devices, exchange(): return lax.ppermute(x, 'replica', perm)  13.6 us
    ppermute x9, starting transfers between devices, exchange(): return lax.ppermute(x, 'replica', perm)  9.39 us
    pallas_call x2, Pallas kernels, on_device(): local(functools.partial(send_kernel, kinds=kinds, **sizes), [smem, pl.Blo...  2.44 us
    ppermute x10, waiting for transfers between devices, twin(): return lax.ppermute(x, 'replica', [(i, i ^ 1) for i in range(reps)])  2.39 us
  transfers between devices with their start and end apart: 19, of which 8 were waited for; matrix products, arithmetic and copies ran while one was open for 0% of the time, Pallas kernels for 1%

profile of v10, /device:TPU:1, one launch (start us, length us, event | category | flops | bytes accessed | tf_op | source)
XLA Modules:
  0.0 104.3 jit_solution(5683381579998975543)
XLA Ops:
  0.0 1.3 %shard_map.48 = bf16[2,4,8,32,128]{4,3,2,1,0:T(8,128)(2,1)S(1)} custom-call(s32[1]{0:T(128)} %bitcast.place, bf16[1,4,32,8192]{3,2,1,0:T(8,128)(2,1)} %grads_ref.7), custom_call_target="tpu_custom_call" | custom-call | tf_op jit(solution)/shard_map/pallas_call | solution.py:231
  1.3 3.3 %collective-permute-start.1 = (bf16[2,4,8,32,128]{4,3,2,1,0:T(8,128)(2,1)S(1)}, bf16[2,4,8,32,128]{4,3,2,1,0:T(8,128)(2,1)S(1)}, u32[]{:S(2)}, u32[]{:S(2)}) collective-permute-start(bf16[2,4,8,32,128]{4,3,2,1,0:T(8,128)(2,1)S(1)} %shard_map.48), channel_id=1, source_target_pairs={{0,32},{32,0},{64,96},{96,64},{128,160},{160,128},{192,224},{224,1... | collective-permute-start | bytes 1572872 | tf_op jit(solution)/shard_map/ppermute | solution.py:208
  4.6 1.1 %shard_map.46 = bf16[2,4,8,32,128]{4,3,2,1,0:T(8,128)(2,1)S(1)} custom-call(s32[1]{0:T(128)} %bitcast.place, bf16[1,4,32,8192]{3,2,1,0:T(8,128)(2,1)} %grads_ref.7), custom_call_target="tpu_custom_call" | custom-call | tf_op jit(solution)/shard_map/pallas_call | solution.py:231
  6.4 1.1 %collective-permute-start.3 = (bf16[4,8,32,128]{3,2,1,0:T(8,128)(2,1)S(1)}, bf16[4,8,32,128]{3,2,1,0:T(8,128)(2,1)S(1)}, u32[]{:S(2)}, u32[]{:S(2)}) collective-permute-start(bf16[4,8,32,128]{3,2,1,0:T(8,128)(2,1)S(1)} %get-tuple-element.17), channel_id=1, source_target_pairs={{0,64},{32,224},{64,0},{96,160},{128,192},{160,96},{192,128},{224,... | collective-permute-start | bytes 786440 | tf_op jit(solution)/shard_map/ppermute | solution.py:212
  7.4 1.7 %collective-permute-start.2 = (bf16[4,8,32,128]{3,2,1,0:T(8,128)(2,1)S(1)}, bf16[4,8,32,128]{3,2,1,0:T(8,128)(2,1)S(1)}, u32[]{:S(2)}, u32[]{:S(2)}) collective-permute-start(bf16[4,8,32,128]{3,2,1,0:T(8,128)(2,1)S(1)} %get-tuple-element.15), channel_id=1, source_target_pairs={{0,64},{32,224},{64,0},{96,160},{128,192},{160,96},{192,128},{224,... | collective-permute-start | bytes 786440 | tf_op jit(solution)/shard_map/ppermute | solution.py:212
  9.3 3.6 %collective-permute-done.3.y_ref = bf16[4,8,32,128]{3,2,1,0:T(8,128)(2,1)S(1)} collective-permute-done((bf16[4,8,32,128]{3,2,1,0:T(8,128)(2,1)S(1)}, bf16[4,8,32,128]{3,2,1,0:T(8,128)(2,1)S(1)}, u32[]{:S(2)}, u32[]{:S(2)}) %collective-permute-start.3) | collective-permute-done | bytes 262176 | tf_op jit(solution)/shard_map/ppermute | solution.py:212
  13.0 2.6 %collective-permute-done.2.refs_1_ = bf16[4,8,32,128]{3,2,1,0:T(8,128)(2,1)S(1)} collective-permute-done((bf16[4,8,32,128]{3,2,1,0:T(8,128)(2,1)S(1)}, bf16[4,8,32,128]{3,2,1,0:T(8,128)(2,1)S(1)}, u32[]{:S(2)}, u32[]{:S(2)}) %collective-permute-start.2) | collective-permute-done | bytes 262176 | tf_op jit(solution)/shard_map/ppermute | solution.py:212
  15.7 2.9 %collective-permute-done.4.refs_2_ = bf16[4,8,32,128]{3,2,1,0:T(8,128)(2,1)S(1)} collective-permute-done((bf16[4,8,32,128]{3,2,1,0:T(8,128)(2,1)S(1)}, bf16[4,8,32,128]{3,2,1,0:T(8,128)(2,1)S(1)}, u32[]{:S(2)}, u32[]{:S(2)}) %collective-permute-start.4) | collective-permute-done | bytes 262176 | tf_op jit(solution)/shard_map/ppermute | solution.py:212
  19.3 23.5 %all_to_all.10.block_ref = bf16[32,2,32,128]{3,2,1,0:T(8,128)(2,1)S(1)} all-to-all(bf16[32,2,32,128]{3,2,1,0:T(8,128)(2,1)S(1)} %shard_map.51), channel_id=1, replica_groups=mesh['replica'=8,'fsdp'=32] {'fsdp'}, dimensions={0} | all-to-all | bytes 1048576 | tf_op jit(solution)/shard_map/all_to_all | solution.py:252
  42.8 1.4 %shard_map.52 = (bf16[2,256,128]{2,1,0:T(8,128)(2,1)S(1)}, bf16[2,256,128]{2,1,0:T(8,128)(2,1)S(1)}, bf16[2,256,128]{2,1,0:T(8,128)(2,1)S(1)}, bf16[2,256,128]{2,1,0:T(8,128)(2,1)S(1)}, f32[2,8,128]{2,1,0:T(8,128)S(1)}) custom-call(s32[1]{0:T(128)} %bitcast.place, bf16[2,1024,1024]{2,1,0:T(8,128)(2,1)S(1)} %copy-done.1, ...), custom_call_target="tpu_custom_call" | custom-call | tf_op jit(solution)/shard_map/pallas_call | solution.py:255
  44.2 3.9 %collective-permute-start.5 = (bf16[2,256,128]{2,1,0:T(8,128)(2,1)S(1)}, bf16[2,256,128]{2,1,0:T(8,128)(2,1)S(1)}, u32[]{:S(2)}, u32[]{:S(2)}) collective-permute-start(bf16[2,256,128]{2,1,0:T(8,128)(2,1)S(1)} %get-tuple-element.19), channel_id=1, source_target_pairs={{0,128},{32,160},{64,192},{96,224},{128,0},{160,32},{192,64},{224,... | collective-permute-start | bytes 393224 | tf_op jit(solution)/shard_map/ppermute | solution.py:212
  48.9 4.2 %collective-permute-start.8 = (bf16[2,256,128]{2,1,0:T(8,128)(2,1)S(1)}, bf16[2,256,128]{2,1,0:T(8,128)(2,1)S(1)}, u32[]{:S(2)}, u32[]{:S(2)}) collective-permute-start(bf16[2,256,128]{2,1,0:T(8,128)(2,1)S(1)} %get-tuple-element.18.refs_0_), channel_id=1, source_target_pairs={{0,32},{32,0},{64,96},{96,64},{128,160},{160,128},{192,224},{224,1... | collective-permute-start | bytes 393224 | tf_op jit(solution)/shard_map/ppermute | solution.py:208
  53.1 3.4 %collective-permute-start.9 = (bf16[2,256,128]{2,1,0:T(8,128)(2,1)S(1)}, bf16[2,256,128]{2,1,0:T(8,128)(2,1)S(1)}, u32[]{:S(2)}, u32[]{:S(2)}) collective-permute-start(bf16[2,256,128]{2,1,0:T(8,128)(2,1)S(1)} %collective-permute-done.5.refs_1_), channel_id=1, source_target_pairs={{0,32},{32,0},{64,96},{96,64},{128,160},{160,128},{192,224},{224,1... | collective-permute-start | bytes 393224 | tf_op jit(solution)/shard_map/ppermute | solution.py:208
  57.2 1.8 %collective-permute-start.10 = (bf16[2,256,128]{2,1,0:T(8,128)(2,1)S(1)}, bf16[2,256,128]{2,1,0:T(8,128)(2,1)S(1)}, u32[]{:S(2)}, u32[]{:S(2)}) collective-permute-start(bf16[2,256,128]{2,1,0:T(8,128)(2,1)S(1)} %collective-permute-done.7.refs_3_), channel_id=1, source_target_pairs={{0,32},{32,0},{64,96},{96,64},{128,160},{160,128},{192,224},{224,1... | collective-permute-start | bytes 393224 | tf_op jit(solution)/shard_map/ppermute | solution.py:208
  59.0 1.0 collective-permute-done.10.refs_6_
  60.0 1.1 %shard_map.53 = bf16[32,8,1152]{2,1,0:T(8,128)(2,1)S(1)} custom-call(s32[1]{0:T(128)} %bitcast.place, bf16[2,256,128]{2,1,0:T(8,128)(2,1)S(1)} %get-tuple-element.18.refs_0_, bf16[2,256,128]{2,1,0:T(8,128)(2,1)S(1)} %collective-permute-done.5.refs_1_, bf16[2,256,128]{2,1,0:T(8,128)(2,1)S(1)} %collective-permute-done.6.refs_2_, ...), custom_call_target="tpu_custom_call" | custom-call | tf_op jit(solution)/shard_map/pallas_call | solution.py:265
  61.1 21.5 %all_to_all.11.back_ref = bf16[32,8,1152]{2,1,0:T(8,128)(2,1)S(1)} all-to-all(bf16[32,8,1152]{2,1,0:T(8,128)(2,1)S(1)} %shard_map.53), channel_id=1, replica_groups=mesh['replica'=8,'fsdp'=32] {'fsdp'}, dimensions={0} | all-to-all | bytes 1179648 | tf_op jit(solution)/shard_map/all_to_all | solution.py:272
  82.7 1.0 shard_map.54.refs_0_
  84.1 0.8 collective-permute-start.12
  84.9 4.0 %collective-permute-done.13.refs_2_ = bf16[130,8,128]{2,1,0:T(8,128)(2,1)S(1)} collective-permute-done((bf16[130,8,128]{2,1,0:T(8,128)(2,1)S(1)}, bf16[130,8,128]{2,1,0:T(8,128)(2,1)S(1)}, u32[]{:S(2)}, u32[]{:S(2)}) %collective-permute-start.13) | collective-permute-done | bytes 266272 | tf_op jit(solution)/shard_map/ppermute | solution.py:212
  89.5 5.8 %collective-permute-start.15 = (bf16[130,8,128]{2,1,0:T(8,128)(2,1)S(1)}, bf16[130,8,128]{2,1,0:T(8,128)(2,1)S(1)}, u32[]{:S(2)}, u32[]{:S(2)}) collective-permute-start(bf16[130,8,128]{2,1,0:T(8,128)(2,1)S(1)} %shard_map.54.refs_0_), channel_id=1, source_target_pairs={{0,32},{32,0},{64,96},{96,64},{128,160},{160,128},{192,224},{224,1... | collective-permute-start | bytes 798728 | tf_op jit(solution)/shard_map/ppermute | solution.py:208
  96.3 5.0 %collective-permute-start.18 = (bf16[130,8,128]{2,1,0:T(8,128)(2,1)S(1)}, bf16[130,8,128]{2,1,0:T(8,128)(2,1)S(1)}, u32[]{:S(2)}, u32[]{:S(2)}) collective-permute-start(bf16[130,8,128]{2,1,0:T(8,128)(2,1)S(1)} %collective-permute-done.14.refs_3_), channel_id=1, source_target_pairs={{0,32},{32,0},{64,96},{96,64},{128,160},{160,128},{192,224},{224,1... | collective-permute-start | bytes 798728 | tf_op jit(solution)/shard_map/ppermute | solution.py:208
  101.4 1.2 %collective-permute-done.18.refs_7_ = bf16[130,8,128]{2,1,0:T(8,128)(2,1)S(1)} collective-permute-done((bf16[130,8,128]{2,1,0:T(8,128)(2,1)S(1)}, bf16[130,8,128]{2,1,0:T(8,128)(2,1)S(1)}, u32[]{:S(2)}, u32[]{:S(2)}) %collective-permute-start.18) | collective-permute-done | bytes 266272 | tf_op jit(solution)/shard_map/ppermute | solution.py:208
  102.5 1.7 %shard_map.55 = bf16[4,32,8192]{2,1,0:T(8,128)(2,1)} custom-call(s32[1]{0:T(128)} %bitcast.place, bf16[130,8,128]{2,1,0:T(8,128)(2,1)S(1)} %shard_map.54.refs_0_, bf16[130,8,128]{2,1,0:T(8,128)(2,1)S(1)} %collective-permute-done.12.refs_1_, bf16[130,8,128]{2,1,0:T(8,128)(2,1)S(1)} %collective-permute-done.13.refs_2_, ...), custom_call_target="tpu_custom_call" | custom-call | tf_op jit(solution)/shard_map/pallas_call | solution.py:281
  (34 shorter events, 5.1 us)
Async XLA Ops:
  0.0 6.2 %copy-start = (bf16[1,4,32,8192]{3,2,1,0:T(8,128)(2,1)S(1)}, bf16[1,4,32,8192]{3,2,1,0:T(8,128)(2,1)}, u32[]{:S(2)}) copy-start(bf16[1,4,32,8192]{3,2,1,0:T(8,128)(2,1)} %grads_ref.7) | copy-start | bytes 6291460
  1.3 17.2 %copy-start.3 = (s32[32]{0:T(128)S(1)}, s32[32]{0:T(128)}, u32[]{:S(2)}) copy-start(s32[32]{0:T(128)} %slot.3) | copy-start | bytes 388
  1.3 4.9 %collective-permute-start.1 = (bf16[2,4,8,32,128]{4,3,2,1,0:T(8,128)(2,1)S(1)}, bf16[2,4,8,32,128]{4,3,2,1,0:T(8,128)(2,1)S(1)}, u32[]{:S(2)}, u32[]{:S(2)}) collective-permute-start(bf16[2,4,8,32,128]{4,3,2,1,0:T(8,128)(2,1)S(1)} %shard_map.48), channel_id=1, source_target_pairs={{0,32},{32,0},{64,96},{96,64},{128,160},{160,128},{192,224},{224,1... | collective-permute-start | bytes 1572872 | tf_op jit(solution)/shard_map/ppermute | solution.py:208
  5.8 37.0 %copy-start.1 = (bf16[2,1024,1024]{2,1,0:T(8,128)(2,1)S(1)}, bf16[2,1024,1024]{2,1,0:T(8,128)(2,1)}, u32[]{:S(2)}) copy-start(bf16[2,1024,1024]{2,1,0:T(8,128)(2,1)} %left_ref.1) | copy-start | bytes 12582916
  5.8 3.3 %collective-permute-start = (bf16[2,4,8,32,128]{4,3,2,1,0:T(8,128)(2,1)S(1)}, bf16[2,4,8,32,128]{4,3,2,1,0:T(8,128)(2,1)S(1)}, u32[]{:S(2)}, u32[]{:S(2)}) collective-permute-start(bf16[2,4,8,32,128]{4,3,2,1,0:T(8,128)(2,1)S(1)} %shard_map.46), channel_id=1, source_target_pairs={{0,32},{32,0},{64,96},{96,64},{128,160},{160,128},{192,224},{224,1... | collective-permute-start | bytes 1572872 | tf_op jit(solution)/shard_map/ppermute | solution.py:208
  6.4 6.5 %collective-permute-start.3 = (bf16[4,8,32,128]{3,2,1,0:T(8,128)(2,1)S(1)}, bf16[4,8,32,128]{3,2,1,0:T(8,128)(2,1)S(1)}, u32[]{:S(2)}, u32[]{:S(2)}) collective-permute-start(bf16[4,8,32,128]{3,2,1,0:T(8,128)(2,1)S(1)} %get-tuple-element.17), channel_id=1, source_target_pairs={{0,64},{32,224},{64,0},{96,160},{128,192},{160,96},{192,128},{224,... | collective-permute-start | bytes 786440 | tf_op jit(solution)/shard_map/ppermute | solution.py:212
  7.4 8.2 %collective-permute-start.2 = (bf16[4,8,32,128]{3,2,1,0:T(8,128)(2,1)S(1)}, bf16[4,8,32,128]{3,2,1,0:T(8,128)(2,1)S(1)}, u32[]{:S(2)}, u32[]{:S(2)}) collective-permute-start(bf16[4,8,32,128]{3,2,1,0:T(8,128)(2,1)S(1)} %get-tuple-element.15), channel_id=1, source_target_pairs={{0,64},{32,224},{64,0},{96,160},{128,192},{160,96},{192,128},{224,... | collective-permute-start | bytes 786440 | tf_op jit(solution)/shard_map/ppermute | solution.py:212
  9.3 50.7 %copy-start.2 = (bf16[2,1024,1024]{2,1,0:T(8,128)(2,1)S(1)}, bf16[2,1024,1024]{2,1,0:T(8,128)(2,1)}, u32[]{:S(2)}) copy-start(bf16[2,1024,1024]{2,1,0:T(8,128)(2,1)} %refs_8_.1) | copy-start | bytes 12582916
  12.9 5.6 %collective-permute-start.4 = (bf16[4,8,32,128]{3,2,1,0:T(8,128)(2,1)S(1)}, bf16[4,8,32,128]{3,2,1,0:T(8,128)(2,1)S(1)}, u32[]{:S(2)}, u32[]{:S(2)}) collective-permute-start(bf16[4,8,32,128]{3,2,1,0:T(8,128)(2,1)S(1)} %shard_map.50), channel_id=1, source_target_pairs={{0,192},{32,96},{64,128},{96,32},{128,64},{160,224},{192,0},{224,1... | collective-permute-start | bytes 786440 | tf_op jit(solution)/shard_map/ppermute | solution.py:212
  44.2 8.8 %collective-permute-start.5 = (bf16[2,256,128]{2,1,0:T(8,128)(2,1)S(1)}, bf16[2,256,128]{2,1,0:T(8,128)(2,1)S(1)}, u32[]{:S(2)}, u32[]{:S(2)}) collective-permute-start(bf16[2,256,128]{2,1,0:T(8,128)(2,1)S(1)} %get-tuple-element.19), channel_id=1, source_target_pairs={{0,128},{32,160},{64,192},{96,224},{128,0},{160,32},{192,64},{224,... | collective-permute-start | bytes 393224 | tf_op jit(solution)/shard_map/ppermute | solution.py:212
  48.1 8.3 %collective-permute-start.6 = (bf16[2,256,128]{2,1,0:T(8,128)(2,1)S(1)}, bf16[2,256,128]{2,1,0:T(8,128)(2,1)S(1)}, u32[]{:S(2)}, u32[]{:S(2)}) collective-permute-start(bf16[2,256,128]{2,1,0:T(8,128)(2,1)S(1)} %get-tuple-element.20), channel_id=1, source_target_pairs={{0,64},{32,224},{64,0},{96,160},{128,192},{160,96},{192,128},{224,... | collective-permute-start | bytes 393224 | tf_op jit(solution)/shard_map/ppermute | solution.py:212
  48.9 8.2 %collective-permute-start.7 = (bf16[2,256,128]{2,1,0:T(8,128)(2,1)S(1)}, bf16[2,256,128]{2,1,0:T(8,128)(2,1)S(1)}, u32[]{:S(2)}, u32[]{:S(2)}) collective-permute-start(bf16[2,256,128]{2,1,0:T(8,128)(2,1)S(1)} %get-tuple-element.21), channel_id=1, source_target_pairs={{0,192},{32,96},{64,128},{96,32},{128,64},{160,224},{192,0},{224,1... | collective-permute-start | bytes 393224 | tf_op jit(solution)/shard_map/ppermute | solution.py:212
  48.9 10.1 %collective-permute-start.8 = (bf16[2,256,128]{2,1,0:T(8,128)(2,1)S(1)}, bf16[2,256,128]{2,1,0:T(8,128)(2,1)S(1)}, u32[]{:S(2)}, u32[]{:S(2)}) collective-permute-start(bf16[2,256,128]{2,1,0:T(8,128)(2,1)S(1)} %get-tuple-element.18.refs_0_), channel_id=1, source_target_pairs={{0,32},{32,0},{64,96},{96,64},{128,160},{160,128},{192,224},{224,1... | collective-permute-start | bytes 393224 | tf_op jit(solution)/shard_map/ppermute | solution.py:208
  53.1 5.9 %collective-permute-start.9 = (bf16[2,256,128]{2,1,0:T(8,128)(2,1)S(1)}, bf16[2,256,128]{2,1,0:T(8,128)(2,1)S(1)}, u32[]{:S(2)}, u32[]{:S(2)}) collective-permute-start(bf16[2,256,128]{2,1,0:T(8,128)(2,1)S(1)} %collective-permute-done.5.refs_1_), channel_id=1, source_target_pairs={{0,32},{32,0},{64,96},{96,64},{128,160},{160,128},{192,224},{224,1... | collective-permute-start | bytes 393224 | tf_op jit(solution)/shard_map/ppermute | solution.py:208
  56.5 2.5 %collective-permute-start.11 = (bf16[2,256,128]{2,1,0:T(8,128)(2,1)S(1)}, bf16[2,256,128]{2,1,0:T(8,128)(2,1)S(1)}, u32[]{:S(2)}, u32[]{:S(2)}) collective-permute-start(bf16[2,256,128]{2,1,0:T(8,128)(2,1)S(1)} %collective-permute-done.6.refs_2_), channel_id=1, source_target_pairs={{0,32},{32,0},{64,96},{96,64},{128,160},{160,128},{192,224},{224,1... | collective-permute-start | bytes 393224 | tf_op jit(solution)/shard_map/ppermute | solution.py:208
  57.2 2.8 %collective-permute-start.10 = (bf16[2,256,128]{2,1,0:T(8,128)(2,1)S(1)}, bf16[2,256,128]{2,1,0:T(8,128)(2,1)S(1)}, u32[]{:S(2)}, u32[]{:S(2)}) collective-permute-start(bf16[2,256,128]{2,1,0:T(8,128)(2,1)S(1)} %collective-permute-done.7.refs_3_), channel_id=1, source_target_pairs={{0,32},{32,0},{64,96},{96,64},{128,160},{160,128},{192,224},{224,1... | collective-permute-start | bytes 393224 | tf_op jit(solution)/shard_map/ppermute | solution.py:208
  83.6 5.3 %collective-permute-start.13 = (bf16[130,8,128]{2,1,0:T(8,128)(2,1)S(1)}, bf16[130,8,128]{2,1,0:T(8,128)(2,1)S(1)}, u32[]{:S(2)}, u32[]{:S(2)}) collective-permute-start(bf16[130,8,128]{2,1,0:T(8,128)(2,1)S(1)} %shard_map.54.refs_0_), channel_id=1, source_target_pairs={{0,192},{32,96},{64,128},{96,32},{128,64},{160,224},{192,0},{224,1... | collective-permute-start | bytes 798728 | tf_op jit(solution)/shard_map/ppermute | solution.py:212
  84.1 11.2 %collective-permute-start.12 = (bf16[130,8,128]{2,1,0:T(8,128)(2,1)S(1)}, bf16[130,8,128]{2,1,0:T(8,128)(2,1)S(1)}, u32[]{:S(2)}, u32[]{:S(2)}) collective-permute-start(bf16[130,8,128]{2,1,0:T(8,128)(2,1)S(1)} %shard_map.54.refs_0_), channel_id=1, source_target_pairs={{0,64},{32,224},{64,0},{96,160},{128,192},{160,96},{192,128},{224,... | collective-permute-start | bytes 798728 | tf_op jit(solution)/shard_map/ppermute | solution.py:212
  89.0 7.3 %collective-permute-start.14 = (bf16[130,8,128]{2,1,0:T(8,128)(2,1)S(1)}, bf16[130,8,128]{2,1,0:T(8,128)(2,1)S(1)}, u32[]{:S(2)}, u32[]{:S(2)}) collective-permute-start(bf16[130,8,128]{2,1,0:T(8,128)(2,1)S(1)} %collective-permute-done.13.refs_2_), channel_id=1, source_target_pairs={{0,64},{32,224},{64,0},{96,160},{128,192},{160,96},{192,128},{224,... | collective-permute-start | bytes 798728 | tf_op jit(solution)/shard_map/ppermute | solution.py:212
  89.5 11.8 %collective-permute-start.15 = (bf16[130,8,128]{2,1,0:T(8,128)(2,1)S(1)}, bf16[130,8,128]{2,1,0:T(8,128)(2,1)S(1)}, u32[]{:S(2)}, u32[]{:S(2)}) collective-permute-start(bf16[130,8,128]{2,1,0:T(8,128)(2,1)S(1)} %shard_map.54.refs_0_), channel_id=1, source_target_pairs={{0,32},{32,0},{64,96},{96,64},{128,160},{160,128},{192,224},{224,1... | collective-permute-start | bytes 798728 | tf_op jit(solution)/shard_map/ppermute | solution.py:208
  95.4 6.0 %collective-permute-start.16 = (bf16[130,8,128]{2,1,0:T(8,128)(2,1)S(1)}, bf16[130,8,128]{2,1,0:T(8,128)(2,1)S(1)}, u32[]{:S(2)}, u32[]{:S(2)}) collective-permute-start(bf16[130,8,128]{2,1,0:T(8,128)(2,1)S(1)} %collective-permute-done.13.refs_2_), channel_id=1, source_target_pairs={{0,32},{32,0},{64,96},{96,64},{128,160},{160,128},{192,224},{224,1... | collective-permute-start | bytes 798728 | tf_op jit(solution)/shard_map/ppermute | solution.py:208
  95.4 6.0 %collective-permute-start.17 = (bf16[130,8,128]{2,1,0:T(8,128)(2,1)S(1)}, bf16[130,8,128]{2,1,0:T(8,128)(2,1)S(1)}, u32[]{:S(2)}, u32[]{:S(2)}) collective-permute-start(bf16[130,8,128]{2,1,0:T(8,128)(2,1)S(1)} %collective-permute-done.12.refs_1_), channel_id=1, source_target_pairs={{0,32},{32,0},{64,96},{96,64},{128,160},{160,128},{192,224},{224,1... | collective-permute-start | bytes 798728 | tf_op jit(solution)/shard_map/ppermute | solution.py:208
  96.3 6.2 %collective-permute-start.18 = (bf16[130,8,128]{2,1,0:T(8,128)(2,1)S(1)}, bf16[130,8,128]{2,1,0:T(8,128)(2,1)S(1)}, u32[]{:S(2)}, u32[]{:S(2)}) collective-permute-start(bf16[130,8,128]{2,1,0:T(8,128)(2,1)S(1)} %collective-permute-done.14.refs_3_), channel_id=1, source_target_pairs={{0,32},{32,0},{64,96},{96,64},{128,160},{160,128},{192,224},{224,1... | collective-permute-start | bytes 798728 | tf_op jit(solution)/shard_map/ppermute | solution.py:208

commit v11 on v4

--- a/solution.py
+++ b/solution.py
@@ -125,43 +125,42 @@
     part, wide = back_ref.shape[1:]
     width = (wide - LANES) // 2
     each = width // LANES
-    blocks = (tiles_ref.shape[0] - 2) // each
-    lane = lax.broadcasted_iota(jnp.int32, (part, LANES), 1)
+    blocks = slot.shape[0]
     line = lax.broadcasted_iota(jnp.int32, (part, LANES), 0)
-    terms = [jnp.zeros((part, LANES), f32)] * 2
-    for b in range(blocks):
-        q, h, pair = slot[b], b % 2, b // 2
-        s = lax.rem(q, 2)
-        for t in range(each):
-            columns = pl.ds(pl.multiple_of(s * width + t * LANES, LANES), LANES)
-            tiles_ref[b * each + t] = back_ref[q // 2, :, columns]
-        tail = back_ref[q // 2, :, 2 * width :].astype(f32)
-        tail = jnp.where(s == h, tail, pltpu.roll(tail, TERMS if h else LANES - TERMS, 1))
-        here = (line == pair % part) & (lane >= TERMS * h) & (lane < TERMS * (h + 1))
-        terms[pair // part] = jnp.where(here, tail, terms[pair // part])
-    for n in range(2):
-        tiles_ref[blocks * each + n] = terms[n].astype(bf16)
-
-
-def finish_kernel(place, *refs, entries):
+    for n in range(blocks // part):
+        terms = jnp.zeros((part, LANES), f32)
+        for b in range(n * part, (n + 1) * part):
+            q = slot[b]
+            s = lax.rem(q, 2)
+            for t in range(each):
+                columns = pl.ds(pl.multiple_of(s * width + t * LANES, LANES), LANES)
+                tiles_ref[b * each + t] = back_ref[q // 2, :, columns]
+            terms = jnp.where(line == b % part, back_ref[q // 2, :, 2 * width :].astype(f32), terms)
+        tiles_ref[blocks * each + n] = terms.astype(bf16)
+
+
+def finish_kernel(place, slot, *refs, entries):
     own_refs, twin_refs = refs[:4], refs[4:8]
     out_ref, ready, ratios, written = refs[8:]
     part = own_refs[0].shape[1]
     mats, rows, full = ready.shape
     blocks = ratios.shape[0]
-    each = (own_refs[0].shape[0] - 2) // blocks
+    each = (own_refs[0].shape[0] - blocks // part) // blocks
     count = blocks // mats
     lane = lax.broadcasted_iota(jnp.int32, (part, LANES), 1)
-    for n in range(2):
+    for n in range(blocks // part):
         tail = sum(ref[blocks * each + n].astype(f32) for ref in own_refs + twin_refs)
+        found = []
         for h in range(2):
             block_square, prec_square = [
                 jnp.sum(jnp.where((lane >= start) & (lane < start + 3), tail, 0.0), axis=1, keepdims=True)
                 for start in (TERMS * h, TERMS * h + 3)
             ]
-            ratio = jnp.sqrt(block_square / entries + EPSILON) / jnp.sqrt(prec_square / entries + EPSILON)
-            for line in range(part):
-                ratios[2 * (n * part + line) + h] = jnp.broadcast_to(ratio[line : line + 1], (part, LANES))
+            found.append(jnp.sqrt(block_square / entries + EPSILON) / jnp.sqrt(prec_square / entries + EPSILON))
+        for line in range(part):
+            b = n * part + line
+            first, second = (jnp.broadcast_to(ratio[line : line + 1], (part, LANES)) for ratio in found)
+            ratios[b] = jnp.where(lax.rem(slot[b], 2) == 0, first, second)
 
     def emit(m, core, odd):
         couples = ((SELF, FAR), (OPPOSITE, NEAR)) if core else ((SELF, NEAR), (OPPOSITE, FAR))
@@ -271,7 +270,7 @@
     )(place, *halves, *handed, right_root, square)
     back = lax.all_to_all(back, "fsdp", 0, 0, tiled=True)
 
-    tiles = blocks * (width // 2 // LANES) + 2
+    tiles = blocks * (width // 2 // LANES) + blocks // part
     mine = local(select_kernel, [smem, vmem], vmem, shape((tiles, part, LANES), bf16))(block_slot, back)
     near = exchange(mine, NEAR)
     far = exchange(mine, FAR)
@@ -280,7 +279,7 @@
     other = [twin(x) for x in (mine, far, near, opposite)]
     return local(
         functools.partial(finish_kernel, entries=height * width),
-        [smem] + [vmem] * 8,
+        [smem] * 2 + [vmem] * 8,
         pl.BlockSpec(memory_space=pl.ANY),
         shape((mats, rows, full), bf16),
         [
@@ -288,7 +287,7 @@
             pltpu.VMEM((blocks, part, LANES), f32),
             pltpu.SemaphoreType.DMA((mats,)),
         ],
-    )(place, *own, *other)
+    )(place, block_slot, *own, *other)
 
 
 def solution(mesh):

time: 104 us -> 105 us (level)
  no operation moved by 1% of the time
where the time goes in v11:
time: 105 us; the launch traced here: 104 us
  blocking collectives  45 us (43%)
  starting transfers between devices  32.3 us (31%)
  waiting for transfers between devices  17.4 us (17%)
  Pallas kernels  9.27 us (9%)
    ppermute x10, starting transfers between devices, twin(): return lax.ppermute(x, 'replica', [(i, i ^ 1) for i in range(reps)])  24.1 us
    all_to_all x1, blocking collectives, on_device(): incoming = lax.all_to_all(outgoing, 'fsdp', 0, 0, tiled=True)  23.5 us
    all_to_all x1, blocking collectives, on_device(): back = lax.all_to_all(back, 'fsdp', 0, 0, tiled=True)  21.5 us
    ppermute x9, waiting for transfers between devices, exchange(): return lax.ppermute(x, 'replica', perm)  15 us
    ppermute x9, starting transfers between devices, exchange(): return lax.ppermute(x, 'replica', perm)  8.25 us
    pallas_call x2, Pallas kernels, on_device(): local(functools.partial(send_kernel, kinds=kinds, **sizes), [smem, pl.Blo...  2.44 us
    ppermute x10, waiting for transfers between devices, twin(): return lax.ppermute(x, 'replica', [(i, i ^ 1) for i in range(reps)])  2.4 us
    pallas_call x1, Pallas kernels, on_device(): local(functools.partial(finish_kernel, entries=height * width), [smem] *...  2.22 us
  transfers between devices with their start and end apart: 19, of which 7 were waited for; matrix products, arithmetic and copies ran while one was open for 0% of the time, Pallas kernels for 1%

profile of v11, /device:TPU:1, one launch (start us, length us, event | category | flops | bytes accessed | tf_op | source)
XLA Modules:
  0.0 104.3 jit_solution(6897235021301061193)
XLA Ops:
  0.0 1.3 %shard_map.48 = bf16[2,4,8,32,128]{4,3,2,1,0:T(8,128)(2,1)S(1)} custom-call(s32[1]{0:T(128)} %bitcast.place, bf16[1,4,32,8192]{3,2,1,0:T(8,128)(2,1)} %grads_ref.7), custom_call_target="tpu_custom_call" | custom-call | tf_op jit(solution)/shard_map/pallas_call | solution.py:230
  1.3 3.3 %collective-permute-start.1 = (bf16[2,4,8,32,128]{4,3,2,1,0:T(8,128)(2,1)S(1)}, bf16[2,4,8,32,128]{4,3,2,1,0:T(8,128)(2,1)S(1)}, u32[]{:S(2)}, u32[]{:S(2)}) collective-permute-start(bf16[2,4,8,32,128]{4,3,2,1,0:T(8,128)(2,1)S(1)} %shard_map.48), channel_id=1, source_target_pairs={{0,32},{32,0},{64,96},{96,64},{128,160},{160,128},{192,224},{224,1... | collective-permute-start | bytes 1572872 | tf_op jit(solution)/shard_map/ppermute | solution.py:207
  4.6 1.1 %shard_map.46 = bf16[2,4,8,32,128]{4,3,2,1,0:T(8,128)(2,1)S(1)} custom-call(s32[1]{0:T(128)} %bitcast.place, bf16[1,4,32,8192]{3,2,1,0:T(8,128)(2,1)} %grads_ref.7), custom_call_target="tpu_custom_call" | custom-call | tf_op jit(solution)/shard_map/pallas_call | solution.py:230
  6.4 1.1 %collective-permute-start.3 = (bf16[4,8,32,128]{3,2,1,0:T(8,128)(2,1)S(1)}, bf16[4,8,32,128]{3,2,1,0:T(8,128)(2,1)S(1)}, u32[]{:S(2)}, u32[]{:S(2)}) collective-permute-start(bf16[4,8,32,128]{3,2,1,0:T(8,128)(2,1)S(1)} %get-tuple-element.17), channel_id=1, source_target_pairs={{0,64},{32,224},{64,0},{96,160},{128,192},{160,96},{192,128},{224,... | collective-permute-start | bytes 786440 | tf_op jit(solution)/shard_map/ppermute | solution.py:211
  7.4 1.7 %collective-permute-start.2 = (bf16[4,8,32,128]{3,2,1,0:T(8,128)(2,1)S(1)}, bf16[4,8,32,128]{3,2,1,0:T(8,128)(2,1)S(1)}, u32[]{:S(2)}, u32[]{:S(2)}) collective-permute-start(bf16[4,8,32,128]{3,2,1,0:T(8,128)(2,1)S(1)} %get-tuple-element.15), channel_id=1, source_target_pairs={{0,64},{32,224},{64,0},{96,160},{128,192},{160,96},{192,128},{224,... | collective-permute-start | bytes 786440 | tf_op jit(solution)/shard_map/ppermute | solution.py:211
  9.3 3.6 %collective-permute-done.3.y_ref = bf16[4,8,32,128]{3,2,1,0:T(8,128)(2,1)S(1)} collective-permute-done((bf16[4,8,32,128]{3,2,1,0:T(8,128)(2,1)S(1)}, bf16[4,8,32,128]{3,2,1,0:T(8,128)(2,1)S(1)}, u32[]{:S(2)}, u32[]{:S(2)}) %collective-permute-start.3) | collective-permute-done | bytes 262176 | tf_op jit(solution)/shard_map/ppermute | solution.py:211
  13.0 2.6 %collective-permute-done.2.refs_1_ = bf16[4,8,32,128]{3,2,1,0:T(8,128)(2,1)S(1)} collective-permute-done((bf16[4,8,32,128]{3,2,1,0:T(8,128)(2,1)S(1)}, bf16[4,8,32,128]{3,2,1,0:T(8,128)(2,1)S(1)}, u32[]{:S(2)}, u32[]{:S(2)}) %collective-permute-start.2) | collective-permute-done | bytes 262176 | tf_op jit(solution)/shard_map/ppermute | solution.py:211
  15.7 2.9 %collective-permute-done.4.refs_2_ = bf16[4,8,32,128]{3,2,1,0:T(8,128)(2,1)S(1)} collective-permute-done((bf16[4,8,32,128]{3,2,1,0:T(8,128)(2,1)S(1)}, bf16[4,8,32,128]{3,2,1,0:T(8,128)(2,1)S(1)}, u32[]{:S(2)}, u32[]{:S(2)}) %collective-permute-start.4) | collective-permute-done | bytes 262176 | tf_op jit(solution)/shard_map/ppermute | solution.py:211
  19.3 23.5 %all_to_all.10.block_ref = bf16[32,2,32,128]{3,2,1,0:T(8,128)(2,1)S(1)} all-to-all(bf16[32,2,32,128]{3,2,1,0:T(8,128)(2,1)S(1)} %shard_map.51), channel_id=1, replica_groups=mesh['replica'=8,'fsdp'=32] {'fsdp'}, dimensions={0} | all-to-all | bytes 1048576 | tf_op jit(solution)/shard_map/all_to_all | solution.py:251
  42.8 1.4 %shard_map.52 = (bf16[2,256,128]{2,1,0:T(8,128)(2,1)S(1)}, bf16[2,256,128]{2,1,0:T(8,128)(2,1)S(1)}, bf16[2,256,128]{2,1,0:T(8,128)(2,1)S(1)}, bf16[2,256,128]{2,1,0:T(8,128)(2,1)S(1)}, f32[2,8,128]{2,1,0:T(8,128)S(1)}) custom-call(s32[1]{0:T(128)} %bitcast.place, bf16[2,1024,1024]{2,1,0:T(8,128)(2,1)S(1)} %copy-done.1, ...), custom_call_target="tpu_custom_call" | custom-call | tf_op jit(solution)/shard_map/pallas_call | solution.py:254
  44.2 3.9 %collective-permute-start.5 = (bf16[2,256,128]{2,1,0:T(8,128)(2,1)S(1)}, bf16[2,256,128]{2,1,0:T(8,128)(2,1)S(1)}, u32[]{:S(2)}, u32[]{:S(2)}) collective-permute-start(bf16[2,256,128]{2,1,0:T(8,128)(2,1)S(1)} %get-tuple-element.19), channel_id=1, source_target_pairs={{0,128},{32,160},{64,192},{96,224},{128,0},{160,32},{192,64},{224,... | collective-permute-start | bytes 393224 | tf_op jit(solution)/shard_map/ppermute | solution.py:211
  48.1 0.8 collective-permute-start.6
  48.9 4.2 %collective-permute-start.8 = (bf16[2,256,128]{2,1,0:T(8,128)(2,1)S(1)}, bf16[2,256,128]{2,1,0:T(8,128)(2,1)S(1)}, u32[]{:S(2)}, u32[]{:S(2)}) collective-permute-start(bf16[2,256,128]{2,1,0:T(8,128)(2,1)S(1)} %get-tuple-element.18.refs_0_), channel_id=1, source_target_pairs={{0,32},{32,0},{64,96},{96,64},{128,160},{160,128},{192,224},{224,1... | collective-permute-start | bytes 393224 | tf_op jit(solution)/shard_map/ppermute | solution.py:207
  53.1 3.4 %collective-permute-start.9 = (bf16[2,256,128]{2,1,0:T(8,128)(2,1)S(1)}, bf16[2,256,128]{2,1,0:T(8,128)(2,1)S(1)}, u32[]{:S(2)}, u32[]{:S(2)}) collective-permute-start(bf16[2,256,128]{2,1,0:T(8,128)(2,1)S(1)} %collective-permute-done.5.refs_1_), channel_id=1, source_target_pairs={{0,32},{32,0},{64,96},{96,64},{128,160},{160,128},{192,224},{224,1... | collective-permute-start | bytes 393224 | tf_op jit(solution)/shard_map/ppermute | solution.py:207
  57.2 1.8 %collective-permute-start.10 = (bf16[2,256,128]{2,1,0:T(8,128)(2,1)S(1)}, bf16[2,256,128]{2,1,0:T(8,128)(2,1)S(1)}, u32[]{:S(2)}, u32[]{:S(2)}) collective-permute-start(bf16[2,256,128]{2,1,0:T(8,128)(2,1)S(1)} %collective-permute-done.7.refs_3_), channel_id=1, source_target_pairs={{0,32},{32,0},{64,96},{96,64},{128,160},{160,128},{192,224},{224,1... | collective-permute-start | bytes 393224 | tf_op jit(solution)/shard_map/ppermute | solution.py:207
  59.0 1.0 collective-permute-done.10.refs_6_
  60.0 1.1 %shard_map.53 = bf16[32,8,1152]{2,1,0:T(8,128)(2,1)S(1)} custom-call(s32[1]{0:T(128)} %bitcast.place, bf16[2,256,128]{2,1,0:T(8,128)(2,1)S(1)} %get-tuple-element.18.refs_0_, bf16[2,256,128]{2,1,0:T(8,128)(2,1)S(1)} %collective-permute-done.5.refs_1_, bf16[2,256,128]{2,1,0:T(8,128)(2,1)S(1)} %collective-permute-done.6.refs_2_, ...), custom_call_target="tpu_custom_call" | custom-call | tf_op jit(solution)/shard_map/pallas_call | solution.py:264
  61.1 21.5 %all_to_all.11.back_ref = bf16[32,8,1152]{2,1,0:T(8,128)(2,1)S(1)} all-to-all(bf16[32,8,1152]{2,1,0:T(8,128)(2,1)S(1)} %shard_map.53), channel_id=1, replica_groups=mesh['replica'=8,'fsdp'=32] {'fsdp'}, dimensions={0} | all-to-all | bytes 1179648 | tf_op jit(solution)/shard_map/all_to_all | solution.py:271
  82.7 0.9 shard_map.54.refs_0_
  84.3 5.9 %collective-permute-done.12.refs_1_ = bf16[132,8,128]{2,1,0:T(8,128)(2,1)S(1)} collective-permute-done((bf16[132,8,128]{2,1,0:T(8,128)(2,1)S(1)}, bf16[132,8,128]{2,1,0:T(8,128)(2,1)S(1)}, u32[]{:S(2)}, u32[]{:S(2)}) %collective-permute-start.12) | collective-permute-done | bytes 270368 | tf_op jit(solution)/shard_map/ppermute | solution.py:211
  90.2 5.9 %collective-permute-start.15 = (bf16[132,8,128]{2,1,0:T(8,128)(2,1)S(1)}, bf16[132,8,128]{2,1,0:T(8,128)(2,1)S(1)}, u32[]{:S(2)}, u32[]{:S(2)}) collective-permute-start(bf16[132,8,128]{2,1,0:T(8,128)(2,1)S(1)} %shard_map.54.refs_0_), channel_id=1, source_target_pairs={{0,32},{32,0},{64,96},{96,64},{128,160},{160,128},{192,224},{224,1... | collective-permute-start | bytes 811016 | tf_op jit(solution)/shard_map/ppermute | solution.py:207
  96.6 4.1 %collective-permute-start.18 = (bf16[132,8,128]{2,1,0:T(8,128)(2,1)S(1)}, bf16[132,8,128]{2,1,0:T(8,128)(2,1)S(1)}, u32[]{:S(2)}, u32[]{:S(2)}) collective-permute-start(bf16[132,8,128]{2,1,0:T(8,128)(2,1)S(1)} %collective-permute-done.14.refs_3_), channel_id=1, source_target_pairs={{0,32},{32,0},{64,96},{96,64},{128,160},{160,128},{192,224},{224,1... | collective-permute-start | bytes 811016 | tf_op jit(solution)/shard_map/ppermute | solution.py:207
  100.8 1.2 %collective-permute-done.18.refs_7_ = bf16[132,8,128]{2,1,0:T(8,128)(2,1)S(1)} collective-permute-done((bf16[132,8,128]{2,1,0:T(8,128)(2,1)S(1)}, bf16[132,8,128]{2,1,0:T(8,128)(2,1)S(1)}, u32[]{:S(2)}, u32[]{:S(2)}) %collective-permute-start.18) | collective-permute-done | bytes 270368 | tf_op jit(solution)/shard_map/ppermute | solution.py:207
  102.0 2.2 %shard_map.55 = bf16[4,32,8192]{2,1,0:T(8,128)(2,1)} custom-call(s32[1]{0:T(128)} %bitcast.place, s32[32]{0:T(128)S(1)} %copy-done.3, bf16[132,8,128]{2,1,0:T(8,128)(2,1)S(1)} %shard_map.54.refs_0_, bf16[132,8,128]{2,1,0:T(8,128)(2,1)S(1)} %collective-permute-done.12.refs_1_, bf16[132,8,128]{2,1,0:T(8,128)(2,1)S(1)} %collective-permute-done.13.refs_2_, ...), custom_call_target="tpu_custom_call" | custom-call | tf_op jit(solution)/shard_map/pallas_call | solution.py:280
  (34 shorter events, 3.6 us)
Async XLA Ops:
  0.0 6.2 %copy-start = (bf16[1,4,32,8192]{3,2,1,0:T(8,128)(2,1)S(1)}, bf16[1,4,32,8192]{3,2,1,0:T(8,128)(2,1)}, u32[]{:S(2)}) copy-start(bf16[1,4,32,8192]{3,2,1,0:T(8,128)(2,1)} %grads_ref.7) | copy-start | bytes 6291460
  1.3 17.2 %copy-start.3 = (s32[32]{0:T(128)S(1)}, s32[32]{0:T(128)}, u32[]{:S(2)}) copy-start(s32[32]{0:T(128)} %slot.5) | copy-start | bytes 388
  1.3 4.9 %collective-permute-start.1 = (bf16[2,4,8,32,128]{4,3,2,1,0:T(8,128)(2,1)S(1)}, bf16[2,4,8,32,128]{4,3,2,1,0:T(8,128)(2,1)S(1)}, u32[]{:S(2)}, u32[]{:S(2)}) collective-permute-start(bf16[2,4,8,32,128]{4,3,2,1,0:T(8,128)(2,1)S(1)} %shard_map.48), channel_id=1, source_target_pairs={{0,32},{32,0},{64,96},{96,64},{128,160},{160,128},{192,224},{224,1... | collective-permute-start | bytes 1572872 | tf_op jit(solution)/shard_map/ppermute | solution.py:207
  5.8 37.0 %copy-start.1 = (bf16[2,1024,1024]{2,1,0:T(8,128)(2,1)S(1)}, bf16[2,1024,1024]{2,1,0:T(8,128)(2,1)}, u32[]{:S(2)}) copy-start(bf16[2,1024,1024]{2,1,0:T(8,128)(2,1)} %left_ref.1) | copy-start | bytes 12582916
  5.8 3.3 %collective-permute-start = (bf16[2,4,8,32,128]{4,3,2,1,0:T(8,128)(2,1)S(1)}, bf16[2,4,8,32,128]{4,3,2,1,0:T(8,128)(2,1)S(1)}, u32[]{:S(2)}, u32[]{:S(2)}) collective-permute-start(bf16[2,4,8,32,128]{4,3,2,1,0:T(8,128)(2,1)S(1)} %shard_map.46), channel_id=1, source_target_pairs={{0,32},{32,0},{64,96},{96,64},{128,160},{160,128},{192,224},{224,1... | collective-permute-start | bytes 1572872 | tf_op jit(solution)/shard_map/ppermute | solution.py:207
  6.4 6.5 %collective-permute-start.3 = (bf16[4,8,32,128]{3,2,1,0:T(8,128)(2,1)S(1)}, bf16[4,8,32,128]{3,2,1,0:T(8,128)(2,1)S(1)}, u32[]{:S(2)}, u32[]{:S(2)}) collective-permute-start(bf16[4,8,32,128]{3,2,1,0:T(8,128)(2,1)S(1)} %get-tuple-element.17), channel_id=1, source_target_pairs={{0,64},{32,224},{64,0},{96,160},{128,192},{160,96},{192,128},{224,... | collective-permute-start | bytes 786440 | tf_op jit(solution)/shard_map/ppermute | solution.py:211
  7.4 8.2 %collective-permute-start.2 = (bf16[4,8,32,128]{3,2,1,0:T(8,128)(2,1)S(1)}, bf16[4,8,32,128]{3,2,1,0:T(8,128)(2,1)S(1)}, u32[]{:S(2)}, u32[]{:S(2)}) collective-permute-start(bf16[4,8,32,128]{3,2,1,0:T(8,128)(2,1)S(1)} %get-tuple-element.15), channel_id=1, source_target_pairs={{0,64},{32,224},{64,0},{96,160},{128,192},{160,96},{192,128},{224,... | collective-permute-start | bytes 786440 | tf_op jit(solution)/shard_map/ppermute | solution.py:211
  9.3 50.7 %copy-start.2 = (bf16[2,1024,1024]{2,1,0:T(8,128)(2,1)S(1)}, bf16[2,1024,1024]{2,1,0:T(8,128)(2,1)}, u32[]{:S(2)}) copy-start(bf16[2,1024,1024]{2,1,0:T(8,128)(2,1)} %refs_8_.1) | copy-start | bytes 12582916
  12.9 5.6 %collective-permute-start.4 = (bf16[4,8,32,128]{3,2,1,0:T(8,128)(2,1)S(1)}, bf16[4,8,32,128]{3,2,1,0:T(8,128)(2,1)S(1)}, u32[]{:S(2)}, u32[]{:S(2)}) collective-permute-start(bf16[4,8,32,128]{3,2,1,0:T(8,128)(2,1)S(1)} %shard_map.50), channel_id=1, source_target_pairs={{0,192},{32,96},{64,128},{96,32},{128,64},{160,224},{192,0},{224,1... | collective-permute-start | bytes 786440 | tf_op jit(solution)/shard_map/ppermute | solution.py:211
  44.2 8.8 %collective-permute-start.5 = (bf16[2,256,128]{2,1,0:T(8,128)(2,1)S(1)}, bf16[2,256,128]{2,1,0:T(8,128)(2,1)S(1)}, u32[]{:S(2)}, u32[]{:S(2)}) collective-permute-start(bf16[2,256,128]{2,1,0:T(8,128)(2,1)S(1)} %get-tuple-element.19), channel_id=1, source_target_pairs={{0,128},{32,160},{64,192},{96,224},{128,0},{160,32},{192,64},{224,... | collective-permute-start | bytes 393224 | tf_op jit(solution)/shard_map/ppermute | solution.py:211
  48.1 8.3 %collective-permute-start.6 = (bf16[2,256,128]{2,1,0:T(8,128)(2,1)S(1)}, bf16[2,256,128]{2,1,0:T(8,128)(2,1)S(1)}, u32[]{:S(2)}, u32[]{:S(2)}) collective-permute-start(bf16[2,256,128]{2,1,0:T(8,128)(2,1)S(1)} %get-tuple-element.20), channel_id=1, source_target_pairs={{0,64},{32,224},{64,0},{96,160},{128,192},{160,96},{192,128},{224,... | collective-permute-start | bytes 393224 | tf_op jit(solution)/shard_map/ppermute | solution.py:211
  48.9 8.2 %collective-permute-start.7 = (bf16[2,256,128]{2,1,0:T(8,128)(2,1)S(1)}, bf16[2,256,128]{2,1,0:T(8,128)(2,1)S(1)}, u32[]{:S(2)}, u32[]{:S(2)}) collective-permute-start(bf16[2,256,128]{2,1,0:T(8,128)(2,1)S(1)} %get-tuple-element.21), channel_id=1, source_target_pairs={{0,192},{32,96},{64,128},{96,32},{128,64},{160,224},{192,0},{224,1... | collective-permute-start | bytes 393224 | tf_op jit(solution)/shard_map/ppermute | solution.py:211
  48.9 10.1 %collective-permute-start.8 = (bf16[2,256,128]{2,1,0:T(8,128)(2,1)S(1)}, bf16[2,256,128]{2,1,0:T(8,128)(2,1)S(1)}, u32[]{:S(2)}, u32[]{:S(2)}) collective-permute-start(bf16[2,256,128]{2,1,0:T(8,128)(2,1)S(1)} %get-tuple-element.18.refs_0_), channel_id=1, source_target_pairs={{0,32},{32,0},{64,96},{96,64},{128,160},{160,128},{192,224},{224,1... | collective-permute-start | bytes 393224 | tf_op jit(solution)/shard_map/ppermute | solution.py:207
  53.1 5.9 %collective-permute-start.9 = (bf16[2,256,128]{2,1,0:T(8,128)(2,1)S(1)}, bf16[2,256,128]{2,1,0:T(8,128)(2,1)S(1)}, u32[]{:S(2)}, u32[]{:S(2)}) collective-permute-start(bf16[2,256,128]{2,1,0:T(8,128)(2,1)S(1)} %collective-permute-done.5.refs_1_), channel_id=1, source_target_pairs={{0,32},{32,0},{64,96},{96,64},{128,160},{160,128},{192,224},{224,1... | collective-permute-start | bytes 393224 | tf_op jit(solution)/shard_map/ppermute | solution.py:207
  56.5 2.5 %collective-permute-start.11 = (bf16[2,256,128]{2,1,0:T(8,128)(2,1)S(1)}, bf16[2,256,128]{2,1,0:T(8,128)(2,1)S(1)}, u32[]{:S(2)}, u32[]{:S(2)}) collective-permute-start(bf16[2,256,128]{2,1,0:T(8,128)(2,1)S(1)} %collective-permute-done.6.refs_2_), channel_id=1, source_target_pairs={{0,32},{32,0},{64,96},{96,64},{128,160},{160,128},{192,224},{224,1... | collective-permute-start | bytes 393224 | tf_op jit(solution)/shard_map/ppermute | solution.py:207
  57.2 2.8 %collective-permute-start.10 = (bf16[2,256,128]{2,1,0:T(8,128)(2,1)S(1)}, bf16[2,256,128]{2,1,0:T(8,128)(2,1)S(1)}, u32[]{:S(2)}, u32[]{:S(2)}) collective-permute-start(bf16[2,256,128]{2,1,0:T(8,128)(2,1)S(1)} %collective-permute-done.7.refs_3_), channel_id=1, source_target_pairs={{0,32},{32,0},{64,96},{96,64},{128,160},{160,128},{192,224},{224,1... | collective-permute-start | bytes 393224 | tf_op jit(solution)/shard_map/ppermute | solution.py:207
  83.6 6.6 %collective-permute-start.12 = (bf16[132,8,128]{2,1,0:T(8,128)(2,1)S(1)}, bf16[132,8,128]{2,1,0:T(8,128)(2,1)S(1)}, u32[]{:S(2)}, u32[]{:S(2)}) collective-permute-start(bf16[132,8,128]{2,1,0:T(8,128)(2,1)S(1)} %shard_map.54.refs_0_), channel_id=1, source_target_pairs={{0,64},{32,224},{64,0},{96,160},{128,192},{160,96},{192,128},{224,... | collective-permute-start | bytes 811016 | tf_op jit(solution)/shard_map/ppermute | solution.py:211
  84.2 11.9 %collective-permute-start.13 = (bf16[132,8,128]{2,1,0:T(8,128)(2,1)S(1)}, bf16[132,8,128]{2,1,0:T(8,128)(2,1)S(1)}, u32[]{:S(2)}, u32[]{:S(2)}) collective-permute-start(bf16[132,8,128]{2,1,0:T(8,128)(2,1)S(1)} %shard_map.54.refs_0_), channel_id=1, source_target_pairs={{0,192},{32,96},{64,128},{96,32},{128,64},{160,224},{192,0},{224,1... | collective-permute-start | bytes 811016 | tf_op jit(solution)/shard_map/ppermute | solution.py:211
  90.2 6.5 %collective-permute-start.14 = (bf16[132,8,128]{2,1,0:T(8,128)(2,1)S(1)}, bf16[132,8,128]{2,1,0:T(8,128)(2,1)S(1)}, u32[]{:S(2)}, u32[]{:S(2)}) collective-permute-start(bf16[132,8,128]{2,1,0:T(8,128)(2,1)S(1)} %collective-permute-done.12.refs_1_), channel_id=1, source_target_pairs={{0,192},{32,96},{64,128},{96,32},{128,64},{160,224},{192,0},{224,1... | collective-permute-start | bytes 811016 | tf_op jit(solution)/shard_map/ppermute | solution.py:211
  90.2 10.6 %collective-permute-start.15 = (bf16[132,8,128]{2,1,0:T(8,128)(2,1)S(1)}, bf16[132,8,128]{2,1,0:T(8,128)(2,1)S(1)}, u32[]{:S(2)}, u32[]{:S(2)}) collective-permute-start(bf16[132,8,128]{2,1,0:T(8,128)(2,1)S(1)} %shard_map.54.refs_0_), channel_id=1, source_target_pairs={{0,32},{32,0},{64,96},{96,64},{128,160},{160,128},{192,224},{224,1... | collective-permute-start | bytes 811016 | tf_op jit(solution)/shard_map/ppermute | solution.py:207
  96.1 4.7 %collective-permute-start.17 = (bf16[132,8,128]{2,1,0:T(8,128)(2,1)S(1)}, bf16[132,8,128]{2,1,0:T(8,128)(2,1)S(1)}, u32[]{:S(2)}, u32[]{:S(2)}) collective-permute-start(bf16[132,8,128]{2,1,0:T(8,128)(2,1)S(1)} %collective-permute-done.12.refs_1_), channel_id=1, source_target_pairs={{0,32},{32,0},{64,96},{96,64},{128,160},{160,128},{192,224},{224,1... | collective-permute-start | bytes 811016 | tf_op jit(solution)/shard_map/ppermute | solution.py:207
  96.1 4.7 %collective-permute-start.16 = (bf16[132,8,128]{2,1,0:T(8,128)(2,1)S(1)}, bf16[132,8,128]{2,1,0:T(8,128)(2,1)S(1)}, u32[]{:S(2)}, u32[]{:S(2)}) collective-permute-start(bf16[132,8,128]{2,1,0:T(8,128)(2,1)S(1)} %collective-permute-done.13.refs_2_), channel_id=1, source_target_pairs={{0,32},{32,0},{64,96},{96,64},{128,160},{160,128},{192,224},{224,1... | collective-permute-start | bytes 811016 | tf_op jit(solution)/shard_map/ppermute | solution.py:207
  96.6 5.3 %collective-permute-start.18 = (bf16[132,8,128]{2,1,0:T(8,128)(2,1)S(1)}, bf16[132,8,128]{2,1,0:T(8,128)(2,1)S(1)}, u32[]{:S(2)}, u32[]{:S(2)}) collective-permute-start(bf16[132,8,128]{2,1,0:T(8,128)(2,1)S(1)} %collective-permute-done.14.refs_3_), channel_id=1, source_target_pairs={{0,32},{32,0},{64,96},{96,64},{128,160},{160,128},{192,224},{224,1... | collective-permute-start | bytes 811016 | tf_op jit(solution)/shard_map/ppermute | solution.py:207

commit v12 on v4

--- a/solution.py
+++ b/solution.py
@@ -16,6 +16,7 @@
 SELF, NEAR, FAR, OPPOSITE = range(4)
 ORDER = (SELF, OPPOSITE, NEAR, FAR)
 TWIN_ORDER = (SELF, OPPOSITE, FAR, NEAR)
+LAST = NEAR
 
 
 def masks(core):
@@ -97,23 +98,39 @@
     return a, b, x - a - b
 
 
+def right_columns(place, right_ref):
+    width = right_ref.shape[2] // 2
+    return pl.ds(pl.multiple_of(lax.rem(place[0], 2) * width, width), width)
+
+
+def strip_lines(place, relative, core, strip):
+    return pl.ds(pl.multiple_of((2 * chip(place, relative) + core) * strip, strip), strip)
+
+
 def right_kernel(place, *refs):
-    own_refs, twin_refs = refs[:4], refs[4:8]
-    right_ref, square_ref, back_ref, half_scratch = refs[8:]
+    *half_refs, right_ref, prec_ref, half_scratch = refs
+    slots, _, strip = half_refs[0].shape
+    core = lax.rem(place[0], 2)
+    known = [(core, k) for k in ORDER] + [(1 - core, k) for k in ORDER if k != LAST]
+    for s in range(slots):
+        half_scratch[s, :, strip_lines(place, LAST, 1 - core, strip)] = jnp.zeros(half_refs[0].shape[1:], bf16)
+        for half_ref, (c, k) in zip(half_refs, known):
+            half_scratch[s, :, strip_lines(place, k, c, strip)] = half_ref[s]
+        prec_ref[s] = jnp.dot(
+            half_scratch[s], right_ref[s, :, right_columns(place, right_ref)], preferred_element_type=f32
+        )
+
+
+def last_strip_kernel(place, half_ref, right_ref, prec_ref, square_ref, back_ref):
     owners, part, wide = back_ref.shape
-    slots = right_ref.shape[0]
+    slots, _, strip = half_ref.shape
     width = (wide - LANES) // slots
-    strip = own_refs[0].shape[2]
-    core = lax.rem(place[0], 2)
     lane = lax.broadcasted_iota(jnp.int32, (part, LANES), 1)
     tail = jnp.zeros((part, LANES), f32)
+    lines = strip_lines(place, LAST, 1 - lax.rem(place[0], 2), strip)
     for s in range(slots):
-        for half_refs, c in ((own_refs, core), (twin_refs, 1 - core)):
-            for k, half_ref in zip(ORDER, half_refs):
-                r = 2 * chip(place, k) + c
-                half_scratch[s, :, pl.ds(pl.multiple_of(r * strip, strip), strip)] = half_ref[s]
-        columns = pl.ds(pl.multiple_of(core * width, width), width)
-        prec = jnp.dot(half_scratch[s], right_ref[s, :, columns], preferred_element_type=f32)
+        root = right_ref[s, lines, right_columns(place, right_ref)]
+        prec = prec_ref[s] + jnp.dot(half_ref[s], root, preferred_element_type=f32)
         back_ref[:, :, s * width : (s + 1) * width] = prec.reshape(owners, part, width).astype(bf16)
         prec_square = jnp.broadcast_to(jnp.sum(prec * prec, keepdims=True), (part, LANES))
         for k, term in enumerate(split3(square_ref[s]) + split3(prec_square)):
@@ -262,13 +279,17 @@
     halves = [half if k == SELF else exchange(half, k) for k, half in zip(ORDER, halves)]
     handed = [twin(halves[ORDER.index(k)]) for k in TWIN_ORDER]
     wide = width + LANES
-    back = local(
+    last = handed.pop(ORDER.index(LAST))
+    prec = local(
         right_kernel,
-        [smem] + [vmem] * 10,
+        [smem] + [vmem] * 8,
         vmem,
-        shape((owners, part, wide), bf16),
+        shape((slots, owners * part, width // 2), f32),
         [pltpu.VMEM((slots, owners * part, width), bf16)],
-    )(place, *halves, *handed, right_root, square)
+    )(place, *halves, *handed, right_root)
+    back = local(last_strip_kernel, [smem] + [vmem] * 4, vmem, shape((owners, part, wide), bf16))(
+        place, last, right_root, prec, square
+    )
     back = lax.all_to_all(back, "fsdp", 0, 0, tiled=True)
 
     tiles = blocks * (width // 2 // LANES) + 2

time: 104 us -> 104 us (level)
  starting transfers between devices: 32.2 us -> 34.1 us
  waiting for transfers between devices: 17.3 us -> 15.7 us
    ppermute x10, starting transfers between devices: 24 us -> 25.2 us  [twin(): return lax.ppermute(x, 'replica', [(i, i ^ 1) for i in range(reps)])]
  transfers between devices with their start and end apart: 19 -> 19, of which waited for: 7 -> 6; matrix products, arithmetic and copies ran while one was open for 0% -> 0% of each run, Pallas kernels for 1% -> 2%
where the time goes in v12:
time: 104 us
  blocking collectives  45 us (43%)
  starting transfers between devices  34.1 us (33%)
  waiting for transfers between devices  15.7 us (15%)
  Pallas kernels  9.09 us (9%)
    ppermute x10, starting transfers between devices, twin(): return lax.ppermute(x, 'replica', [(i, i ^ 1) for i in range(reps)])  25.2 us
    all_to_all x1, blocking collectives, on_device(): incoming = lax.all_to_all(outgoing, 'fsdp', 0, 0, tiled=True)  23.5 us
    all_to_all x1, blocking collectives, on_device(): back = lax.all_to_all(back, 'fsdp', 0, 0, tiled=True)  21.5 us
    ppermute x9, waiting for transfers between devices, exchange(): return lax.ppermute(x, 'replica', perm)  14.3 us
    ppermute x9, starting transfers between devices, exchange(): return lax.ppermute(x, 'replica', perm)  8.9 us
    pallas_call x2, Pallas kernels, on_device(): local(functools.partial(send_kernel, kinds=kinds, **sizes), [smem, pl.Blo...  2.44 us
  transfers between devices with their start and end apart: 19, of which 6 were waited for; matrix products, arithmetic and copies ran while one was open for 0% of the time, Pallas kernels for 2%

profile of v12, /device:TPU:1, one launch (start us, length us, event | category | flops | bytes accessed | tf_op | source)
XLA Modules:
  0.0 104.2 jit_solution(15614674449587103862)
XLA Ops:
  0.0 1.3 %shard_map.48 = bf16[2,4,8,32,128]{4,3,2,1,0:T(8,128)(2,1)S(1)} custom-call(s32[1]{0:T(128)} %bitcast.place, bf16[1,4,32,8192]{3,2,1,0:T(8,128)(2,1)} %grads_ref.7), custom_call_target="tpu_custom_call" | custom-call | tf_op jit(solution)/shard_map/pallas_call | solution.py:248
  1.3 3.3 %collective-permute-start.1 = (bf16[2,4,8,32,128]{4,3,2,1,0:T(8,128)(2,1)S(1)}, bf16[2,4,8,32,128]{4,3,2,1,0:T(8,128)(2,1)S(1)}, u32[]{:S(2)}, u32[]{:S(2)}) collective-permute-start(bf16[2,4,8,32,128]{4,3,2,1,0:T(8,128)(2,1)S(1)} %shard_map.48), channel_id=1, source_target_pairs={{0,32},{32,0},{64,96},{96,64},{128,160},{160,128},{192,224},{224,1... | collective-permute-start | bytes 1572872 | tf_op jit(solution)/shard_map/ppermute | solution.py:225
  4.6 1.1 %shard_map.46 = bf16[2,4,8,32,128]{4,3,2,1,0:T(8,128)(2,1)S(1)} custom-call(s32[1]{0:T(128)} %bitcast.place, bf16[1,4,32,8192]{3,2,1,0:T(8,128)(2,1)} %grads_ref.7), custom_call_target="tpu_custom_call" | custom-call | tf_op jit(solution)/shard_map/pallas_call | solution.py:248
  6.4 1.1 %collective-permute-start.3 = (bf16[4,8,32,128]{3,2,1,0:T(8,128)(2,1)S(1)}, bf16[4,8,32,128]{3,2,1,0:T(8,128)(2,1)S(1)}, u32[]{:S(2)}, u32[]{:S(2)}) collective-permute-start(bf16[4,8,32,128]{3,2,1,0:T(8,128)(2,1)S(1)} %get-tuple-element.17), channel_id=1, source_target_pairs={{0,64},{32,224},{64,0},{96,160},{128,192},{160,96},{192,128},{224,... | collective-permute-start | bytes 786440 | tf_op jit(solution)/shard_map/ppermute | solution.py:229
  7.4 1.7 %collective-permute-start.2 = (bf16[4,8,32,128]{3,2,1,0:T(8,128)(2,1)S(1)}, bf16[4,8,32,128]{3,2,1,0:T(8,128)(2,1)S(1)}, u32[]{:S(2)}, u32[]{:S(2)}) collective-permute-start(bf16[4,8,32,128]{3,2,1,0:T(8,128)(2,1)S(1)} %get-tuple-element.15), channel_id=1, source_target_pairs={{0,64},{32,224},{64,0},{96,160},{128,192},{160,96},{192,128},{224,... | collective-permute-start | bytes 786440 | tf_op jit(solution)/shard_map/ppermute | solution.py:229
  9.3 3.6 %collective-permute-done.3.y_ref = bf16[4,8,32,128]{3,2,1,0:T(8,128)(2,1)S(1)} collective-permute-done((bf16[4,8,32,128]{3,2,1,0:T(8,128)(2,1)S(1)}, bf16[4,8,32,128]{3,2,1,0:T(8,128)(2,1)S(1)}, u32[]{:S(2)}, u32[]{:S(2)}) %collective-permute-start.3) | collective-permute-done | bytes 262176 | tf_op jit(solution)/shard_map/ppermute | solution.py:229
  13.0 2.6 %collective-permute-done.2.refs_1_ = bf16[4,8,32,128]{3,2,1,0:T(8,128)(2,1)S(1)} collective-permute-done((bf16[4,8,32,128]{3,2,1,0:T(8,128)(2,1)S(1)}, bf16[4,8,32,128]{3,2,1,0:T(8,128)(2,1)S(1)}, u32[]{:S(2)}, u32[]{:S(2)}) %collective-permute-start.2) | collective-permute-done | bytes 262176 | tf_op jit(solution)/shard_map/ppermute | solution.py:229
  15.7 2.9 %collective-permute-done.4.refs_2_ = bf16[4,8,32,128]{3,2,1,0:T(8,128)(2,1)S(1)} collective-permute-done((bf16[4,8,32,128]{3,2,1,0:T(8,128)(2,1)S(1)}, bf16[4,8,32,128]{3,2,1,0:T(8,128)(2,1)S(1)}, u32[]{:S(2)}, u32[]{:S(2)}) %collective-permute-start.4) | collective-permute-done | bytes 262176 | tf_op jit(solution)/shard_map/ppermute | solution.py:229
  19.3 23.5 %all_to_all.10.block_ref = bf16[32,2,32,128]{3,2,1,0:T(8,128)(2,1)S(1)} all-to-all(bf16[32,2,32,128]{3,2,1,0:T(8,128)(2,1)S(1)} %shard_map.51), channel_id=1, replica_groups=mesh['replica'=8,'fsdp'=32] {'fsdp'}, dimensions={0} | all-to-all | bytes 1048576 | tf_op jit(solution)/shard_map/all_to_all | solution.py:269
  42.8 1.4 %shard_map.52 = (bf16[2,256,128]{2,1,0:T(8,128)(2,1)S(1)}, bf16[2,256,128]{2,1,0:T(8,128)(2,1)S(1)}, bf16[2,256,128]{2,1,0:T(8,128)(2,1)S(1)}, bf16[2,256,128]{2,1,0:T(8,128)(2,1)S(1)}, f32[2,8,128]{2,1,0:T(8,128)S(1)}) custom-call(s32[1]{0:T(128)} %bitcast.place, bf16[2,1024,1024]{2,1,0:T(8,128)(2,1)S(1)} %copy-done.2, ...), custom_call_target="tpu_custom_call" | custom-call | tf_op jit(solution)/shard_map/pallas_call | solution.py:272
  44.2 3.9 %collective-permute-start.7 = (bf16[2,256,128]{2,1,0:T(8,128)(2,1)S(1)}, bf16[2,256,128]{2,1,0:T(8,128)(2,1)S(1)}, u32[]{:S(2)}, u32[]{:S(2)}) collective-permute-start(bf16[2,256,128]{2,1,0:T(8,128)(2,1)S(1)} %get-tuple-element.20), channel_id=1, source_target_pairs={{0,128},{32,160},{64,192},{96,224},{128,0},{160,32},{192,64},{224,... | collective-permute-start | bytes 393224 | tf_op jit(solution)/shard_map/ppermute | solution.py:229
  48.1 0.8 collective-permute-start.8
  48.9 4.2 %collective-permute-start.9 = (bf16[2,256,128]{2,1,0:T(8,128)(2,1)S(1)}, bf16[2,256,128]{2,1,0:T(8,128)(2,1)S(1)}, u32[]{:S(2)}, u32[]{:S(2)}) collective-permute-start(bf16[2,256,128]{2,1,0:T(8,128)(2,1)S(1)} %get-tuple-element.19.refs_0_), channel_id=1, source_target_pairs={{0,32},{32,0},{64,96},{96,64},{128,160},{160,128},{192,224},{224,1... | collective-permute-start | bytes 393224 | tf_op jit(solution)/shard_map/ppermute | solution.py:225
  53.1 3.4 %collective-permute-start.10 = (bf16[2,256,128]{2,1,0:T(8,128)(2,1)S(1)}, bf16[2,256,128]{2,1,0:T(8,128)(2,1)S(1)}, u32[]{:S(2)}, u32[]{:S(2)}) collective-permute-start(bf16[2,256,128]{2,1,0:T(8,128)(2,1)S(1)} %collective-permute-done.7.refs_1_), channel_id=1, source_target_pairs={{0,32},{32,0},{64,96},{96,64},{128,160},{160,128},{192,224},{224,1... | collective-permute-start | bytes 393224 | tf_op jit(solution)/shard_map/ppermute | solution.py:225
  57.2 1.8 %collective-permute-start.6 = (bf16[2,256,128]{2,1,0:T(8,128)(2,1)S(1)}, bf16[2,256,128]{2,1,0:T(8,128)(2,1)S(1)}, u32[]{:S(2)}, u32[]{:S(2)}) collective-permute-start(bf16[2,256,128]{2,1,0:T(8,128)(2,1)S(1)} %collective-permute-done.5.refs_3_), channel_id=1, source_target_pairs={{0,32},{32,0},{64,96},{96,64},{128,160},{160,128},{192,224},{224,1... | collective-permute-start | bytes 393224 | tf_op jit(solution)/shard_map/ppermute | solution.py:225
  59.0 0.9 shard_map.53.prec_ref
  60.5 21.5 %all_to_all.11.back_ref = bf16[32,8,1152]{2,1,0:T(8,128)(2,1)S(1)} all-to-all(bf16[32,8,1152]{2,1,0:T(8,128)(2,1)S(1)} %shard_map.54), channel_id=1, replica_groups=mesh['replica'=8,'fsdp'=32] {'fsdp'}, dimensions={0} | all-to-all | bytes 1179648 | tf_op jit(solution)/shard_map/all_to_all | solution.py:293
  82.0 1.0 shard_map.55.refs_0_
  83.0 1.4 %collective-permute-start.12 = (bf16[130,8,128]{2,1,0:T(8,128)(2,1)S(1)}, bf16[130,8,128]{2,1,0:T(8,128)(2,1)S(1)}, u32[]{:S(2)}, u32[]{:S(2)}) collective-permute-start(bf16[130,8,128]{2,1,0:T(8,128)(2,1)S(1)} %shard_map.55.refs_0_), channel_id=1, source_target_pairs={{0,64},{32,224},{64,0},{96,160},{128,192},{160,96},{192,128},{224,... | collective-permute-start | bytes 798728 | tf_op jit(solution)/shard_map/ppermute | solution.py:229
  84.3 5.2 %collective-permute-done.12.refs_1_ = bf16[130,8,128]{2,1,0:T(8,128)(2,1)S(1)} collective-permute-done((bf16[130,8,128]{2,1,0:T(8,128)(2,1)S(1)}, bf16[130,8,128]{2,1,0:T(8,128)(2,1)S(1)}, u32[]{:S(2)}, u32[]{:S(2)}) %collective-permute-start.12) | collective-permute-done | bytes 266272 | tf_op jit(solution)/shard_map/ppermute | solution.py:229
  89.5 5.8 %collective-permute-start.15 = (bf16[130,8,128]{2,1,0:T(8,128)(2,1)S(1)}, bf16[130,8,128]{2,1,0:T(8,128)(2,1)S(1)}, u32[]{:S(2)}, u32[]{:S(2)}) collective-permute-start(bf16[130,8,128]{2,1,0:T(8,128)(2,1)S(1)} %shard_map.55.refs_0_), channel_id=1, source_target_pairs={{0,32},{32,0},{64,96},{96,64},{128,160},{160,128},{192,224},{224,1... | collective-permute-start | bytes 798728 | tf_op jit(solution)/shard_map/ppermute | solution.py:225
  95.9 5.4 %collective-permute-start.18 = (bf16[130,8,128]{2,1,0:T(8,128)(2,1)S(1)}, bf16[130,8,128]{2,1,0:T(8,128)(2,1)S(1)}, u32[]{:S(2)}, u32[]{:S(2)}) collective-permute-start(bf16[130,8,128]{2,1,0:T(8,128)(2,1)S(1)} %collective-permute-done.14.refs_3_), channel_id=1, source_target_pairs={{0,32},{32,0},{64,96},{96,64},{128,160},{160,128},{192,224},{224,1... | collective-permute-start | bytes 798728 | tf_op jit(solution)/shard_map/ppermute | solution.py:225
  101.2 1.2 %collective-permute-done.18.refs_7_ = bf16[130,8,128]{2,1,0:T(8,128)(2,1)S(1)} collective-permute-done((bf16[130,8,128]{2,1,0:T(8,128)(2,1)S(1)}, bf16[130,8,128]{2,1,0:T(8,128)(2,1)S(1)}, u32[]{:S(2)}, u32[]{:S(2)}) %collective-permute-start.18) | collective-permute-done | bytes 266272 | tf_op jit(solution)/shard_map/ppermute | solution.py:225
  102.4 1.7 %shard_map.56 = bf16[4,32,8192]{2,1,0:T(8,128)(2,1)} custom-call(s32[1]{0:T(128)} %bitcast.place, bf16[130,8,128]{2,1,0:T(8,128)(2,1)S(1)} %shard_map.55.refs_0_, bf16[130,8,128]{2,1,0:T(8,128)(2,1)S(1)} %collective-permute-done.12.refs_1_, bf16[130,8,128]{2,1,0:T(8,128)(2,1)S(1)} %collective-permute-done.13.refs_2_, ...), custom_call_target="tpu_custom_call" | custom-call | tf_op jit(solution)/shard_map/pallas_call | solution.py:302
  (35 shorter events, 3.4 us)
Async XLA Ops:
  0.0 6.2 %copy-start = (bf16[1,4,32,8192]{3,2,1,0:T(8,128)(2,1)S(1)}, bf16[1,4,32,8192]{3,2,1,0:T(8,128)(2,1)}, u32[]{:S(2)}) copy-start(bf16[1,4,32,8192]{3,2,1,0:T(8,128)(2,1)} %grads_ref.7) | copy-start | bytes 6291460
  1.3 17.2 %copy-start.3 = (s32[32]{0:T(128)S(1)}, s32[32]{0:T(128)}, u32[]{:S(2)}) copy-start(s32[32]{0:T(128)} %slot.3) | copy-start | bytes 388
  1.3 4.9 %collective-permute-start.1 = (bf16[2,4,8,32,128]{4,3,2,1,0:T(8,128)(2,1)S(1)}, bf16[2,4,8,32,128]{4,3,2,1,0:T(8,128)(2,1)S(1)}, u32[]{:S(2)}, u32[]{:S(2)}) collective-permute-start(bf16[2,4,8,32,128]{4,3,2,1,0:T(8,128)(2,1)S(1)} %shard_map.48), channel_id=1, source_target_pairs={{0,32},{32,0},{64,96},{96,64},{128,160},{160,128},{192,224},{224,1... | collective-permute-start | bytes 1572872 | tf_op jit(solution)/shard_map/ppermute | solution.py:225
  5.8 37.0 %copy-start.2 = (bf16[2,1024,1024]{2,1,0:T(8,128)(2,1)S(1)}, bf16[2,1024,1024]{2,1,0:T(8,128)(2,1)}, u32[]{:S(2)}) copy-start(bf16[2,1024,1024]{2,1,0:T(8,128)(2,1)} %left_ref.1) | copy-start | bytes 12582916
  5.8 3.3 %collective-permute-start = (bf16[2,4,8,32,128]{4,3,2,1,0:T(8,128)(2,1)S(1)}, bf16[2,4,8,32,128]{4,3,2,1,0:T(8,128)(2,1)S(1)}, u32[]{:S(2)}, u32[]{:S(2)}) collective-permute-start(bf16[2,4,8,32,128]{4,3,2,1,0:T(8,128)(2,1)S(1)} %shard_map.46), channel_id=1, source_target_pairs={{0,32},{32,0},{64,96},{96,64},{128,160},{160,128},{192,224},{224,1... | collective-permute-start | bytes 1572872 | tf_op jit(solution)/shard_map/ppermute | solution.py:225
  6.4 6.5 %collective-permute-start.3 = (bf16[4,8,32,128]{3,2,1,0:T(8,128)(2,1)S(1)}, bf16[4,8,32,128]{3,2,1,0:T(8,128)(2,1)S(1)}, u32[]{:S(2)}, u32[]{:S(2)}) collective-permute-start(bf16[4,8,32,128]{3,2,1,0:T(8,128)(2,1)S(1)} %get-tuple-element.17), channel_id=1, source_target_pairs={{0,64},{32,224},{64,0},{96,160},{128,192},{160,96},{192,128},{224,... | collective-permute-start | bytes 786440 | tf_op jit(solution)/shard_map/ppermute | solution.py:229
  7.4 8.2 %collective-permute-start.2 = (bf16[4,8,32,128]{3,2,1,0:T(8,128)(2,1)S(1)}, bf16[4,8,32,128]{3,2,1,0:T(8,128)(2,1)S(1)}, u32[]{:S(2)}, u32[]{:S(2)}) collective-permute-start(bf16[4,8,32,128]{3,2,1,0:T(8,128)(2,1)S(1)} %get-tuple-element.15), channel_id=1, source_target_pairs={{0,64},{32,224},{64,0},{96,160},{128,192},{160,96},{192,128},{224,... | collective-permute-start | bytes 786440 | tf_op jit(solution)/shard_map/ppermute | solution.py:229
  9.3 49.7 %copy-start.1 = (bf16[2,1024,1024]{2,1,0:T(8,128)(2,1)S(1)}, bf16[2,1024,1024]{2,1,0:T(8,128)(2,1)}, u32[]{:S(2)}) copy-start(bf16[2,1024,1024]{2,1,0:T(8,128)(2,1)} %right_ref.1) | copy-start | bytes 12582916
  12.9 5.6 %collective-permute-start.4 = (bf16[4,8,32,128]{3,2,1,0:T(8,128)(2,1)S(1)}, bf16[4,8,32,128]{3,2,1,0:T(8,128)(2,1)S(1)}, u32[]{:S(2)}, u32[]{:S(2)}) collective-permute-start(bf16[4,8,32,128]{3,2,1,0:T(8,128)(2,1)S(1)} %shard_map.50), channel_id=1, source_target_pairs={{0,192},{32,96},{64,128},{96,32},{128,64},{160,224},{192,0},{224,1... | collective-permute-start | bytes 786440 | tf_op jit(solution)/shard_map/ppermute | solution.py:229
  44.2 8.8 %collective-permute-start.7 = (bf16[2,256,128]{2,1,0:T(8,128)(2,1)S(1)}, bf16[2,256,128]{2,1,0:T(8,128)(2,1)S(1)}, u32[]{:S(2)}, u32[]{:S(2)}) collective-permute-start(bf16[2,256,128]{2,1,0:T(8,128)(2,1)S(1)} %get-tuple-element.20), channel_id=1, source_target_pairs={{0,128},{32,160},{64,192},{96,224},{128,0},{160,32},{192,64},{224,... | collective-permute-start | bytes 393224 | tf_op jit(solution)/shard_map/ppermute | solution.py:229
  48.1 8.3 %collective-permute-start.8 = (bf16[2,256,128]{2,1,0:T(8,128)(2,1)S(1)}, bf16[2,256,128]{2,1,0:T(8,128)(2,1)S(1)}, u32[]{:S(2)}, u32[]{:S(2)}) collective-permute-start(bf16[2,256,128]{2,1,0:T(8,128)(2,1)S(1)} %get-tuple-element.21), channel_id=1, source_target_pairs={{0,64},{32,224},{64,0},{96,160},{128,192},{160,96},{192,128},{224,... | collective-permute-start | bytes 393224 | tf_op jit(solution)/shard_map/ppermute | solution.py:229
  48.9 8.2 %collective-permute-start.5 = (bf16[2,256,128]{2,1,0:T(8,128)(2,1)S(1)}, bf16[2,256,128]{2,1,0:T(8,128)(2,1)S(1)}, u32[]{:S(2)}, u32[]{:S(2)}) collective-permute-start(bf16[2,256,128]{2,1,0:T(8,128)(2,1)S(1)} %get-tuple-element.18), channel_id=1, source_target_pairs={{0,192},{32,96},{64,128},{96,32},{128,64},{160,224},{192,0},{224,1... | collective-permute-start | bytes 393224 | tf_op jit(solution)/shard_map/ppermute | solution.py:229
  48.9 10.1 %collective-permute-start.9 = (bf16[2,256,128]{2,1,0:T(8,128)(2,1)S(1)}, bf16[2,256,128]{2,1,0:T(8,128)(2,1)S(1)}, u32[]{:S(2)}, u32[]{:S(2)}) collective-permute-start(bf16[2,256,128]{2,1,0:T(8,128)(2,1)S(1)} %get-tuple-element.19.refs_0_), channel_id=1, source_target_pairs={{0,32},{32,0},{64,96},{96,64},{128,160},{160,128},{192,224},{224,1... | collective-permute-start | bytes 393224 | tf_op jit(solution)/shard_map/ppermute | solution.py:225
  53.1 5.9 %collective-permute-start.10 = (bf16[2,256,128]{2,1,0:T(8,128)(2,1)S(1)}, bf16[2,256,128]{2,1,0:T(8,128)(2,1)S(1)}, u32[]{:S(2)}, u32[]{:S(2)}) collective-permute-start(bf16[2,256,128]{2,1,0:T(8,128)(2,1)S(1)} %collective-permute-done.7.refs_1_), channel_id=1, source_target_pairs={{0,32},{32,0},{64,96},{96,64},{128,160},{160,128},{192,224},{224,1... | collective-permute-start | bytes 393224 | tf_op jit(solution)/shard_map/ppermute | solution.py:225
  56.5 2.5 %collective-permute-start.11 = (bf16[2,256,128]{2,1,0:T(8,128)(2,1)S(1)}, bf16[2,256,128]{2,1,0:T(8,128)(2,1)S(1)}, u32[]{:S(2)}, u32[]{:S(2)}) collective-permute-start(bf16[2,256,128]{2,1,0:T(8,128)(2,1)S(1)} %collective-permute-done.8.refs_2_), channel_id=1, source_target_pairs={{0,32},{32,0},{64,96},{96,64},{128,160},{160,128},{192,224},{224,1... | collective-permute-start | bytes 393224 | tf_op jit(solution)/shard_map/ppermute | solution.py:225
  57.2 2.8 %collective-permute-start.6 = (bf16[2,256,128]{2,1,0:T(8,128)(2,1)S(1)}, bf16[2,256,128]{2,1,0:T(8,128)(2,1)S(1)}, u32[]{:S(2)}, u32[]{:S(2)}) collective-permute-start(bf16[2,256,128]{2,1,0:T(8,128)(2,1)S(1)} %collective-permute-done.5.refs_3_), channel_id=1, source_target_pairs={{0,32},{32,0},{64,96},{96,64},{128,160},{160,128},{192,224},{224,1... | collective-permute-start | bytes 393224 | tf_op jit(solution)/shard_map/ppermute | solution.py:225
  83.0 6.5 %collective-permute-start.12 = (bf16[130,8,128]{2,1,0:T(8,128)(2,1)S(1)}, bf16[130,8,128]{2,1,0:T(8,128)(2,1)S(1)}, u32[]{:S(2)}, u32[]{:S(2)}) collective-permute-start(bf16[130,8,128]{2,1,0:T(8,128)(2,1)S(1)} %shard_map.55.refs_0_), channel_id=1, source_target_pairs={{0,64},{32,224},{64,0},{96,160},{128,192},{160,96},{192,128},{224,... | collective-permute-start | bytes 798728 | tf_op jit(solution)/shard_map/ppermute | solution.py:229
  84.3 11.0 %collective-permute-start.13 = (bf16[130,8,128]{2,1,0:T(8,128)(2,1)S(1)}, bf16[130,8,128]{2,1,0:T(8,128)(2,1)S(1)}, u32[]{:S(2)}, u32[]{:S(2)}) collective-permute-start(bf16[130,8,128]{2,1,0:T(8,128)(2,1)S(1)} %shard_map.55.refs_0_), channel_id=1, source_target_pairs={{0,192},{32,96},{64,128},{96,32},{128,64},{160,224},{192,0},{224,1... | collective-permute-start | bytes 798728 | tf_op jit(solution)/shard_map/ppermute | solution.py:229
  89.5 6.4 %collective-permute-start.14 = (bf16[130,8,128]{2,1,0:T(8,128)(2,1)S(1)}, bf16[130,8,128]{2,1,0:T(8,128)(2,1)S(1)}, u32[]{:S(2)}, u32[]{:S(2)}) collective-permute-start(bf16[130,8,128]{2,1,0:T(8,128)(2,1)S(1)} %collective-permute-done.12.refs_1_), channel_id=1, source_target_pairs={{0,192},{32,96},{64,128},{96,32},{128,64},{160,224},{192,0},{224,1... | collective-permute-start | bytes 798728 | tf_op jit(solution)/shard_map/ppermute | solution.py:229
  89.5 11.7 %collective-permute-start.15 = (bf16[130,8,128]{2,1,0:T(8,128)(2,1)S(1)}, bf16[130,8,128]{2,1,0:T(8,128)(2,1)S(1)}, u32[]{:S(2)}, u32[]{:S(2)}) collective-permute-start(bf16[130,8,128]{2,1,0:T(8,128)(2,1)S(1)} %shard_map.55.refs_0_), channel_id=1, source_target_pairs={{0,32},{32,0},{64,96},{96,64},{128,160},{160,128},{192,224},{224,1... | collective-permute-start | bytes 798728 | tf_op jit(solution)/shard_map/ppermute | solution.py:225
  95.3 5.9 %collective-permute-start.17 = (bf16[130,8,128]{2,1,0:T(8,128)(2,1)S(1)}, bf16[130,8,128]{2,1,0:T(8,128)(2,1)S(1)}, u32[]{:S(2)}, u32[]{:S(2)}) collective-permute-start(bf16[130,8,128]{2,1,0:T(8,128)(2,1)S(1)} %collective-permute-done.12.refs_1_), channel_id=1, source_target_pairs={{0,32},{32,0},{64,96},{96,64},{128,160},{160,128},{192,224},{224,1... | collective-permute-start | bytes 798728 | tf_op jit(solution)/shard_map/ppermute | solution.py:225
  95.3 5.9 %collective-permute-start.16 = (bf16[130,8,128]{2,1,0:T(8,128)(2,1)S(1)}, bf16[130,8,128]{2,1,0:T(8,128)(2,1)S(1)}, u32[]{:S(2)}, u32[]{:S(2)}) collective-permute-start(bf16[130,8,128]{2,1,0:T(8,128)(2,1)S(1)} %collective-permute-done.13.refs_2_), channel_id=1, source_target_pairs={{0,32},{32,0},{64,96},{96,64},{128,160},{160,128},{192,224},{224,1... | collective-permute-start | bytes 798728 | tf_op jit(solution)/shard_map/ppermute | solution.py:225
  95.9 6.5 %collective-permute-start.18 = (bf16[130,8,128]{2,1,0:T(8,128)(2,1)S(1)}, bf16[130,8,128]{2,1,0:T(8,128)(2,1)S(1)}, u32[]{:S(2)}, u32[]{:S(2)}) collective-permute-start(bf16[130,8,128]{2,1,0:T(8,128)(2,1)S(1)} %collective-permute-done.14.refs_3_), channel_id=1, source_target_pairs={{0,32},{32,0},{64,96},{96,64},{128,160},{160,128},{192,224},{224,1... | collective-permute-start | bytes 798728 | tf_op jit(solution)/shard_map/ppermute | solution.py:225
